TPU v7x, 256 devices: a whole 4x4x8 slice. The times are simulated.
256 devices in a mesh: depth: 16 (over z_hi, x, core), rows: 16 (over y, z_lo).
Axes of the slice: x: 4, y: 4, z: 8 (z_hi: 2, z_lo: 4; z = z_hi * 4 + z_lo), core: 2. Of those that a mesh axis runs over, the one named last changes fastest.
Arguments:
- volume: bfloat16 [32, 64, 128, 128], P('depth', 'rows'), may hold values from -6 to 6
- fine_filters: bfloat16 [3, 3, 3, 128, 128], replicated, may hold values from -0.109375 to 0.109375
- fine_bias: float32 [128], replicated, may hold values from -0.5 to 0.5
- coarse_filters: bfloat16 [3, 3, 3, 128, 256], P(None, None, None, None, 'rows'), may hold values from -0.109375 to 0.109375
- coarse_bias: float32 [256], P('rows'), may hold values from -0.5 to 0.5
Outputs:
- encoded: bfloat16 [256, 16, 2048], P('rows', 'depth')
All inputs are finite; a program needn't handle non-finite values.
Results may differ from a plain program's by a relative error of at most 0.0049.
Values may be sent and summed in bfloat16 or wider, within the bound.
No kernel may reach another device: no remote copies, remote signals or barrier semaphores. Data moves between devices by JAX's collectives and lax.ppermute only.
A program may use at most 64 MiB of HBM per device.

v0:
```python
import jax
import jax.numpy as jnp
from jax import lax
from jax.sharding import PartitionSpec as P


def padded_2(cells, sides, width):
    for axis, dim in sides:
        count = lax.axis_size(axis)
        ends = count - 1
        head = lax.slice_in_dim(cells, 0, width, axis=dim)
        tail = lax.slice_in_dim(cells, cells.shape[dim] - width, cells.shape[dim], axis=dim)
        cells = jnp.concatenate(
            [
                lax.ppermute(tail, axis, [(i, (i + 1) % count) for i in range(ends)]),
                cells,
                lax.ppermute(head, axis, [((i + 1) % count, i) for i in range(ends)]),
            ],
            axis=dim,
        )
    return cells


def widen(padded):
    shifted = jnp.pad(padded, ((0, 0), (0, 0), (1, 1), (0, 0)))
    return jnp.concatenate([shifted[:, :, :-2], shifted[:, :, 1:-1], shifted[:, :, 2:]], axis=-1)


def conv_cells(padded, kernel):
    widened = widen(padded)
    planes = padded.shape[0] - 2
    lines = padded.shape[1] - 2
    kernel = kernel.reshape(3, 3, 3 * kernel.shape[3], kernel.shape[4])
    summed = None
    for kd in range(3):
        for kh in range(3):
            window = widened[kd : kd + planes, kh : kh + lines].reshape(-1, widened.shape[3])
            term = jnp.einsum(
                "vk,ko->ov", window, kernel[kd, kh], preferred_element_type=jnp.float32
            )
            summed = term if summed is None else summed + term
    return summed


def body(volume, fine_filters, fine_bias, coarse_filters, coarse_bias):
    planes, lines, columns, chans = volume.shape
    padded = padded_2(volume, (("depth", 0), ("rows", 1)), 1)
    fine_sum = conv_cells(padded, fine_filters)
    active = jnp.maximum(fine_sum + fine_bias[:, None], 0.0).astype(jnp.bfloat16)
    active = jnp.transpose(active).reshape(planes // 2, 2, lines // 2, 2, columns // 2, 2, chans)
    pooled = active.max(axis=(1, 3, 5))
    gathered = lax.all_gather(pooled, "rows", axis=1, tiled=True)
    deeper = padded_2(gathered, (("depth", 0),), 1)
    deeper = jnp.pad(deeper, ((0, 0), (1, 1), (0, 0), (0, 0)))
    coarse_sum = conv_cells(deeper, coarse_filters)
    result = jnp.maximum(coarse_sum + coarse_bias[:, None], 0.0).astype(jnp.bfloat16)
    return result.reshape(coarse_filters.shape[4], planes // 2, gathered.shape[1] * (columns // 2))


def solution(mesh):
    placed = (
        P("depth", "rows", None, None),
        P(),
        P(),
        P(None, None, None, None, "rows"),
        P("rows"),
    )
    return jax.shard_map(
        body, mesh=mesh, in_specs=placed, out_specs=P("rows", "depth", None), check_vma=False
    )
```

profile of v0, /device:TPU:39, one launch (start us, length us, event | category | flops | bytes accessed | tf_op | source)
XLA Modules:
  0.0 116.6 jit_solution(14518402746034474325)
XLA Ops:
  0.0 1.0 fusion.39
  1.0 8.4 %collective-permute-start = (bf16[1,4,128,128]{3,2,1,0:T(8,128)(2,1)S(1)}, bf16[1,4,128,128]{3,2,1,0:T(8,128)(2,1)S(1)}, u32[]{:S(2)}, u32[]{:S(2)}) collective-permute-start(bf16[1,4,128,128]{3,2,1,0:T(8,128)(2,1)S(1)} %get-tuple-element.30), channel_id=1, source_target_pairs={{0,16},{16,32},{32,48},{48,64},{64,80},{80,96},{96,112},{112,128},... | collective-permute-start | bytes 393224 | tf_op jit(solution)/shard_map/ppermute | solution.py:15
  9.4 1.9 %collective-permute-start.1 = (bf16[1,4,128,128]{3,2,1,0:T(8,128)(2,1)S(1)}, bf16[1,4,128,128]{3,2,1,0:T(8,128)(2,1)S(1)}, u32[]{:S(2)}, u32[]{:S(2)}) collective-permute-start(bf16[1,4,128,128]{3,2,1,0:T(8,128)(2,1)S(1)} %get-tuple-element.29), channel_id=1, source_target_pairs={{16,0},{32,16},{48,32},{64,48},{80,64},{96,80},{112,96},{128,112},... | collective-permute-start | bytes 393224 | tf_op jit(solution)/shard_map/ppermute | solution.py:17
  11.4 1.4 %collective-permute-done = bf16[1,4,128,128]{3,2,1,0:T(8,128)(2,1)S(1)} collective-permute-done((bf16[1,4,128,128]{3,2,1,0:T(8,128)(2,1)S(1)}, bf16[1,4,128,128]{3,2,1,0:T(8,128)(2,1)S(1)}, u32[]{:S(2)}, u32[]{:S(2)}) %collective-permute-start) | collective-permute-done | bytes 131104 | tf_op jit(solution)/shard_map/ppermute | solution.py:15
  12.7 1.0 constant_dynamic-update-slice_fusion.1
  13.7 9.4 %collective-permute-done.1 = bf16[1,4,128,128]{3,2,1,0:T(8,128)(2,1)S(1)} collective-permute-done((bf16[1,4,128,128]{3,2,1,0:T(8,128)(2,1)S(1)}, bf16[1,4,128,128]{3,2,1,0:T(8,128)(2,1)S(1)}, u32[]{:S(2)}, u32[]{:S(2)}) %collective-permute-start.1) | collective-permute-done | bytes 131104 | tf_op jit(solution)/shard_map/ppermute | solution.py:17
  23.2 3.6 %collective-permute-start.2 = (bf16[4,1,128,128]{3,2,1,0:T(8,128)(2,1)S(1)}, bf16[4,1,128,128]{3,2,1,0:T(8,128)(2,1)S(1)}, u32[]{:S(2)}, u32[]{:S(2)}) collective-permute-start(bf16[4,1,128,128]{3,2,1,0:T(8,128)(2,1)S(1)} %get-tuple-element.27), channel_id=1, source_target_pairs={{0,1},{1,2},{2,3},{3,4},{4,5},{5,6},{6,7},{7,8},{8,9},{9,10},{10,1... | collective-permute-start | bytes 393224 | tf_op jit(solution)/shard_map/ppermute | solution.py:15
  26.8 1.9 %collective-permute-start.3 = (bf16[4,1,128,128]{3,2,1,0:T(8,128)(2,1)S(1)}, bf16[4,1,128,128]{3,2,1,0:T(8,128)(2,1)S(1)}, u32[]{:S(2)}, u32[]{:S(2)}) collective-permute-start(bf16[4,1,128,128]{3,2,1,0:T(8,128)(2,1)S(1)} %get-tuple-element.28), channel_id=1, source_target_pairs={{1,0},{2,1},{3,2},{4,3},{5,4},{6,5},{7,6},{8,7},{9,8},{10,9},{11,1... | collective-permute-start | bytes 393224 | tf_op jit(solution)/shard_map/ppermute | solution.py:17
  28.9 3.6 %collective-permute-done.3 = bf16[4,1,128,128]{3,2,1,0:T(8,128)(2,1)S(1)} collective-permute-done((bf16[4,1,128,128]{3,2,1,0:T(8,128)(2,1)S(1)}, bf16[4,1,128,128]{3,2,1,0:T(8,128)(2,1)S(1)}, u32[]{:S(2)}, u32[]{:S(2)}) %collective-permute-start.3) | collective-permute-done | bytes 131104 | tf_op jit(solution)/shard_map/ppermute | solution.py:17
  33.7 1.1 fusion.36
  38.6 35.4 %all-gather = bf16[32,64,128]{2,1,0:T(8,128)(2,1)S(1)} all-gather(bf16[2,64,128]{2,1,0:T(8,128)(2,1)S(1)} %reduce_max.11), channel_id=2, replica_groups=mesh['depth'=16,'rows'=16] {'rows'}, dimensions={0}, use_global_device_ids=true | all-gather | bytes 557056 | tf_op jit(solution)/shard_map/all_gather | solution.py:52
  74.0 10.0 %collective-permute-start.4 = (bf16[1,32,64,128]{3,2,1,0:T(8,128)(2,1)S(1)}, bf16[1,32,64,128]{3,2,1,0:T(8,128)(2,1)S(1)}, u32[]{:S(2)}, u32[]{:S(2)}) collective-permute-start(bf16[1,32,64,128]{3,2,1,0:T(8,128)(2,1)S(1)} %bitcast.120), channel_id=1, source_target_pairs={{0,16},{16,32},{32,48},{48,64},{64,80},{80,96},{96,112},{112,128},... | collective-permute-start | bytes 1572872 | tf_op jit(solution)/shard_map/ppermute | solution.py:15
  84.1 1.9 %collective-permute-start.5 = (bf16[1,32,64,128]{3,2,1,0:T(8,128)(2,1)S(1)}, bf16[1,32,64,128]{3,2,1,0:T(8,128)(2,1)S(1)}, u32[]{:S(2)}, u32[]{:S(2)}) collective-permute-start(bf16[1,32,64,128]{3,2,1,0:T(8,128)(2,1)S(1)} %bitcast.121), channel_id=1, source_target_pairs={{16,0},{32,16},{48,32},{64,48},{80,64},{96,80},{112,96},{128,112},... | collective-permute-start | bytes 1572872 | tf_op jit(solution)/shard_map/ppermute | solution.py:17
  86.1 9.1 %collective-permute-done.4 = bf16[1,32,64,128]{3,2,1,0:T(8,128)(2,1)S(1)} collective-permute-done((bf16[1,32,64,128]{3,2,1,0:T(8,128)(2,1)S(1)}, bf16[1,32,64,128]{3,2,1,0:T(8,128)(2,1)S(1)}, u32[]{:S(2)}, u32[]{:S(2)}) %collective-permute-start.4) | collective-permute-done | bytes 524320 | tf_op jit(solution)/shard_map/ppermute | solution.py:15
  95.2 10.4 %collective-permute-done.5 = bf16[1,32,64,128]{3,2,1,0:T(8,128)(2,1)S(1)} collective-permute-done((bf16[1,32,64,128]{3,2,1,0:T(8,128)(2,1)S(1)}, bf16[1,32,64,128]{3,2,1,0:T(8,128)(2,1)S(1)}, u32[]{:S(2)}, u32[]{:S(2)}) %collective-permute-start.5) | collective-permute-done | bytes 524320 | tf_op jit(solution)/shard_map/ppermute | solution.py:17
  105.8 2.4 %pad_slice_fusion.1 = (bf16[3,34,64,128]{3,2,1,0:T(8,128)(2,1)S(1)}, bf16[3,34,64,128]{3,2,1,0:T(8,128)(2,1)S(1)}) fusion(bf16[3,34,64,128]{3,2,1,0:T(8,128)(2,1)S(1)} %fusion.9), kind=kLoop, calls=%fused_computation.23 | loop fusion | bytes 5013504 | tf_op jit(solution)/shard_map/slice | solution.py:26
  108.2 0.8 pad_maximum_fusion
  109.0 2.2 %fusion.35 = (bf16[1,32,64,384]{3,2,1,0:T(8,128)(2,1)S(1)}, bf16[1,32,64,384]{3,2,1,0:T(8,128)(2,1)S(1)}, bf16[1,32,64,384]{3,2,1,0:T(8,128)(2,1)S(1)}, bf16[1,3...) fusion(bf16[3,34,64,384]{3,2,1,0:T(8,128)(2,1)S(1)} %pad_maximu, ...), kind=kLoop, calls=%fused_computation.74 | loop fusion | bytes 28311552 | tf_op jit(solution)/shard_map/slice | solution.py:37
  111.7 0.5 convolution_add_fusion.7
  112.3 0.5 convolution_add_fusion.6
  112.8 0.5 convolution_add_fusion.5
  113.3 0.5 convolution_add_fusion.4
  113.8 0.5 convolution_add_fusion.3
  115.4 1.2 %fusion.4 = bf16[16,1,2048]{2,0,1:T(8,128)(2,1)} fusion(f32[2048,16]{0,1:T(8,128)S(1)} %convolution_add_fusion.1, bf16[2048,384]{1,0:T(8,128)(2,1)S(1)} %bitcast.102, f32[16]{0:T(128)S(1)} %copy-done.3, bf16[3,3,384,16]{2,3,1,0:T(8,128)(2,1)S(1)} %copy_bitcast_fusion), kind=kOutput, calls=%fused_computation.18 | convolution fusion | flops 25296896 | bytes 1782272 | tf_op jit(solution)/shard_map/vk,ko->ov/dot_general | solution.py:38
  (30 shorter events, 6.8 us)
Async XLA Ops:
  0.0 86.0 %copy-start = (bf16[3,3,3,128,16]{3,4,2,1,0:T(8,128)(2,1)S(1)}, bf16[3,3,3,128,16]{3,4,2,1,0:T(8,128)(2,1)}, u32[]{:S(2)}) copy-start(bf16[3,3,3,128,16]{3,4,2,1,0:T(8,128)(2,1)} %param.8) | copy-start | bytes 331780
  1.0 11.7 %collective-permute-start = (bf16[1,4,128,128]{3,2,1,0:T(8,128)(2,1)S(1)}, bf16[1,4,128,128]{3,2,1,0:T(8,128)(2,1)S(1)}, u32[]{:S(2)}, u32[]{:S(2)}) collective-permute-start(bf16[1,4,128,128]{3,2,1,0:T(8,128)(2,1)S(1)} %get-tuple-element.30), channel_id=1, source_target_pairs={{0,16},{16,32},{32,48},{48,64},{64,80},{80,96},{96,112},{112,128},... | collective-permute-start | bytes 393224 | tf_op jit(solution)/shard_map/ppermute | solution.py:15
  9.4 13.7 %collective-permute-start.1 = (bf16[1,4,128,128]{3,2,1,0:T(8,128)(2,1)S(1)}, bf16[1,4,128,128]{3,2,1,0:T(8,128)(2,1)S(1)}, u32[]{:S(2)}, u32[]{:S(2)}) collective-permute-start(bf16[1,4,128,128]{3,2,1,0:T(8,128)(2,1)S(1)} %get-tuple-element.29), channel_id=1, source_target_pairs={{16,0},{32,16},{48,32},{64,48},{80,64},{96,80},{112,96},{128,112},... | collective-permute-start | bytes 393224 | tf_op jit(solution)/shard_map/ppermute | solution.py:17
  23.2 5.7 %collective-permute-start.2 = (bf16[4,1,128,128]{3,2,1,0:T(8,128)(2,1)S(1)}, bf16[4,1,128,128]{3,2,1,0:T(8,128)(2,1)S(1)}, u32[]{:S(2)}, u32[]{:S(2)}) collective-permute-start(bf16[4,1,128,128]{3,2,1,0:T(8,128)(2,1)S(1)} %get-tuple-element.27), channel_id=1, source_target_pairs={{0,1},{1,2},{2,3},{3,4},{4,5},{5,6},{6,7},{7,8},{8,9},{9,10},{10,1... | collective-permute-start | bytes 393224 | tf_op jit(solution)/shard_map/ppermute | solution.py:15
  26.8 5.7 %collective-permute-start.3 = (bf16[4,1,128,128]{3,2,1,0:T(8,128)(2,1)S(1)}, bf16[4,1,128,128]{3,2,1,0:T(8,128)(2,1)S(1)}, u32[]{:S(2)}, u32[]{:S(2)}) collective-permute-start(bf16[4,1,128,128]{3,2,1,0:T(8,128)(2,1)S(1)} %get-tuple-element.28), channel_id=1, source_target_pairs={{1,0},{2,1},{3,2},{4,3},{5,4},{6,5},{7,6},{8,7},{9,8},{10,9},{11,1... | collective-permute-start | bytes 393224 | tf_op jit(solution)/shard_map/ppermute | solution.py:17
  33.6 1.2 %copy-start.1 = (bf16[3,3,3,128,128]{4,3,2,1,0:T(8,128)(2,1)S(1)}, bf16[3,3,3,128,128]{4,3,2,1,0:T(8,128)(2,1)}, u32[]{:S(2)}) copy-start(bf16[3,3,3,128,128]{4,3,2,1,0:T(8,128)(2,1)} %param.6) | copy-start | bytes 2654212
  37.0 0.8 copy-start.2
  74.0 21.1 %collective-permute-start.4 = (bf16[1,32,64,128]{3,2,1,0:T(8,128)(2,1)S(1)}, bf16[1,32,64,128]{3,2,1,0:T(8,128)(2,1)S(1)}, u32[]{:S(2)}, u32[]{:S(2)}) collective-permute-start(bf16[1,32,64,128]{3,2,1,0:T(8,128)(2,1)S(1)} %bitcast.120), channel_id=1, source_target_pairs={{0,16},{16,32},{32,48},{48,64},{64,80},{80,96},{96,112},{112,128},... | collective-permute-start | bytes 1572872 | tf_op jit(solution)/shard_map/ppermute | solution.py:15
  84.1 21.5 %collective-permute-start.5 = (bf16[1,32,64,128]{3,2,1,0:T(8,128)(2,1)S(1)}, bf16[1,32,64,128]{3,2,1,0:T(8,128)(2,1)S(1)}, u32[]{:S(2)}, u32[]{:S(2)}) collective-permute-start(bf16[1,32,64,128]{3,2,1,0:T(8,128)(2,1)S(1)} %bitcast.121), channel_id=1, source_target_pairs={{16,0},{32,16},{48,32},{64,48},{80,64},{96,80},{112,96},{128,112},... | collective-permute-start | bytes 1572872 | tf_op jit(solution)/shard_map/ppermute | solution.py:17
  114.4 1.1 copy-start.3
where the time goes:
time: 117 us
  blocking collectives  35.4 us (30%)
  waiting for transfers between devices  34.1 us (29%)
  starting transfers between devices  27.8 us (24%)
  matrix products  8.69 us (7%)
  local copies, waits for them, and re-layouts  8.34 us (7%)
  other arithmetic  2.01 us (2%)
    all_gather x1, blocking collectives, body(): gathered = lax.all_gather(pooled, 'rows', axis=1, tiled=True)  35.4 us
    ppermute x3, waiting for transfers between devices, padded_2(): lax.ppermute(head, axis, [((i + 1) % count, i) for i in range(ends)])  23.4 us
    ppermute x3, starting transfers between devices, padded_2(): lax.ppermute(tail, axis, [(i, (i + 1) % count) for i in range(ends)])  22 us
    ppermute x3, waiting for transfers between devices, padded_2(): lax.ppermute(tail, axis, [(i, (i + 1) % count) for i in range(ends)])  10.7 us
    dot_general x18, matrix products, conv_cells(): jnp.einsum('vk,ko->ov', window, kernel[kd, kh], preferred_element_type=jn...  8.69 us
    ppermute x3, starting transfers between devices, padded_2(): lax.ppermute(head, axis, [((i + 1) % count, i) for i in range(ends)])  5.76 us
    slice x2, local copies, waits for them, and re-layouts, conv_cells(): widened[kd:kd + planes, kh:kh + lines].reshape(-1, widened.shape[3])  3.34 us
    slice x2, local copies, waits for them, and re-layouts, widen(): shifted[:, :, :-2]  2.92 us
  transfers between devices with their start and end apart: 6, of which 6 were waited for; matrix products, arithmetic and copies ran while one was open for 1% of the time, Pallas kernels for 0%

commit v1 on v0

v1 whole, which is shorter than its diff:
```python
import jax
import jax.numpy as jnp
from jax import lax
from jax.experimental import pallas as pl
from jax.experimental.pallas import tpu as pltpu
from jax.sharding import PartitionSpec as P

BF16 = jnp.bfloat16
F32 = jnp.float32


def near_pairs(count):
    return [(i, i ^ 1) for i in range(count)]


def far_pairs(count):
    return [(i, ((i - 1) ^ 1) + 1) for i in range(1, count - 1)]


def fine_kernel(odd, vol, x1, x2, r1, r2, c1, c2, w, bias, out, cells, peak):
    pd = odd[0]
    pr = odd[1]
    for j in range(4):
        for i in range(6):
            row = (i - 1) + pr * (5 - 2 * i)
            if j in (1, 2):
                plane = (j - 1) + pd * (3 - 2 * j)
                piece = r2[plane] if i == 0 else r1[plane] if i == 5 else vol[plane, row]
            else:
                side, slot = (x2, 1) if j == 0 else (x1, 0)
                piece = c2[slot] if i == 0 else c1[slot] if i == 5 else side[row]
            cells[j, i] = piece
    taps = [(a, b) for a in range(3) for b in range(3)]
    groups = [taps[i : i + 2] for i in range(0, 9, 2)]
    parts = []
    for s in range(2):
        total = None
        for group in groups:
            lhs = jnp.concatenate(
                [cells[s + a, b : b + 4].reshape(512, 128) for a, b in group], axis=1
            )
            rhs = jnp.concatenate(
                [
                    jnp.concatenate(
                        [w[a + pd * (2 - 2 * a), b + pr * (2 - 2 * b), c] for c in range(3)], axis=1
                    )
                    for a, b in group
                ],
                axis=0,
            )
            term = jnp.dot(lhs, rhs, preferred_element_type=F32)
            total = term if total is None else total + term
        parts.append(total)
    col = lax.broadcasted_iota(jnp.int32, (128, 128), 0)
    for q in range(2):
        best = None
        for s in range(2):
            for t in range(2):
                line = parts[s][(2 * q + t) * 128 : (2 * q + t + 1) * 128]
                left = jnp.where(col == 0, 0.0, pltpu.roll(line[:, :128], 1, 0))
                right = jnp.where(col == 127, 0.0, pltpu.roll(line[:, 256:], 127, 0))
                value = line[:, 128:256] + left + right
                best = value if best is None else jnp.maximum(best, value)
        peak[...] = best
        pooled = jnp.maximum(peak[pl.ds(0, 64, stride=2), :], peak[pl.ds(1, 64, stride=2), :])
        out[q + pr * (1 - 2 * q)] = jnp.maximum(pooled + bias[...], 0.0).astype(BF16)


def fine_level(odd, vol, x1, x2, r1, r2, c1, c2, w, bias):
    vmem = pl.BlockSpec(memory_space=pltpu.VMEM)
    return pl.pallas_call(
        fine_kernel,
        out_shape=jax.ShapeDtypeStruct((2, 64, 128), BF16),
        in_specs=[pl.BlockSpec(memory_space=pltpu.SMEM)] + [vmem] * 9,
        out_specs=vmem,
        scratch_shapes=[pltpu.VMEM((4, 6, 128, 128), BF16), pltpu.VMEM((128, 128), F32)],
        compiler_params=pltpu.CompilerParams(vmem_limit_bytes=32 * 1024 * 1024),
    )(odd, vol, x1, x2, r1, r2, c1, c2, w, bias)


def coarse_kernel(place, g0, g1, g2, g3, w, out, cells):
    y = place[0]
    z = place[1]
    cells[0] = jnp.zeros((64, 128), BF16)
    cells[33] = jnp.zeros((64, 128), BF16)
    for m, block in enumerate((g0, g1, g2, g3)):
        for k in range(4):
            row = lax.rem(y - m + 4, 4) * 8 + lax.rem(z - k + 4, 4) * 2
            cells[pl.ds(row + 1, 2)] = block[k]
    lines = 8
    size = lines * 64
    lane = lax.rem(lax.broadcasted_iota(jnp.int32, (48, size), 1), 64)
    for t in range(32 // lines):
        rhs = jnp.concatenate(
            [cells[t * lines + b : t * lines + b + lines].reshape(size, 128) for b in range(3)], axis=1
        )
        term = lax.dot_general(w[...], rhs, (((1,), (1,)), ((), ())), preferred_element_type=F32)
        left = jnp.where(lane == 0, 0.0, pltpu.roll(term[:48], 1, 1))
        right = jnp.where(lane == 63, 0.0, pltpu.roll(term[96:], size - 1, 1))
        value = term[48:96] + left + right
        for n in range(3):
            out[n, :, t * size : (t + 1) * size] = value[16 * n : 16 * n + 16]


def coarse_level(place, g0, g1, g2, g3, w):
    vmem = pl.BlockSpec(memory_space=pltpu.VMEM)
    return pl.pallas_call(
        coarse_kernel,
        out_shape=jax.ShapeDtypeStruct((3, 16, 2048), F32),
        in_specs=[pl.BlockSpec(memory_space=pltpu.SMEM)] + [vmem] * 5,
        out_specs=vmem,
        scratch_shapes=[pltpu.VMEM((34, 64, 128), BF16)],
        compiler_params=pltpu.CompilerParams(vmem_limit_bytes=32 * 1024 * 1024),
    )(place, g0, g1, g2, g3, w)


def body(volume, fine_filters, fine_bias, coarse_filters, coarse_bias):
    d = lax.axis_index("depth")
    r = lax.axis_index("rows")
    pd = lax.rem(d, 2)
    pr = lax.rem(r, 2)
    depth_near, depth_far = near_pairs(16), far_pairs(16)
    rows_near, rows_far = near_pairs(16), far_pairs(16)

    x2 = lax.ppermute(lax.dynamic_index_in_dim(volume, pd, 0, False), "depth", depth_far)
    x1 = lax.ppermute(lax.dynamic_index_in_dim(volume, 1 - pd, 0, False), "depth", depth_near)
    r2 = lax.ppermute(lax.dynamic_index_in_dim(volume, 3 * pr, 1, False), "rows", rows_far)
    r1 = lax.ppermute(lax.dynamic_index_in_dim(volume, 3 - 3 * pr, 1, False), "rows", rows_near)
    sides = jnp.stack([x1, x2])
    c2 = lax.ppermute(lax.dynamic_index_in_dim(sides, 3 * pr, 1, False), "rows", rows_far)
    c1 = lax.ppermute(lax.dynamic_index_in_dim(sides, 3 - 3 * pr, 1, False), "rows", rows_near)
    odd = jnp.stack([pd, pr]).astype(jnp.int32)
    pooled = fine_level(odd, volume, x1, x2, r1, r2, c1, c2, fine_filters, fine_bias.reshape(1, 128))

    def along_z(k):
        return [(y * 4 + z, y * 4 + (z + k) % 4) for y in range(4) for z in range(4)]

    def along_y(k):
        return [(y * 4 + z, (y + k) % 4 * 4 + z) for y in range(4) for z in range(4)]

    zs = {k: lax.ppermute(pooled, "rows", along_z(k)) for k in (2, 1, 3)}
    g0 = jnp.stack([pooled, zs[1], zs[2], zs[3]])
    gs = {k: lax.ppermute(g0, "rows", along_y(k)) for k in (2, 1, 3)}

    up, own, down = coarse_filters[0], coarse_filters[1], coarse_filters[2]
    near = jnp.where(pd == 0, up, down)
    far = jnp.where(pd == 0, down, up)
    w = jnp.stack([near, far, own])
    w = jnp.transpose(w, (2, 0, 4, 1, 3)).reshape(144, 384)
    place = jnp.stack([r // 4, lax.rem(r, 4)]).astype(jnp.int32)
    sums = coarse_level(place, g0, gs[1], gs[2], gs[3], w)
    far_sum = lax.ppermute(sums[1], "depth", depth_far)
    near_sum = lax.ppermute(sums[0], "depth", depth_near)
    total = sums[2] + near_sum + far_sum
    result = jnp.maximum(total + coarse_bias[:, None], 0.0).astype(BF16)
    return result.reshape(16, 1, 2048)


def solution(mesh):
    placed = (
        P("depth", "rows", None, None),
        P(),
        P(),
        P(None, None, None, None, "rows"),
        P("rows"),
    )
    return jax.shard_map(
        body, mesh=mesh, in_specs=placed, out_specs=P("rows", "depth", None), check_vma=False
    )
```

time: 117 us -> 61 us (0.52)
  the two profiles are of different devices: /device:TPU:39 before, /device:TPU:7 now
where the time goes in v1:
time: 61 us; the launch traced here: 60.8 us
  starting transfers between devices  38.2 us (63%)
  waiting for transfers between devices  16.9 us (28%)
  Pallas kernels  3.38 us (6%)
  local copies, waits for them, and re-layouts  1.21 us (2%)
  other arithmetic  0.92 us (2%)
    ppermute x1, starting transfers between devices, body(): lax.ppermute(lax.dynamic_index_in_dim(volume, pd, 0, False), 'depth', dep...  9.29 us
    ppermute x1, starting transfers between devices, body(): far_sum = lax.ppermute(sums[1], 'depth', depth_far)  6.61 us
    ppermute x3, starting transfers between devices, body(): zs = {k: lax.ppermute(pooled, 'rows', along_z(k)) for k in (2, 1, 3)}  5.89 us
    ppermute x1, waiting for transfers between devices, body(): far_sum = lax.ppermute(sums[1], 'depth', depth_far)  5.66 us
    ppermute x3, waiting for transfers between devices, body(): gs = {k: lax.ppermute(g0, 'rows', along_y(k)) for k in (2, 1, 3)}  5.46 us
    ppermute x1, starting transfers between devices, body(): lax.ppermute(lax.dynamic_index_in_dim(sides, 3 - 3 * pr, 1, False), 'rows...  4.7 us
    ppermute x3, waiting for transfers between devices, body(): zs = {k: lax.ppermute(pooled, 'rows', along_z(k)) for k in (2, 1, 3)}  4.16 us
    ppermute x3, starting transfers between devices, body(): gs = {k: lax.ppermute(g0, 'rows', along_y(k)) for k in (2, 1, 3)}  3.83 us
  transfers between devices with their start and end apart: 14, of which 8 were waited for; matrix products, arithmetic and copies ran while one was open for 0% of the time, Pallas kernels for 0%

profile of v1, /device:TPU:7, one launch (start us, length us, event | category | flops | bytes accessed | tf_op | source)
XLA Modules:
  0.0 60.8 jit_solution(3439460111381729977)
XLA Ops:
  0.0 1.1 %dynamic-slice_bitcast_fusion = (bf16[4,128,128]{2,1,0:T(8,128)(2,1)S(1)}, bf16[4,128,128]{2,1,0:T(8,128)(2,1)S(1)}) fusion(bf16[2,4,128,128]{3,2,1,0:T(8,128)(2,1)} %vol.1, s32[]{:T(128)S(6)} %select_n.37, s32[]{:T(128)S(6)} %select_n.36), kind=kLoop, calls=%fused_computation.13 | loop fusion | bytes 524296 | tf_op jit(solution)/shard_map/jit(dynamic_index_in_dim)/squeeze | solution.py:125
  1.1 9.3 %collective-permute-start.1 = (bf16[4,128,128]{2,1,0:T(8,128)(2,1)S(1)}, bf16[4,128,128]{2,1,0:T(8,128)(2,1)S(1)}, u32[]{:S(2)}, u32[]{:S(2)}) collective-permute-start(bf16[4,128,128]{2,1,0:T(8,128)(2,1)S(1)} %get-tuple-element.11), channel_id=1, source_target_pairs={{16,32},{32,16},{48,64},{64,48},{80,96},{96,80},{112,128},{128,112... | collective-permute-start | bytes 393224 | tf_op jit(solution)/shard_map/ppermute | solution.py:125
  10.5 0.7 %collective-permute-start.3 = (bf16[2,128,128]{2,1,0:T(8,128)(2,1)S(1)}, bf16[2,128,128]{2,1,0:T(8,128)(2,1)S(1)}, u32[]{:S(2)}, u32[]{:S(2)}) collective-permute-start(bf16[2,128,128]{2,1,0:T(8,128)(2,1)S(1)} %get-tuple-element.9), channel_id=1, source_target_pairs={{1,2},{2,1},{3,4},{4,3},{5,6},{6,5},{7,8},{8,7},{9,10},{10,9},{11,... | collective-permute-start | bytes 196616 | tf_op jit(solution)/shard_map/ppermute | solution.py:127
  11.2 2.8 %collective-permute-start.2 = (bf16[2,128,128]{2,1,0:T(8,128)(2,1)S(1)}, bf16[2,128,128]{2,1,0:T(8,128)(2,1)S(1)}, u32[]{:S(2)}, u32[]{:S(2)}) collective-permute-start(bf16[2,128,128]{2,1,0:T(8,128)(2,1)S(1)} %get-tuple-element.10), channel_id=1, source_target_pairs={{0,1},{1,0},{2,3},{3,2},{4,5},{5,4},{6,7},{7,6},{8,9},{9,8},{10,11... | collective-permute-start | bytes 196616 | tf_op jit(solution)/shard_map/ppermute | solution.py:128
  14.0 0.7 %collective-permute-start.5 = (bf16[2,128,128]{2,1,0:T(8,128)(2,1)S(1)}, bf16[2,128,128]{2,1,0:T(8,128)(2,1)S(1)}, u32[]{:S(2)}, u32[]{:S(2)}) collective-permute-start(bf16[2,128,128]{2,1,0:T(8,128)(2,1)S(1)} %get-tuple-element.7), channel_id=1, source_target_pairs={{1,2},{2,1},{3,4},{4,3},{5,6},{6,5},{7,8},{8,7},{9,10},{10,9},{11,... | collective-permute-start | bytes 196616 | tf_op jit(solution)/shard_map/ppermute | solution.py:130
  14.7 4.7 %collective-permute-start.4 = (bf16[2,128,128]{2,1,0:T(8,128)(2,1)S(1)}, bf16[2,128,128]{2,1,0:T(8,128)(2,1)S(1)}, u32[]{:S(2)}, u32[]{:S(2)}) collective-permute-start(bf16[2,128,128]{2,1,0:T(8,128)(2,1)S(1)} %get-tuple-element.8), channel_id=1, source_target_pairs={{0,1},{1,0},{2,3},{3,2},{4,5},{5,4},{6,7},{7,6},{8,9},{9,8},{10,11... | collective-permute-start | bytes 196616 | tf_op jit(solution)/shard_map/ppermute | solution.py:131
  19.5 1.6 %collective-permute-done.4.c1 = bf16[2,128,128]{2,1,0:T(8,128)(2,1)S(1)} collective-permute-done((bf16[2,128,128]{2,1,0:T(8,128)(2,1)S(1)}, bf16[2,128,128]{2,1,0:T(8,128)(2,1)S(1)}, u32[]{:S(2)}, u32[]{:S(2)}) %collective-permute-start.4) | collective-permute-done | bytes 65568 | tf_op jit(solution)/shard_map/ppermute | solution.py:131
  21.1 2.1 %shard_map.55 = bf16[2,64,128]{2,1,0:T(8,128)(2,1)S(1)} custom-call(s32[2]{0:T(128)S(1)} %pad_add_fusion.1.odd, bf16[2,4,128,128]{3,2,1,0:T(8,128)(2,1)S(1)} %copy-done, bf16[4,128,128]{2,1,0:T(8,128)(2,1)S(1)} %collective-permute-done.x1, bf16[4,128,128]{2,1,0:T(8,128)(2,1)S(1)} %collective-permute-done.1.x2, ...), custom_call_target="tpu_custom_call" | custom-call | tf_op jit(solution)/shard_map/pallas_call | solution.py:71
  23.1 5.5 %collective-permute-start.8 = (bf16[2,64,128]{2,1,0:T(8,128)(2,1)S(1)}, bf16[2,64,128]{2,1,0:T(8,128)(2,1)S(1)}, u32[]{:S(2)}, u32[]{:S(2)}) collective-permute-start(bf16[2,64,128]{2,1,0:T(8,128)(2,1)S(1)} %shard_map.55), channel_id=1, source_target_pairs={{0,3},{1,0},{2,1},{3,2},{4,7},{5,4},{6,5},{7,6},{8,11},{9,8},{10,9... | collective-permute-start | bytes 98312 | tf_op jit(solution)/shard_map/ppermute | solution.py:141
  28.6 0.4 collective-permute-start.6
  29.0 0.6 %collective-permute-done.8 = bf16[2,64,128]{2,1,0:T(8,128)(2,1)S(1)} collective-permute-done((bf16[2,64,128]{2,1,0:T(8,128)(2,1)S(1)}, bf16[2,64,128]{2,1,0:T(8,128)(2,1)S(1)}, u32[]{:S(2)}, u32[]{:S(2)}) %collective-permute-start.8) | collective-permute-done | bytes 32800 | tf_op jit(solution)/shard_map/ppermute | solution.py:141
  29.7 2.6 %collective-permute-done.7 = bf16[2,64,128]{2,1,0:T(8,128)(2,1)S(1)} collective-permute-done((bf16[2,64,128]{2,1,0:T(8,128)(2,1)S(1)}, bf16[2,64,128]{2,1,0:T(8,128)(2,1)S(1)}, u32[]{:S(2)}, u32[]{:S(2)}) %collective-permute-start.7) | collective-permute-done | bytes 32800 | tf_op jit(solution)/shard_map/ppermute | solution.py:141
  32.3 0.9 %collective-permute-done.6 = bf16[2,64,128]{2,1,0:T(8,128)(2,1)S(1)} collective-permute-done((bf16[2,64,128]{2,1,0:T(8,128)(2,1)S(1)}, bf16[2,64,128]{2,1,0:T(8,128)(2,1)S(1)}, u32[]{:S(2)}, u32[]{:S(2)}) %collective-permute-start.6) | collective-permute-done | bytes 32800 | tf_op jit(solution)/shard_map/ppermute | solution.py:141
  33.2 2.8 %collective-permute-start.11 = (bf16[4,2,64,128]{3,2,1,0:T(8,128)(2,1)S(1)}, bf16[4,2,64,128]{3,2,1,0:T(8,128)(2,1)S(1)}, u32[]{:S(2)}, u32[]{:S(2)}) collective-permute-start(bf16[4,2,64,128]{3,2,1,0:T(8,128)(2,1)S(1)} %pad_maximum_fusion.g0), channel_id=1, source_target_pairs={{0,12},{1,13},{2,14},{3,15},{4,0},{5,1},{6,2},{7,3},{8,4},{9,5},{1... | collective-permute-start | bytes 393224 | tf_op jit(solution)/shard_map/ppermute | solution.py:143
  36.1 0.2 collective-permute-start.10
  36.3 0.8 %collective-permute-start.9 = (bf16[4,2,64,128]{3,2,1,0:T(8,128)(2,1)S(1)}, bf16[4,2,64,128]{3,2,1,0:T(8,128)(2,1)S(1)}, u32[]{:S(2)}, u32[]{:S(2)}) collective-permute-start(bf16[4,2,64,128]{3,2,1,0:T(8,128)(2,1)S(1)} %pad_maximum_fusion.g0), channel_id=1, source_target_pairs={{0,4},{1,5},{2,6},{3,7},{4,8},{5,9},{6,10},{7,11},{8,12},{9,13},{1... | collective-permute-start | bytes 393224 | tf_op jit(solution)/shard_map/ppermute | solution.py:143
  37.3 1.5 %collective-permute-done.11.g3 = bf16[4,2,64,128]{3,2,1,0:T(8,128)(2,1)S(1)} collective-permute-done((bf16[4,2,64,128]{3,2,1,0:T(8,128)(2,1)S(1)}, bf16[4,2,64,128]{3,2,1,0:T(8,128)(2,1)S(1)}, u32[]{:S(2)}, u32[]{:S(2)}) %collective-permute-start.11) | collective-permute-done | bytes 131104 | tf_op jit(solution)/shard_map/ppermute | solution.py:143
  38.8 2.7 %collective-permute-done.10.g2 = bf16[4,2,64,128]{3,2,1,0:T(8,128)(2,1)S(1)} collective-permute-done((bf16[4,2,64,128]{3,2,1,0:T(8,128)(2,1)S(1)}, bf16[4,2,64,128]{3,2,1,0:T(8,128)(2,1)S(1)}, u32[]{:S(2)}, u32[]{:S(2)}) %collective-permute-start.10) | collective-permute-done | bytes 131104 | tf_op jit(solution)/shard_map/ppermute | solution.py:143
  41.5 1.2 %collective-permute-done.9.g1 = bf16[4,2,64,128]{3,2,1,0:T(8,128)(2,1)S(1)} collective-permute-done((bf16[4,2,64,128]{3,2,1,0:T(8,128)(2,1)S(1)}, bf16[4,2,64,128]{3,2,1,0:T(8,128)(2,1)S(1)}, u32[]{:S(2)}, u32[]{:S(2)}) %collective-permute-start.9) | collective-permute-done | bytes 131104 | tf_op jit(solution)/shard_map/ppermute | solution.py:143
  42.7 1.3 %shard_map.56 = f32[3,16,2048]{2,1,0:T(8,128)S(1)} custom-call(s32[2]{0:T(128)S(1)} %pad_add_fusion.place, bf16[4,2,64,128]{3,2,1,0:T(8,128)(2,1)S(1)} %pad_maximum_fusion.g0, bf16[4,2,64,128]{3,2,1,0:T(8,128)(2,1)S(1)} %collective-permute-done.9.g1, bf16[4,2,64,128]{3,2,1,0:T(8,128)(2,1)S(1)} %collective-permute-done.10.g2, ...), custom_call_target="tpu_custom_call" | custom-call | tf_op jit(solution)/shard_map/pallas_call | solution.py:107
  44.1 3.7 %collective-permute-start.12 = (f32[16,2048]{1,0:T(8,128)S(1)}, f32[16,2048]{1,0:T(8,128)S(1)}, u32[]{:S(2)}, u32[]{:S(2)}) collective-permute-start(f32[16,2048]{1,0:T(8,128)S(1)} %get-tuple-element.5), channel_id=1, source_target_pairs={{0,16},{16,0},{32,48},{48,32},{64,80},{80,64},{96,112},{112,96},{1... | collective-permute-start | bytes 393224 | tf_op jit(solution)/shard_map/ppermute | solution.py:153
  47.8 6.6 %collective-permute-start.13 = (f32[16,2048]{1,0:T(8,128)S(1)}, f32[16,2048]{1,0:T(8,128)S(1)}, u32[]{:S(2)}, u32[]{:S(2)}) collective-permute-start(f32[16,2048]{1,0:T(8,128)S(1)} %get-tuple-element.6), channel_id=1, source_target_pairs={{16,32},{32,16},{48,64},{64,48},{80,96},{96,80},{112,128},{128,112... | collective-permute-start | bytes 393224 | tf_op jit(solution)/shard_map/ppermute | solution.py:152
  54.4 5.7 %collective-permute-done.13 = f32[16,2048]{1,0:T(8,128)S(1)} collective-permute-done((f32[16,2048]{1,0:T(8,128)S(1)}, f32[16,2048]{1,0:T(8,128)S(1)}, u32[]{:S(2)}, u32[]{:S(2)}) %collective-permute-start.13) | collective-permute-done | bytes 131104 | tf_op jit(solution)/shard_map/ppermute | solution.py:152
  60.1 0.7 %fusion.5 = bf16[16,1,2048]{2,0,1:T(8,128)(2,1)} fusion(f32[16,2048]{1,0:T(8,128)S(1)} %collective-permute-done.13, f32[16,2048]{1,0:T(8,128)S(1)} %collective-permute-done.12, f32[3,16,2048]{2,1,0:T(8,128)S(1)} %shard_map.56, f32[16]{0:T(128)S(1)} %copy-done.4), kind=kLoop, calls=%fused_computation.17 | loop fusion | flops 163840 | bytes 458816 | tf_op jit(solution)/shard_map/reshape | solution.py:156
  (28 shorter events, 0.5 us)
Async XLA Ops:
  0.0 10.5 %copy-start = (bf16[2,4,128,128]{3,2,1,0:T(8,128)(2,1)S(1)}, bf16[2,4,128,128]{3,2,1,0:T(8,128)(2,1)}, u32[]{:S(2)}) copy-start(bf16[2,4,128,128]{3,2,1,0:T(8,128)(2,1)} %vol.1) | copy-start | bytes 786436
  0.0 21.1 %copy-start.1 = (bf16[3,3,3,128,128]{4,3,2,1,0:T(8,128)(2,1)S(1)}, bf16[3,3,3,128,128]{4,3,2,1,0:T(8,128)(2,1)}, u32[]{:S(2)}) copy-start(bf16[3,3,3,128,128]{4,3,2,1,0:T(8,128)(2,1)} %w.1) | copy-start | bytes 2654212
  1.1 12.9 %collective-permute-start.1 = (bf16[4,128,128]{2,1,0:T(8,128)(2,1)S(1)}, bf16[4,128,128]{2,1,0:T(8,128)(2,1)S(1)}, u32[]{:S(2)}, u32[]{:S(2)}) collective-permute-start(bf16[4,128,128]{2,1,0:T(8,128)(2,1)S(1)} %get-tuple-element.11), channel_id=1, source_target_pairs={{16,32},{32,16},{48,64},{64,48},{80,96},{96,80},{112,128},{128,112... | collective-permute-start | bytes 393224 | tf_op jit(solution)/shard_map/ppermute | solution.py:125
  10.4 3.6 %collective-permute-start = (bf16[4,128,128]{2,1,0:T(8,128)(2,1)S(1)}, bf16[4,128,128]{2,1,0:T(8,128)(2,1)S(1)}, u32[]{:S(2)}, u32[]{:S(2)}) collective-permute-start(bf16[4,128,128]{2,1,0:T(8,128)(2,1)S(1)} %get-tuple-element.12), channel_id=1, source_target_pairs={{0,16},{16,0},{32,48},{48,32},{64,80},{80,64},{96,112},{112,96},{1... | collective-permute-start | bytes 393224 | tf_op jit(solution)/shard_map/ppermute | solution.py:126
  10.5 9.0 %collective-permute-start.3 = (bf16[2,128,128]{2,1,0:T(8,128)(2,1)S(1)}, bf16[2,128,128]{2,1,0:T(8,128)(2,1)S(1)}, u32[]{:S(2)}, u32[]{:S(2)}) collective-permute-start(bf16[2,128,128]{2,1,0:T(8,128)(2,1)S(1)} %get-tuple-element.9), channel_id=1, source_target_pairs={{1,2},{2,1},{3,4},{4,3},{5,6},{6,5},{7,8},{8,7},{9,10},{10,9},{11,... | collective-permute-start | bytes 196616 | tf_op jit(solution)/shard_map/ppermute | solution.py:127
  11.2 8.3 %collective-permute-start.2 = (bf16[2,128,128]{2,1,0:T(8,128)(2,1)S(1)}, bf16[2,128,128]{2,1,0:T(8,128)(2,1)S(1)}, u32[]{:S(2)}, u32[]{:S(2)}) collective-permute-start(bf16[2,128,128]{2,1,0:T(8,128)(2,1)S(1)} %get-tuple-element.10), channel_id=1, source_target_pairs={{0,1},{1,0},{2,3},{3,2},{4,5},{5,4},{6,7},{7,6},{8,9},{9,8},{10,11... | collective-permute-start | bytes 196616 | tf_op jit(solution)/shard_map/ppermute | solution.py:128
  14.0 5.5 %collective-permute-start.5 = (bf16[2,128,128]{2,1,0:T(8,128)(2,1)S(1)}, bf16[2,128,128]{2,1,0:T(8,128)(2,1)S(1)}, u32[]{:S(2)}, u32[]{:S(2)}) collective-permute-start(bf16[2,128,128]{2,1,0:T(8,128)(2,1)S(1)} %get-tuple-element.7), channel_id=1, source_target_pairs={{1,2},{2,1},{3,4},{4,3},{5,6},{6,5},{7,8},{8,7},{9,10},{10,9},{11,... | collective-permute-start | bytes 196616 | tf_op jit(solution)/shard_map/ppermute | solution.py:130
  14.7 6.4 %collective-permute-start.4 = (bf16[2,128,128]{2,1,0:T(8,128)(2,1)S(1)}, bf16[2,128,128]{2,1,0:T(8,128)(2,1)S(1)}, u32[]{:S(2)}, u32[]{:S(2)}) collective-permute-start(bf16[2,128,128]{2,1,0:T(8,128)(2,1)S(1)} %get-tuple-element.8), channel_id=1, source_target_pairs={{0,1},{1,0},{2,3},{3,2},{4,5},{5,4},{6,7},{7,6},{8,9},{9,8},{10,11... | collective-permute-start | bytes 196616 | tf_op jit(solution)/shard_map/ppermute | solution.py:131
  19.5 1.6 %copy-start.2 = (f32[128]{0:T(128)S(1)}, f32[128]{0:T(128)}, u32[]{:S(2)}) copy-start(f32[128]{0:T(128)} %param.7) | copy-start | bytes 1540
  21.1 7.9 %copy-start.3 = (bf16[3,3,3,128,16]{3,4,2,1,0:T(8,128)(2,1)S(1)}, bf16[3,3,3,128,16]{3,4,2,1,0:T(8,128)(2,1)}, u32[]{:S(2)}) copy-start(bf16[3,3,3,128,16]{3,4,2,1,0:T(8,128)(2,1)} %param.8) | copy-start | bytes 331780
  23.1 6.5 %collective-permute-start.8 = (bf16[2,64,128]{2,1,0:T(8,128)(2,1)S(1)}, bf16[2,64,128]{2,1,0:T(8,128)(2,1)S(1)}, u32[]{:S(2)}, u32[]{:S(2)}) collective-permute-start(bf16[2,64,128]{2,1,0:T(8,128)(2,1)S(1)} %shard_map.55), channel_id=1, source_target_pairs={{0,3},{1,0},{2,1},{3,2},{4,7},{5,4},{6,5},{7,6},{8,11},{9,8},{10,9... | collective-permute-start | bytes 98312 | tf_op jit(solution)/shard_map/ppermute | solution.py:141
  28.6 3.7 %collective-permute-start.7 = (bf16[2,64,128]{2,1,0:T(8,128)(2,1)S(1)}, bf16[2,64,128]{2,1,0:T(8,128)(2,1)S(1)}, u32[]{:S(2)}, u32[]{:S(2)}) collective-permute-start(bf16[2,64,128]{2,1,0:T(8,128)(2,1)S(1)} %shard_map.55), channel_id=1, source_target_pairs={{0,2},{1,3},{2,0},{3,1},{4,6},{5,7},{6,4},{7,5},{8,10},{9,11},{10,... | collective-permute-start | bytes 98312 | tf_op jit(solution)/shard_map/ppermute | solution.py:141
  28.6 4.6 %collective-permute-start.6 = (bf16[2,64,128]{2,1,0:T(8,128)(2,1)S(1)}, bf16[2,64,128]{2,1,0:T(8,128)(2,1)S(1)}, u32[]{:S(2)}, u32[]{:S(2)}) collective-permute-start(bf16[2,64,128]{2,1,0:T(8,128)(2,1)S(1)} %shard_map.55), channel_id=1, source_target_pairs={{0,1},{1,2},{2,3},{3,0},{4,5},{5,6},{6,7},{7,4},{8,9},{9,10},{10,1... | collective-permute-start | bytes 98312 | tf_op jit(solution)/shard_map/ppermute | solution.py:141
  33.2 5.6 %collective-permute-start.11 = (bf16[4,2,64,128]{3,2,1,0:T(8,128)(2,1)S(1)}, bf16[4,2,64,128]{3,2,1,0:T(8,128)(2,1)S(1)}, u32[]{:S(2)}, u32[]{:S(2)}) collective-permute-start(bf16[4,2,64,128]{3,2,1,0:T(8,128)(2,1)S(1)} %pad_maximum_fusion.g0), channel_id=1, source_target_pairs={{0,12},{1,13},{2,14},{3,15},{4,0},{5,1},{6,2},{7,3},{8,4},{9,5},{1... | collective-permute-start | bytes 393224 | tf_op jit(solution)/shard_map/ppermute | solution.py:143
  36.1 5.4 %collective-permute-start.10 = (bf16[4,2,64,128]{3,2,1,0:T(8,128)(2,1)S(1)}, bf16[4,2,64,128]{3,2,1,0:T(8,128)(2,1)S(1)}, u32[]{:S(2)}, u32[]{:S(2)}) collective-permute-start(bf16[4,2,64,128]{3,2,1,0:T(8,128)(2,1)S(1)} %pad_maximum_fusion.g0), channel_id=1, source_target_pairs={{0,8},{1,9},{2,10},{3,11},{4,12},{5,13},{6,14},{7,15},{8,0},{9,1},... | collective-permute-start | bytes 393224 | tf_op jit(solution)/shard_map/ppermute | solution.py:143
  36.3 6.4 %collective-permute-start.9 = (bf16[4,2,64,128]{3,2,1,0:T(8,128)(2,1)S(1)}, bf16[4,2,64,128]{3,2,1,0:T(8,128)(2,1)S(1)}, u32[]{:S(2)}, u32[]{:S(2)}) collective-permute-start(bf16[4,2,64,128]{3,2,1,0:T(8,128)(2,1)S(1)} %pad_maximum_fusion.g0), channel_id=1, source_target_pairs={{0,4},{1,5},{2,6},{3,7},{4,8},{5,9},{6,10},{7,11},{8,12},{9,13},{1... | collective-permute-start | bytes 393224 | tf_op jit(solution)/shard_map/ppermute | solution.py:143
  44.1 16.0 %copy-start.4 = (f32[16]{0:T(128)S(1)}, f32[16]{0:T(128)}, u32[]{:S(2)}) copy-start(f32[16]{0:T(128)} %param.9) | copy-start | bytes 196
  44.1 10.3 %collective-permute-start.12 = (f32[16,2048]{1,0:T(8,128)S(1)}, f32[16,2048]{1,0:T(8,128)S(1)}, u32[]{:S(2)}, u32[]{:S(2)}) collective-permute-start(f32[16,2048]{1,0:T(8,128)S(1)} %get-tuple-element.5), channel_id=1, source_target_pairs={{0,16},{16,0},{32,48},{48,32},{64,80},{80,64},{96,112},{112,96},{1... | collective-permute-start | bytes 393224 | tf_op jit(solution)/shard_map/ppermute | solution.py:153
  47.8 12.3 %collective-permute-start.13 = (f32[16,2048]{1,0:T(8,128)S(1)}, f32[16,2048]{1,0:T(8,128)S(1)}, u32[]{:S(2)}, u32[]{:S(2)}) collective-permute-start(f32[16,2048]{1,0:T(8,128)S(1)} %get-tuple-element.6), channel_id=1, source_target_pairs={{16,32},{32,16},{48,64},{64,48},{80,96},{96,80},{112,128},{128,112... | collective-permute-start | bytes 393224 | tf_op jit(solution)/shard_map/ppermute | solution.py:152

commit v2 on v1

--- a/solution.py
+++ b/solution.py
@@ -17,9 +17,9 @@
     return [(i, ((i - 1) ^ 1) + 1) for i in range(1, count - 1)]
 
 
-def fine_kernel(odd, vol, x1, x2, r1, r2, c1, c2, w, bias, out, cells, peak):
-    pd = odd[0]
-    pr = odd[1]
+def fine_kernel(vol, x1, x2, r1, r2, c1, c2, w, bias, out, cells, peak):
+    pd = lax.rem(lax.axis_index("depth"), 2)
+    pr = lax.rem(lax.axis_index("rows"), 2)
     for j in range(4):
         for i in range(6):
             row = (i - 1) + pr * (5 - 2 * i)
@@ -66,52 +66,94 @@
         out[q + pr * (1 - 2 * q)] = jnp.maximum(pooled + bias[...], 0.0).astype(BF16)
 
 
-def fine_level(odd, vol, x1, x2, r1, r2, c1, c2, w, bias):
+def fine_level(vol, x1, x2, r1, r2, c1, c2, w, bias):
     vmem = pl.BlockSpec(memory_space=pltpu.VMEM)
     return pl.pallas_call(
         fine_kernel,
         out_shape=jax.ShapeDtypeStruct((2, 64, 128), BF16),
-        in_specs=[pl.BlockSpec(memory_space=pltpu.SMEM)] + [vmem] * 9,
+        in_specs=[vmem] * 9,
         out_specs=vmem,
         scratch_shapes=[pltpu.VMEM((4, 6, 128, 128), BF16), pltpu.VMEM((128, 128), F32)],
         compiler_params=pltpu.CompilerParams(vmem_limit_bytes=32 * 1024 * 1024),
-    )(odd, vol, x1, x2, r1, r2, c1, c2, w, bias)
-
-
-def coarse_kernel(place, g0, g1, g2, g3, w, out, cells):
-    y = place[0]
-    z = place[1]
-    cells[0] = jnp.zeros((64, 128), BF16)
-    cells[33] = jnp.zeros((64, 128), BF16)
-    for m, block in enumerate((g0, g1, g2, g3)):
-        for k in range(4):
-            row = lax.rem(y - m + 4, 4) * 8 + lax.rem(z - k + 4, 4) * 2
-            cells[pl.ds(row + 1, 2)] = block[k]
-    lines = 8
-    size = lines * 64
-    lane = lax.rem(lax.broadcasted_iota(jnp.int32, (48, size), 1), 64)
-    for t in range(32 // lines):
-        rhs = jnp.concatenate(
-            [cells[t * lines + b : t * lines + b + lines].reshape(size, 128) for b in range(3)], axis=1
-        )
-        term = lax.dot_general(w[...], rhs, (((1,), (1,)), ((), ())), preferred_element_type=F32)
-        left = jnp.where(lane == 0, 0.0, pltpu.roll(term[:48], 1, 1))
-        right = jnp.where(lane == 63, 0.0, pltpu.roll(term[96:], size - 1, 1))
-        value = term[48:96] + left + right
-        for n in range(3):
-            out[n, :, t * size : (t + 1) * size] = value[16 * n : 16 * n + 16]
-
-
-def coarse_level(place, g0, g1, g2, g3, w):
+    )(vol, x1, x2, r1, r2, c1, c2, w, bias)
+
+
+def coarse_kernel(p0, p1, p2, p3, w0, w1, w2, w3, o0, o1, o2, o3, cells):
+    pd = lax.rem(lax.axis_index("depth"), 2)
+    z = lax.rem(lax.axis_index("rows"), 4)
+    for a in range(3):
+        for i in (0, 1, 10, 11):
+            cells[a, i] = jnp.zeros((64, 128), BF16)
+    for k, piece in enumerate((p0, p1, p2, p3)):
+        cells[:, pl.ds(2 + 2 * (z ^ k), 2)] = piece[...]
+    lhs = jnp.concatenate(
+        [
+            jnp.concatenate(
+                [w[9 * (a + pd * (2 - 2 * a)) + 3 * b + c] for a in range(3) for b in range(3)], axis=1
+            )
+            for c in range(3)
+            for w in (w0, w1, w2, w3)
+        ],
+        axis=0,
+    )
+    for start, size in ((0, 256), (256, 256), (512, 128)):
+        if start < 512:
+            first = start // 64 + 1
+            blocks = [
+                cells[a, first + b : first + b + 4].reshape(256, 128) for a in range(3) for b in range(3)
+            ]
+        else:
+            blocks = [
+                jnp.concatenate([cells[a, 9 + b], cells[a, b]], axis=0) for a in range(3) for b in range(3)
+            ]
+        rhs = jnp.concatenate(blocks, axis=1)
+        term = lax.dot_general(lhs, rhs, (((1,), (1,)), ((), ())), preferred_element_type=F32)
+        lane = lax.rem(lax.broadcasted_iota(jnp.int32, (64, size), 1), 64)
+        left = jnp.where(lane == 0, 0.0, pltpu.roll(term[:64], 1, 1))
+        right = jnp.where(lane == 63, 0.0, pltpu.roll(term[128:], size - 1, 1))
+        value = term[64:128] + left + right
+        for k, out in enumerate((o0, o1, o2, o3)):
+            out[:, start : start + size] = value[16 * k : 16 * k + 16]
+
+
+def coarse_level(pieces, weights):
     vmem = pl.BlockSpec(memory_space=pltpu.VMEM)
     return pl.pallas_call(
         coarse_kernel,
-        out_shape=jax.ShapeDtypeStruct((3, 16, 2048), F32),
-        in_specs=[pl.BlockSpec(memory_space=pltpu.SMEM)] + [vmem] * 5,
+        out_shape=[jax.ShapeDtypeStruct((16, 640), F32)] * 4,
+        in_specs=[vmem] * 8,
+        out_specs=[vmem] * 4,
+        scratch_shapes=[pltpu.VMEM((3, 12, 64, 128), BF16)],
+        compiler_params=pltpu.CompilerParams(vmem_limit_bytes=32 * 1024 * 1024),
+    )(*pieces, *weights)
+
+
+def join_kernel(s0, s1, s2, s3, bias, out, held):
+    y = lax.div(lax.axis_index("rows"), 4)
+    for k, part in enumerate((s0, s1, s2, s3)):
+        held[y ^ k] = part[...]
+    low = lax.broadcasted_iota(jnp.int32, (16, 128), 1) < 64
+    for m in range(4):
+        tiles = [held[m, :, 128 * i : 128 * i + 128] for i in range(4)]
+        if m > 0:
+            tiles[0] = tiles[0] + jnp.where(low, held[m - 1, :, 512:], 0.0)
+        if m < 3:
+            tiles[3] = tiles[3] + jnp.where(low, 0.0, held[m + 1, :, 512:])
+        for i in range(4):
+            value = jnp.maximum(tiles[i] + bias[...], 0.0).astype(BF16)
+            out[:, 512 * m + 128 * i : 512 * m + 128 * i + 128] = value
+
+
+def join(parts, bias):
+    vmem = pl.BlockSpec(memory_space=pltpu.VMEM)
+    return pl.pallas_call(
+        join_kernel,
+        out_shape=jax.ShapeDtypeStruct((16, 2048), BF16),
+        in_specs=[vmem] * 5,
         out_specs=vmem,
-        scratch_shapes=[pltpu.VMEM((34, 64, 128), BF16)],
+        scratch_shapes=[pltpu.VMEM((4, 16, 640), F32)],
         compiler_params=pltpu.CompilerParams(vmem_limit_bytes=32 * 1024 * 1024),
-    )(place, g0, g1, g2, g3, w)
+    )(*parts, bias)
 
 
 def body(volume, fine_filters, fine_bias, coarse_filters, coarse_bias):
@@ -129,30 +171,30 @@
     sides = jnp.stack([x1, x2])
     c2 = lax.ppermute(lax.dynamic_index_in_dim(sides, 3 * pr, 1, False), "rows", rows_far)
     c1 = lax.ppermute(lax.dynamic_index_in_dim(sides, 3 - 3 * pr, 1, False), "rows", rows_near)
-    odd = jnp.stack([pd, pr]).astype(jnp.int32)
-    pooled = fine_level(odd, volume, x1, x2, r1, r2, c1, c2, fine_filters, fine_bias.reshape(1, 128))
+    pooled = fine_level(volume, x1, x2, r1, r2, c1, c2, fine_filters, fine_bias.reshape(1, 128))
 
     def along_z(k):
-        return [(y * 4 + z, y * 4 + (z + k) % 4) for y in range(4) for z in range(4)]
+        return [(i, i ^ k) for i in range(16)]
 
     def along_y(k):
-        return [(y * 4 + z, (y + k) % 4 * 4 + z) for y in range(4) for z in range(4)]
-
-    zs = {k: lax.ppermute(pooled, "rows", along_z(k)) for k in (2, 1, 3)}
-    g0 = jnp.stack([pooled, zs[1], zs[2], zs[3]])
-    gs = {k: lax.ppermute(g0, "rows", along_y(k)) for k in (2, 1, 3)}
-
-    up, own, down = coarse_filters[0], coarse_filters[1], coarse_filters[2]
-    near = jnp.where(pd == 0, up, down)
-    far = jnp.where(pd == 0, down, up)
-    w = jnp.stack([near, far, own])
-    w = jnp.transpose(w, (2, 0, 4, 1, 3)).reshape(144, 384)
-    place = jnp.stack([r // 4, lax.rem(r, 4)]).astype(jnp.int32)
-    sums = coarse_level(place, g0, gs[1], gs[2], gs[3], w)
-    far_sum = lax.ppermute(sums[1], "depth", depth_far)
-    near_sum = lax.ppermute(sums[0], "depth", depth_near)
-    total = sums[2] + near_sum + far_sum
-    result = jnp.maximum(total + coarse_bias[:, None], 0.0).astype(BF16)
+        return [(i, i ^ (4 * k)) for i in range(16)]
+
+    w = jnp.transpose(coarse_filters, (0, 1, 2, 4, 3)).reshape(27, 16, 128)
+    weights = [w] + [None] * 3
+    for k in (2, 1, 3):
+        weights[k] = lax.ppermute(w, "rows", along_y(k))
+
+    far = lax.ppermute(pooled, "depth", depth_far)
+    near = lax.ppermute(pooled, "depth", depth_near)
+    planes = jnp.stack([far, pooled, near])
+    pieces = [planes] + [None] * 3
+    for k in (3, 2, 1):
+        pieces[k] = lax.ppermute(planes, "rows", along_z(k))
+    sums = coarse_level(pieces, weights)
+    parts = [sums[0]] + [None] * 3
+    for k in (2, 1, 3):
+        parts[k] = lax.ppermute(sums[k], "rows", along_y(k))
+    result = join(parts, jnp.broadcast_to(coarse_bias[:, None], (16, 128)))
     return result.reshape(16, 1, 2048)
 
 

time: 61 us -> 58.6 us (0.961)
  the two profiles are of different devices: /device:TPU:7 before, /device:TPU:192 now
where the time goes in v2:
time: 58.6 us; the launch traced here: 58.4 us
  starting transfers between devices  34.4 us (59%)
  waiting for transfers between devices  19.6 us (33%)
  Pallas kernels  2.97 us (5%)
  local copies, waits for them, and re-layouts  1.19 us (2%)
    ppermute x3, starting transfers between devices, body(): pieces[k] = lax.ppermute(planes, 'rows', along_z(k))  7.52 us
    ppermute x3, starting transfers between devices, body(): parts[k] = lax.ppermute(sums[k], 'rows', along_y(k))  5.65 us
    ppermute x1, waiting for transfers between devices, body(): lax.ppermute(lax.dynamic_index_in_dim(volume, pd, 0, False), 'depth', dep...  5.31 us
    ppermute x3, starting transfers between devices, body(): weights[k] = lax.ppermute(w, 'rows', along_y(k))  4.79 us
    ppermute x1, starting transfers between devices, body(): lax.ppermute(lax.dynamic_index_in_dim(volume, pd, 0, False), 'depth', dep...  4.73 us
    ppermute x3, waiting for transfers between devices, body(): pieces[k] = lax.ppermute(planes, 'rows', along_z(k))  4.68 us
    ppermute x3, waiting for transfers between devices, body(): parts[k] = lax.ppermute(sums[k], 'rows', along_y(k))  4.45 us
    ppermute x1, starting transfers between devices, body(): far = lax.ppermute(pooled, 'depth', depth_far)  3.76 us
  transfers between devices with their start and end apart: 17, of which 9 were waited for; matrix products, arithmetic and copies ran while one was open for 0% of the time, Pallas kernels for 0%

profile of v2, /device:TPU:192, one launch (start us, length us, event | category | flops | bytes accessed | tf_op | source)
XLA Modules:
  0.0 58.4 jit_solution(4042935973545123699)
XLA Ops:
  0.0 1.1 %dynamic-slice_bitcast_fusion = (bf16[4,128,128]{2,1,0:T(8,128)(2,1)S(1)}, bf16[4,128,128]{2,1,0:T(8,128)(2,1)S(1)}) fusion(bf16[2,4,128,128]{3,2,1,0:T(8,128)(2,1)} %vol.1, s32[]{:T(128)S(6)} %select_n.17, s32[]{:T(128)S(6)} %select_n.16), kind=kLoop, calls=%fused_computation.4 | loop fusion | bytes 524296 | tf_op jit(solution)/shard_map/jit(dynamic_index_in_dim)/squeeze | solution.py:167
  1.2 4.7 %collective-permute-start.1 = (bf16[4,128,128]{2,1,0:T(8,128)(2,1)S(1)}, bf16[4,128,128]{2,1,0:T(8,128)(2,1)S(1)}, u32[]{:S(2)}, u32[]{:S(2)}) collective-permute-start(bf16[4,128,128]{2,1,0:T(8,128)(2,1)S(1)} %get-tuple-element.17), channel_id=1, source_target_pairs={{16,32},{32,16},{48,64},{64,48},{80,96},{96,80},{112,128},{128,112... | collective-permute-start | bytes 393224 | tf_op jit(solution)/shard_map/ppermute | solution.py:167
  6.0 2.0 %collective-permute-start.2 = (bf16[2,128,128]{2,1,0:T(8,128)(2,1)S(1)}, bf16[2,128,128]{2,1,0:T(8,128)(2,1)S(1)}, u32[]{:S(2)}, u32[]{:S(2)}) collective-permute-start(bf16[2,128,128]{2,1,0:T(8,128)(2,1)S(1)} %get-tuple-element.16), channel_id=1, source_target_pairs={{0,1},{1,0},{2,3},{3,2},{4,5},{5,4},{6,7},{7,6},{8,9},{9,8},{10,11... | collective-permute-start | bytes 196616 | tf_op jit(solution)/shard_map/ppermute | solution.py:170
  8.0 1.9 %collective-permute-start.3 = (bf16[2,128,128]{2,1,0:T(8,128)(2,1)S(1)}, bf16[2,128,128]{2,1,0:T(8,128)(2,1)S(1)}, u32[]{:S(2)}, u32[]{:S(2)}) collective-permute-start(bf16[2,128,128]{2,1,0:T(8,128)(2,1)S(1)} %get-tuple-element.15), channel_id=1, source_target_pairs={{1,2},{2,1},{3,4},{4,3},{5,6},{6,5},{7,8},{8,7},{9,10},{10,9},{11,... | collective-permute-start | bytes 196616 | tf_op jit(solution)/shard_map/ppermute | solution.py:169
  9.9 5.3 %collective-permute-done.1.x2 = bf16[4,128,128]{2,1,0:T(8,128)(2,1)S(1)} collective-permute-done((bf16[4,128,128]{2,1,0:T(8,128)(2,1)S(1)}, bf16[4,128,128]{2,1,0:T(8,128)(2,1)S(1)}, u32[]{:S(2)}, u32[]{:S(2)}) %collective-permute-start.1) | collective-permute-done | bytes 131104 | tf_op jit(solution)/shard_map/ppermute | solution.py:167
  15.3 3.8 %collective-permute-start.5 = (bf16[2,128,128]{2,1,0:T(8,128)(2,1)S(1)}, bf16[2,128,128]{2,1,0:T(8,128)(2,1)S(1)}, u32[]{:S(2)}, u32[]{:S(2)}) collective-permute-start(bf16[2,128,128]{2,1,0:T(8,128)(2,1)S(1)} %get-tuple-element.13), channel_id=1, source_target_pairs={{1,2},{2,1},{3,4},{4,3},{5,6},{6,5},{7,8},{8,7},{9,10},{10,9},{11,... | collective-permute-start | bytes 196616 | tf_op jit(solution)/shard_map/ppermute | solution.py:172
  19.6 1.9 %collective-permute-done.5.c2 = bf16[2,128,128]{2,1,0:T(8,128)(2,1)S(1)} collective-permute-done((bf16[2,128,128]{2,1,0:T(8,128)(2,1)S(1)}, bf16[2,128,128]{2,1,0:T(8,128)(2,1)S(1)}, u32[]{:S(2)}, u32[]{:S(2)}) %collective-permute-start.5) | collective-permute-done | bytes 65568 | tf_op jit(solution)/shard_map/ppermute | solution.py:172
  21.5 1.5 %shard_map.55 = bf16[2,64,128]{2,1,0:T(8,128)(2,1)S(1)} custom-call(bf16[2,4,128,128]{3,2,1,0:T(8,128)(2,1)S(1)} %copy-done, bf16[4,128,128]{2,1,0:T(8,128)(2,1)S(1)} %collective-permute-done.x1, bf16[4,128,128]{2,1,0:T(8,128)(2,1)S(1)} %collective-permute-done.1.x2, bf16[2,128,128]{2,1,0:T(8,128)(2,1)S(1)} %collective-permute-done.2.r1, ...), custom_call_target="tpu_custom_call" | custom-call | tf_op jit(solution)/shard_map/pallas_call | solution.py:71
  23.1 3.8 %collective-permute-start.6 = (bf16[2,64,128]{2,1,0:T(8,128)(2,1)S(1)}, bf16[2,64,128]{2,1,0:T(8,128)(2,1)S(1)}, u32[]{:S(2)}, u32[]{:S(2)}) collective-permute-start(bf16[2,64,128]{2,1,0:T(8,128)(2,1)S(1)} %shard_map.55), channel_id=1, source_target_pairs={{16,32},{32,16},{48,64},{64,48},{80,96},{96,80},{112,128},{128,112... | collective-permute-start | bytes 98312 | tf_op jit(solution)/shard_map/ppermute | solution.py:187
  26.9 1.6 %collective-permute-start.11 = (bf16[27,16,128]{2,1,0:T(8,128)(2,1)S(1)}, bf16[27,16,128]{2,1,0:T(8,128)(2,1)S(1)}, u32[]{:S(2)}, u32[]{:S(2)}) collective-permute-start(bf16[27,16,128]{2,1,0:T(8,128)(2,1)S(1)} %bitcast.25), channel_id=1, source_target_pairs={{0,4},{1,5},{2,6},{3,7},{4,0},{5,1},{6,2},{7,3},{8,12},{9,13},{10,... | collective-permute-start | bytes 331784 | tf_op jit(solution)/shard_map/ppermute | solution.py:185
  28.5 2.9 %collective-permute-start.12 = (bf16[27,16,128]{2,1,0:T(8,128)(2,1)S(1)}, bf16[27,16,128]{2,1,0:T(8,128)(2,1)S(1)}, u32[]{:S(2)}, u32[]{:S(2)}) collective-permute-start(bf16[27,16,128]{2,1,0:T(8,128)(2,1)S(1)} %bitcast.26), channel_id=1, source_target_pairs={{0,8},{1,9},{2,10},{3,11},{4,12},{5,13},{6,14},{7,15},{8,0},{9,1},... | collective-permute-start | bytes 331784 | tf_op jit(solution)/shard_map/ppermute | solution.py:185
  31.7 2.8 %collective-permute-done.6 = bf16[2,64,128]{2,1,0:T(8,128)(2,1)S(1)} collective-permute-done((bf16[2,64,128]{2,1,0:T(8,128)(2,1)S(1)}, bf16[2,64,128]{2,1,0:T(8,128)(2,1)S(1)}, u32[]{:S(2)}, u32[]{:S(2)}) %collective-permute-start.6) | collective-permute-done | bytes 32800 | tf_op jit(solution)/shard_map/ppermute | solution.py:187
  34.5 2.0 %collective-permute-start.10 = (bf16[3,2,64,128]{3,2,1,0:T(8,128)(2,1)S(1)}, bf16[3,2,64,128]{3,2,1,0:T(8,128)(2,1)S(1)}, u32[]{:S(2)}, u32[]{:S(2)}) collective-permute-start(bf16[3,2,64,128]{3,2,1,0:T(8,128)(2,1)S(1)} %pad_maximum_fusion.p0), channel_id=1, source_target_pairs={{0,3},{1,2},{2,1},{3,0},{4,7},{5,6},{6,5},{7,4},{8,11},{9,10},{10,... | collective-permute-start | bytes 294920 | tf_op jit(solution)/shard_map/ppermute | solution.py:192
  36.5 3.2 %collective-permute-start.8 = (bf16[3,2,64,128]{3,2,1,0:T(8,128)(2,1)S(1)}, bf16[3,2,64,128]{3,2,1,0:T(8,128)(2,1)S(1)}, u32[]{:S(2)}, u32[]{:S(2)}) collective-permute-start(bf16[3,2,64,128]{3,2,1,0:T(8,128)(2,1)S(1)} %pad_maximum_fusion.p0), channel_id=1, source_target_pairs={{0,1},{1,0},{2,3},{3,2},{4,5},{5,4},{6,7},{7,6},{8,9},{9,8},{10,11... | collective-permute-start | bytes 294920 | tf_op jit(solution)/shard_map/ppermute | solution.py:192
  39.8 2.3 %collective-permute-start.9 = (bf16[3,2,64,128]{3,2,1,0:T(8,128)(2,1)S(1)}, bf16[3,2,64,128]{3,2,1,0:T(8,128)(2,1)S(1)}, u32[]{:S(2)}, u32[]{:S(2)}) collective-permute-start(bf16[3,2,64,128]{3,2,1,0:T(8,128)(2,1)S(1)} %pad_maximum_fusion.p0), channel_id=1, source_target_pairs={{0,2},{1,3},{2,0},{3,1},{4,6},{5,7},{6,4},{7,5},{8,10},{9,11},{10,... | collective-permute-start | bytes 294920 | tf_op jit(solution)/shard_map/ppermute | solution.py:192
  42.3 1.0 %collective-permute-done.8.p1 = bf16[3,2,64,128]{3,2,1,0:T(8,128)(2,1)S(1)} collective-permute-done((bf16[3,2,64,128]{3,2,1,0:T(8,128)(2,1)S(1)}, bf16[3,2,64,128]{3,2,1,0:T(8,128)(2,1)S(1)}, u32[]{:S(2)}, u32[]{:S(2)}) %collective-permute-start.8) | collective-permute-done | bytes 98336 | tf_op jit(solution)/shard_map/ppermute | solution.py:192
  43.3 3.4 %collective-permute-done.9.p2 = bf16[3,2,64,128]{3,2,1,0:T(8,128)(2,1)S(1)} collective-permute-done((bf16[3,2,64,128]{3,2,1,0:T(8,128)(2,1)S(1)}, bf16[3,2,64,128]{3,2,1,0:T(8,128)(2,1)S(1)}, u32[]{:S(2)}, u32[]{:S(2)}) %collective-permute-start.9) | collective-permute-done | bytes 98336 | tf_op jit(solution)/shard_map/ppermute | solution.py:192
  46.7 0.8 %shard_map.56 = (f32[16,640]{1,0:T(8,128)S(1)}, f32[16,640]{1,0:T(8,128)S(1)}, f32[16,640]{1,0:T(8,128)S(1)}, f32[16,640]{1,0:T(8,128)S(1)}) custom-call(bf16[3,2,64,128]{3,2,1,0:T(8,128)(2,1)S(1)} %pad_maximum_fusion.p0, bf16[3,2,64,128]{3,2,1,0:T(8,128)(2,1)S(1)} %collective-permute-done.8.p1, bf16[3,2,64,128]{3,2,1,0:T(8,128)(2,1)S(1)} %collective-permute-done.9.p2, ...), custom_call_target="tpu_custom_call" | custom-call | tf_op jit(solution)/shard_map/pallas_call | solution.py:121
  47.5 2.9 %collective-permute-start.14 = (f32[16,640]{1,0:T(8,128)S(1)}, f32[16,640]{1,0:T(8,128)S(1)}, u32[]{:S(2)}, u32[]{:S(2)}) collective-permute-start(f32[16,640]{1,0:T(8,128)S(1)} %get-tuple-element.10), channel_id=1, source_target_pairs={{0,4},{1,5},{2,6},{3,7},{4,0},{5,1},{6,2},{7,3},{8,12},{9,13},{10,... | collective-permute-start | bytes 122888 | tf_op jit(solution)/shard_map/ppermute | solution.py:196
  50.4 2.0 %collective-permute-start.15 = (f32[16,640]{1,0:T(8,128)S(1)}, f32[16,640]{1,0:T(8,128)S(1)}, u32[]{:S(2)}, u32[]{:S(2)}) collective-permute-start(f32[16,640]{1,0:T(8,128)S(1)} %get-tuple-element.11), channel_id=1, source_target_pairs={{0,8},{1,9},{2,10},{3,11},{4,12},{5,13},{6,14},{7,15},{8,0},{9,1},... | collective-permute-start | bytes 122888 | tf_op jit(solution)/shard_map/ppermute | solution.py:196
  52.4 0.8 %collective-permute-start.16 = (f32[16,640]{1,0:T(8,128)S(1)}, f32[16,640]{1,0:T(8,128)S(1)}, u32[]{:S(2)}, u32[]{:S(2)}) collective-permute-start(f32[16,640]{1,0:T(8,128)S(1)} %get-tuple-element.12), channel_id=1, source_target_pairs={{0,12},{1,13},{2,14},{3,15},{4,8},{5,9},{6,10},{7,11},{8,4},{9,5},... | collective-permute-start | bytes 122888 | tf_op jit(solution)/shard_map/ppermute | solution.py:196
  53.2 2.7 %collective-permute-done.15.s2 = f32[16,640]{1,0:T(8,128)S(1)} collective-permute-done((f32[16,640]{1,0:T(8,128)S(1)}, f32[16,640]{1,0:T(8,128)S(1)}, u32[]{:S(2)}, u32[]{:S(2)}) %collective-permute-start.15) | collective-permute-done | bytes 40992 | tf_op jit(solution)/shard_map/ppermute | solution.py:196
  55.9 1.7 %collective-permute-done.16.s3 = f32[16,640]{1,0:T(8,128)S(1)} collective-permute-done((f32[16,640]{1,0:T(8,128)S(1)}, f32[16,640]{1,0:T(8,128)S(1)}, u32[]{:S(2)}, u32[]{:S(2)}) %collective-permute-start.16) | collective-permute-done | bytes 40992 | tf_op jit(solution)/shard_map/ppermute | solution.py:196
  57.7 0.7 %shard_map.57 = bf16[16,2048]{1,0:T(8,128)(2,1)} custom-call(f32[16,640]{1,0:T(8,128)S(1)} %get-tuple-element.9.s0, f32[16,640]{1,0:T(8,128)S(1)} %collective-permute-done.14.s1, f32[16,640]{1,0:T(8,128)S(1)} %collective-permute-done.15.s2, f32[16,640]{1,0:T(8,128)S(1)} %collective-permute-done.16.s3, f32[16,128]{1,0:T(8,128)S(1)} %broadcast_in_dim.2.bias), custom_call_target="tpu_custom_call" | custom-call | tf_op jit(solution)/shard_map/pallas_call | solution.py:149
  (28 shorter events, 1.4 us)
Async XLA Ops:
  0.0 5.9 %copy-start = (bf16[2,4,128,128]{3,2,1,0:T(8,128)(2,1)S(1)}, bf16[2,4,128,128]{3,2,1,0:T(8,128)(2,1)}, u32[]{:S(2)}) copy-start(bf16[2,4,128,128]{3,2,1,0:T(8,128)(2,1)} %vol.1) | copy-start | bytes 786436
  0.0 21.5 %copy-start.1 = (bf16[3,3,3,128,128]{4,3,2,1,0:T(8,128)(2,1)S(1)}, bf16[3,3,3,128,128]{4,3,2,1,0:T(8,128)(2,1)}, u32[]{:S(2)}) copy-start(bf16[3,3,3,128,128]{4,3,2,1,0:T(8,128)(2,1)} %w.1) | copy-start | bytes 2654212
  1.1 8.8 %collective-permute-start = (bf16[4,128,128]{2,1,0:T(8,128)(2,1)S(1)}, bf16[4,128,128]{2,1,0:T(8,128)(2,1)S(1)}, u32[]{:S(2)}, u32[]{:S(2)}) collective-permute-start(bf16[4,128,128]{2,1,0:T(8,128)(2,1)S(1)} %get-tuple-element.18), channel_id=1, source_target_pairs={{0,16},{16,0},{32,48},{48,32},{64,80},{80,64},{96,112},{112,96},{1... | collective-permute-start | bytes 393224 | tf_op jit(solution)/shard_map/ppermute | solution.py:168
  1.2 14.0 %collective-permute-start.1 = (bf16[4,128,128]{2,1,0:T(8,128)(2,1)S(1)}, bf16[4,128,128]{2,1,0:T(8,128)(2,1)S(1)}, u32[]{:S(2)}, u32[]{:S(2)}) collective-permute-start(bf16[4,128,128]{2,1,0:T(8,128)(2,1)S(1)} %get-tuple-element.17), channel_id=1, source_target_pairs={{16,32},{32,16},{48,64},{64,48},{80,96},{96,80},{112,128},{128,112... | collective-permute-start | bytes 393224 | tf_op jit(solution)/shard_map/ppermute | solution.py:167
  6.0 13.1 %collective-permute-start.2 = (bf16[2,128,128]{2,1,0:T(8,128)(2,1)S(1)}, bf16[2,128,128]{2,1,0:T(8,128)(2,1)S(1)}, u32[]{:S(2)}, u32[]{:S(2)}) collective-permute-start(bf16[2,128,128]{2,1,0:T(8,128)(2,1)S(1)} %get-tuple-element.16), channel_id=1, source_target_pairs={{0,1},{1,0},{2,3},{3,2},{4,5},{5,4},{6,7},{7,6},{8,9},{9,8},{10,11... | collective-permute-start | bytes 196616 | tf_op jit(solution)/shard_map/ppermute | solution.py:170
  8.0 11.1 %collective-permute-start.3 = (bf16[2,128,128]{2,1,0:T(8,128)(2,1)S(1)}, bf16[2,128,128]{2,1,0:T(8,128)(2,1)S(1)}, u32[]{:S(2)}, u32[]{:S(2)}) collective-permute-start(bf16[2,128,128]{2,1,0:T(8,128)(2,1)S(1)} %get-tuple-element.15), channel_id=1, source_target_pairs={{1,2},{2,1},{3,4},{4,3},{5,6},{6,5},{7,8},{8,7},{9,10},{10,9},{11,... | collective-permute-start | bytes 196616 | tf_op jit(solution)/shard_map/ppermute | solution.py:169
  15.2 4.4 %collective-permute-start.4 = (bf16[2,128,128]{2,1,0:T(8,128)(2,1)S(1)}, bf16[2,128,128]{2,1,0:T(8,128)(2,1)S(1)}, u32[]{:S(2)}, u32[]{:S(2)}) collective-permute-start(bf16[2,128,128]{2,1,0:T(8,128)(2,1)S(1)} %get-tuple-element.14), channel_id=1, source_target_pairs={{0,1},{1,0},{2,3},{3,2},{4,5},{5,4},{6,7},{7,6},{8,9},{9,8},{10,11... | collective-permute-start | bytes 196616 | tf_op jit(solution)/shard_map/ppermute | solution.py:173
  15.3 6.2 %copy-start.3 = (f32[128]{0:T(128)S(1)}, f32[128]{0:T(128)}, u32[]{:S(2)}) copy-start(f32[128]{0:T(128)} %param.7) | copy-start | bytes 1540
  15.3 6.2 %collective-permute-start.5 = (bf16[2,128,128]{2,1,0:T(8,128)(2,1)S(1)}, bf16[2,128,128]{2,1,0:T(8,128)(2,1)S(1)}, u32[]{:S(2)}, u32[]{:S(2)}) collective-permute-start(bf16[2,128,128]{2,1,0:T(8,128)(2,1)S(1)} %get-tuple-element.13), channel_id=1, source_target_pairs={{1,2},{2,1},{3,4},{4,3},{5,6},{6,5},{7,8},{8,7},{9,10},{10,9},{11,... | collective-permute-start | bytes 196616 | tf_op jit(solution)/shard_map/ppermute | solution.py:172
  21.5 5.4 %copy-start.2 = (bf16[3,3,3,128,16]{3,4,2,1,0:T(8,128)(2,1)S(1)}, bf16[3,3,3,128,16]{3,4,2,1,0:T(8,128)(2,1)}, u32[]{:S(2)}) copy-start(bf16[3,3,3,128,16]{3,4,2,1,0:T(8,128)(2,1)} %param.8) | copy-start | bytes 331780
  23.0 8.7 %collective-permute-start.7 = (bf16[2,64,128]{2,1,0:T(8,128)(2,1)S(1)}, bf16[2,64,128]{2,1,0:T(8,128)(2,1)S(1)}, u32[]{:S(2)}, u32[]{:S(2)}) collective-permute-start(bf16[2,64,128]{2,1,0:T(8,128)(2,1)S(1)} %shard_map.55), channel_id=1, source_target_pairs={{0,16},{16,0},{32,48},{48,32},{64,80},{80,64},{96,112},{112,96},{1... | collective-permute-start | bytes 98312 | tf_op jit(solution)/shard_map/ppermute | solution.py:188
  23.1 11.4 %collective-permute-start.6 = (bf16[2,64,128]{2,1,0:T(8,128)(2,1)S(1)}, bf16[2,64,128]{2,1,0:T(8,128)(2,1)S(1)}, u32[]{:S(2)}, u32[]{:S(2)}) collective-permute-start(bf16[2,64,128]{2,1,0:T(8,128)(2,1)S(1)} %shard_map.55), channel_id=1, source_target_pairs={{16,32},{32,16},{48,64},{64,48},{80,96},{96,80},{112,128},{128,112... | collective-permute-start | bytes 98312 | tf_op jit(solution)/shard_map/ppermute | solution.py:187
  26.9 12.9 %collective-permute-start.11 = (bf16[27,16,128]{2,1,0:T(8,128)(2,1)S(1)}, bf16[27,16,128]{2,1,0:T(8,128)(2,1)S(1)}, u32[]{:S(2)}, u32[]{:S(2)}) collective-permute-start(bf16[27,16,128]{2,1,0:T(8,128)(2,1)S(1)} %bitcast.25), channel_id=1, source_target_pairs={{0,4},{1,5},{2,6},{3,7},{4,0},{5,1},{6,2},{7,3},{8,12},{9,13},{10,... | collective-permute-start | bytes 331784 | tf_op jit(solution)/shard_map/ppermute | solution.py:185
  28.5 13.5 %collective-permute-start.12 = (bf16[27,16,128]{2,1,0:T(8,128)(2,1)S(1)}, bf16[27,16,128]{2,1,0:T(8,128)(2,1)S(1)}, u32[]{:S(2)}, u32[]{:S(2)}) collective-permute-start(bf16[27,16,128]{2,1,0:T(8,128)(2,1)S(1)} %bitcast.26), channel_id=1, source_target_pairs={{0,8},{1,9},{2,10},{3,11},{4,12},{5,13},{6,14},{7,15},{8,0},{9,1},... | collective-permute-start | bytes 331784 | tf_op jit(solution)/shard_map/ppermute | solution.py:185
  31.4 10.6 %collective-permute-start.13 = (bf16[27,16,128]{2,1,0:T(8,128)(2,1)S(1)}, bf16[27,16,128]{2,1,0:T(8,128)(2,1)S(1)}, u32[]{:S(2)}, u32[]{:S(2)}) collective-permute-start(bf16[27,16,128]{2,1,0:T(8,128)(2,1)S(1)} %bitcast.27), channel_id=1, source_target_pairs={{0,12},{1,13},{2,14},{3,15},{4,8},{5,9},{6,10},{7,11},{8,4},{9,5},... | collective-permute-start | bytes 331784 | tf_op jit(solution)/shard_map/ppermute | solution.py:185
  34.5 7.8 %collective-permute-start.10 = (bf16[3,2,64,128]{3,2,1,0:T(8,128)(2,1)S(1)}, bf16[3,2,64,128]{3,2,1,0:T(8,128)(2,1)S(1)}, u32[]{:S(2)}, u32[]{:S(2)}) collective-permute-start(bf16[3,2,64,128]{3,2,1,0:T(8,128)(2,1)S(1)} %pad_maximum_fusion.p0), channel_id=1, source_target_pairs={{0,3},{1,2},{2,1},{3,0},{4,7},{5,6},{6,5},{7,4},{8,11},{9,10},{10,... | collective-permute-start | bytes 294920 | tf_op jit(solution)/shard_map/ppermute | solution.py:192
  36.5 6.8 %collective-permute-start.8 = (bf16[3,2,64,128]{3,2,1,0:T(8,128)(2,1)S(1)}, bf16[3,2,64,128]{3,2,1,0:T(8,128)(2,1)S(1)}, u32[]{:S(2)}, u32[]{:S(2)}) collective-permute-start(bf16[3,2,64,128]{3,2,1,0:T(8,128)(2,1)S(1)} %pad_maximum_fusion.p0), channel_id=1, source_target_pairs={{0,1},{1,0},{2,3},{3,2},{4,5},{5,4},{6,7},{7,6},{8,9},{9,8},{10,11... | collective-permute-start | bytes 294920 | tf_op jit(solution)/shard_map/ppermute | solution.py:192
  39.8 7.0 %collective-permute-start.9 = (bf16[3,2,64,128]{3,2,1,0:T(8,128)(2,1)S(1)}, bf16[3,2,64,128]{3,2,1,0:T(8,128)(2,1)S(1)}, u32[]{:S(2)}, u32[]{:S(2)}) collective-permute-start(bf16[3,2,64,128]{3,2,1,0:T(8,128)(2,1)S(1)} %pad_maximum_fusion.p0), channel_id=1, source_target_pairs={{0,2},{1,3},{2,0},{3,1},{4,6},{5,7},{6,4},{7,5},{8,10},{9,11},{10,... | collective-permute-start | bytes 294920 | tf_op jit(solution)/shard_map/ppermute | solution.py:192
  47.5 5.7 %collective-permute-start.14 = (f32[16,640]{1,0:T(8,128)S(1)}, f32[16,640]{1,0:T(8,128)S(1)}, u32[]{:S(2)}, u32[]{:S(2)}) collective-permute-start(f32[16,640]{1,0:T(8,128)S(1)} %get-tuple-element.10), channel_id=1, source_target_pairs={{0,4},{1,5},{2,6},{3,7},{4,0},{5,1},{6,2},{7,3},{8,12},{9,13},{10,... | collective-permute-start | bytes 122888 | tf_op jit(solution)/shard_map/ppermute | solution.py:196
  50.4 5.5 %collective-permute-start.15 = (f32[16,640]{1,0:T(8,128)S(1)}, f32[16,640]{1,0:T(8,128)S(1)}, u32[]{:S(2)}, u32[]{:S(2)}) collective-permute-start(f32[16,640]{1,0:T(8,128)S(1)} %get-tuple-element.11), channel_id=1, source_target_pairs={{0,8},{1,9},{2,10},{3,11},{4,12},{5,13},{6,14},{7,15},{8,0},{9,1},... | collective-permute-start | bytes 122888 | tf_op jit(solution)/shard_map/ppermute | solution.py:196
  52.4 5.2 %copy-start.4 = (f32[16]{0:T(128)S(1)}, f32[16]{0:T(128)}, u32[]{:S(2)}) copy-start(f32[16]{0:T(128)} %param.9) | copy-start | bytes 196
  52.4 5.2 %collective-permute-start.16 = (f32[16,640]{1,0:T(8,128)S(1)}, f32[16,640]{1,0:T(8,128)S(1)}, u32[]{:S(2)}, u32[]{:S(2)}) collective-permute-start(f32[16,640]{1,0:T(8,128)S(1)} %get-tuple-element.12), channel_id=1, source_target_pairs={{0,12},{1,13},{2,14},{3,15},{4,8},{5,9},{6,10},{7,11},{8,4},{9,5},... | collective-permute-start | bytes 122888 | tf_op jit(solution)/shard_map/ppermute | solution.py:196

commit v3 on v2

--- a/solution.py
+++ b/solution.py
@@ -15,6 +15,45 @@
 
 def far_pairs(count):
     return [(i, ((i - 1) ^ 1) + 1) for i in range(1, count - 1)]
+
+
+def bridge_pairs():
+    pairs = []
+    for d, e in far_pairs(16):
+        for r in range(16):
+            y, z = r // 4, r % 4
+            if min(d, e) != 7:
+                pairs.append((d * 16 + r, e * 16 + r))
+            elif z in (0, 3):
+                pairs.append((d * 16 + r, e * 16 + y * 4 + 3 - z))
+    return pairs
+
+
+def relay_pairs():
+    pairs = []
+    for d in (7, 8):
+        for y in range(4):
+            for z, t in ((0, 1), (3, 2)):
+                pairs.append((d * 16 + y * 4 + z, d * 16 + y * 4 + t))
+    return pairs
+
+
+def edges_kernel(x1, x2, far_edge, near_edge):
+    pr = lax.rem(lax.axis_index("rows"), 2)
+    for k, side in enumerate((x1, x2)):
+        far_edge[k] = side[3 * pr]
+        near_edge[k] = side[3 - 3 * pr]
+
+def edges(x1, x2):
+    vmem = pl.BlockSpec(memory_space=pltpu.VMEM)
+    edge = jax.ShapeDtypeStruct((2, 128, 128), BF16)
+    return pl.pallas_call(
+        edges_kernel,
+        out_shape=[edge, edge],
+        in_specs=[vmem] * 2,
+        out_specs=[vmem] * 2,
+        compiler_params=pltpu.CompilerParams(vmem_limit_bytes=8 * 1024 * 1024),
+    )(x1, x2)
 
 
 def fine_kernel(vol, x1, x2, r1, r2, c1, c2, w, bias, out, cells, peak):
@@ -78,14 +117,37 @@
     )(vol, x1, x2, r1, r2, c1, c2, w, bias)
 
 
-def coarse_kernel(p0, p1, p2, p3, w0, w1, w2, w3, o0, o1, o2, o3, cells):
+def assemble_kernel(p0, p1, p2, p3, w, plane, kept):
+    for k, piece in enumerate((p0, p1, p2, p3)):
+        plane[k] = piece[...]
+    kept[...] = w[...]
+
+
+def assemble(pieces, w):
+    vmem = pl.BlockSpec(memory_space=pltpu.VMEM)
+    return pl.pallas_call(
+        assemble_kernel,
+        out_shape=[jax.ShapeDtypeStruct((4, 2, 64, 128), BF16), jax.ShapeDtypeStruct(w.shape, BF16)],
+        in_specs=[vmem] * 5,
+        out_specs=[vmem] * 2,
+        compiler_params=pltpu.CompilerParams(vmem_limit_bytes=8 * 1024 * 1024),
+    )(*pieces, w)
+
+
+def coarse_kernel(own, near, far, via, w0, w1, w2, w3, o0, o1, o2, o3, cells):
     pd = lax.rem(lax.axis_index("depth"), 2)
+    d = lax.axis_index("depth")
     z = lax.rem(lax.axis_index("rows"), 4)
+    split = (d == 7) | (d == 8)
+    relayed = split & ((z == 1) | (z == 2))
+    far_z = jnp.where(split, jnp.where(z < 2, 3, 0), z)
     for a in range(3):
         for i in (0, 1, 10, 11):
             cells[a, i] = jnp.zeros((64, 128), BF16)
-    for k, piece in enumerate((p0, p1, p2, p3)):
-        cells[:, pl.ds(2 + 2 * (z ^ k), 2)] = piece[...]
+    for k in range(4):
+        cells[0, pl.ds(2 + 2 * (far_z ^ k), 2)] = jnp.where(relayed, via[k], far[k])
+        cells[1, pl.ds(2 + 2 * (z ^ k), 2)] = own[k]
+        cells[2, pl.ds(2 + 2 * (z ^ k), 2)] = near[k]
     lhs = jnp.concatenate(
         [
             jnp.concatenate(
@@ -168,10 +230,9 @@
     x1 = lax.ppermute(lax.dynamic_index_in_dim(volume, 1 - pd, 0, False), "depth", depth_near)
     r2 = lax.ppermute(lax.dynamic_index_in_dim(volume, 3 * pr, 1, False), "rows", rows_far)
     r1 = lax.ppermute(lax.dynamic_index_in_dim(volume, 3 - 3 * pr, 1, False), "rows", rows_near)
-    sides = jnp.stack([x1, x2])
-    c2 = lax.ppermute(lax.dynamic_index_in_dim(sides, 3 * pr, 1, False), "rows", rows_far)
-    c1 = lax.ppermute(lax.dynamic_index_in_dim(sides, 3 - 3 * pr, 1, False), "rows", rows_near)
-    pooled = fine_level(volume, x1, x2, r1, r2, c1, c2, fine_filters, fine_bias.reshape(1, 128))
+    far_edge, near_edge = edges(x1, x2)
+    c2 = lax.ppermute(far_edge, "rows", rows_far)
+    c1 = lax.ppermute(near_edge, "rows", rows_near)
 
     def along_z(k):
         return [(i, i ^ k) for i in range(16)]
@@ -179,18 +240,23 @@
     def along_y(k):
         return [(i, i ^ (4 * k)) for i in range(16)]
 
+    pooled = fine_level(
+        volume, x1, x2, r1, r2, c1, c2, fine_filters, fine_bias.reshape(1, 128)
+    )
+
+    pieces = [pooled] + [None] * 3
+    for k in (3, 2, 1):
+        pieces[k] = lax.ppermute(pooled, "rows", along_z(k))
     w = jnp.transpose(coarse_filters, (0, 1, 2, 4, 3)).reshape(27, 16, 128)
+    plane, w = assemble(pieces, w)
     weights = [w] + [None] * 3
     for k in (2, 1, 3):
         weights[k] = lax.ppermute(w, "rows", along_y(k))
-
-    far = lax.ppermute(pooled, "depth", depth_far)
-    near = lax.ppermute(pooled, "depth", depth_near)
-    planes = jnp.stack([far, pooled, near])
-    pieces = [planes] + [None] * 3
-    for k in (3, 2, 1):
-        pieces[k] = lax.ppermute(planes, "rows", along_z(k))
-    sums = coarse_level(pieces, weights)
+    both = ("depth", "rows")
+    far = lax.ppermute(plane, both, bridge_pairs())
+    near = lax.ppermute(plane, "depth", depth_near)
+    via = lax.ppermute(far, both, relay_pairs())
+    sums = coarse_level((plane, near, far, via), weights)
     parts = [sums[0]] + [None] * 3
     for k in (2, 1, 3):
         parts[k] = lax.ppermute(sums[k], "rows", along_y(k))

time: 58.6 us -> 68.3 us (1.17)
  the two profiles are of different devices: /device:TPU:192 before, /device:TPU:6 now
where the time goes in v3:
time: 68.3 us; the launch traced here: 67 us
  starting transfers between devices  40.5 us (59%)
  waiting for transfers between devices  21 us (31%)
  Pallas kernels  3.01 us (4%)
  local copies, waits for them, and re-layouts  2.3 us (3%)
    ppermute x1, starting transfers between devices, body(): near = lax.ppermute(plane, 'depth', depth_near)  9.78 us
    ppermute x3, waiting for transfers between devices, body(): weights[k] = lax.ppermute(w, 'rows', along_y(k))  7.4 us
    ppermute x3, starting transfers between devices, body(): weights[k] = lax.ppermute(w, 'rows', along_y(k))  6.72 us
    ppermute x3, starting transfers between devices, body(): pieces[k] = lax.ppermute(pooled, 'rows', along_z(k))  5.86 us
    ppermute x3, waiting for transfers between devices, body(): pieces[k] = lax.ppermute(pooled, 'rows', along_z(k))  5.71 us
    ppermute x3, starting transfers between devices, body(): parts[k] = lax.ppermute(sums[k], 'rows', along_y(k))  4.78 us
    ppermute x1, starting transfers between devices, body(): c1 = lax.ppermute(near_edge, 'rows', rows_near)  4.46 us
    ppermute x1, waiting for transfers between devices, body(): c1 = lax.ppermute(near_edge, 'rows', rows_near)  3.97 us
  transfers between devices with their start and end apart: 18, of which 8 were waited for; matrix products, arithmetic and copies ran while one was open for 0% of the time, Pallas kernels for 0%

profile of v3, /device:TPU:6, one launch (start us, length us, event | category | flops | bytes accessed | tf_op | source)
XLA Modules:
  0.0 67.0 jit_solution(13195600589593725532)
XLA Ops:
  0.0 1.0 %dynamic-slice_bitcast_fusion = (bf16[4,128,128]{2,1,0:T(8,128)(2,1)S(1)}, bf16[4,128,128]{2,1,0:T(8,128)(2,1)S(1)}) fusion(bf16[2,4,128,128]{3,2,1,0:T(8,128)(2,1)} %vol.1, s32[]{:T(128)S(6)} %select_n.15, s32[]{:T(128)S(6)} %select_n.14), kind=kLoop, calls=%fused_computation | loop fusion | bytes 524296 | tf_op jit(solution)/shard_map/jit(dynamic_index_in_dim)/squeeze | solution.py:229
  1.1 2.8 %collective-permute-start.1 = (bf16[4,128,128]{2,1,0:T(8,128)(2,1)S(1)}, bf16[4,128,128]{2,1,0:T(8,128)(2,1)S(1)}, u32[]{:S(2)}, u32[]{:S(2)}) collective-permute-start(bf16[4,128,128]{2,1,0:T(8,128)(2,1)S(1)} %get-tuple-element.23), channel_id=1, source_target_pairs={{16,32},{32,16},{48,64},{64,48},{80,96},{96,80},{112,128},{128,112... | collective-permute-start | bytes 393224 | tf_op jit(solution)/shard_map/ppermute | solution.py:229
  4.0 2.0 %collective-permute-start.2 = (bf16[2,128,128]{2,1,0:T(8,128)(2,1)S(1)}, bf16[2,128,128]{2,1,0:T(8,128)(2,1)S(1)}, u32[]{:S(2)}, u32[]{:S(2)}) collective-permute-start(bf16[2,128,128]{2,1,0:T(8,128)(2,1)S(1)} %get-tuple-element.22), channel_id=1, source_target_pairs={{0,1},{1,0},{2,3},{3,2},{4,5},{5,4},{6,7},{7,6},{8,9},{9,8},{10,11... | collective-permute-start | bytes 196616 | tf_op jit(solution)/shard_map/ppermute | solution.py:232
  6.7 0.7 %collective-permute-done.1.x2 = bf16[4,128,128]{2,1,0:T(8,128)(2,1)S(1)} collective-permute-done((bf16[4,128,128]{2,1,0:T(8,128)(2,1)S(1)}, bf16[4,128,128]{2,1,0:T(8,128)(2,1)S(1)}, u32[]{:S(2)}, u32[]{:S(2)}) %collective-permute-start.1) | collective-permute-done | bytes 131104 | tf_op jit(solution)/shard_map/ppermute | solution.py:229
  7.4 4.5 %collective-permute-start.4 = (bf16[2,128,128]{2,1,0:T(8,128)(2,1)S(1)}, bf16[2,128,128]{2,1,0:T(8,128)(2,1)S(1)}, u32[]{:S(2)}, u32[]{:S(2)}) collective-permute-start(bf16[2,128,128]{2,1,0:T(8,128)(2,1)S(1)} %get-tuple-element.13), channel_id=1, source_target_pairs={{0,1},{1,0},{2,3},{3,2},{4,5},{5,4},{6,7},{7,6},{8,9},{9,8},{10,11... | collective-permute-start | bytes 196616 | tf_op jit(solution)/shard_map/ppermute | solution.py:235
  11.9 0.8 %collective-permute-start.5 = (bf16[2,128,128]{2,1,0:T(8,128)(2,1)S(1)}, bf16[2,128,128]{2,1,0:T(8,128)(2,1)S(1)}, u32[]{:S(2)}, u32[]{:S(2)}) collective-permute-start(bf16[2,128,128]{2,1,0:T(8,128)(2,1)S(1)} %get-tuple-element.14), channel_id=1, source_target_pairs={{1,2},{2,1},{3,4},{4,3},{5,6},{6,5},{7,8},{8,7},{9,10},{10,9},{11,... | collective-permute-start | bytes 196616 | tf_op jit(solution)/shard_map/ppermute | solution.py:234
  12.7 4.0 %collective-permute-done.4.c1 = bf16[2,128,128]{2,1,0:T(8,128)(2,1)S(1)} collective-permute-done((bf16[2,128,128]{2,1,0:T(8,128)(2,1)S(1)}, bf16[2,128,128]{2,1,0:T(8,128)(2,1)S(1)}, u32[]{:S(2)}, u32[]{:S(2)}) %collective-permute-start.4) | collective-permute-done | bytes 65568 | tf_op jit(solution)/shard_map/ppermute | solution.py:235
  16.7 1.2 %copy-done.1 = bf16[3,3,3,128,128]{4,3,2,1,0:T(8,128)(2,1)S(1)} copy-done((bf16[3,3,3,128,128]{4,3,2,1,0:T(8,128)(2,1)S(1)}, bf16[3,3,3,128,128]{4,3,2,1,0:T(8,128)(2,1)}, u32[]{:S(2)}) %copy-start.1) | copy-done | bytes 884760
  17.9 1.5 %shard_map.56.p0 = bf16[2,64,128]{2,1,0:T(8,128)(2,1)S(1)} custom-call(bf16[2,4,128,128]{3,2,1,0:T(8,128)(2,1)S(1)} %copy-done, bf16[4,128,128]{2,1,0:T(8,128)(2,1)S(1)} %collective-permute-done.x1, bf16[4,128,128]{2,1,0:T(8,128)(2,1)S(1)} %collective-permute-done.1.x2, bf16[2,128,128]{2,1,0:T(8,128)(2,1)S(1)} %collective-permute-done.2.r1, ...), custom_call_target="tpu_custom_call" | custom-call | tf_op jit(solution)/shard_map/pallas_call | solution.py:110
  19.4 1.7 %collective-permute-start.6 = (bf16[2,64,128]{2,1,0:T(8,128)(2,1)S(1)}, bf16[2,64,128]{2,1,0:T(8,128)(2,1)S(1)}, u32[]{:S(2)}, u32[]{:S(2)}) collective-permute-start(bf16[2,64,128]{2,1,0:T(8,128)(2,1)S(1)} %shard_map.56.p0), channel_id=1, source_target_pairs={{0,1},{1,0},{2,3},{3,2},{4,5},{5,4},{6,7},{7,6},{8,9},{9,8},{10,11... | collective-permute-start | bytes 98312 | tf_op jit(solution)/shard_map/ppermute | solution.py:249
  21.1 4.2 %collective-permute-start.7 = (bf16[2,64,128]{2,1,0:T(8,128)(2,1)S(1)}, bf16[2,64,128]{2,1,0:T(8,128)(2,1)S(1)}, u32[]{:S(2)}, u32[]{:S(2)}) collective-permute-start(bf16[2,64,128]{2,1,0:T(8,128)(2,1)S(1)} %shard_map.56.p0), channel_id=1, source_target_pairs={{0,2},{1,3},{2,0},{3,1},{4,6},{5,7},{6,4},{7,5},{8,10},{9,11},{10,... | collective-permute-start | bytes 98312 | tf_op jit(solution)/shard_map/ppermute | solution.py:249
  25.2 2.1 %collective-permute-done.7.p2 = bf16[2,64,128]{2,1,0:T(8,128)(2,1)S(1)} collective-permute-done((bf16[2,64,128]{2,1,0:T(8,128)(2,1)S(1)}, bf16[2,64,128]{2,1,0:T(8,128)(2,1)S(1)}, u32[]{:S(2)}, u32[]{:S(2)}) %collective-permute-start.7) | collective-permute-done | bytes 32800 | tf_op jit(solution)/shard_map/ppermute | solution.py:249
  27.3 3.6 %collective-permute-done.8.p3 = bf16[2,64,128]{2,1,0:T(8,128)(2,1)S(1)} collective-permute-done((bf16[2,64,128]{2,1,0:T(8,128)(2,1)S(1)}, bf16[2,64,128]{2,1,0:T(8,128)(2,1)S(1)}, u32[]{:S(2)}, u32[]{:S(2)}) %collective-permute-start.8) | collective-permute-done | bytes 32800 | tf_op jit(solution)/shard_map/ppermute | solution.py:249
  31.0 1.9 %collective-permute-start.10 = (bf16[4,2,64,128]{3,2,1,0:T(8,128)(2,1)S(1)}, bf16[4,2,64,128]{3,2,1,0:T(8,128)(2,1)S(1)}, u32[]{:S(2)}, u32[]{:S(2)}) collective-permute-start(bf16[4,2,64,128]{3,2,1,0:T(8,128)(2,1)S(1)} %get-tuple-element.15.own), channel_id=1, source_target_pairs={{16,32},{17,33},{18,34},{19,35},{20,36},{21,37},{22,38},{23,39},{2... | collective-permute-start | bytes 393224 | tf_op jit(solution)/shard_map/ppermute | solution.py:256
  32.9 9.8 %collective-permute-start.9 = (bf16[4,2,64,128]{3,2,1,0:T(8,128)(2,1)S(1)}, bf16[4,2,64,128]{3,2,1,0:T(8,128)(2,1)S(1)}, u32[]{:S(2)}, u32[]{:S(2)}) collective-permute-start(bf16[4,2,64,128]{3,2,1,0:T(8,128)(2,1)S(1)} %get-tuple-element.15.own), channel_id=1, source_target_pairs={{0,16},{16,0},{32,48},{48,32},{64,80},{80,64},{96,112},{112,96},{1... | collective-permute-start | bytes 393224 | tf_op jit(solution)/shard_map/ppermute | solution.py:257
  43.3 3.9 %collective-permute-start.12 = (bf16[27,16,128]{2,1,0:T(8,128)(2,1)S(1)}, bf16[27,16,128]{2,1,0:T(8,128)(2,1)S(1)}, u32[]{:S(2)}, u32[]{:S(2)}) collective-permute-start(bf16[27,16,128]{2,1,0:T(8,128)(2,1)S(1)} %get-tuple-element.16.w0), channel_id=1, source_target_pairs={{0,4},{1,5},{2,6},{3,7},{4,0},{5,1},{6,2},{7,3},{8,12},{9,13},{10,... | collective-permute-start | bytes 331784 | tf_op jit(solution)/shard_map/ppermute | solution.py:254
  47.3 2.4 %collective-permute-start.13 = (bf16[27,16,128]{2,1,0:T(8,128)(2,1)S(1)}, bf16[27,16,128]{2,1,0:T(8,128)(2,1)S(1)}, u32[]{:S(2)}, u32[]{:S(2)}) collective-permute-start(bf16[27,16,128]{2,1,0:T(8,128)(2,1)S(1)} %get-tuple-element.16.w0), channel_id=1, source_target_pairs={{0,8},{1,9},{2,10},{3,11},{4,12},{5,13},{6,14},{7,15},{8,0},{9,1},... | collective-permute-start | bytes 331784 | tf_op jit(solution)/shard_map/ppermute | solution.py:254
  50.1 3.6 %collective-permute-done.13.w2 = bf16[27,16,128]{2,1,0:T(8,128)(2,1)S(1)} collective-permute-done((bf16[27,16,128]{2,1,0:T(8,128)(2,1)S(1)}, bf16[27,16,128]{2,1,0:T(8,128)(2,1)S(1)}, u32[]{:S(2)}, u32[]{:S(2)}) %collective-permute-start.13) | collective-permute-done | bytes 110624 | tf_op jit(solution)/shard_map/ppermute | solution.py:254
  53.7 3.8 %collective-permute-done.14.w3 = bf16[27,16,128]{2,1,0:T(8,128)(2,1)S(1)} collective-permute-done((bf16[27,16,128]{2,1,0:T(8,128)(2,1)S(1)}, bf16[27,16,128]{2,1,0:T(8,128)(2,1)S(1)}, u32[]{:S(2)}, u32[]{:S(2)}) %collective-permute-start.14) | collective-permute-done | bytes 110624 | tf_op jit(solution)/shard_map/ppermute | solution.py:254
  57.5 0.8 %shard_map.58 = (f32[16,640]{1,0:T(8,128)S(1)}, f32[16,640]{1,0:T(8,128)S(1)}, f32[16,640]{1,0:T(8,128)S(1)}, f32[16,640]{1,0:T(8,128)S(1)}) custom-call(bf16[4,2,64,128]{3,2,1,0:T(8,128)(2,1)S(1)} %get-tuple-element.15.own, bf16[4,2,64,128]{3,2,1,0:T(8,128)(2,1)S(1)} %collective-permute-done.9.near, ...), custom_call_target="tpu_custom_call" | custom-call | tf_op jit(solution)/shard_map/pallas_call | solution.py:183
  58.4 2.7 %collective-permute-start.16 = (f32[16,640]{1,0:T(8,128)S(1)}, f32[16,640]{1,0:T(8,128)S(1)}, u32[]{:S(2)}, u32[]{:S(2)}) collective-permute-start(f32[16,640]{1,0:T(8,128)S(1)} %get-tuple-element.19), channel_id=1, source_target_pairs={{0,8},{1,9},{2,10},{3,11},{4,12},{5,13},{6,14},{7,15},{8,0},{9,1},... | collective-permute-start | bytes 122888 | tf_op jit(solution)/shard_map/ppermute | solution.py:262
  61.1 2.0 %collective-permute-start.17 = (f32[16,640]{1,0:T(8,128)S(1)}, f32[16,640]{1,0:T(8,128)S(1)}, u32[]{:S(2)}, u32[]{:S(2)}) collective-permute-start(f32[16,640]{1,0:T(8,128)S(1)} %get-tuple-element.20), channel_id=1, source_target_pairs={{0,12},{1,13},{2,14},{3,15},{4,8},{5,9},{6,10},{7,11},{8,4},{9,5},... | collective-permute-start | bytes 122888 | tf_op jit(solution)/shard_map/ppermute | solution.py:262
  63.1 0.9 %collective-permute-done.16.s2 = f32[16,640]{1,0:T(8,128)S(1)} collective-permute-done((f32[16,640]{1,0:T(8,128)S(1)}, f32[16,640]{1,0:T(8,128)S(1)}, u32[]{:S(2)}, u32[]{:S(2)}) %collective-permute-start.16) | collective-permute-done | bytes 40992 | tf_op jit(solution)/shard_map/ppermute | solution.py:262
  64.0 2.3 %collective-permute-done.17.s3 = f32[16,640]{1,0:T(8,128)S(1)} collective-permute-done((f32[16,640]{1,0:T(8,128)S(1)}, f32[16,640]{1,0:T(8,128)S(1)}, u32[]{:S(2)}, u32[]{:S(2)}) %collective-permute-start.17) | collective-permute-done | bytes 40992 | tf_op jit(solution)/shard_map/ppermute | solution.py:262
  (30 shorter events, 2.7 us)
Async XLA Ops:
  0.0 4.0 %copy-start = (bf16[2,4,128,128]{3,2,1,0:T(8,128)(2,1)S(1)}, bf16[2,4,128,128]{3,2,1,0:T(8,128)(2,1)}, u32[]{:S(2)}) copy-start(bf16[2,4,128,128]{3,2,1,0:T(8,128)(2,1)} %vol.1) | copy-start | bytes 786436
  1.0 5.6 %collective-permute-start = (bf16[4,128,128]{2,1,0:T(8,128)(2,1)S(1)}, bf16[4,128,128]{2,1,0:T(8,128)(2,1)S(1)}, u32[]{:S(2)}, u32[]{:S(2)}) collective-permute-start(bf16[4,128,128]{2,1,0:T(8,128)(2,1)S(1)} %get-tuple-element.24), channel_id=1, source_target_pairs={{0,16},{16,0},{32,48},{48,32},{64,80},{80,64},{96,112},{112,96},{1... | collective-permute-start | bytes 393224 | tf_op jit(solution)/shard_map/ppermute | solution.py:230
  1.1 6.3 %collective-permute-start.1 = (bf16[4,128,128]{2,1,0:T(8,128)(2,1)S(1)}, bf16[4,128,128]{2,1,0:T(8,128)(2,1)S(1)}, u32[]{:S(2)}, u32[]{:S(2)}) collective-permute-start(bf16[4,128,128]{2,1,0:T(8,128)(2,1)S(1)} %get-tuple-element.23), channel_id=1, source_target_pairs={{16,32},{32,16},{48,64},{64,48},{80,96},{96,80},{112,128},{128,112... | collective-permute-start | bytes 393224 | tf_op jit(solution)/shard_map/ppermute | solution.py:229
  4.0 8.7 %collective-permute-start.2 = (bf16[2,128,128]{2,1,0:T(8,128)(2,1)S(1)}, bf16[2,128,128]{2,1,0:T(8,128)(2,1)S(1)}, u32[]{:S(2)}, u32[]{:S(2)}) collective-permute-start(bf16[2,128,128]{2,1,0:T(8,128)(2,1)S(1)} %get-tuple-element.22), channel_id=1, source_target_pairs={{0,1},{1,0},{2,3},{3,2},{4,5},{5,4},{6,7},{7,6},{8,9},{9,8},{10,11... | collective-permute-start | bytes 196616 | tf_op jit(solution)/shard_map/ppermute | solution.py:232
  6.0 6.7 %collective-permute-start.3 = (bf16[2,128,128]{2,1,0:T(8,128)(2,1)S(1)}, bf16[2,128,128]{2,1,0:T(8,128)(2,1)S(1)}, u32[]{:S(2)}, u32[]{:S(2)}) collective-permute-start(bf16[2,128,128]{2,1,0:T(8,128)(2,1)S(1)} %get-tuple-element.21), channel_id=1, source_target_pairs={{1,2},{2,1},{3,4},{4,3},{5,6},{6,5},{7,8},{8,7},{9,10},{10,9},{11,... | collective-permute-start | bytes 196616 | tf_op jit(solution)/shard_map/ppermute | solution.py:231
  7.4 9.2 %collective-permute-start.4 = (bf16[2,128,128]{2,1,0:T(8,128)(2,1)S(1)}, bf16[2,128,128]{2,1,0:T(8,128)(2,1)S(1)}, u32[]{:S(2)}, u32[]{:S(2)}) collective-permute-start(bf16[2,128,128]{2,1,0:T(8,128)(2,1)S(1)} %get-tuple-element.13), channel_id=1, source_target_pairs={{0,1},{1,0},{2,3},{3,2},{4,5},{5,4},{6,7},{7,6},{8,9},{9,8},{10,11... | collective-permute-start | bytes 196616 | tf_op jit(solution)/shard_map/ppermute | solution.py:235
  11.9 4.8 %copy-start.3 = (f32[128]{0:T(128)S(1)}, f32[128]{0:T(128)}, u32[]{:S(2)}) copy-start(f32[128]{0:T(128)} %param.7) | copy-start | bytes 1540
  11.9 4.8 %collective-permute-start.5 = (bf16[2,128,128]{2,1,0:T(8,128)(2,1)S(1)}, bf16[2,128,128]{2,1,0:T(8,128)(2,1)S(1)}, u32[]{:S(2)}, u32[]{:S(2)}) collective-permute-start(bf16[2,128,128]{2,1,0:T(8,128)(2,1)S(1)} %get-tuple-element.14), channel_id=1, source_target_pairs={{1,2},{2,1},{3,4},{4,3},{5,6},{6,5},{7,8},{8,7},{9,10},{10,9},{11,... | collective-permute-start | bytes 196616 | tf_op jit(solution)/shard_map/ppermute | solution.py:234
  16.7 1.2 %copy-start.1 = (bf16[3,3,3,128,128]{4,3,2,1,0:T(8,128)(2,1)S(1)}, bf16[3,3,3,128,128]{4,3,2,1,0:T(8,128)(2,1)}, u32[]{:S(2)}) copy-start(bf16[3,3,3,128,128]{4,3,2,1,0:T(8,128)(2,1)} %w.1) | copy-start | bytes 2654212
  17.9 13.1 %copy-start.2 = (bf16[3,3,3,128,16]{3,4,2,1,0:T(8,128)(2,1)S(1)}, bf16[3,3,3,128,16]{3,4,2,1,0:T(8,128)(2,1)}, u32[]{:S(2)}) copy-start(bf16[3,3,3,128,16]{3,4,2,1,0:T(8,128)(2,1)} %param.8) | copy-start | bytes 331780
  19.4 5.9 %collective-permute-start.6 = (bf16[2,64,128]{2,1,0:T(8,128)(2,1)S(1)}, bf16[2,64,128]{2,1,0:T(8,128)(2,1)S(1)}, u32[]{:S(2)}, u32[]{:S(2)}) collective-permute-start(bf16[2,64,128]{2,1,0:T(8,128)(2,1)S(1)} %shard_map.56.p0), channel_id=1, source_target_pairs={{0,1},{1,0},{2,3},{3,2},{4,5},{5,4},{6,7},{7,6},{8,9},{9,8},{10,11... | collective-permute-start | bytes 98312 | tf_op jit(solution)/shard_map/ppermute | solution.py:249
  21.1 6.3 %collective-permute-start.7 = (bf16[2,64,128]{2,1,0:T(8,128)(2,1)S(1)}, bf16[2,64,128]{2,1,0:T(8,128)(2,1)S(1)}, u32[]{:S(2)}, u32[]{:S(2)}) collective-permute-start(bf16[2,64,128]{2,1,0:T(8,128)(2,1)S(1)} %shard_map.56.p0), channel_id=1, source_target_pairs={{0,2},{1,3},{2,0},{3,1},{4,6},{5,7},{6,4},{7,5},{8,10},{9,11},{10,... | collective-permute-start | bytes 98312 | tf_op jit(solution)/shard_map/ppermute | solution.py:249
  25.2 5.7 %collective-permute-start.8 = (bf16[2,64,128]{2,1,0:T(8,128)(2,1)S(1)}, bf16[2,64,128]{2,1,0:T(8,128)(2,1)S(1)}, u32[]{:S(2)}, u32[]{:S(2)}) collective-permute-start(bf16[2,64,128]{2,1,0:T(8,128)(2,1)S(1)} %shard_map.56.p0), channel_id=1, source_target_pairs={{0,3},{1,2},{2,1},{3,0},{4,7},{5,6},{6,5},{7,4},{8,11},{9,10},{10,... | collective-permute-start | bytes 98312 | tf_op jit(solution)/shard_map/ppermute | solution.py:249
  31.0 11.7 %collective-permute-start.10 = (bf16[4,2,64,128]{3,2,1,0:T(8,128)(2,1)S(1)}, bf16[4,2,64,128]{3,2,1,0:T(8,128)(2,1)S(1)}, u32[]{:S(2)}, u32[]{:S(2)}) collective-permute-start(bf16[4,2,64,128]{3,2,1,0:T(8,128)(2,1)S(1)} %get-tuple-element.15.own), channel_id=1, source_target_pairs={{16,32},{17,33},{18,34},{19,35},{20,36},{21,37},{22,38},{23,39},{2... | collective-permute-start | bytes 393224 | tf_op jit(solution)/shard_map/ppermute | solution.py:256
  32.9 24.6 %collective-permute-start.9 = (bf16[4,2,64,128]{3,2,1,0:T(8,128)(2,1)S(1)}, bf16[4,2,64,128]{3,2,1,0:T(8,128)(2,1)S(1)}, u32[]{:S(2)}, u32[]{:S(2)}) collective-permute-start(bf16[4,2,64,128]{3,2,1,0:T(8,128)(2,1)S(1)} %get-tuple-element.15.own), channel_id=1, source_target_pairs={{0,16},{16,0},{32,48},{48,32},{64,80},{80,64},{96,112},{112,96},{1... | collective-permute-start | bytes 393224 | tf_op jit(solution)/shard_map/ppermute | solution.py:257
  42.7 14.8 %collective-permute-start.11 = (bf16[4,2,64,128]{3,2,1,0:T(8,128)(2,1)S(1)}, bf16[4,2,64,128]{3,2,1,0:T(8,128)(2,1)S(1)}, u32[]{:S(2)}, u32[]{:S(2)}) collective-permute-start(bf16[4,2,64,128]{3,2,1,0:T(8,128)(2,1)S(1)} %collective-permute-done.10.far), channel_id=1, source_target_pairs={{112,113},{115,114},{116,117},{119,118},{120,121},{123,122},{124,1... | collective-permute-start | bytes 393224 | tf_op jit(solution)/shard_map/ppermute | solution.py:258
  43.3 6.7 %collective-permute-start.12 = (bf16[27,16,128]{2,1,0:T(8,128)(2,1)S(1)}, bf16[27,16,128]{2,1,0:T(8,128)(2,1)S(1)}, u32[]{:S(2)}, u32[]{:S(2)}) collective-permute-start(bf16[27,16,128]{2,1,0:T(8,128)(2,1)S(1)} %get-tuple-element.16.w0), channel_id=1, source_target_pairs={{0,4},{1,5},{2,6},{3,7},{4,0},{5,1},{6,2},{7,3},{8,12},{9,13},{10,... | collective-permute-start | bytes 331784 | tf_op jit(solution)/shard_map/ppermute | solution.py:254
  47.3 6.4 %collective-permute-start.13 = (bf16[27,16,128]{2,1,0:T(8,128)(2,1)S(1)}, bf16[27,16,128]{2,1,0:T(8,128)(2,1)S(1)}, u32[]{:S(2)}, u32[]{:S(2)}) collective-permute-start(bf16[27,16,128]{2,1,0:T(8,128)(2,1)S(1)} %get-tuple-element.16.w0), channel_id=1, source_target_pairs={{0,8},{1,9},{2,10},{3,11},{4,12},{5,13},{6,14},{7,15},{8,0},{9,1},... | collective-permute-start | bytes 331784 | tf_op jit(solution)/shard_map/ppermute | solution.py:254
  49.7 7.8 %collective-permute-start.14 = (bf16[27,16,128]{2,1,0:T(8,128)(2,1)S(1)}, bf16[27,16,128]{2,1,0:T(8,128)(2,1)S(1)}, u32[]{:S(2)}, u32[]{:S(2)}) collective-permute-start(bf16[27,16,128]{2,1,0:T(8,128)(2,1)S(1)} %get-tuple-element.16.w0), channel_id=1, source_target_pairs={{0,12},{1,13},{2,14},{3,15},{4,8},{5,9},{6,10},{7,11},{8,4},{9,5},... | collective-permute-start | bytes 331784 | tf_op jit(solution)/shard_map/ppermute | solution.py:254
  58.3 4.8 %collective-permute-start.15 = (f32[16,640]{1,0:T(8,128)S(1)}, f32[16,640]{1,0:T(8,128)S(1)}, u32[]{:S(2)}, u32[]{:S(2)}) collective-permute-start(f32[16,640]{1,0:T(8,128)S(1)} %get-tuple-element.18), channel_id=1, source_target_pairs={{0,4},{1,5},{2,6},{3,7},{4,0},{5,1},{6,2},{7,3},{8,12},{9,13},{10,... | collective-permute-start | bytes 122888 | tf_op jit(solution)/shard_map/ppermute | solution.py:262
  58.4 5.6 %collective-permute-start.16 = (f32[16,640]{1,0:T(8,128)S(1)}, f32[16,640]{1,0:T(8,128)S(1)}, u32[]{:S(2)}, u32[]{:S(2)}) collective-permute-start(f32[16,640]{1,0:T(8,128)S(1)} %get-tuple-element.19), channel_id=1, source_target_pairs={{0,8},{1,9},{2,10},{3,11},{4,12},{5,13},{6,14},{7,15},{8,0},{9,1},... | collective-permute-start | bytes 122888 | tf_op jit(solution)/shard_map/ppermute | solution.py:262
  61.0 5.2 %copy-start.4 = (f32[16]{0:T(128)S(1)}, f32[16]{0:T(128)}, u32[]{:S(2)}) copy-start(f32[16]{0:T(128)} %param.9) | copy-start | bytes 196
  61.1 5.2 %collective-permute-start.17 = (f32[16,640]{1,0:T(8,128)S(1)}, f32[16,640]{1,0:T(8,128)S(1)}, u32[]{:S(2)}, u32[]{:S(2)}) collective-permute-start(f32[16,640]{1,0:T(8,128)S(1)} %get-tuple-element.20), channel_id=1, source_target_pairs={{0,12},{1,13},{2,14},{3,15},{4,8},{5,9},{6,10},{7,11},{8,4},{9,5},... | collective-permute-start | bytes 122888 | tf_op jit(solution)/shard_map/ppermute | solution.py:262

commit v4 on v2

--- a/solution.py
+++ b/solution.py
@@ -14,12 +14,20 @@
 
 
 def far_pairs(count):
-    return [(i, ((i - 1) ^ 1) + 1) for i in range(1, count - 1)]
+    return [(i, min(max(((i - 1) ^ 1) + 1, 0), count - 1)) for i in range(count)]
+
+
+def inner(axis):
+    i = lax.axis_index(axis)
+    return (i > 0) & (i < 15)
 
 
 def fine_kernel(vol, x1, x2, r1, r2, c1, c2, w, bias, out, cells, peak):
     pd = lax.rem(lax.axis_index("depth"), 2)
     pr = lax.rem(lax.axis_index("rows"), 2)
+    inner_d = inner("depth")
+    inner_r = inner("rows")
+    zero = jnp.zeros((128, 128), BF16)
     for j in range(4):
         for i in range(6):
             row = (i - 1) + pr * (5 - 2 * i)
@@ -29,6 +37,10 @@
             else:
                 side, slot = (x2, 1) if j == 0 else (x1, 0)
                 piece = c2[slot] if i == 0 else c1[slot] if i == 5 else side[row]
+            if i == 0:
+                piece = jnp.where(inner_r, piece, zero)
+            if j == 0:
+                piece = jnp.where(inner_d, piece, zero)
             cells[j, i] = piece
     taps = [(a, b) for a in range(3) for b in range(3)]
     groups = [taps[i : i + 2] for i in range(0, 9, 2)]
@@ -78,14 +90,34 @@
     )(vol, x1, x2, r1, r2, c1, c2, w, bias)
 
 
-def coarse_kernel(p0, p1, p2, p3, w0, w1, w2, w3, o0, o1, o2, o3, cells):
+def assemble_kernel(p0, p1, p2, p3, w, plane, kept):
+    for k, piece in enumerate((p0, p1, p2, p3)):
+        plane[k] = piece[...]
+    kept[...] = w[...]
+
+
+def assemble(pieces, w):
+    vmem = pl.BlockSpec(memory_space=pltpu.VMEM)
+    return pl.pallas_call(
+        assemble_kernel,
+        out_shape=[jax.ShapeDtypeStruct((4, 2, 64, 128), BF16), jax.ShapeDtypeStruct(w.shape, BF16)],
+        in_specs=[vmem] * 5,
+        out_specs=[vmem] * 2,
+        compiler_params=pltpu.CompilerParams(vmem_limit_bytes=8 * 1024 * 1024),
+    )(*pieces, w)
+
+
+def coarse_kernel(own, near, far, w0, w1, w2, w3, o0, o1, o2, o3, cells):
     pd = lax.rem(lax.axis_index("depth"), 2)
     z = lax.rem(lax.axis_index("rows"), 4)
+    inner_d = inner("depth")
     for a in range(3):
         for i in (0, 1, 10, 11):
             cells[a, i] = jnp.zeros((64, 128), BF16)
-    for k, piece in enumerate((p0, p1, p2, p3)):
-        cells[:, pl.ds(2 + 2 * (z ^ k), 2)] = piece[...]
+    for k in range(4):
+        cells[0, pl.ds(2 + 2 * (z ^ k), 2)] = jnp.where(inner_d, far[k], jnp.zeros_like(far[k]))
+        cells[1, pl.ds(2 + 2 * (z ^ k), 2)] = own[k]
+        cells[2, pl.ds(2 + 2 * (z ^ k), 2)] = near[k]
     lhs = jnp.concatenate(
         [
             jnp.concatenate(
@@ -121,7 +153,7 @@
     return pl.pallas_call(
         coarse_kernel,
         out_shape=[jax.ShapeDtypeStruct((16, 640), F32)] * 4,
-        in_specs=[vmem] * 8,
+        in_specs=[vmem] * 7,
         out_specs=[vmem] * 4,
         scratch_shapes=[pltpu.VMEM((3, 12, 64, 128), BF16)],
         compiler_params=pltpu.CompilerParams(vmem_limit_bytes=32 * 1024 * 1024),
@@ -171,7 +203,6 @@
     sides = jnp.stack([x1, x2])
     c2 = lax.ppermute(lax.dynamic_index_in_dim(sides, 3 * pr, 1, False), "rows", rows_far)
     c1 = lax.ppermute(lax.dynamic_index_in_dim(sides, 3 - 3 * pr, 1, False), "rows", rows_near)
-    pooled = fine_level(volume, x1, x2, r1, r2, c1, c2, fine_filters, fine_bias.reshape(1, 128))
 
     def along_z(k):
         return [(i, i ^ k) for i in range(16)]
@@ -179,18 +210,21 @@
     def along_y(k):
         return [(i, i ^ (4 * k)) for i in range(16)]
 
+    pooled = fine_level(
+        volume, x1, x2, r1, r2, c1, c2, fine_filters, fine_bias.reshape(1, 128)
+    )
+
+    pieces = [pooled] + [None] * 3
+    for k in (3, 2, 1):
+        pieces[k] = lax.ppermute(pooled, "rows", along_z(k))
     w = jnp.transpose(coarse_filters, (0, 1, 2, 4, 3)).reshape(27, 16, 128)
+    plane, w = assemble(pieces, w)
     weights = [w] + [None] * 3
     for k in (2, 1, 3):
         weights[k] = lax.ppermute(w, "rows", along_y(k))
-
-    far = lax.ppermute(pooled, "depth", depth_far)
-    near = lax.ppermute(pooled, "depth", depth_near)
-    planes = jnp.stack([far, pooled, near])
-    pieces = [planes] + [None] * 3
-    for k in (3, 2, 1):
-        pieces[k] = lax.ppermute(planes, "rows", along_z(k))
-    sums = coarse_level(pieces, weights)
+    far = lax.ppermute(plane, "depth", depth_far)
+    near = lax.ppermute(plane, "depth", depth_near)
+    sums = coarse_level((plane, near, far), weights)
     parts = [sums[0]] + [None] * 3
     for k in (2, 1, 3):
         parts[k] = lax.ppermute(sums[k], "rows", along_y(k))

time: 58.6 us -> 66.5 us (1.13)
  the two profiles are of different devices: /device:TPU:192 before, /device:TPU:6 now
where the time goes in v4:
time: 66.5 us; the launch traced here: 66.3 us
  starting transfers between devices  41.4 us (62%)
  waiting for transfers between devices  20.6 us (31%)
  Pallas kernels  3.02 us (5%)
  local copies, waits for them, and re-layouts  1.19 us (2%)
    ppermute x1, starting transfers between devices, body(): near = lax.ppermute(plane, 'depth', depth_near)  12.7 us
    ppermute x3, waiting for transfers between devices, body(): weights[k] = lax.ppermute(w, 'rows', along_y(k))  6.95 us
    ppermute x3, starting transfers between devices, body(): pieces[k] = lax.ppermute(pooled, 'rows', along_z(k))  5.84 us
    ppermute x3, waiting for transfers between devices, body(): pieces[k] = lax.ppermute(pooled, 'rows', along_z(k))  5.71 us
    ppermute x3, starting transfers between devices, body(): weights[k] = lax.ppermute(w, 'rows', along_y(k))  5.29 us
    ppermute x3, starting transfers between devices, body(): parts[k] = lax.ppermute(sums[k], 'rows', along_y(k))  4.79 us
    ppermute x1, starting transfers between devices, body(): lax.ppermute(lax.dynamic_index_in_dim(sides, 3 - 3 * pr, 1, False), 'rows...  4.46 us
    ppermute x1, waiting for transfers between devices, body(): lax.ppermute(lax.dynamic_index_in_dim(sides, 3 - 3 * pr, 1, False), 'rows...  3.97 us
  transfers between devices with their start and end apart: 17, of which 9 were waited for; matrix products, arithmetic and copies ran while one was open for 0% of the time, Pallas kernels for 0%

profile of v4, /device:TPU:6, one launch (start us, length us, event | category | flops | bytes accessed | tf_op | source)
XLA Modules:
  0.0 66.3 jit_solution(14798363003822910657)
XLA Ops:
  0.0 1.1 %dynamic-slice_bitcast_fusion = (bf16[4,128,128]{2,1,0:T(8,128)(2,1)S(1)}, bf16[4,128,128]{2,1,0:T(8,128)(2,1)S(1)}) fusion(bf16[2,4,128,128]{3,2,1,0:T(8,128)(2,1)} %vol.1, s32[]{:T(128)S(6)} %select_n.17, s32[]{:T(128)S(6)} %select_n.16), kind=kLoop, calls=%fused_computation.4 | loop fusion | bytes 524296 | tf_op jit(solution)/shard_map/jit(dynamic_index_in_dim)/squeeze | solution.py:199
  1.2 2.8 %collective-permute-start.1 = (bf16[4,128,128]{2,1,0:T(8,128)(2,1)S(1)}, bf16[4,128,128]{2,1,0:T(8,128)(2,1)S(1)}, u32[]{:S(2)}, u32[]{:S(2)}) collective-permute-start(bf16[4,128,128]{2,1,0:T(8,128)(2,1)S(1)} %get-tuple-element.21), channel_id=1, source_target_pairs={{0,0},{16,32},{32,16},{48,64},{64,48},{80,96},{96,80},{112,128},{1... | collective-permute-start | bytes 393224 | tf_op jit(solution)/shard_map/ppermute | solution.py:199
  4.1 2.0 %collective-permute-start.2 = (bf16[2,128,128]{2,1,0:T(8,128)(2,1)S(1)}, bf16[2,128,128]{2,1,0:T(8,128)(2,1)S(1)}, u32[]{:S(2)}, u32[]{:S(2)}) collective-permute-start(bf16[2,128,128]{2,1,0:T(8,128)(2,1)S(1)} %get-tuple-element.20), channel_id=1, source_target_pairs={{0,1},{1,0},{2,3},{3,2},{4,5},{5,4},{6,7},{7,6},{8,9},{9,8},{10,11... | collective-permute-start | bytes 196616 | tf_op jit(solution)/shard_map/ppermute | solution.py:202
  6.7 0.7 %collective-permute-done.1.x2 = bf16[4,128,128]{2,1,0:T(8,128)(2,1)S(1)} collective-permute-done((bf16[4,128,128]{2,1,0:T(8,128)(2,1)S(1)}, bf16[4,128,128]{2,1,0:T(8,128)(2,1)S(1)}, u32[]{:S(2)}, u32[]{:S(2)}) %collective-permute-start.1) | collective-permute-done | bytes 131104 | tf_op jit(solution)/shard_map/ppermute | solution.py:199
  7.5 4.5 %collective-permute-start.4 = (bf16[2,128,128]{2,1,0:T(8,128)(2,1)S(1)}, bf16[2,128,128]{2,1,0:T(8,128)(2,1)S(1)}, u32[]{:S(2)}, u32[]{:S(2)}) collective-permute-start(bf16[2,128,128]{2,1,0:T(8,128)(2,1)S(1)} %get-tuple-element.18), channel_id=1, source_target_pairs={{0,1},{1,0},{2,3},{3,2},{4,5},{5,4},{6,7},{7,6},{8,9},{9,8},{10,11... | collective-permute-start | bytes 196616 | tf_op jit(solution)/shard_map/ppermute | solution.py:205
  12.0 0.8 %collective-permute-start.5 = (bf16[2,128,128]{2,1,0:T(8,128)(2,1)S(1)}, bf16[2,128,128]{2,1,0:T(8,128)(2,1)S(1)}, u32[]{:S(2)}, u32[]{:S(2)}) collective-permute-start(bf16[2,128,128]{2,1,0:T(8,128)(2,1)S(1)} %get-tuple-element.17), channel_id=1, source_target_pairs={{0,0},{1,2},{2,1},{3,4},{4,3},{5,6},{6,5},{7,8},{8,7},{9,10},{10,9... | collective-permute-start | bytes 196616 | tf_op jit(solution)/shard_map/ppermute | solution.py:204
  12.8 4.0 %collective-permute-done.4.c1 = bf16[2,128,128]{2,1,0:T(8,128)(2,1)S(1)} collective-permute-done((bf16[2,128,128]{2,1,0:T(8,128)(2,1)S(1)}, bf16[2,128,128]{2,1,0:T(8,128)(2,1)S(1)}, u32[]{:S(2)}, u32[]{:S(2)}) %collective-permute-start.4) | collective-permute-done | bytes 65568 | tf_op jit(solution)/shard_map/ppermute | solution.py:205
  16.8 1.5 %shard_map.55.p0 = bf16[2,64,128]{2,1,0:T(8,128)(2,1)S(1)} custom-call(bf16[2,4,128,128]{3,2,1,0:T(8,128)(2,1)S(1)} %copy-done, bf16[4,128,128]{2,1,0:T(8,128)(2,1)S(1)} %collective-permute-done.x1, bf16[4,128,128]{2,1,0:T(8,128)(2,1)S(1)} %collective-permute-done.1.x2, bf16[2,128,128]{2,1,0:T(8,128)(2,1)S(1)} %collective-permute-done.2.r1, ...), custom_call_target="tpu_custom_call" | custom-call | tf_op jit(solution)/shard_map/pallas_call | solution.py:83
  18.3 1.7 %collective-permute-start.6 = (bf16[2,64,128]{2,1,0:T(8,128)(2,1)S(1)}, bf16[2,64,128]{2,1,0:T(8,128)(2,1)S(1)}, u32[]{:S(2)}, u32[]{:S(2)}) collective-permute-start(bf16[2,64,128]{2,1,0:T(8,128)(2,1)S(1)} %shard_map.55.p0), channel_id=1, source_target_pairs={{0,1},{1,0},{2,3},{3,2},{4,5},{5,4},{6,7},{7,6},{8,9},{9,8},{10,11... | collective-permute-start | bytes 98312 | tf_op jit(solution)/shard_map/ppermute | solution.py:219
  20.0 4.2 %collective-permute-start.7 = (bf16[2,64,128]{2,1,0:T(8,128)(2,1)S(1)}, bf16[2,64,128]{2,1,0:T(8,128)(2,1)S(1)}, u32[]{:S(2)}, u32[]{:S(2)}) collective-permute-start(bf16[2,64,128]{2,1,0:T(8,128)(2,1)S(1)} %shard_map.55.p0), channel_id=1, source_target_pairs={{0,2},{1,3},{2,0},{3,1},{4,6},{5,7},{6,4},{7,5},{8,10},{9,11},{10,... | collective-permute-start | bytes 98312 | tf_op jit(solution)/shard_map/ppermute | solution.py:219
  24.1 2.1 %collective-permute-done.7.p2 = bf16[2,64,128]{2,1,0:T(8,128)(2,1)S(1)} collective-permute-done((bf16[2,64,128]{2,1,0:T(8,128)(2,1)S(1)}, bf16[2,64,128]{2,1,0:T(8,128)(2,1)S(1)}, u32[]{:S(2)}, u32[]{:S(2)}) %collective-permute-start.7) | collective-permute-done | bytes 32800 | tf_op jit(solution)/shard_map/ppermute | solution.py:219
  26.3 3.6 %collective-permute-done.8.p3 = bf16[2,64,128]{2,1,0:T(8,128)(2,1)S(1)} collective-permute-done((bf16[2,64,128]{2,1,0:T(8,128)(2,1)S(1)}, bf16[2,64,128]{2,1,0:T(8,128)(2,1)S(1)}, u32[]{:S(2)}, u32[]{:S(2)}) %collective-permute-start.8) | collective-permute-done | bytes 32800 | tf_op jit(solution)/shard_map/ppermute | solution.py:219
  29.9 1.9 %collective-permute-start.10 = (bf16[4,2,64,128]{3,2,1,0:T(8,128)(2,1)S(1)}, bf16[4,2,64,128]{3,2,1,0:T(8,128)(2,1)S(1)}, u32[]{:S(2)}, u32[]{:S(2)}) collective-permute-start(bf16[4,2,64,128]{3,2,1,0:T(8,128)(2,1)S(1)} %get-tuple-element.11.own), channel_id=1, source_target_pairs={{0,0},{16,32},{32,16},{48,64},{64,48},{80,96},{96,80},{112,128},{1... | collective-permute-start | bytes 393224 | tf_op jit(solution)/shard_map/ppermute | solution.py:225
  31.8 12.7 %collective-permute-start.9 = (bf16[4,2,64,128]{3,2,1,0:T(8,128)(2,1)S(1)}, bf16[4,2,64,128]{3,2,1,0:T(8,128)(2,1)S(1)}, u32[]{:S(2)}, u32[]{:S(2)}) collective-permute-start(bf16[4,2,64,128]{3,2,1,0:T(8,128)(2,1)S(1)} %get-tuple-element.11.own), channel_id=1, source_target_pairs={{0,16},{16,0},{32,48},{48,32},{64,80},{80,64},{96,112},{112,96},{1... | collective-permute-start | bytes 393224 | tf_op jit(solution)/shard_map/ppermute | solution.py:226
  44.5 2.6 %collective-permute-start.11 = (bf16[27,16,128]{2,1,0:T(8,128)(2,1)S(1)}, bf16[27,16,128]{2,1,0:T(8,128)(2,1)S(1)}, u32[]{:S(2)}, u32[]{:S(2)}) collective-permute-start(bf16[27,16,128]{2,1,0:T(8,128)(2,1)S(1)} %get-tuple-element.12.w0), channel_id=1, source_target_pairs={{0,4},{1,5},{2,6},{3,7},{4,0},{5,1},{6,2},{7,3},{8,12},{9,13},{10,... | collective-permute-start | bytes 331784 | tf_op jit(solution)/shard_map/ppermute | solution.py:224
  47.1 1.6 %collective-permute-start.12 = (bf16[27,16,128]{2,1,0:T(8,128)(2,1)S(1)}, bf16[27,16,128]{2,1,0:T(8,128)(2,1)S(1)}, u32[]{:S(2)}, u32[]{:S(2)}) collective-permute-start(bf16[27,16,128]{2,1,0:T(8,128)(2,1)S(1)} %get-tuple-element.12.w0), channel_id=1, source_target_pairs={{0,8},{1,9},{2,10},{3,11},{4,12},{5,13},{6,14},{7,15},{8,0},{9,1},... | collective-permute-start | bytes 331784 | tf_op jit(solution)/shard_map/ppermute | solution.py:224
  48.8 1.1 %collective-permute-start.13 = (bf16[27,16,128]{2,1,0:T(8,128)(2,1)S(1)}, bf16[27,16,128]{2,1,0:T(8,128)(2,1)S(1)}, u32[]{:S(2)}, u32[]{:S(2)}) collective-permute-start(bf16[27,16,128]{2,1,0:T(8,128)(2,1)S(1)} %get-tuple-element.12.w0), channel_id=1, source_target_pairs={{0,12},{1,13},{2,14},{3,15},{4,8},{5,9},{6,10},{7,11},{8,4},{9,5},... | collective-permute-start | bytes 331784 | tf_op jit(solution)/shard_map/ppermute | solution.py:224
  50.5 4.1 %collective-permute-done.12.w2 = bf16[27,16,128]{2,1,0:T(8,128)(2,1)S(1)} collective-permute-done((bf16[27,16,128]{2,1,0:T(8,128)(2,1)S(1)}, bf16[27,16,128]{2,1,0:T(8,128)(2,1)S(1)}, u32[]{:S(2)}, u32[]{:S(2)}) %collective-permute-start.12) | collective-permute-done | bytes 110624 | tf_op jit(solution)/shard_map/ppermute | solution.py:224
  54.6 2.2 %collective-permute-done.13.w3 = bf16[27,16,128]{2,1,0:T(8,128)(2,1)S(1)} collective-permute-done((bf16[27,16,128]{2,1,0:T(8,128)(2,1)S(1)}, bf16[27,16,128]{2,1,0:T(8,128)(2,1)S(1)}, u32[]{:S(2)}, u32[]{:S(2)}) %collective-permute-start.13) | collective-permute-done | bytes 110624 | tf_op jit(solution)/shard_map/ppermute | solution.py:224
  56.8 0.8 %shard_map.57 = (f32[16,640]{1,0:T(8,128)S(1)}, f32[16,640]{1,0:T(8,128)S(1)}, f32[16,640]{1,0:T(8,128)S(1)}, f32[16,640]{1,0:T(8,128)S(1)}) custom-call(bf16[4,2,64,128]{3,2,1,0:T(8,128)(2,1)S(1)} %get-tuple-element.11.own, bf16[4,2,64,128]{3,2,1,0:T(8,128)(2,1)S(1)} %collective-permute-done.9.near, ...), custom_call_target="tpu_custom_call" | custom-call | tf_op jit(solution)/shard_map/pallas_call | solution.py:153
  58.0 2.4 %collective-permute-start.15 = (f32[16,640]{1,0:T(8,128)S(1)}, f32[16,640]{1,0:T(8,128)S(1)}, u32[]{:S(2)}, u32[]{:S(2)}) collective-permute-start(f32[16,640]{1,0:T(8,128)S(1)} %get-tuple-element.15), channel_id=1, source_target_pairs={{0,8},{1,9},{2,10},{3,11},{4,12},{5,13},{6,14},{7,15},{8,0},{9,1},... | collective-permute-start | bytes 122888 | tf_op jit(solution)/shard_map/ppermute | solution.py:230
  60.4 2.0 %collective-permute-start.16 = (f32[16,640]{1,0:T(8,128)S(1)}, f32[16,640]{1,0:T(8,128)S(1)}, u32[]{:S(2)}, u32[]{:S(2)}) collective-permute-start(f32[16,640]{1,0:T(8,128)S(1)} %get-tuple-element.16), channel_id=1, source_target_pairs={{0,12},{1,13},{2,14},{3,15},{4,8},{5,9},{6,10},{7,11},{8,4},{9,5},... | collective-permute-start | bytes 122888 | tf_op jit(solution)/shard_map/ppermute | solution.py:230
  62.4 1.1 %collective-permute-done.15.s2 = f32[16,640]{1,0:T(8,128)S(1)} collective-permute-done((f32[16,640]{1,0:T(8,128)S(1)}, f32[16,640]{1,0:T(8,128)S(1)}, u32[]{:S(2)}, u32[]{:S(2)}) %collective-permute-start.15) | collective-permute-done | bytes 40992 | tf_op jit(solution)/shard_map/ppermute | solution.py:230
  63.5 2.1 %collective-permute-done.16.s3 = f32[16,640]{1,0:T(8,128)S(1)} collective-permute-done((f32[16,640]{1,0:T(8,128)S(1)}, f32[16,640]{1,0:T(8,128)S(1)}, u32[]{:S(2)}, u32[]{:S(2)}) %collective-permute-start.16) | collective-permute-done | bytes 40992 | tf_op jit(solution)/shard_map/ppermute | solution.py:230
  (28 shorter events, 2.6 us)
Async XLA Ops:
  0.0 4.0 %copy-start = (bf16[2,4,128,128]{3,2,1,0:T(8,128)(2,1)S(1)}, bf16[2,4,128,128]{3,2,1,0:T(8,128)(2,1)}, u32[]{:S(2)}) copy-start(bf16[2,4,128,128]{3,2,1,0:T(8,128)(2,1)} %vol.1) | copy-start | bytes 786436
  0.0 16.7 %copy-start.1 = (bf16[3,3,3,128,128]{4,3,2,1,0:T(8,128)(2,1)S(1)}, bf16[3,3,3,128,128]{4,3,2,1,0:T(8,128)(2,1)}, u32[]{:S(2)}) copy-start(bf16[3,3,3,128,128]{4,3,2,1,0:T(8,128)(2,1)} %w.1) | copy-start | bytes 2654212
  1.1 5.6 %collective-permute-start = (bf16[4,128,128]{2,1,0:T(8,128)(2,1)S(1)}, bf16[4,128,128]{2,1,0:T(8,128)(2,1)S(1)}, u32[]{:S(2)}, u32[]{:S(2)}) collective-permute-start(bf16[4,128,128]{2,1,0:T(8,128)(2,1)S(1)} %get-tuple-element.22), channel_id=1, source_target_pairs={{0,16},{16,0},{32,48},{48,32},{64,80},{80,64},{96,112},{112,96},{1... | collective-permute-start | bytes 393224 | tf_op jit(solution)/shard_map/ppermute | solution.py:200
  1.2 6.3 %collective-permute-start.1 = (bf16[4,128,128]{2,1,0:T(8,128)(2,1)S(1)}, bf16[4,128,128]{2,1,0:T(8,128)(2,1)S(1)}, u32[]{:S(2)}, u32[]{:S(2)}) collective-permute-start(bf16[4,128,128]{2,1,0:T(8,128)(2,1)S(1)} %get-tuple-element.21), channel_id=1, source_target_pairs={{0,0},{16,32},{32,16},{48,64},{64,48},{80,96},{96,80},{112,128},{1... | collective-permute-start | bytes 393224 | tf_op jit(solution)/shard_map/ppermute | solution.py:199
  4.1 8.7 %collective-permute-start.2 = (bf16[2,128,128]{2,1,0:T(8,128)(2,1)S(1)}, bf16[2,128,128]{2,1,0:T(8,128)(2,1)S(1)}, u32[]{:S(2)}, u32[]{:S(2)}) collective-permute-start(bf16[2,128,128]{2,1,0:T(8,128)(2,1)S(1)} %get-tuple-element.20), channel_id=1, source_target_pairs={{0,1},{1,0},{2,3},{3,2},{4,5},{5,4},{6,7},{7,6},{8,9},{9,8},{10,11... | collective-permute-start | bytes 196616 | tf_op jit(solution)/shard_map/ppermute | solution.py:202
  6.1 6.7 %collective-permute-start.3 = (bf16[2,128,128]{2,1,0:T(8,128)(2,1)S(1)}, bf16[2,128,128]{2,1,0:T(8,128)(2,1)S(1)}, u32[]{:S(2)}, u32[]{:S(2)}) collective-permute-start(bf16[2,128,128]{2,1,0:T(8,128)(2,1)S(1)} %get-tuple-element.19), channel_id=1, source_target_pairs={{0,0},{1,2},{2,1},{3,4},{4,3},{5,6},{6,5},{7,8},{8,7},{9,10},{10,9... | collective-permute-start | bytes 196616 | tf_op jit(solution)/shard_map/ppermute | solution.py:201
  7.5 9.2 %collective-permute-start.4 = (bf16[2,128,128]{2,1,0:T(8,128)(2,1)S(1)}, bf16[2,128,128]{2,1,0:T(8,128)(2,1)S(1)}, u32[]{:S(2)}, u32[]{:S(2)}) collective-permute-start(bf16[2,128,128]{2,1,0:T(8,128)(2,1)S(1)} %get-tuple-element.18), channel_id=1, source_target_pairs={{0,1},{1,0},{2,3},{3,2},{4,5},{5,4},{6,7},{7,6},{8,9},{9,8},{10,11... | collective-permute-start | bytes 196616 | tf_op jit(solution)/shard_map/ppermute | solution.py:205
  11.9 4.8 %copy-start.3 = (f32[128]{0:T(128)S(1)}, f32[128]{0:T(128)}, u32[]{:S(2)}) copy-start(f32[128]{0:T(128)} %param.7) | copy-start | bytes 1540
  12.0 4.8 %collective-permute-start.5 = (bf16[2,128,128]{2,1,0:T(8,128)(2,1)S(1)}, bf16[2,128,128]{2,1,0:T(8,128)(2,1)S(1)}, u32[]{:S(2)}, u32[]{:S(2)}) collective-permute-start(bf16[2,128,128]{2,1,0:T(8,128)(2,1)S(1)} %get-tuple-element.17), channel_id=1, source_target_pairs={{0,0},{1,2},{2,1},{3,4},{4,3},{5,6},{6,5},{7,8},{8,7},{9,10},{10,9... | collective-permute-start | bytes 196616 | tf_op jit(solution)/shard_map/ppermute | solution.py:204
  16.7 13.1 %copy-start.2 = (bf16[3,3,3,128,16]{3,4,2,1,0:T(8,128)(2,1)S(1)}, bf16[3,3,3,128,16]{3,4,2,1,0:T(8,128)(2,1)}, u32[]{:S(2)}) copy-start(bf16[3,3,3,128,16]{3,4,2,1,0:T(8,128)(2,1)} %param.8) | copy-start | bytes 331780
  18.3 5.8 %collective-permute-start.6 = (bf16[2,64,128]{2,1,0:T(8,128)(2,1)S(1)}, bf16[2,64,128]{2,1,0:T(8,128)(2,1)S(1)}, u32[]{:S(2)}, u32[]{:S(2)}) collective-permute-start(bf16[2,64,128]{2,1,0:T(8,128)(2,1)S(1)} %shard_map.55.p0), channel_id=1, source_target_pairs={{0,1},{1,0},{2,3},{3,2},{4,5},{5,4},{6,7},{7,6},{8,9},{9,8},{10,11... | collective-permute-start | bytes 98312 | tf_op jit(solution)/shard_map/ppermute | solution.py:219
  20.0 6.3 %collective-permute-start.7 = (bf16[2,64,128]{2,1,0:T(8,128)(2,1)S(1)}, bf16[2,64,128]{2,1,0:T(8,128)(2,1)S(1)}, u32[]{:S(2)}, u32[]{:S(2)}) collective-permute-start(bf16[2,64,128]{2,1,0:T(8,128)(2,1)S(1)} %shard_map.55.p0), channel_id=1, source_target_pairs={{0,2},{1,3},{2,0},{3,1},{4,6},{5,7},{6,4},{7,5},{8,10},{9,11},{10,... | collective-permute-start | bytes 98312 | tf_op jit(solution)/shard_map/ppermute | solution.py:219
  24.1 5.7 %collective-permute-start.8 = (bf16[2,64,128]{2,1,0:T(8,128)(2,1)S(1)}, bf16[2,64,128]{2,1,0:T(8,128)(2,1)S(1)}, u32[]{:S(2)}, u32[]{:S(2)}) collective-permute-start(bf16[2,64,128]{2,1,0:T(8,128)(2,1)S(1)} %shard_map.55.p0), channel_id=1, source_target_pairs={{0,3},{1,2},{2,1},{3,0},{4,7},{5,6},{6,5},{7,4},{8,11},{9,10},{10,... | collective-permute-start | bytes 98312 | tf_op jit(solution)/shard_map/ppermute | solution.py:219
  29.9 26.9 %collective-permute-start.10 = (bf16[4,2,64,128]{3,2,1,0:T(8,128)(2,1)S(1)}, bf16[4,2,64,128]{3,2,1,0:T(8,128)(2,1)S(1)}, u32[]{:S(2)}, u32[]{:S(2)}) collective-permute-start(bf16[4,2,64,128]{3,2,1,0:T(8,128)(2,1)S(1)} %get-tuple-element.11.own), channel_id=1, source_target_pairs={{0,0},{16,32},{32,16},{48,64},{64,48},{80,96},{96,80},{112,128},{1... | collective-permute-start | bytes 393224 | tf_op jit(solution)/shard_map/ppermute | solution.py:225
  31.8 25.0 %collective-permute-start.9 = (bf16[4,2,64,128]{3,2,1,0:T(8,128)(2,1)S(1)}, bf16[4,2,64,128]{3,2,1,0:T(8,128)(2,1)S(1)}, u32[]{:S(2)}, u32[]{:S(2)}) collective-permute-start(bf16[4,2,64,128]{3,2,1,0:T(8,128)(2,1)S(1)} %get-tuple-element.11.own), channel_id=1, source_target_pairs={{0,16},{16,0},{32,48},{48,32},{64,80},{80,64},{96,112},{112,96},{1... | collective-permute-start | bytes 393224 | tf_op jit(solution)/shard_map/ppermute | solution.py:226
  44.5 5.9 %collective-permute-start.11 = (bf16[27,16,128]{2,1,0:T(8,128)(2,1)S(1)}, bf16[27,16,128]{2,1,0:T(8,128)(2,1)S(1)}, u32[]{:S(2)}, u32[]{:S(2)}) collective-permute-start(bf16[27,16,128]{2,1,0:T(8,128)(2,1)S(1)} %get-tuple-element.12.w0), channel_id=1, source_target_pairs={{0,4},{1,5},{2,6},{3,7},{4,0},{5,1},{6,2},{7,3},{8,12},{9,13},{10,... | collective-permute-start | bytes 331784 | tf_op jit(solution)/shard_map/ppermute | solution.py:224
  47.1 7.4 %collective-permute-start.12 = (bf16[27,16,128]{2,1,0:T(8,128)(2,1)S(1)}, bf16[27,16,128]{2,1,0:T(8,128)(2,1)S(1)}, u32[]{:S(2)}, u32[]{:S(2)}) collective-permute-start(bf16[27,16,128]{2,1,0:T(8,128)(2,1)S(1)} %get-tuple-element.12.w0), channel_id=1, source_target_pairs={{0,8},{1,9},{2,10},{3,11},{4,12},{5,13},{6,14},{7,15},{8,0},{9,1},... | collective-permute-start | bytes 331784 | tf_op jit(solution)/shard_map/ppermute | solution.py:224
  48.8 8.0 %collective-permute-start.13 = (bf16[27,16,128]{2,1,0:T(8,128)(2,1)S(1)}, bf16[27,16,128]{2,1,0:T(8,128)(2,1)S(1)}, u32[]{:S(2)}, u32[]{:S(2)}) collective-permute-start(bf16[27,16,128]{2,1,0:T(8,128)(2,1)S(1)} %get-tuple-element.12.w0), channel_id=1, source_target_pairs={{0,12},{1,13},{2,14},{3,15},{4,8},{5,9},{6,10},{7,11},{8,4},{9,5},... | collective-permute-start | bytes 331784 | tf_op jit(solution)/shard_map/ppermute | solution.py:224
  57.6 4.8 %collective-permute-start.14 = (f32[16,640]{1,0:T(8,128)S(1)}, f32[16,640]{1,0:T(8,128)S(1)}, u32[]{:S(2)}, u32[]{:S(2)}) collective-permute-start(f32[16,640]{1,0:T(8,128)S(1)} %get-tuple-element.14), channel_id=1, source_target_pairs={{0,4},{1,5},{2,6},{3,7},{4,0},{5,1},{6,2},{7,3},{8,12},{9,13},{10,... | collective-permute-start | bytes 122888 | tf_op jit(solution)/shard_map/ppermute | solution.py:230
  58.0 5.5 %collective-permute-start.15 = (f32[16,640]{1,0:T(8,128)S(1)}, f32[16,640]{1,0:T(8,128)S(1)}, u32[]{:S(2)}, u32[]{:S(2)}) collective-permute-start(f32[16,640]{1,0:T(8,128)S(1)} %get-tuple-element.15), channel_id=1, source_target_pairs={{0,8},{1,9},{2,10},{3,11},{4,12},{5,13},{6,14},{7,15},{8,0},{9,1},... | collective-permute-start | bytes 122888 | tf_op jit(solution)/shard_map/ppermute | solution.py:230
  60.4 5.2 %copy-start.4 = (f32[16]{0:T(128)S(1)}, f32[16]{0:T(128)}, u32[]{:S(2)}) copy-start(f32[16]{0:T(128)} %param.9) | copy-start | bytes 196
  60.4 5.2 %collective-permute-start.16 = (f32[16,640]{1,0:T(8,128)S(1)}, f32[16,640]{1,0:T(8,128)S(1)}, u32[]{:S(2)}, u32[]{:S(2)}) collective-permute-start(f32[16,640]{1,0:T(8,128)S(1)} %get-tuple-element.16), channel_id=1, source_target_pairs={{0,12},{1,13},{2,14},{3,15},{4,8},{5,9},{6,10},{7,11},{8,4},{9,5},... | collective-permute-start | bytes 122888 | tf_op jit(solution)/shard_map/ppermute | solution.py:230

commit v5 on v4

--- a/solution.py
+++ b/solution.py
@@ -22,7 +22,7 @@
     return (i > 0) & (i < 15)
 
 
-def fine_kernel(vol, x1, x2, r1, r2, c1, c2, w, bias, out, cells, peak):
+def fine_kernel(vol, x2, x1, r2, r1, w2, c2, c1, w, bias, out, cells, peak):
     pd = lax.rem(lax.axis_index("depth"), 2)
     pr = lax.rem(lax.axis_index("rows"), 2)
     inner_d = inner("depth")
@@ -35,7 +35,7 @@
                 plane = (j - 1) + pd * (3 - 2 * j)
                 piece = r2[plane] if i == 0 else r1[plane] if i == 5 else vol[plane, row]
             else:
-                side, slot = (x2, 1) if j == 0 else (x1, 0)
+                side, slot = (x2, 0) if j == 0 else (x1, 1)
                 piece = c2[slot] if i == 0 else c1[slot] if i == 5 else side[row]
             if i == 0:
                 piece = jnp.where(inner_r, piece, zero)
@@ -78,16 +78,16 @@
         out[q + pr * (1 - 2 * q)] = jnp.maximum(pooled + bias[...], 0.0).astype(BF16)
 
 
-def fine_level(vol, x1, x2, r1, r2, c1, c2, w, bias):
+def fine_level(vol, x2, x1, r2, r1, w2, c2, c1, w, bias):
     vmem = pl.BlockSpec(memory_space=pltpu.VMEM)
     return pl.pallas_call(
         fine_kernel,
         out_shape=jax.ShapeDtypeStruct((2, 64, 128), BF16),
-        in_specs=[vmem] * 9,
+        in_specs=[vmem] * 5 + [pl.BlockSpec(memory_space=pl.ANY)] + [vmem] * 4,
         out_specs=vmem,
         scratch_shapes=[pltpu.VMEM((4, 6, 128, 128), BF16), pltpu.VMEM((128, 128), F32)],
         compiler_params=pltpu.CompilerParams(vmem_limit_bytes=32 * 1024 * 1024),
-    )(vol, x1, x2, r1, r2, c1, c2, w, bias)
+    )(vol, x2, x1, r2, r1, w2, c2, c1, w, bias)
 
 
 def assemble_kernel(p0, p1, p2, p3, w, plane, kept):
@@ -107,17 +107,17 @@
     )(*pieces, w)
 
 
-def coarse_kernel(own, near, far, w0, w1, w2, w3, o0, o1, o2, o3, cells):
+def coarse_kernel(own, far, near, w0, w1, w2, w3, o0, o1, o2, o3, cells):
     pd = lax.rem(lax.axis_index("depth"), 2)
     z = lax.rem(lax.axis_index("rows"), 4)
     inner_d = inner("depth")
     for a in range(3):
         for i in (0, 1, 10, 11):
             cells[a, i] = jnp.zeros((64, 128), BF16)
-    for k in range(4):
-        cells[0, pl.ds(2 + 2 * (z ^ k), 2)] = jnp.where(inner_d, far[k], jnp.zeros_like(far[k]))
-        cells[1, pl.ds(2 + 2 * (z ^ k), 2)] = own[k]
-        cells[2, pl.ds(2 + 2 * (z ^ k), 2)] = near[k]
+    for m, k in enumerate((0, 3, 2, 1)):
+        cells[0, pl.ds(2 + 2 * (z ^ k), 2)] = jnp.where(inner_d, far[m], jnp.zeros_like(far[m]))
+        cells[1, pl.ds(2 + 2 * (z ^ k), 2)] = own[m]
+        cells[2, pl.ds(2 + 2 * (z ^ k), 2)] = near[m]
     lhs = jnp.concatenate(
         [
             jnp.concatenate(
@@ -160,7 +160,7 @@
     )(*pieces, *weights)
 
 
-def join_kernel(s0, s1, s2, s3, bias, out, held):
+def join_kernel(s0, s2, s1, s3, bias, out, held):
     y = lax.div(lax.axis_index("rows"), 4)
     for k, part in enumerate((s0, s1, s2, s3)):
         held[y ^ k] = part[...]
@@ -200,7 +200,7 @@
     x1 = lax.ppermute(lax.dynamic_index_in_dim(volume, 1 - pd, 0, False), "depth", depth_near)
     r2 = lax.ppermute(lax.dynamic_index_in_dim(volume, 3 * pr, 1, False), "rows", rows_far)
     r1 = lax.ppermute(lax.dynamic_index_in_dim(volume, 3 - 3 * pr, 1, False), "rows", rows_near)
-    sides = jnp.stack([x1, x2])
+    sides = jnp.stack([x2, x1])
     c2 = lax.ppermute(lax.dynamic_index_in_dim(sides, 3 * pr, 1, False), "rows", rows_far)
     c1 = lax.ppermute(lax.dynamic_index_in_dim(sides, 3 - 3 * pr, 1, False), "rows", rows_near)
 
@@ -210,24 +210,18 @@
     def along_y(k):
         return [(i, i ^ (4 * k)) for i in range(16)]
 
+    w = jnp.transpose(coarse_filters, (0, 1, 2, 4, 3)).reshape(27, 16, 128)
+    w2 = lax.ppermute(w, "rows", along_y(2))
     pooled = fine_level(
-        volume, x1, x2, r1, r2, c1, c2, fine_filters, fine_bias.reshape(1, 128)
-    )
-
-    pieces = [pooled] + [None] * 3
-    for k in (3, 2, 1):
-        pieces[k] = lax.ppermute(pooled, "rows", along_z(k))
-    w = jnp.transpose(coarse_filters, (0, 1, 2, 4, 3)).reshape(27, 16, 128)
-    plane, w = assemble(pieces, w)
-    weights = [w] + [None] * 3
-    for k in (2, 1, 3):
-        weights[k] = lax.ppermute(w, "rows", along_y(k))
+        volume, x2, x1, r2, r1, w2, c2, c1, fine_filters, fine_bias.reshape(1, 128)
+    )
+
+    plane, kept = assemble([pooled] + [lax.ppermute(pooled, "rows", along_z(k)) for k in (3, 2, 1)], w)
+    w1, w3 = [lax.ppermute(kept, "rows", along_y(k)) for k in (1, 3)]
     far = lax.ppermute(plane, "depth", depth_far)
     near = lax.ppermute(plane, "depth", depth_near)
-    sums = coarse_level((plane, near, far), weights)
-    parts = [sums[0]] + [None] * 3
-    for k in (2, 1, 3):
-        parts[k] = lax.ppermute(sums[k], "rows", along_y(k))
+    sums = coarse_level((plane, far, near), (w, w1, w2, w3))
+    parts = [sums[0]] + [lax.ppermute(sums[k], "rows", along_y(k)) for k in (2, 1, 3)]
     result = join(parts, jnp.broadcast_to(coarse_bias[:, None], (16, 128)))
     return result.reshape(16, 1, 2048)
 

time: 66.5 us -> 57.8 us (0.87)
  waiting for transfers between devices: 20.6 us -> 14.2 us
  starting transfers between devices: 41.4 us -> 39.1 us
    ppermute x1, starting transfers between devices: 12.7 us -> 2.84 us  [body(): near = lax.ppermute(plane, 'depth', depth_near)]
    ppermute x1, starting transfers between devices: 0.09 us -> 7.04 us  [body(): lax.ppermute(lax.dynamic_index_in_dim(volume, 1 - pd, 0, False), 'depth',...]
    ppermute x9, waiting for transfers between devices: 15.9 us -> 11.3 us  [the longest x3 3.99 us: body(): lax.ppermute(sums[k], 'rows', along_y(k))]
    ppermute x1, starting transfers between devices: 2 us -> 3.37 us  [body(): lax.ppermute(lax.dynamic_index_in_dim(volume, 3 - 3 * pr, 1, False), 'row...]
    ppermute x1, waiting for transfers between devices: 3.97 us -> 2.92 us  [body(): lax.ppermute(lax.dynamic_index_in_dim(sides, 3 - 3 * pr, 1, False), 'rows...]
    ppermute x1, waiting for transfers between devices: 0.73 us -> 0.01 us  [body(): lax.ppermute(lax.dynamic_index_in_dim(volume, pd, 0, False), 'depth', dep...]
  transfers between devices with their start and end apart: 17 -> 17, of which waited for: 9 -> 7; matrix products, arithmetic and copies ran while one was open for 0% -> 0% of each run, Pallas kernels for 0% -> 0%
where the time goes in v5:
time: 57.8 us; the launch traced here: 57.6 us
  starting transfers between devices  39.1 us (68%)
  waiting for transfers between devices  14.2 us (25%)
  Pallas kernels  3 us (5%)
  local copies, waits for them, and re-layouts  1.19 us (2%)
    ppermute x1, starting transfers between devices, body(): lax.ppermute(lax.dynamic_index_in_dim(volume, 1 - pd, 0, False), 'depth',...  7.04 us
    ppermute x1, starting transfers between devices, body(): lax.ppermute(lax.dynamic_index_in_dim(sides, 3 - 3 * pr, 1, False), 'rows...  4.96 us
    ppermute x3, starting transfers between devices, body(): lax.ppermute(pooled, 'rows', along_z(k))  4.47 us
    ppermute x3, starting transfers between devices, body(): lax.ppermute(sums[k], 'rows', along_y(k))  4.18 us
    ppermute x3, waiting for transfers between devices, body(): lax.ppermute(sums[k], 'rows', along_y(k))  3.99 us
    ppermute x2, waiting for transfers between devices, body(): w1, w3 = [lax.ppermute(kept, 'rows', along_y(k)) for k in (1, 3)]  3.98 us
    ppermute x2, starting transfers between devices, body(): w1, w3 = [lax.ppermute(kept, 'rows', along_y(k)) for k in (1, 3)]  3.59 us
    ppermute x1, starting transfers between devices, body(): lax.ppermute(lax.dynamic_index_in_dim(volume, 3 - 3 * pr, 1, False), 'row...  3.37 us
  transfers between devices with their start and end apart: 17, of which 7 were waited for; matrix products, arithmetic and copies ran while one was open for 0% of the time, Pallas kernels for 0%

profile of v5, /device:TPU:6, one launch (start us, length us, event | category | flops | bytes accessed | tf_op | source)
XLA Modules:
  0.0 57.6 jit_solution(1499075139675296904)
XLA Ops:
  0.0 1.1 %dynamic-slice_bitcast_fusion = (bf16[4,128,128]{2,1,0:T(8,128)(2,1)S(1)}, bf16[4,128,128]{2,1,0:T(8,128)(2,1)S(1)}) fusion(bf16[2,4,128,128]{3,2,1,0:T(8,128)(2,1)} %vol.1, s32[]{:T(128)S(6)} %select_n.17, s32[]{:T(128)S(6)} %select_n.16), kind=kLoop, calls=%fused_computation.4 | loop fusion | bytes 524296 | tf_op jit(solution)/shard_map/jit(dynamic_index_in_dim)/squeeze | solution.py:200
  1.1 2.2 %collective-permute-start = (bf16[4,128,128]{2,1,0:T(8,128)(2,1)S(1)}, bf16[4,128,128]{2,1,0:T(8,128)(2,1)S(1)}, u32[]{:S(2)}, u32[]{:S(2)}) collective-permute-start(bf16[4,128,128]{2,1,0:T(8,128)(2,1)S(1)} %get-tuple-element.22), channel_id=1, source_target_pairs={{0,0},{16,32},{32,16},{48,64},{64,48},{80,96},{96,80},{112,128},{1... | collective-permute-start | bytes 393224 | tf_op jit(solution)/shard_map/ppermute | solution.py:199
  3.3 7.0 %collective-permute-start.1 = (bf16[4,128,128]{2,1,0:T(8,128)(2,1)S(1)}, bf16[4,128,128]{2,1,0:T(8,128)(2,1)S(1)}, u32[]{:S(2)}, u32[]{:S(2)}) collective-permute-start(bf16[4,128,128]{2,1,0:T(8,128)(2,1)S(1)} %get-tuple-element.21), channel_id=1, source_target_pairs={{0,16},{16,0},{32,48},{48,32},{64,80},{80,64},{96,112},{112,96},{1... | collective-permute-start | bytes 393224 | tf_op jit(solution)/shard_map/ppermute | solution.py:200
  11.0 3.4 %collective-permute-start.3 = (bf16[2,128,128]{2,1,0:T(8,128)(2,1)S(1)}, bf16[2,128,128]{2,1,0:T(8,128)(2,1)S(1)}, u32[]{:S(2)}, u32[]{:S(2)}) collective-permute-start(bf16[2,128,128]{2,1,0:T(8,128)(2,1)S(1)} %get-tuple-element.19), channel_id=1, source_target_pairs={{0,1},{1,0},{2,3},{3,2},{4,5},{5,4},{6,7},{7,6},{8,9},{9,8},{10,11... | collective-permute-start | bytes 196616 | tf_op jit(solution)/shard_map/ppermute | solution.py:202
  14.4 3.2 %collective-permute-start.4 = (bf16[27,16,128]{2,1,0:T(8,128)(2,1)S(1)}, bf16[27,16,128]{2,1,0:T(8,128)(2,1)S(1)}, u32[]{:S(2)}, u32[]{:S(2)}) collective-permute-start(bf16[27,16,128]{2,1,0:T(8,128)(2,1)S(1)} %bitcast.21), channel_id=1, source_target_pairs={{0,8},{1,9},{2,10},{3,11},{4,12},{5,13},{6,14},{7,15},{8,0},{9,1},... | collective-permute-start | bytes 331784 | tf_op jit(solution)/shard_map/ppermute | solution.py:214
  18.3 5.0 %collective-permute-start.6 = (bf16[2,128,128]{2,1,0:T(8,128)(2,1)S(1)}, bf16[2,128,128]{2,1,0:T(8,128)(2,1)S(1)}, u32[]{:S(2)}, u32[]{:S(2)}) collective-permute-start(bf16[2,128,128]{2,1,0:T(8,128)(2,1)S(1)} %get-tuple-element.17), channel_id=1, source_target_pairs={{0,1},{1,0},{2,3},{3,2},{4,5},{5,4},{6,7},{7,6},{8,9},{9,8},{10,11... | collective-permute-start | bytes 196616 | tf_op jit(solution)/shard_map/ppermute | solution.py:205
  23.3 2.9 %collective-permute-done.6.c1 = bf16[2,128,128]{2,1,0:T(8,128)(2,1)S(1)} collective-permute-done((bf16[2,128,128]{2,1,0:T(8,128)(2,1)S(1)}, bf16[2,128,128]{2,1,0:T(8,128)(2,1)S(1)}, u32[]{:S(2)}, u32[]{:S(2)}) %collective-permute-start.6) | collective-permute-done | bytes 65568 | tf_op jit(solution)/shard_map/ppermute | solution.py:205
  26.2 1.5 %shard_map.55.p0 = bf16[2,64,128]{2,1,0:T(8,128)(2,1)S(1)} custom-call(bf16[2,4,128,128]{3,2,1,0:T(8,128)(2,1)S(1)} %copy-done, bf16[4,128,128]{2,1,0:T(8,128)(2,1)S(1)} %collective-permute-done.x2, bf16[4,128,128]{2,1,0:T(8,128)(2,1)S(1)} %collective-permute-done.1.x1, bf16[2,128,128]{2,1,0:T(8,128)(2,1)S(1)} %collective-permute-done.2.r2, ...), custom_call_target="tpu_custom_call" | custom-call | tf_op jit(solution)/shard_map/pallas_call | solution.py:83
  27.7 3.0 %collective-permute-start.7 = (bf16[2,64,128]{2,1,0:T(8,128)(2,1)S(1)}, bf16[2,64,128]{2,1,0:T(8,128)(2,1)S(1)}, u32[]{:S(2)}, u32[]{:S(2)}) collective-permute-start(bf16[2,64,128]{2,1,0:T(8,128)(2,1)S(1)} %shard_map.55.p0), channel_id=1, source_target_pairs={{0,3},{1,2},{2,1},{3,0},{4,7},{5,6},{6,5},{7,4},{8,11},{9,10},{10,... | collective-permute-start | bytes 98312 | tf_op jit(solution)/shard_map/ppermute | solution.py:219
  30.7 1.5 %collective-permute-start.9 = (bf16[2,64,128]{2,1,0:T(8,128)(2,1)S(1)}, bf16[2,64,128]{2,1,0:T(8,128)(2,1)S(1)}, u32[]{:S(2)}, u32[]{:S(2)}) collective-permute-start(bf16[2,64,128]{2,1,0:T(8,128)(2,1)S(1)} %shard_map.55.p0), channel_id=1, source_target_pairs={{0,1},{1,0},{2,3},{3,2},{4,5},{5,4},{6,7},{7,6},{8,9},{9,8},{10,11... | collective-permute-start | bytes 98312 | tf_op jit(solution)/shard_map/ppermute | solution.py:219
  32.2 1.3 %collective-permute-done.7.p1 = bf16[2,64,128]{2,1,0:T(8,128)(2,1)S(1)} collective-permute-done((bf16[2,64,128]{2,1,0:T(8,128)(2,1)S(1)}, bf16[2,64,128]{2,1,0:T(8,128)(2,1)S(1)}, u32[]{:S(2)}, u32[]{:S(2)}) %collective-permute-start.7) | collective-permute-done | bytes 32800 | tf_op jit(solution)/shard_map/ppermute | solution.py:219
  33.5 2.0 %collective-permute-done.8.p2 = bf16[2,64,128]{2,1,0:T(8,128)(2,1)S(1)} collective-permute-done((bf16[2,64,128]{2,1,0:T(8,128)(2,1)S(1)}, bf16[2,64,128]{2,1,0:T(8,128)(2,1)S(1)}, u32[]{:S(2)}, u32[]{:S(2)}) %collective-permute-start.8) | collective-permute-done | bytes 32800 | tf_op jit(solution)/shard_map/ppermute | solution.py:219
  35.5 1.9 %collective-permute-start.10 = (bf16[4,2,64,128]{3,2,1,0:T(8,128)(2,1)S(1)}, bf16[4,2,64,128]{3,2,1,0:T(8,128)(2,1)S(1)}, u32[]{:S(2)}, u32[]{:S(2)}) collective-permute-start(bf16[4,2,64,128]{3,2,1,0:T(8,128)(2,1)S(1)} %get-tuple-element.11.own), channel_id=1, source_target_pairs={{0,0},{16,32},{32,16},{48,64},{64,48},{80,96},{96,80},{112,128},{1... | collective-permute-start | bytes 393224 | tf_op jit(solution)/shard_map/ppermute | solution.py:221
  37.5 2.8 %collective-permute-start.11 = (bf16[4,2,64,128]{3,2,1,0:T(8,128)(2,1)S(1)}, bf16[4,2,64,128]{3,2,1,0:T(8,128)(2,1)S(1)}, u32[]{:S(2)}, u32[]{:S(2)}) collective-permute-start(bf16[4,2,64,128]{3,2,1,0:T(8,128)(2,1)S(1)} %get-tuple-element.11.own), channel_id=1, source_target_pairs={{0,16},{16,0},{32,48},{48,32},{64,80},{80,64},{96,112},{112,96},{1... | collective-permute-start | bytes 393224 | tf_op jit(solution)/shard_map/ppermute | solution.py:222
  40.3 1.6 %collective-permute-start.12 = (bf16[27,16,128]{2,1,0:T(8,128)(2,1)S(1)}, bf16[27,16,128]{2,1,0:T(8,128)(2,1)S(1)}, u32[]{:S(2)}, u32[]{:S(2)}) collective-permute-start(bf16[27,16,128]{2,1,0:T(8,128)(2,1)S(1)} %get-tuple-element.12), channel_id=1, source_target_pairs={{0,4},{1,5},{2,6},{3,7},{4,0},{5,1},{6,2},{7,3},{8,12},{9,13},{10,... | collective-permute-start | bytes 331784 | tf_op jit(solution)/shard_map/ppermute | solution.py:220
  41.9 2.0 %collective-permute-start.13 = (bf16[27,16,128]{2,1,0:T(8,128)(2,1)S(1)}, bf16[27,16,128]{2,1,0:T(8,128)(2,1)S(1)}, u32[]{:S(2)}, u32[]{:S(2)}) collective-permute-start(bf16[27,16,128]{2,1,0:T(8,128)(2,1)S(1)} %get-tuple-element.12), channel_id=1, source_target_pairs={{0,12},{1,13},{2,14},{3,15},{4,8},{5,9},{6,10},{7,11},{8,4},{9,5},... | collective-permute-start | bytes 331784 | tf_op jit(solution)/shard_map/ppermute | solution.py:220
  43.9 1.5 %collective-permute-done.12.w1 = bf16[27,16,128]{2,1,0:T(8,128)(2,1)S(1)} collective-permute-done((bf16[27,16,128]{2,1,0:T(8,128)(2,1)S(1)}, bf16[27,16,128]{2,1,0:T(8,128)(2,1)S(1)}, u32[]{:S(2)}, u32[]{:S(2)}) %collective-permute-start.12) | collective-permute-done | bytes 110624 | tf_op jit(solution)/shard_map/ppermute | solution.py:220
  45.4 2.5 %collective-permute-done.13.w3 = bf16[27,16,128]{2,1,0:T(8,128)(2,1)S(1)} collective-permute-done((bf16[27,16,128]{2,1,0:T(8,128)(2,1)S(1)}, bf16[27,16,128]{2,1,0:T(8,128)(2,1)S(1)}, u32[]{:S(2)}, u32[]{:S(2)}) %collective-permute-start.13) | collective-permute-done | bytes 110624 | tf_op jit(solution)/shard_map/ppermute | solution.py:220
  47.9 0.8 %shard_map.57 = (f32[16,640]{1,0:T(8,128)S(1)}, f32[16,640]{1,0:T(8,128)S(1)}, f32[16,640]{1,0:T(8,128)S(1)}, f32[16,640]{1,0:T(8,128)S(1)}) custom-call(bf16[4,2,64,128]{3,2,1,0:T(8,128)(2,1)S(1)} %get-tuple-element.11.own, bf16[4,2,64,128]{3,2,1,0:T(8,128)(2,1)S(1)} %collective-permute-done.10.far, ...), custom_call_target="tpu_custom_call" | custom-call | tf_op jit(solution)/shard_map/pallas_call | solution.py:153
  48.7 1.4 %collective-permute-start.14 = (f32[16,640]{1,0:T(8,128)S(1)}, f32[16,640]{1,0:T(8,128)S(1)}, u32[]{:S(2)}, u32[]{:S(2)}) collective-permute-start(f32[16,640]{1,0:T(8,128)S(1)} %get-tuple-element.14), channel_id=1, source_target_pairs={{0,8},{1,9},{2,10},{3,11},{4,12},{5,13},{6,14},{7,15},{8,0},{9,1},... | collective-permute-start | bytes 122888 | tf_op jit(solution)/shard_map/ppermute | solution.py:224
  50.1 1.6 %collective-permute-start.15 = (f32[16,640]{1,0:T(8,128)S(1)}, f32[16,640]{1,0:T(8,128)S(1)}, u32[]{:S(2)}, u32[]{:S(2)}) collective-permute-start(f32[16,640]{1,0:T(8,128)S(1)} %get-tuple-element.15), channel_id=1, source_target_pairs={{0,4},{1,5},{2,6},{3,7},{4,0},{5,1},{6,2},{7,3},{8,12},{9,13},{10,... | collective-permute-start | bytes 122888 | tf_op jit(solution)/shard_map/ppermute | solution.py:224
  51.7 1.2 %collective-permute-start.16 = (f32[16,640]{1,0:T(8,128)S(1)}, f32[16,640]{1,0:T(8,128)S(1)}, u32[]{:S(2)}, u32[]{:S(2)}) collective-permute-start(f32[16,640]{1,0:T(8,128)S(1)} %get-tuple-element.16), channel_id=1, source_target_pairs={{0,12},{1,13},{2,14},{3,15},{4,8},{5,9},{6,10},{7,11},{8,4},{9,5},... | collective-permute-start | bytes 122888 | tf_op jit(solution)/shard_map/ppermute | solution.py:224
  52.9 1.5 %collective-permute-done.14.s2 = f32[16,640]{1,0:T(8,128)S(1)} collective-permute-done((f32[16,640]{1,0:T(8,128)S(1)}, f32[16,640]{1,0:T(8,128)S(1)}, u32[]{:S(2)}, u32[]{:S(2)}) %collective-permute-start.14) | collective-permute-done | bytes 40992 | tf_op jit(solution)/shard_map/ppermute | solution.py:224
  54.4 2.5 %collective-permute-done.16.s3 = f32[16,640]{1,0:T(8,128)S(1)} collective-permute-done((f32[16,640]{1,0:T(8,128)S(1)}, f32[16,640]{1,0:T(8,128)S(1)}, u32[]{:S(2)}, u32[]{:S(2)}) %collective-permute-start.16) | collective-permute-done | bytes 40992 | tf_op jit(solution)/shard_map/ppermute | solution.py:224
  (28 shorter events, 2.2 us)
Async XLA Ops:
  0.0 14.4 %copy-start.2 = (bf16[3,3,3,128,16]{3,4,2,1,0:T(8,128)(2,1)S(1)}, bf16[3,3,3,128,16]{3,4,2,1,0:T(8,128)(2,1)}, u32[]{:S(2)}) copy-start(bf16[3,3,3,128,16]{3,4,2,1,0:T(8,128)(2,1)} %param.8) | copy-start | bytes 331780
  0.0 10.3 %copy-start = (bf16[2,4,128,128]{3,2,1,0:T(8,128)(2,1)S(1)}, bf16[2,4,128,128]{3,2,1,0:T(8,128)(2,1)}, u32[]{:S(2)}) copy-start(bf16[2,4,128,128]{3,2,1,0:T(8,128)(2,1)} %vol.1) | copy-start | bytes 786436
  0.0 26.2 %copy-start.1 = (bf16[3,3,3,128,128]{4,3,2,1,0:T(8,128)(2,1)S(1)}, bf16[3,3,3,128,128]{4,3,2,1,0:T(8,128)(2,1)}, u32[]{:S(2)}) copy-start(bf16[3,3,3,128,128]{4,3,2,1,0:T(8,128)(2,1)} %w.1) | copy-start | bytes 2654212
  1.1 16.5 %collective-permute-start = (bf16[4,128,128]{2,1,0:T(8,128)(2,1)S(1)}, bf16[4,128,128]{2,1,0:T(8,128)(2,1)S(1)}, u32[]{:S(2)}, u32[]{:S(2)}) collective-permute-start(bf16[4,128,128]{2,1,0:T(8,128)(2,1)S(1)} %get-tuple-element.22), channel_id=1, source_target_pairs={{0,0},{16,32},{32,16},{48,64},{64,48},{80,96},{96,80},{112,128},{1... | collective-permute-start | bytes 393224 | tf_op jit(solution)/shard_map/ppermute | solution.py:199
  3.3 14.3 %collective-permute-start.1 = (bf16[4,128,128]{2,1,0:T(8,128)(2,1)S(1)}, bf16[4,128,128]{2,1,0:T(8,128)(2,1)S(1)}, u32[]{:S(2)}, u32[]{:S(2)}) collective-permute-start(bf16[4,128,128]{2,1,0:T(8,128)(2,1)S(1)} %get-tuple-element.21), channel_id=1, source_target_pairs={{0,16},{16,0},{32,48},{48,32},{64,80},{80,64},{96,112},{112,96},{1... | collective-permute-start | bytes 393224 | tf_op jit(solution)/shard_map/ppermute | solution.py:200
  10.3 12.9 %collective-permute-start.2 = (bf16[2,128,128]{2,1,0:T(8,128)(2,1)S(1)}, bf16[2,128,128]{2,1,0:T(8,128)(2,1)S(1)}, u32[]{:S(2)}, u32[]{:S(2)}) collective-permute-start(bf16[2,128,128]{2,1,0:T(8,128)(2,1)S(1)} %get-tuple-element.20), channel_id=1, source_target_pairs={{0,0},{1,2},{2,1},{3,4},{4,3},{5,6},{6,5},{7,8},{8,7},{9,10},{10,9... | collective-permute-start | bytes 196616 | tf_op jit(solution)/shard_map/ppermute | solution.py:201
  11.0 12.2 %collective-permute-start.3 = (bf16[2,128,128]{2,1,0:T(8,128)(2,1)S(1)}, bf16[2,128,128]{2,1,0:T(8,128)(2,1)S(1)}, u32[]{:S(2)}, u32[]{:S(2)}) collective-permute-start(bf16[2,128,128]{2,1,0:T(8,128)(2,1)S(1)} %get-tuple-element.19), channel_id=1, source_target_pairs={{0,1},{1,0},{2,3},{3,2},{4,5},{5,4},{6,7},{7,6},{8,9},{9,8},{10,11... | collective-permute-start | bytes 196616 | tf_op jit(solution)/shard_map/ppermute | solution.py:202
  14.4 8.9 %collective-permute-start.4 = (bf16[27,16,128]{2,1,0:T(8,128)(2,1)S(1)}, bf16[27,16,128]{2,1,0:T(8,128)(2,1)S(1)}, u32[]{:S(2)}, u32[]{:S(2)}) collective-permute-start(bf16[27,16,128]{2,1,0:T(8,128)(2,1)S(1)} %bitcast.21), channel_id=1, source_target_pairs={{0,8},{1,9},{2,10},{3,11},{4,12},{5,13},{6,14},{7,15},{8,0},{9,1},... | collective-permute-start | bytes 331784 | tf_op jit(solution)/shard_map/ppermute | solution.py:214
  17.6 5.7 %collective-permute-start.5 = (bf16[2,128,128]{2,1,0:T(8,128)(2,1)S(1)}, bf16[2,128,128]{2,1,0:T(8,128)(2,1)S(1)}, u32[]{:S(2)}, u32[]{:S(2)}) collective-permute-start(bf16[2,128,128]{2,1,0:T(8,128)(2,1)S(1)} %get-tuple-element.18), channel_id=1, source_target_pairs={{0,0},{1,2},{2,1},{3,4},{4,3},{5,6},{6,5},{7,8},{8,7},{9,10},{10,9... | collective-permute-start | bytes 196616 | tf_op jit(solution)/shard_map/ppermute | solution.py:204
  18.3 7.9 %copy-start.3 = (f32[128]{0:T(128)S(1)}, f32[128]{0:T(128)}, u32[]{:S(2)}) copy-start(f32[128]{0:T(128)} %param.7) | copy-start | bytes 1540
  18.3 7.9 %collective-permute-start.6 = (bf16[2,128,128]{2,1,0:T(8,128)(2,1)S(1)}, bf16[2,128,128]{2,1,0:T(8,128)(2,1)S(1)}, u32[]{:S(2)}, u32[]{:S(2)}) collective-permute-start(bf16[2,128,128]{2,1,0:T(8,128)(2,1)S(1)} %get-tuple-element.17), channel_id=1, source_target_pairs={{0,1},{1,0},{2,3},{3,2},{4,5},{5,4},{6,7},{7,6},{8,9},{9,8},{10,11... | collective-permute-start | bytes 196616 | tf_op jit(solution)/shard_map/ppermute | solution.py:205
  27.7 5.8 %collective-permute-start.7 = (bf16[2,64,128]{2,1,0:T(8,128)(2,1)S(1)}, bf16[2,64,128]{2,1,0:T(8,128)(2,1)S(1)}, u32[]{:S(2)}, u32[]{:S(2)}) collective-permute-start(bf16[2,64,128]{2,1,0:T(8,128)(2,1)S(1)} %shard_map.55.p0), channel_id=1, source_target_pairs={{0,3},{1,2},{2,1},{3,0},{4,7},{5,6},{6,5},{7,4},{8,11},{9,10},{10,... | collective-permute-start | bytes 98312 | tf_op jit(solution)/shard_map/ppermute | solution.py:219
  30.7 4.8 %collective-permute-start.8 = (bf16[2,64,128]{2,1,0:T(8,128)(2,1)S(1)}, bf16[2,64,128]{2,1,0:T(8,128)(2,1)S(1)}, u32[]{:S(2)}, u32[]{:S(2)}) collective-permute-start(bf16[2,64,128]{2,1,0:T(8,128)(2,1)S(1)} %shard_map.55.p0), channel_id=1, source_target_pairs={{0,2},{1,3},{2,0},{3,1},{4,6},{5,7},{6,4},{7,5},{8,10},{9,11},{10,... | collective-permute-start | bytes 98312 | tf_op jit(solution)/shard_map/ppermute | solution.py:219
  30.7 4.8 %collective-permute-start.9 = (bf16[2,64,128]{2,1,0:T(8,128)(2,1)S(1)}, bf16[2,64,128]{2,1,0:T(8,128)(2,1)S(1)}, u32[]{:S(2)}, u32[]{:S(2)}) collective-permute-start(bf16[2,64,128]{2,1,0:T(8,128)(2,1)S(1)} %shard_map.55.p0), channel_id=1, source_target_pairs={{0,1},{1,0},{2,3},{3,2},{4,5},{5,4},{6,7},{7,6},{8,9},{9,8},{10,11... | collective-permute-start | bytes 98312 | tf_op jit(solution)/shard_map/ppermute | solution.py:219
  35.5 12.3 %collective-permute-start.10 = (bf16[4,2,64,128]{3,2,1,0:T(8,128)(2,1)S(1)}, bf16[4,2,64,128]{3,2,1,0:T(8,128)(2,1)S(1)}, u32[]{:S(2)}, u32[]{:S(2)}) collective-permute-start(bf16[4,2,64,128]{3,2,1,0:T(8,128)(2,1)S(1)} %get-tuple-element.11.own), channel_id=1, source_target_pairs={{0,0},{16,32},{32,16},{48,64},{64,48},{80,96},{96,80},{112,128},{1... | collective-permute-start | bytes 393224 | tf_op jit(solution)/shard_map/ppermute | solution.py:221
  37.5 10.4 %collective-permute-start.11 = (bf16[4,2,64,128]{3,2,1,0:T(8,128)(2,1)S(1)}, bf16[4,2,64,128]{3,2,1,0:T(8,128)(2,1)S(1)}, u32[]{:S(2)}, u32[]{:S(2)}) collective-permute-start(bf16[4,2,64,128]{3,2,1,0:T(8,128)(2,1)S(1)} %get-tuple-element.11.own), channel_id=1, source_target_pairs={{0,16},{16,0},{32,48},{48,32},{64,80},{80,64},{96,112},{112,96},{1... | collective-permute-start | bytes 393224 | tf_op jit(solution)/shard_map/ppermute | solution.py:222
  40.3 5.1 %collective-permute-start.12 = (bf16[27,16,128]{2,1,0:T(8,128)(2,1)S(1)}, bf16[27,16,128]{2,1,0:T(8,128)(2,1)S(1)}, u32[]{:S(2)}, u32[]{:S(2)}) collective-permute-start(bf16[27,16,128]{2,1,0:T(8,128)(2,1)S(1)} %get-tuple-element.12), channel_id=1, source_target_pairs={{0,4},{1,5},{2,6},{3,7},{4,0},{5,1},{6,2},{7,3},{8,12},{9,13},{10,... | collective-permute-start | bytes 331784 | tf_op jit(solution)/shard_map/ppermute | solution.py:220
  41.9 6.0 %collective-permute-start.13 = (bf16[27,16,128]{2,1,0:T(8,128)(2,1)S(1)}, bf16[27,16,128]{2,1,0:T(8,128)(2,1)S(1)}, u32[]{:S(2)}, u32[]{:S(2)}) collective-permute-start(bf16[27,16,128]{2,1,0:T(8,128)(2,1)S(1)} %get-tuple-element.12), channel_id=1, source_target_pairs={{0,12},{1,13},{2,14},{3,15},{4,8},{5,9},{6,10},{7,11},{8,4},{9,5},... | collective-permute-start | bytes 331784 | tf_op jit(solution)/shard_map/ppermute | solution.py:220
  48.7 5.7 %collective-permute-start.14 = (f32[16,640]{1,0:T(8,128)S(1)}, f32[16,640]{1,0:T(8,128)S(1)}, u32[]{:S(2)}, u32[]{:S(2)}) collective-permute-start(f32[16,640]{1,0:T(8,128)S(1)} %get-tuple-element.14), channel_id=1, source_target_pairs={{0,8},{1,9},{2,10},{3,11},{4,12},{5,13},{6,14},{7,15},{8,0},{9,1},... | collective-permute-start | bytes 122888 | tf_op jit(solution)/shard_map/ppermute | solution.py:224
  50.1 4.3 %collective-permute-start.15 = (f32[16,640]{1,0:T(8,128)S(1)}, f32[16,640]{1,0:T(8,128)S(1)}, u32[]{:S(2)}, u32[]{:S(2)}) collective-permute-start(f32[16,640]{1,0:T(8,128)S(1)} %get-tuple-element.15), channel_id=1, source_target_pairs={{0,4},{1,5},{2,6},{3,7},{4,0},{5,1},{6,2},{7,3},{8,12},{9,13},{10,... | collective-permute-start | bytes 122888 | tf_op jit(solution)/shard_map/ppermute | solution.py:224
  51.7 5.2 %copy-start.4 = (f32[16]{0:T(128)S(1)}, f32[16]{0:T(128)}, u32[]{:S(2)}) copy-start(f32[16]{0:T(128)} %param.9) | copy-start | bytes 196
  51.7 5.2 %collective-permute-start.16 = (f32[16,640]{1,0:T(8,128)S(1)}, f32[16,640]{1,0:T(8,128)S(1)}, u32[]{:S(2)}, u32[]{:S(2)}) collective-permute-start(f32[16,640]{1,0:T(8,128)S(1)} %get-tuple-element.16), channel_id=1, source_target_pairs={{0,12},{1,13},{2,14},{3,15},{4,8},{5,9},{6,10},{7,11},{8,4},{9,5},... | collective-permute-start | bytes 122888 | tf_op jit(solution)/shard_map/ppermute | solution.py:224

commit v6 on v5

--- a/solution.py
+++ b/solution.py
@@ -17,12 +17,17 @@
     return [(i, min(max(((i - 1) ^ 1) + 1, 0), count - 1)) for i in range(count)]
 
 
+def far_and_z():
+    pairs = [(d, d + 1) for d in range(1, 15, 2)] + [(15, 0)]
+    return [[d * 16 + 4 * y + z for d in pair for z in range(4)] for pair in pairs for y in range(4)]
+
+
 def inner(axis):
     i = lax.axis_index(axis)
     return (i > 0) & (i < 15)
 
 
-def fine_kernel(vol, x2, x1, r2, r1, w2, c2, c1, w, bias, out, cells, peak):
+def fine_kernel(vol, x2, x1, r2, r1, c2, c1, other, w, bias, out, cells, peak):
     pd = lax.rem(lax.axis_index("depth"), 2)
     pr = lax.rem(lax.axis_index("rows"), 2)
     inner_d = inner("depth")
@@ -75,56 +80,41 @@
                 best = value if best is None else jnp.maximum(best, value)
         peak[...] = best
         pooled = jnp.maximum(peak[pl.ds(0, 64, stride=2), :], peak[pl.ds(1, 64, stride=2), :])
-        out[q + pr * (1 - 2 * q)] = jnp.maximum(pooled + bias[...], 0.0).astype(BF16)
-
-
-def fine_level(vol, x2, x1, r2, r1, w2, c2, c1, w, bias):
+        value = jnp.maximum(pooled + bias[...], 0.0).astype(BF16)
+        for k in range(8):
+            out[k, q + pr * (1 - 2 * q)] = value
+
+
+def fine_level(vol, x2, x1, r2, r1, c2, c1, other, w, bias):
     vmem = pl.BlockSpec(memory_space=pltpu.VMEM)
     return pl.pallas_call(
         fine_kernel,
-        out_shape=jax.ShapeDtypeStruct((2, 64, 128), BF16),
-        in_specs=[vmem] * 5 + [pl.BlockSpec(memory_space=pl.ANY)] + [vmem] * 4,
+        out_shape=jax.ShapeDtypeStruct((8, 2, 64, 128), BF16),
+        in_specs=[vmem] * 7 + [pl.BlockSpec(memory_space=pl.ANY)] + [vmem] * 2,
         out_specs=vmem,
         scratch_shapes=[pltpu.VMEM((4, 6, 128, 128), BF16), pltpu.VMEM((128, 128), F32)],
         compiler_params=pltpu.CompilerParams(vmem_limit_bytes=32 * 1024 * 1024),
-    )(vol, x2, x1, r2, r1, w2, c2, c1, w, bias)
-
-
-def assemble_kernel(p0, p1, p2, p3, w, plane, kept):
-    for k, piece in enumerate((p0, p1, p2, p3)):
-        plane[k] = piece[...]
-    kept[...] = w[...]
-
-
-def assemble(pieces, w):
-    vmem = pl.BlockSpec(memory_space=pltpu.VMEM)
-    return pl.pallas_call(
-        assemble_kernel,
-        out_shape=[jax.ShapeDtypeStruct((4, 2, 64, 128), BF16), jax.ShapeDtypeStruct(w.shape, BF16)],
-        in_specs=[vmem] * 5,
-        out_specs=[vmem] * 2,
-        compiler_params=pltpu.CompilerParams(vmem_limit_bytes=8 * 1024 * 1024),
-    )(*pieces, w)
-
-
-def coarse_kernel(own, far, near, w0, w1, w2, w3, o0, o1, o2, o3, cells):
+    )(vol, x2, x1, r2, r1, c2, c1, other, w, bias)
+
+
+def coarse_kernel(both, near, pair, other, o0, o1, o2, o3, cells):
     pd = lax.rem(lax.axis_index("depth"), 2)
-    z = lax.rem(lax.axis_index("rows"), 4)
     inner_d = inner("depth")
     for a in range(3):
         for i in (0, 1, 10, 11):
             cells[a, i] = jnp.zeros((64, 128), BF16)
-    for m, k in enumerate((0, 3, 2, 1)):
-        cells[0, pl.ds(2 + 2 * (z ^ k), 2)] = jnp.where(inner_d, far[m], jnp.zeros_like(far[m]))
-        cells[1, pl.ds(2 + 2 * (z ^ k), 2)] = own[m]
-        cells[2, pl.ds(2 + 2 * (z ^ k), 2)] = near[m]
+    for k in range(4):
+        far = both[pd, k]
+        cells[0, 2 + 2 * k : 4 + 2 * k] = jnp.where(inner_d, far, jnp.zeros_like(far))
+        cells[1, 2 + 2 * k : 4 + 2 * k] = both[1 - pd, k]
+        cells[2, 2 + 2 * k : 4 + 2 * k] = near[k]
     lhs = jnp.concatenate(
         [
             jnp.concatenate(
-                [w[9 * (a + pd * (2 - 2 * a)) + 3 * b + c] for a in range(3) for b in range(3)], axis=1
+                [w[m, 9 * (a + pd * (2 - 2 * a)) + 3 * b + c] for a in range(3) for b in range(3)], axis=1
             )
             for c in range(3)
-            for w in (w0, w1, w2, w3)
+            for w, m in ((pair, 0), (pair, 1), (other, 0), (other, 1))
         ],
         axis=0,
     )
@@ -148,16 +138,16 @@
             out[:, start : start + size] = value[16 * k : 16 * k + 16]
 
 
-def coarse_level(pieces, weights):
+def coarse_level(both, near, pair, other):
     vmem = pl.BlockSpec(memory_space=pltpu.VMEM)
     return pl.pallas_call(
         coarse_kernel,
         out_shape=[jax.ShapeDtypeStruct((16, 640), F32)] * 4,
-        in_specs=[vmem] * 7,
+        in_specs=[vmem] * 4,
         out_specs=[vmem] * 4,
         scratch_shapes=[pltpu.VMEM((3, 12, 64, 128), BF16)],
         compiler_params=pltpu.CompilerParams(vmem_limit_bytes=32 * 1024 * 1024),
-    )(*pieces, *weights)
+    )(both, near, pair, other)
 
 
 def join_kernel(s0, s2, s1, s3, bias, out, held):
@@ -204,23 +194,21 @@
     c2 = lax.ppermute(lax.dynamic_index_in_dim(sides, 3 * pr, 1, False), "rows", rows_far)
     c1 = lax.ppermute(lax.dynamic_index_in_dim(sides, 3 - 3 * pr, 1, False), "rows", rows_near)
 
-    def along_z(k):
-        return [(i, i ^ k) for i in range(16)]
-
     def along_y(k):
         return [(i, i ^ (4 * k)) for i in range(16)]
 
     w = jnp.transpose(coarse_filters, (0, 1, 2, 4, 3)).reshape(27, 16, 128)
-    w2 = lax.ppermute(w, "rows", along_y(2))
+    pair = jnp.stack([w, lax.ppermute(w, "rows", along_y(1))])
+    other = lax.ppermute(pair, "rows", along_y(2))
     pooled = fine_level(
-        volume, x2, x1, r2, r1, w2, c2, c1, fine_filters, fine_bias.reshape(1, 128)
-    )
-
-    plane, kept = assemble([pooled] + [lax.ppermute(pooled, "rows", along_z(k)) for k in (3, 2, 1)], w)
-    w1, w3 = [lax.ppermute(kept, "rows", along_y(k)) for k in (1, 3)]
-    far = lax.ppermute(plane, "depth", depth_far)
-    near = lax.ppermute(plane, "depth", depth_near)
-    sums = coarse_level((plane, far, near), (w, w1, w2, w3))
+        volume, x2, x1, r2, r1, c2, c1, other, fine_filters, fine_bias.reshape(1, 128)
+    )
+
+    both = lax.all_to_all(
+        pooled, ("depth", "rows"), 0, 0, axis_index_groups=far_and_z(), tiled=True
+    ).reshape(2, 4, 2, 64, 128)
+    near = lax.ppermute(lax.dynamic_index_in_dim(both, 1 - pd, 0, False), "depth", depth_near)
+    sums = coarse_level(both, near, pair, other)
     parts = [sums[0]] + [lax.ppermute(sums[k], "rows", along_y(k)) for k in (2, 1, 3)]
     result = join(parts, jnp.broadcast_to(coarse_bias[:, None], (16, 128)))
     return result.reshape(16, 1, 2048)

time: 57.8 us -> 56.6 us (0.979)
  blocking collectives: 0 us -> 13.5 us
  starting transfers between devices: 39.1 us -> 29.3 us
  waiting for transfers between devices: 14.2 us -> 9.21 us
    all_to_all x0 -> x1, blocking collectives: none -> 13.5 us  [body(): lax.all_to_all(pooled, ('depth', 'rows'), 0, 0, axis_index_groups=far_and...]
    ppermute x8 -> x3, starting transfers between devices: 16 us -> 7.01 us  [the longest x1 2.99 us: body(): other = lax.ppermute(pair, 'rows', along_y(2))]
    ppermute x8 -> x3, waiting for transfers between devices: 7.31 us -> 0.99 us  [the longest x1 0.99 us: body(): lax.ppermute(lax.dynamic_index_in_dim(both, 1 - pd, 0, False), 'depth', d...]
    ppermute x3, waiting for transfers between devices: 3.99 us -> 5.27 us  [body(): lax.ppermute(sums[k], 'rows', along_y(k))]
    ppermute x1, starting transfers between devices: 4.96 us -> 3.82 us  [body(): lax.ppermute(lax.dynamic_index_in_dim(sides, 3 - 3 * pr, 1, False), 'rows...]
    pallas_call x2 -> x1, Pallas kernels: 1.52 us -> 1.52 us  [fine_level(): pl.pallas_call(fine_kernel, out_shape=jax.ShapeDtypeStruct((8, 2, 64, 128...]
  transfers between devices with their start and end apart: 17 -> 12, of which waited for: 7 -> 4; matrix products, arithmetic and copies ran while one was open for 0% -> 2% of each run, Pallas kernels for 0% -> 0%
where the time goes in v6:
time: 56.6 us; the launch traced here: 56.3 us
  starting transfers between devices  29.3 us (52%)
  blocking collectives  13.5 us (24%)
  waiting for transfers between devices  9.21 us (16%)
  Pallas kernels  2.97 us (5%)
  local copies, waits for them, and re-layouts  1.13 us (2%)
    all_to_all x1, blocking collectives, body(): lax.all_to_all(pooled, ('depth', 'rows'), 0, 0, axis_index_groups=far_and...  13.5 us
    ppermute x1, starting transfers between devices, body(): lax.ppermute(lax.dynamic_index_in_dim(volume, 1 - pd, 0, False), 'depth',...  7.29 us
    ppermute x3, waiting for transfers between devices, body(): lax.ppermute(sums[k], 'rows', along_y(k))  5.27 us
    ppermute x3, starting transfers between devices, body(): lax.ppermute(sums[k], 'rows', along_y(k))  4.47 us
    ppermute x1, starting transfers between devices, body(): lax.ppermute(lax.dynamic_index_in_dim(sides, 3 - 3 * pr, 1, False), 'rows...  3.82 us
    ppermute x1, starting transfers between devices, body(): lax.ppermute(lax.dynamic_index_in_dim(volume, 3 - 3 * pr, 1, False), 'row...  3.37 us
    ppermute x1, starting transfers between devices, body(): other = lax.ppermute(pair, 'rows', along_y(2))  2.99 us
    ppermute x1, waiting for transfers between devices, body(): lax.ppermute(lax.dynamic_index_in_dim(sides, 3 - 3 * pr, 1, False), 'rows...  2.94 us
  transfers between devices with their start and end apart: 12, of which 4 were waited for; matrix products, arithmetic and copies ran while one was open for 2% of the time, Pallas kernels for 0%

profile of v6, /device:TPU:6, one launch (start us, length us, event | category | flops | bytes accessed | tf_op | source)
XLA Modules:
  0.0 56.3 jit_solution(14527678965518125859)
XLA Ops:
  0.0 1.6 %collective-permute-start.6 = (bf16[27,16,128]{2,1,0:T(8,128)(2,1)}, bf16[27,16,128]{2,1,0:T(8,128)(2,1)S(1)}, u32[]{:S(2)}, u32[]{:S(2)}) collective-permute-start(bf16[27,16,128]{2,1,0:T(8,128)(2,1)} %bitcast.30), channel_id=1, source_target_pairs={{0,4},{1,5},{2,6},{3,7},{4,0},{5,1},{6,2},{7,3},{8,12},{9,13},{10,... | collective-permute-start | bytes 331784 | tf_op jit(solution)/shard_map/ppermute | solution.py:201
  1.6 1.0 %dynamic-slice_bitcast_fusion.1 = (bf16[4,128,128]{2,1,0:T(8,128)(2,1)S(1)}, bf16[4,128,128]{2,1,0:T(8,128)(2,1)S(1)}) fusion(bf16[2,4,128,128]{3,2,1,0:T(8,128)(2,1)} %vol.1, s32[]{:T(128)S(6)} %select_n.19, s32[]{:T(128)S(6)} %select_n.18), kind=kLoop, calls=%fused_computation.6 | loop fusion | bytes 524296 | tf_op jit(solution)/shard_map/jit(dynamic_index_in_dim)/squeeze | solution.py:190
  2.6 0.0 copy-start
  2.6 2.1 %collective-permute-start = (bf16[4,128,128]{2,1,0:T(8,128)(2,1)S(1)}, bf16[4,128,128]{2,1,0:T(8,128)(2,1)S(1)}, u32[]{:S(2)}, u32[]{:S(2)}) collective-permute-start(bf16[4,128,128]{2,1,0:T(8,128)(2,1)S(1)} %get-tuple-element.18), channel_id=1, source_target_pairs={{0,0},{16,32},{32,16},{48,64},{64,48},{80,96},{96,80},{112,128},{1... | collective-permute-start | bytes 393224 | tf_op jit(solution)/shard_map/ppermute | solution.py:189
  4.7 7.3 %collective-permute-start.1 = (bf16[4,128,128]{2,1,0:T(8,128)(2,1)S(1)}, bf16[4,128,128]{2,1,0:T(8,128)(2,1)S(1)}, u32[]{:S(2)}, u32[]{:S(2)}) collective-permute-start(bf16[4,128,128]{2,1,0:T(8,128)(2,1)S(1)} %get-tuple-element.17), channel_id=1, source_target_pairs={{0,16},{16,0},{32,48},{48,32},{64,80},{80,64},{96,112},{112,96},{1... | collective-permute-start | bytes 393224 | tf_op jit(solution)/shard_map/ppermute | solution.py:190
  12.0 3.0 %collective-permute-start.7 = (bf16[2,27,16,128]{3,2,1,0:T(8,128)(2,1)S(1)}, bf16[2,27,16,128]{3,2,1,0:T(8,128)(2,1)S(1)}, u32[]{:S(2)}, u32[]{:S(2)}) collective-permute-start(bf16[2,27,16,128]{3,2,1,0:T(8,128)(2,1)S(1)} %pad_maximum_fusion.pair), channel_id=1, source_target_pairs={{0,8},{1,9},{2,10},{3,11},{4,12},{5,13},{6,14},{7,15},{8,0},{9,1},... | collective-permute-start | bytes 663560 | tf_op jit(solution)/shard_map/ppermute | solution.py:202
  15.0 0.7 %collective-permute-start.2 = (bf16[2,128,128]{2,1,0:T(8,128)(2,1)S(1)}, bf16[2,128,128]{2,1,0:T(8,128)(2,1)S(1)}, u32[]{:S(2)}, u32[]{:S(2)}) collective-permute-start(bf16[2,128,128]{2,1,0:T(8,128)(2,1)S(1)} %get-tuple-element.16), channel_id=1, source_target_pairs={{0,0},{1,2},{2,1},{3,4},{4,3},{5,6},{6,5},{7,8},{8,7},{9,10},{10,9... | collective-permute-start | bytes 196616 | tf_op jit(solution)/shard_map/ppermute | solution.py:191
  15.7 3.4 %collective-permute-start.3 = (bf16[2,128,128]{2,1,0:T(8,128)(2,1)S(1)}, bf16[2,128,128]{2,1,0:T(8,128)(2,1)S(1)}, u32[]{:S(2)}, u32[]{:S(2)}) collective-permute-start(bf16[2,128,128]{2,1,0:T(8,128)(2,1)S(1)} %get-tuple-element.15), channel_id=1, source_target_pairs={{0,1},{1,0},{2,3},{3,2},{4,5},{5,4},{6,7},{7,6},{8,9},{9,8},{10,11... | collective-permute-start | bytes 196616 | tf_op jit(solution)/shard_map/ppermute | solution.py:192
  19.1 0.7 %collective-permute-start.4 = (bf16[2,128,128]{2,1,0:T(8,128)(2,1)S(1)}, bf16[2,128,128]{2,1,0:T(8,128)(2,1)S(1)}, u32[]{:S(2)}, u32[]{:S(2)}) collective-permute-start(bf16[2,128,128]{2,1,0:T(8,128)(2,1)S(1)} %get-tuple-element.14), channel_id=1, source_target_pairs={{0,0},{1,2},{2,1},{3,4},{4,3},{5,6},{6,5},{7,8},{8,7},{9,10},{10,9... | collective-permute-start | bytes 196616 | tf_op jit(solution)/shard_map/ppermute | solution.py:194
  19.8 0.0 copy-start.2
  19.8 3.8 %collective-permute-start.5 = (bf16[2,128,128]{2,1,0:T(8,128)(2,1)S(1)}, bf16[2,128,128]{2,1,0:T(8,128)(2,1)S(1)}, u32[]{:S(2)}, u32[]{:S(2)}) collective-permute-start(bf16[2,128,128]{2,1,0:T(8,128)(2,1)S(1)} %get-tuple-element.13), channel_id=1, source_target_pairs={{0,1},{1,0},{2,3},{3,2},{4,5},{5,4},{6,7},{7,6},{8,9},{9,8},{10,11... | collective-permute-start | bytes 196616 | tf_op jit(solution)/shard_map/ppermute | solution.py:195
  23.6 2.9 %collective-permute-done.5.c1 = bf16[2,128,128]{2,1,0:T(8,128)(2,1)S(1)} collective-permute-done((bf16[2,128,128]{2,1,0:T(8,128)(2,1)S(1)}, bf16[2,128,128]{2,1,0:T(8,128)(2,1)S(1)}, u32[]{:S(2)}, u32[]{:S(2)}) %collective-permute-start.5) | collective-permute-done | bytes 65568 | tf_op jit(solution)/shard_map/ppermute | solution.py:195
  26.5 1.5 %shard_map.55 = bf16[8,2,64,128]{3,2,1,0:T(8,128)(2,1)S(1)} custom-call(bf16[2,4,128,128]{3,2,1,0:T(8,128)(2,1)S(1)} %copy-done, bf16[4,128,128]{2,1,0:T(8,128)(2,1)S(1)} %collective-permute-done.x2, bf16[4,128,128]{2,1,0:T(8,128)(2,1)S(1)} %collective-permute-done.1.x1, bf16[2,128,128]{2,1,0:T(8,128)(2,1)S(1)} %collective-permute-done.2.r2, ...), custom_call_target="tpu_custom_call" | custom-call | tf_op jit(solution)/shard_map/pallas_call | solution.py:90
  28.1 13.5 %all_to_all.5 = bf16[8,2,64,128]{3,2,1,0:T(8,128)(2,1)S(1)} all-to-all(bf16[8,2,64,128]{3,2,1,0:T(8,128)(2,1)S(1)} %shard_map.55), channel_id=1, replica_groups={{16,17,18,19,32,33,34,35},{20,21,22,23,36,37,38,39},{24,25,26,27,40,41,..., dimensions={0} | all-to-all | bytes 524288 | tf_op jit(solution)/shard_map/all_to_all | solution.py:207
  41.6 2.4 %collective-permute-start.8 = (bf16[4,2,64,128]{3,2,1,0:T(8,128)(2,1)S(1)}, bf16[4,2,64,128]{3,2,1,0:T(8,128)(2,1)S(1)}, u32[]{:S(2)}, u32[]{:S(2)}) collective-permute-start(bf16[4,2,64,128]{3,2,1,0:T(8,128)(2,1)S(1)} %dynamic-slice_bitcast_fusion), channel_id=1, source_target_pairs={{0,16},{16,0},{32,48},{48,32},{64,80},{80,64},{96,112},{112,96},{1... | collective-permute-start | bytes 393224 | tf_op jit(solution)/shard_map/ppermute | solution.py:210
  44.0 1.0 %collective-permute-done.8.near = bf16[4,2,64,128]{3,2,1,0:T(8,128)(2,1)S(1)} collective-permute-done((bf16[4,2,64,128]{3,2,1,0:T(8,128)(2,1)S(1)}, bf16[4,2,64,128]{3,2,1,0:T(8,128)(2,1)S(1)}, u32[]{:S(2)}, u32[]{:S(2)}) %collective-permute-start.8) | collective-permute-done | bytes 131104 | tf_op jit(solution)/shard_map/ppermute | solution.py:210
  45.0 0.8 %shard_map.56 = (f32[16,640]{1,0:T(8,128)S(1)}, f32[16,640]{1,0:T(8,128)S(1)}, f32[16,640]{1,0:T(8,128)S(1)}, f32[16,640]{1,0:T(8,128)S(1)}) custom-call(bf16[2,4,2,64,128]{4,3,2,1,0:T(8,128)(2,1)S(1)} %bitcast.26, bf16[4,2,64,128]{3,2,1,0:T(8,128)(2,1)S(1)} %collective-permute-done.8.near, bf16[2,27,16,128]{3,2,1,0:T(8,128)(2,1)S(1)} %pad_maximum_fusion.pair, ...), custom_call_target="tpu_custom_call" | custom-call | tf_op jit(solution)/shard_map/pallas_call | solution.py:143
  45.8 2.2 %collective-permute-start.10 = (f32[16,640]{1,0:T(8,128)S(1)}, f32[16,640]{1,0:T(8,128)S(1)}, u32[]{:S(2)}, u32[]{:S(2)}) collective-permute-start(f32[16,640]{1,0:T(8,128)S(1)} %get-tuple-element.11), channel_id=1, source_target_pairs={{0,4},{1,5},{2,6},{3,7},{4,0},{5,1},{6,2},{7,3},{8,12},{9,13},{10,... | collective-permute-start | bytes 122888 | tf_op jit(solution)/shard_map/ppermute | solution.py:212
  48.0 2.0 %collective-permute-start.11 = (f32[16,640]{1,0:T(8,128)S(1)}, f32[16,640]{1,0:T(8,128)S(1)}, u32[]{:S(2)}, u32[]{:S(2)}) collective-permute-start(f32[16,640]{1,0:T(8,128)S(1)} %get-tuple-element.12), channel_id=1, source_target_pairs={{0,12},{1,13},{2,14},{3,15},{4,8},{5,9},{6,10},{7,11},{8,4},{9,5},... | collective-permute-start | bytes 122888 | tf_op jit(solution)/shard_map/ppermute | solution.py:212
  50.0 0.2 collective-permute-start.9
  50.3 2.9 %collective-permute-done.11.s3 = f32[16,640]{1,0:T(8,128)S(1)} collective-permute-done((f32[16,640]{1,0:T(8,128)S(1)}, f32[16,640]{1,0:T(8,128)S(1)}, u32[]{:S(2)}, u32[]{:S(2)}) %collective-permute-start.11) | collective-permute-done | bytes 40992 | tf_op jit(solution)/shard_map/ppermute | solution.py:212
  53.2 2.3 %collective-permute-done.9.s2 = f32[16,640]{1,0:T(8,128)S(1)} collective-permute-done((f32[16,640]{1,0:T(8,128)S(1)}, f32[16,640]{1,0:T(8,128)S(1)}, u32[]{:S(2)}, u32[]{:S(2)}) %collective-permute-start.9) | collective-permute-done | bytes 40992 | tf_op jit(solution)/shard_map/ppermute | solution.py:212
  55.6 0.1 broadcast_in_dim.2.bias
  55.6 0.7 %shard_map.57 = bf16[16,2048]{1,0:T(8,128)(2,1)} custom-call(f32[16,640]{1,0:T(8,128)S(1)} %get-tuple-element.9.s0, f32[16,640]{1,0:T(8,128)S(1)} %collective-permute-done.9.s2, f32[16,640]{1,0:T(8,128)S(1)} %collective-permute-done.10.s1, f32[16,640]{1,0:T(8,128)S(1)} %collective-permute-done.11.s3, f32[16,128]{1,0:T(8,128)S(1)} %broadcast_in_dim.2.bias), custom_call_target="tpu_custom_call" | custom-call | tf_op jit(solution)/shard_map/pallas_call | solution.py:171
  (20 shorter events, 0.1 us)
Async XLA Ops:
  0.0 12.0 %collective-permute-start.6 = (bf16[27,16,128]{2,1,0:T(8,128)(2,1)}, bf16[27,16,128]{2,1,0:T(8,128)(2,1)S(1)}, u32[]{:S(2)}, u32[]{:S(2)}) collective-permute-start(bf16[27,16,128]{2,1,0:T(8,128)(2,1)} %bitcast.30), channel_id=1, source_target_pairs={{0,4},{1,5},{2,6},{3,7},{4,0},{5,1},{6,2},{7,3},{8,12},{9,13},{10,... | collective-permute-start | bytes 331784 | tf_op jit(solution)/shard_map/ppermute | solution.py:201
  1.6 10.4 %copy-start.3 = (bf16[3,3,3,128,16]{3,4,2,1,0:T(8,128)(2,1)S(1)}, bf16[3,3,3,128,16]{3,4,2,1,0:T(8,128)(2,1)}, u32[]{:S(2)}) copy-start(bf16[3,3,3,128,16]{3,4,2,1,0:T(8,128)(2,1)} %param.8) | copy-start | bytes 331780
  2.6 12.4 %copy-start = (bf16[2,4,128,128]{3,2,1,0:T(8,128)(2,1)S(1)}, bf16[2,4,128,128]{3,2,1,0:T(8,128)(2,1)}, u32[]{:S(2)}) copy-start(bf16[2,4,128,128]{3,2,1,0:T(8,128)(2,1)} %vol.1) | copy-start | bytes 786436
  2.6 23.9 %copy-start.1 = (bf16[3,3,3,128,128]{4,3,2,1,0:T(8,128)(2,1)S(1)}, bf16[3,3,3,128,128]{4,3,2,1,0:T(8,128)(2,1)}, u32[]{:S(2)}) copy-start(bf16[3,3,3,128,128]{4,3,2,1,0:T(8,128)(2,1)} %w.1) | copy-start | bytes 2654212
  2.6 16.4 %collective-permute-start = (bf16[4,128,128]{2,1,0:T(8,128)(2,1)S(1)}, bf16[4,128,128]{2,1,0:T(8,128)(2,1)S(1)}, u32[]{:S(2)}, u32[]{:S(2)}) collective-permute-start(bf16[4,128,128]{2,1,0:T(8,128)(2,1)S(1)} %get-tuple-element.18), channel_id=1, source_target_pairs={{0,0},{16,32},{32,16},{48,64},{64,48},{80,96},{96,80},{112,128},{1... | collective-permute-start | bytes 393224 | tf_op jit(solution)/shard_map/ppermute | solution.py:189
  4.7 14.4 %collective-permute-start.1 = (bf16[4,128,128]{2,1,0:T(8,128)(2,1)S(1)}, bf16[4,128,128]{2,1,0:T(8,128)(2,1)S(1)}, u32[]{:S(2)}, u32[]{:S(2)}) collective-permute-start(bf16[4,128,128]{2,1,0:T(8,128)(2,1)S(1)} %get-tuple-element.17), channel_id=1, source_target_pairs={{0,16},{16,0},{32,48},{48,32},{64,80},{80,64},{96,112},{112,96},{1... | collective-permute-start | bytes 393224 | tf_op jit(solution)/shard_map/ppermute | solution.py:190
  12.0 14.5 %collective-permute-start.7 = (bf16[2,27,16,128]{3,2,1,0:T(8,128)(2,1)S(1)}, bf16[2,27,16,128]{3,2,1,0:T(8,128)(2,1)S(1)}, u32[]{:S(2)}, u32[]{:S(2)}) collective-permute-start(bf16[2,27,16,128]{3,2,1,0:T(8,128)(2,1)S(1)} %pad_maximum_fusion.pair), channel_id=1, source_target_pairs={{0,8},{1,9},{2,10},{3,11},{4,12},{5,13},{6,14},{7,15},{8,0},{9,1},... | collective-permute-start | bytes 663560 | tf_op jit(solution)/shard_map/ppermute | solution.py:202
  15.0 8.6 %collective-permute-start.2 = (bf16[2,128,128]{2,1,0:T(8,128)(2,1)S(1)}, bf16[2,128,128]{2,1,0:T(8,128)(2,1)S(1)}, u32[]{:S(2)}, u32[]{:S(2)}) collective-permute-start(bf16[2,128,128]{2,1,0:T(8,128)(2,1)S(1)} %get-tuple-element.16), channel_id=1, source_target_pairs={{0,0},{1,2},{2,1},{3,4},{4,3},{5,6},{6,5},{7,8},{8,7},{9,10},{10,9... | collective-permute-start | bytes 196616 | tf_op jit(solution)/shard_map/ppermute | solution.py:191
  15.7 7.9 %collective-permute-start.3 = (bf16[2,128,128]{2,1,0:T(8,128)(2,1)S(1)}, bf16[2,128,128]{2,1,0:T(8,128)(2,1)S(1)}, u32[]{:S(2)}, u32[]{:S(2)}) collective-permute-start(bf16[2,128,128]{2,1,0:T(8,128)(2,1)S(1)} %get-tuple-element.15), channel_id=1, source_target_pairs={{0,1},{1,0},{2,3},{3,2},{4,5},{5,4},{6,7},{7,6},{8,9},{9,8},{10,11... | collective-permute-start | bytes 196616 | tf_op jit(solution)/shard_map/ppermute | solution.py:192
  19.1 4.5 %collective-permute-start.4 = (bf16[2,128,128]{2,1,0:T(8,128)(2,1)S(1)}, bf16[2,128,128]{2,1,0:T(8,128)(2,1)S(1)}, u32[]{:S(2)}, u32[]{:S(2)}) collective-permute-start(bf16[2,128,128]{2,1,0:T(8,128)(2,1)S(1)} %get-tuple-element.14), channel_id=1, source_target_pairs={{0,0},{1,2},{2,1},{3,4},{4,3},{5,6},{6,5},{7,8},{8,7},{9,10},{10,9... | collective-permute-start | bytes 196616 | tf_op jit(solution)/shard_map/ppermute | solution.py:194
  19.8 6.8 %copy-start.2 = (f32[128]{0:T(128)S(1)}, f32[128]{0:T(128)}, u32[]{:S(2)}) copy-start(f32[128]{0:T(128)} %param.7) | copy-start | bytes 1540
  19.8 6.8 %collective-permute-start.5 = (bf16[2,128,128]{2,1,0:T(8,128)(2,1)S(1)}, bf16[2,128,128]{2,1,0:T(8,128)(2,1)S(1)}, u32[]{:S(2)}, u32[]{:S(2)}) collective-permute-start(bf16[2,128,128]{2,1,0:T(8,128)(2,1)S(1)} %get-tuple-element.13), channel_id=1, source_target_pairs={{0,1},{1,0},{2,3},{3,2},{4,5},{5,4},{6,7},{7,6},{8,9},{9,8},{10,11... | collective-permute-start | bytes 196616 | tf_op jit(solution)/shard_map/ppermute | solution.py:195
  41.6 3.4 %collective-permute-start.8 = (bf16[4,2,64,128]{3,2,1,0:T(8,128)(2,1)S(1)}, bf16[4,2,64,128]{3,2,1,0:T(8,128)(2,1)S(1)}, u32[]{:S(2)}, u32[]{:S(2)}) collective-permute-start(bf16[4,2,64,128]{3,2,1,0:T(8,128)(2,1)S(1)} %dynamic-slice_bitcast_fusion), channel_id=1, source_target_pairs={{0,16},{16,0},{32,48},{48,32},{64,80},{80,64},{96,112},{112,96},{1... | collective-permute-start | bytes 393224 | tf_op jit(solution)/shard_map/ppermute | solution.py:210
  45.8 4.5 %collective-permute-start.10 = (f32[16,640]{1,0:T(8,128)S(1)}, f32[16,640]{1,0:T(8,128)S(1)}, u32[]{:S(2)}, u32[]{:S(2)}) collective-permute-start(f32[16,640]{1,0:T(8,128)S(1)} %get-tuple-element.11), channel_id=1, source_target_pairs={{0,4},{1,5},{2,6},{3,7},{4,0},{5,1},{6,2},{7,3},{8,12},{9,13},{10,... | collective-permute-start | bytes 122888 | tf_op jit(solution)/shard_map/ppermute | solution.py:212
  48.0 5.2 %collective-permute-start.11 = (f32[16,640]{1,0:T(8,128)S(1)}, f32[16,640]{1,0:T(8,128)S(1)}, u32[]{:S(2)}, u32[]{:S(2)}) collective-permute-start(f32[16,640]{1,0:T(8,128)S(1)} %get-tuple-element.12), channel_id=1, source_target_pairs={{0,12},{1,13},{2,14},{3,15},{4,8},{5,9},{6,10},{7,11},{8,4},{9,5},... | collective-permute-start | bytes 122888 | tf_op jit(solution)/shard_map/ppermute | solution.py:212
  50.0 5.5 %copy-start.4 = (f32[16]{0:T(128)S(1)}, f32[16]{0:T(128)}, u32[]{:S(2)}) copy-start(f32[16]{0:T(128)} %param.9) | copy-start | bytes 196
  50.0 5.5 %collective-permute-start.9 = (f32[16,640]{1,0:T(8,128)S(1)}, f32[16,640]{1,0:T(8,128)S(1)}, u32[]{:S(2)}, u32[]{:S(2)}) collective-permute-start(f32[16,640]{1,0:T(8,128)S(1)} %get-tuple-element.10), channel_id=1, source_target_pairs={{0,8},{1,9},{2,10},{3,11},{4,12},{5,13},{6,14},{7,15},{8,0},{9,1},... | collective-permute-start | bytes 122888 | tf_op jit(solution)/shard_map/ppermute | solution.py:212

commit v7 on v6

--- a/solution.py
+++ b/solution.py
@@ -27,7 +27,13 @@
     return (i > 0) & (i < 15)
 
 
-def fine_kernel(vol, x2, x1, r2, r1, c2, c1, other, w, bias, out, cells, peak):
+def spread(line, col):
+    left = jnp.where(col == 0, 0.0, pltpu.roll(line[:, :128], 1, 0))
+    right = jnp.where(col == 127, 0.0, pltpu.roll(line[:, 256:], 127, 0))
+    return line[:, 128:256] + left + right
+
+
+def fine_kernel(vol, x2, x1, r2, r1, w, out, cells):
     pd = lax.rem(lax.axis_index("depth"), 2)
     pr = lax.rem(lax.axis_index("rows"), 2)
     inner_d = inner("depth")
@@ -39,9 +45,10 @@
             if j in (1, 2):
                 plane = (j - 1) + pd * (3 - 2 * j)
                 piece = r2[plane] if i == 0 else r1[plane] if i == 5 else vol[plane, row]
+            elif i in (0, 5):
+                piece = zero
             else:
-                side, slot = (x2, 0) if j == 0 else (x1, 1)
-                piece = c2[slot] if i == 0 else c1[slot] if i == 5 else side[row]
+                piece = (x2 if j == 0 else x1)[row]
             if i == 0:
                 piece = jnp.where(inner_r, piece, zero)
             if j == 0:
@@ -49,7 +56,7 @@
             cells[j, i] = piece
     taps = [(a, b) for a in range(3) for b in range(3)]
     groups = [taps[i : i + 2] for i in range(0, 9, 2)]
-    parts = []
+    col = lax.broadcasted_iota(jnp.int32, (128, 128), 0)
     for s in range(2):
         total = None
         for group in groups:
@@ -67,38 +74,68 @@
             )
             term = jnp.dot(lhs, rhs, preferred_element_type=F32)
             total = term if total is None else total + term
-        parts.append(total)
+        for t in range(4):
+            out[s, t] = spread(total[t * 128 : (t + 1) * 128], col)
+
+
+def fine_level(vol, x2, x1, r2, r1, w):
+    vmem = pl.BlockSpec(memory_space=pltpu.VMEM)
+    return pl.pallas_call(
+        fine_kernel,
+        out_shape=jax.ShapeDtypeStruct((2, 4, 128, 128), F32),
+        in_specs=[vmem] * 6,
+        out_specs=vmem,
+        scratch_shapes=[pltpu.VMEM((4, 6, 128, 128), BF16)],
+        compiler_params=pltpu.CompilerParams(vmem_limit_bytes=32 * 1024 * 1024),
+        cost_estimate=pl.CostEstimate(flops=20_000_000_000, bytes_accessed=0, transcendentals=0),
+    )(vol, x2, x1, r2, r1, w)
+
+
+def finish_kernel(sums, c2, c1, w, bias, out, peak):
+    pd = lax.rem(lax.axis_index("depth"), 2)
+    pr = lax.rem(lax.axis_index("rows"), 2)
+    inner_d = inner("depth")
+    inner_r = inner("rows")
+    zero = jnp.zeros((128, 128), BF16)
     col = lax.broadcasted_iota(jnp.int32, (128, 128), 0)
     for q in range(2):
+        edge = 2 * q
         best = None
         for s in range(2):
-            for t in range(2):
-                line = parts[s][(2 * q + t) * 128 : (2 * q + t + 1) * 128]
-                left = jnp.where(col == 0, 0.0, pltpu.roll(line[:, :128], 1, 0))
-                right = jnp.where(col == 127, 0.0, pltpu.roll(line[:, 256:], 127, 0))
-                value = line[:, 128:256] + left + right
-                best = value if best is None else jnp.maximum(best, value)
+            side = 2 * s
+            piece = (c2, c1)[q][s]
+            if q == 0:
+                piece = jnp.where(inner_r, piece, zero)
+            if s == 0:
+                piece = jnp.where(inner_d, piece, zero)
+            rhs = jnp.concatenate(
+                [w[side + pd * (2 - 2 * side), edge + pr * (2 - 2 * edge), c] for c in range(3)], axis=1
+            )
+            corner = spread(jnp.dot(piece, rhs, preferred_element_type=F32), col)
+            value = jnp.maximum(sums[s, 3 * q] + corner, sums[s, q + 1])
+            best = value if best is None else jnp.maximum(best, value)
         peak[...] = best
         pooled = jnp.maximum(peak[pl.ds(0, 64, stride=2), :], peak[pl.ds(1, 64, stride=2), :])
-        value = jnp.maximum(pooled + bias[...], 0.0).astype(BF16)
+        pooled = jnp.maximum(pooled + bias[...], 0.0).astype(BF16)
         for k in range(8):
-            out[k, q + pr * (1 - 2 * q)] = value
-
-
-def fine_level(vol, x2, x1, r2, r1, c2, c1, other, w, bias):
-    vmem = pl.BlockSpec(memory_space=pltpu.VMEM)
-    return pl.pallas_call(
-        fine_kernel,
+            out[k, q + pr * (1 - 2 * q)] = pooled
+
+
+def finish(sums, c2, c1, w, bias):
+    vmem = pl.BlockSpec(memory_space=pltpu.VMEM)
+    return pl.pallas_call(
+        finish_kernel,
         out_shape=jax.ShapeDtypeStruct((8, 2, 64, 128), BF16),
-        in_specs=[vmem] * 7 + [pl.BlockSpec(memory_space=pl.ANY)] + [vmem] * 2,
-        out_specs=vmem,
-        scratch_shapes=[pltpu.VMEM((4, 6, 128, 128), BF16), pltpu.VMEM((128, 128), F32)],
-        compiler_params=pltpu.CompilerParams(vmem_limit_bytes=32 * 1024 * 1024),
-    )(vol, x2, x1, r2, r1, c2, c1, other, w, bias)
-
-
-def coarse_kernel(both, near, pair, other, o0, o1, o2, o3, cells):
+        in_specs=[vmem] * 5,
+        out_specs=vmem,
+        scratch_shapes=[pltpu.VMEM((128, 128), F32)],
+        compiler_params=pltpu.CompilerParams(vmem_limit_bytes=32 * 1024 * 1024),
+    )(sums, c2, c1, w, bias)
+
+
+def coarse_kernel(both, near, pair, other, out, cells):
     pd = lax.rem(lax.axis_index("depth"), 2)
+    y = lax.div(lax.axis_index("rows"), 4)
     inner_d = inner("depth")
     for a in range(3):
         for i in (0, 1, 10, 11):
@@ -134,26 +171,23 @@
         left = jnp.where(lane == 0, 0.0, pltpu.roll(term[:64], 1, 1))
         right = jnp.where(lane == 63, 0.0, pltpu.roll(term[128:], size - 1, 1))
         value = term[64:128] + left + right
-        for k, out in enumerate((o0, o1, o2, o3)):
-            out[:, start : start + size] = value[16 * k : 16 * k + 16]
+        for k in range(4):
+            out[y ^ k, :, start : start + size] = value[16 * k : 16 * k + 16]
 
 
 def coarse_level(both, near, pair, other):
     vmem = pl.BlockSpec(memory_space=pltpu.VMEM)
     return pl.pallas_call(
         coarse_kernel,
-        out_shape=[jax.ShapeDtypeStruct((16, 640), F32)] * 4,
+        out_shape=jax.ShapeDtypeStruct((4, 16, 640), F32),
         in_specs=[vmem] * 4,
-        out_specs=[vmem] * 4,
+        out_specs=vmem,
         scratch_shapes=[pltpu.VMEM((3, 12, 64, 128), BF16)],
         compiler_params=pltpu.CompilerParams(vmem_limit_bytes=32 * 1024 * 1024),
     )(both, near, pair, other)
 
 
-def join_kernel(s0, s2, s1, s3, bias, out, held):
-    y = lax.div(lax.axis_index("rows"), 4)
-    for k, part in enumerate((s0, s1, s2, s3)):
-        held[y ^ k] = part[...]
+def join_kernel(held, bias, out):
     low = lax.broadcasted_iota(jnp.int32, (16, 128), 1) < 64
     for m in range(4):
         tiles = [held[m, :, 128 * i : 128 * i + 128] for i in range(4)]
@@ -171,11 +205,10 @@
     return pl.pallas_call(
         join_kernel,
         out_shape=jax.ShapeDtypeStruct((16, 2048), BF16),
-        in_specs=[vmem] * 5,
-        out_specs=vmem,
-        scratch_shapes=[pltpu.VMEM((4, 16, 640), F32)],
-        compiler_params=pltpu.CompilerParams(vmem_limit_bytes=32 * 1024 * 1024),
-    )(*parts, bias)
+        in_specs=[vmem] * 2,
+        out_specs=vmem,
+        compiler_params=pltpu.CompilerParams(vmem_limit_bytes=32 * 1024 * 1024),
+    )(parts, bias)
 
 
 def body(volume, fine_filters, fine_bias, coarse_filters, coarse_bias):
@@ -200,16 +233,17 @@
     w = jnp.transpose(coarse_filters, (0, 1, 2, 4, 3)).reshape(27, 16, 128)
     pair = jnp.stack([w, lax.ppermute(w, "rows", along_y(1))])
     other = lax.ppermute(pair, "rows", along_y(2))
-    pooled = fine_level(
-        volume, x2, x1, r2, r1, c2, c1, other, fine_filters, fine_bias.reshape(1, 128)
-    )
+    main = fine_level(volume, x2, x1, r2, r1, fine_filters)
+    pooled = finish(main, c2, c1, fine_filters, fine_bias.reshape(1, 128))
 
     both = lax.all_to_all(
         pooled, ("depth", "rows"), 0, 0, axis_index_groups=far_and_z(), tiled=True
     ).reshape(2, 4, 2, 64, 128)
     near = lax.ppermute(lax.dynamic_index_in_dim(both, 1 - pd, 0, False), "depth", depth_near)
     sums = coarse_level(both, near, pair, other)
-    parts = [sums[0]] + [lax.ppermute(sums[k], "rows", along_y(k)) for k in (2, 1, 3)]
+    parts = lax.all_to_all(
+        sums, "rows", 0, 0, axis_index_groups=[[4 * y + z for y in range(4)] for z in range(4)], tiled=True
+    )
     result = join(parts, jnp.broadcast_to(coarse_bias[:, None], (16, 128)))
     return result.reshape(16, 1, 2048)
 

time: 56.6 us -> 58.1 us (1.027)
  blocking collectives: 13.5 us -> 10.2 us
  starting transfers between devices: 29.3 us -> 32.1 us
  Pallas kernels: 2.97 us -> 3.93 us
  local copies, waits for them, and re-layouts: 1.13 us -> 2.05 us
    all_to_all x0 -> x1, starting transfers between devices: none -> 6.18 us  [body(): lax.all_to_all(pooled, ('depth', 'rows'), 0, 0, axis_index_groups=far_and...]
    ppermute x3 -> x0, waiting for transfers between devices: 5.27 us -> none  [body(): lax.ppermute(sums[k], 'rows', along_y(k))]
    ppermute x3 -> x0, starting transfers between devices: 4.47 us -> none  [body(): lax.ppermute(sums[k], 'rows', along_y(k))]
    ppermute x1, waiting for transfers between devices: 0.01 us -> 4.37 us  [body(): pair = jnp.stack([w, lax.ppermute(w, 'rows', along_y(1))])]
    ppermute x1, waiting for transfers between devices: 0.01 us -> 3.94 us  [body(): other = lax.ppermute(pair, 'rows', along_y(2))]
    all_to_all x1, blocking collectives: 13.5 us -> 10.2 us  [body(): lax.all_to_all(sums, 'rows', 0, 0, axis_index_groups=[[4 * y + z for y in...]
    ppermute x1, waiting for transfers between devices: 2.94 us -> 0.9 us  [body(): lax.ppermute(lax.dynamic_index_in_dim(sides, 3 - 3 * pr, 1, False), 'rows...]
    ppermute x1, starting transfers between devices: 3.82 us -> 5.26 us  [body(): lax.ppermute(lax.dynamic_index_in_dim(sides, 3 - 3 * pr, 1, False), 'rows...]
  transfers between devices with their start and end apart: 12 -> 10, of which waited for: 4 -> 3; matrix products, arithmetic and copies ran while one was open for 2% -> 2% of each run, Pallas kernels for 0% -> 3%
where the time goes in v7:
time: 58.1 us; the launch traced here: 57.7 us
  starting transfers between devices  32.1 us (55%)
  blocking collectives  10.2 us (18%)
  waiting for transfers between devices  9.23 us (16%)
  Pallas kernels  3.93 us (7%)
  local copies, waits for them, and re-layouts  2.05 us (4%)
    all_to_all x1, blocking collectives, body(): lax.all_to_all(sums, 'rows', 0, 0, axis_index_groups=[[4 * y + z for y in...  10.2 us
    ppermute x1, starting transfers between devices, body(): lax.ppermute(lax.dynamic_index_in_dim(volume, 1 - pd, 0, False), 'depth',...  7.04 us
    all_to_all x1, starting transfers between devices, body(): lax.all_to_all(pooled, ('depth', 'rows'), 0, 0, axis_index_groups=far_and...  6.18 us
    ppermute x1, starting transfers between devices, body(): lax.ppermute(lax.dynamic_index_in_dim(sides, 3 - 3 * pr, 1, False), 'rows...  5.26 us
    ppermute x1, waiting for transfers between devices, body(): pair = jnp.stack([w, lax.ppermute(w, 'rows', along_y(1))])  4.37 us
    ppermute x1, waiting for transfers between devices, body(): other = lax.ppermute(pair, 'rows', along_y(2))  3.94 us
    ppermute x1, starting transfers between devices, body(): lax.ppermute(lax.dynamic_index_in_dim(volume, 3 - 3 * pr, 1, False), 'row...  3.37 us
    ppermute x1, starting transfers between devices, body(): other = lax.ppermute(pair, 'rows', along_y(2))  2.83 us
  transfers between devices with their start and end apart: 10, of which 3 were waited for; matrix products, arithmetic and copies ran while one was open for 2% of the time, Pallas kernels for 3%

profile of v7, /device:TPU:6, one launch (start us, length us, event | category | flops | bytes accessed | tf_op | source)
XLA Modules:
  0.0 57.7 jit_solution(994357200046800510)
XLA Ops:
  0.0 1.1 %dynamic-slice_bitcast_fusion.1 = (bf16[4,128,128]{2,1,0:T(8,128)(2,1)S(1)}, bf16[4,128,128]{2,1,0:T(8,128)(2,1)S(1)}) fusion(bf16[2,4,128,128]{3,2,1,0:T(8,128)(2,1)} %vol.1, s32[]{:T(128)S(6)} %select_n.19, s32[]{:T(128)S(6)} %select_n.18), kind=kLoop, calls=%fused_computation.6 | loop fusion | bytes 524296 | tf_op jit(solution)/shard_map/jit(dynamic_index_in_dim)/squeeze | solution.py:223
  1.1 2.2 %collective-permute-start = (bf16[4,128,128]{2,1,0:T(8,128)(2,1)S(1)}, bf16[4,128,128]{2,1,0:T(8,128)(2,1)S(1)}, u32[]{:S(2)}, u32[]{:S(2)}) collective-permute-start(bf16[4,128,128]{2,1,0:T(8,128)(2,1)S(1)} %get-tuple-element.10), channel_id=1, source_target_pairs={{0,0},{16,32},{32,16},{48,64},{64,48},{80,96},{96,80},{112,128},{1... | collective-permute-start | bytes 393224 | tf_op jit(solution)/shard_map/ppermute | solution.py:222
  3.3 7.0 %collective-permute-start.1 = (bf16[4,128,128]{2,1,0:T(8,128)(2,1)S(1)}, bf16[4,128,128]{2,1,0:T(8,128)(2,1)S(1)}, u32[]{:S(2)}, u32[]{:S(2)}) collective-permute-start(bf16[4,128,128]{2,1,0:T(8,128)(2,1)S(1)} %get-tuple-element.9), channel_id=1, source_target_pairs={{0,16},{16,0},{32,48},{48,32},{64,80},{80,64},{96,112},{112,96},{1... | collective-permute-start | bytes 393224 | tf_op jit(solution)/shard_map/ppermute | solution.py:223
  10.3 0.9 %dynamic-slice_bitcast_fusion.3 = (bf16[2,128,128]{2,1,0:T(8,128)(2,1)S(1)}, bf16[2,128,128]{2,1,0:T(8,128)(2,1)S(1)}) fusion(bf16[2,4,128,128]{3,2,1,0:T(8,128)(2,1)} %vol.1, s32[]{:T(128)S(6)} %select_n.21, s32[]{:T(128)S(6)} %select_n.20), kind=kLoop, calls=%fused_computation.12 | loop fusion | bytes 262152 | tf_op jit(solution)/shard_map/jit(dynamic_index_in_dim)/squeeze | solution.py:225
  11.2 0.0 copy-start.1
  11.2 0.8 %collective-permute-start.2 = (bf16[2,128,128]{2,1,0:T(8,128)(2,1)S(1)}, bf16[2,128,128]{2,1,0:T(8,128)(2,1)S(1)}, u32[]{:S(2)}, u32[]{:S(2)}) collective-permute-start(bf16[2,128,128]{2,1,0:T(8,128)(2,1)S(1)} %get-tuple-element.8), channel_id=1, source_target_pairs={{0,0},{1,2},{2,1},{3,4},{4,3},{5,6},{6,5},{7,8},{8,7},{9,10},{10,9... | collective-permute-start | bytes 196616 | tf_op jit(solution)/shard_map/ppermute | solution.py:224
  12.0 3.4 %collective-permute-start.3 = (bf16[2,128,128]{2,1,0:T(8,128)(2,1)S(1)}, bf16[2,128,128]{2,1,0:T(8,128)(2,1)S(1)}, u32[]{:S(2)}, u32[]{:S(2)}) collective-permute-start(bf16[2,128,128]{2,1,0:T(8,128)(2,1)S(1)} %get-tuple-element.7), channel_id=1, source_target_pairs={{0,1},{1,0},{2,3},{3,2},{4,5},{5,4},{6,7},{7,6},{8,9},{9,8},{10,11... | collective-permute-start | bytes 196616 | tf_op jit(solution)/shard_map/ppermute | solution.py:225
  15.4 0.7 %collective-permute-start.4 = (bf16[2,128,128]{2,1,0:T(8,128)(2,1)S(1)}, bf16[2,128,128]{2,1,0:T(8,128)(2,1)S(1)}, u32[]{:S(2)}, u32[]{:S(2)}) collective-permute-start(bf16[2,128,128]{2,1,0:T(8,128)(2,1)S(1)} %get-tuple-element.6), channel_id=1, source_target_pairs={{0,0},{1,2},{2,1},{3,4},{4,3},{5,6},{6,5},{7,8},{8,7},{9,10},{10,9... | collective-permute-start | bytes 196616 | tf_op jit(solution)/shard_map/ppermute | solution.py:227
  16.1 5.3 %collective-permute-start.5 = (bf16[2,128,128]{2,1,0:T(8,128)(2,1)S(1)}, bf16[2,128,128]{2,1,0:T(8,128)(2,1)S(1)}, u32[]{:S(2)}, u32[]{:S(2)}) collective-permute-start(bf16[2,128,128]{2,1,0:T(8,128)(2,1)S(1)} %get-tuple-element.5), channel_id=1, source_target_pairs={{0,1},{1,0},{2,3},{3,2},{4,5},{5,4},{6,7},{7,6},{8,9},{9,8},{10,11... | collective-permute-start | bytes 196616 | tf_op jit(solution)/shard_map/ppermute | solution.py:228
  21.3 1.5 %shard_map.55.sums = f32[2,4,128,128]{3,2,1,0:T(8,128)S(1)} custom-call(bf16[2,4,128,128]{3,2,1,0:T(8,128)(2,1)S(1)} %copy-done.1, bf16[4,128,128]{2,1,0:T(8,128)(2,1)S(1)} %collective-permute-done.x2, bf16[4,128,128]{2,1,0:T(8,128)(2,1)S(1)} %collective-permute-done.1.x1, bf16[2,128,128]{2,1,0:T(8,128)(2,1)S(1)} %collective-permute-done.2.r2, ...), custom_call_target="tpu_custom_call" | custom-call | flops 20000000000 | tf_op jit(solution)/shard_map/pallas_call | solution.py:83
  22.8 0.0 copy-start.2
  22.9 0.9 %collective-permute-done.5.c1 = bf16[2,128,128]{2,1,0:T(8,128)(2,1)S(1)} collective-permute-done((bf16[2,128,128]{2,1,0:T(8,128)(2,1)S(1)}, bf16[2,128,128]{2,1,0:T(8,128)(2,1)S(1)}, u32[]{:S(2)}, u32[]{:S(2)}) %collective-permute-start.5) | collective-permute-done | bytes 65568 | tf_op jit(solution)/shard_map/ppermute | solution.py:228
  23.8 1.0 %shard_map.56 = bf16[8,2,64,128]{3,2,1,0:T(8,128)(2,1)} custom-call(f32[2,4,128,128]{3,2,1,0:T(8,128)S(1)} %shard_map.55.sums, bf16[2,128,128]{2,1,0:T(8,128)(2,1)S(1)} %collective-permute-done.4.c2, bf16[2,128,128]{2,1,0:T(8,128)(2,1)S(1)} %collective-permute-done.5.c1, bf16[3,3,3,128,128]{4,3,2,1,0:T(8,128)(2,1)S(1)} %copy-done, f32[1,128]{1,0:T(1,128)S(1)} %bitcast.29), custom_call_target="tpu_custom_call" | custom-call | tf_op jit(solution)/shard_map/pallas_call | solution.py:126
  24.8 6.2 %all-to-all-start = ((bf16[8,2,64,128]{3,2,1,0:T(8,128)(2,1)}), bf16[8,2,64,128]{3,2,1,0:T(8,128)(2,1)S(1)}, u32[]{:S(2)}, u32[]{:S(2)}) async-start(bf16[8,2,64,128]{3,2,1,0:T(8,128)(2,1)} %shard_map.56), calls=%async_computation | async-start | bytes 524288 | tf_op jit(solution)/shard_map/all_to_all | solution.py:239
  31.0 1.5 %collective-permute-start.7 = (bf16[27,16,128]{2,1,0:T(8,128)(2,1)S(1)}, bf16[27,16,128]{2,1,0:T(8,128)(2,1)S(1)}, u32[]{:S(2)}, u32[]{:S(2)}) collective-permute-start(bf16[27,16,128]{2,1,0:T(8,128)(2,1)S(1)} %bitcast.30), channel_id=1, source_target_pairs={{0,4},{1,5},{2,6},{3,7},{4,0},{5,1},{6,2},{7,3},{8,12},{9,13},{10,... | collective-permute-start | bytes 331784 | tf_op jit(solution)/shard_map/ppermute | solution.py:234
  32.5 4.4 %collective-permute-done.7 = bf16[27,16,128]{2,1,0:T(8,128)(2,1)S(1)} collective-permute-done((bf16[27,16,128]{2,1,0:T(8,128)(2,1)S(1)}, bf16[27,16,128]{2,1,0:T(8,128)(2,1)S(1)}, u32[]{:S(2)}, u32[]{:S(2)}) %collective-permute-start.7) | collective-permute-done | bytes 110624 | tf_op jit(solution)/shard_map/ppermute | solution.py:234
  36.9 2.8 %collective-permute-start.8 = (bf16[2,27,16,128]{3,2,1,0:T(8,128)(2,1)S(1)}, bf16[2,27,16,128]{3,2,1,0:T(8,128)(2,1)S(1)}, u32[]{:S(2)}, u32[]{:S(2)}) collective-permute-start(bf16[2,27,16,128]{3,2,1,0:T(8,128)(2,1)S(1)} %pad_maximum_fusion.pair), channel_id=1, source_target_pairs={{0,8},{1,9},{2,10},{3,11},{4,12},{5,13},{6,14},{7,15},{8,0},{9,1},... | collective-permute-start | bytes 663560 | tf_op jit(solution)/shard_map/ppermute | solution.py:235
  39.8 2.2 %collective-permute-start.6 = (bf16[4,2,64,128]{3,2,1,0:T(8,128)(2,1)S(1)}, bf16[4,2,64,128]{3,2,1,0:T(8,128)(2,1)S(1)}, u32[]{:S(2)}, u32[]{:S(2)}) collective-permute-start(bf16[4,2,64,128]{3,2,1,0:T(8,128)(2,1)S(1)} %dynamic-slice_bitcast_fusion), channel_id=1, source_target_pairs={{0,16},{16,0},{32,48},{48,32},{64,80},{80,64},{96,112},{112,96},{1... | collective-permute-start | bytes 393224 | tf_op jit(solution)/shard_map/ppermute | solution.py:242
  42.0 3.9 %collective-permute-done.8.other = bf16[2,27,16,128]{3,2,1,0:T(8,128)(2,1)S(1)} collective-permute-done((bf16[2,27,16,128]{3,2,1,0:T(8,128)(2,1)S(1)}, bf16[2,27,16,128]{3,2,1,0:T(8,128)(2,1)S(1)}, u32[]{:S(2)}, u32[]{:S(2)}) %collective-permute-start.8) | collective-permute-done | bytes 221216 | tf_op jit(solution)/shard_map/ppermute | solution.py:235
  45.9 0.8 %shard_map.57 = f32[4,16,640]{2,1,0:T(8,128)S(1)} custom-call(bf16[2,4,2,64,128]{4,3,2,1,0:T(8,128)(2,1)S(1)} %bitcast.26, bf16[4,2,64,128]{3,2,1,0:T(8,128)(2,1)S(1)} %collective-permute-done.6.near, bf16[2,27,16,128]{3,2,1,0:T(8,128)(2,1)S(1)} %pad_maximum_fusion.pair, bf16[2,27,16,128]{3,2,1,0:T(8,128)(2,1)S(1)} %collective-permute-done.8.other), custom_call_target="tpu_custom_call" | custom-call | tf_op jit(solution)/shard_map/pallas_call | solution.py:180
  46.7 0.0 copy-start.4
  46.7 10.2 %all_to_all.10.held = f32[4,16,640]{2,1,0:T(8,128)S(1)} all-to-all(f32[4,16,640]{2,1,0:T(8,128)S(1)} %shard_map.57), channel_id=1, replica_groups={{0,4,8,12},{1,5,9,13},{2,6,10,14},{3,7,11,15},{16,20,24,28},{17,21,25,2..., dimensions={0} | all-to-all | bytes 327680 | tf_op jit(solution)/shard_map/all_to_all | solution.py:244
  57.0 0.1 broadcast_in_dim.2.bias
  57.0 0.7 %shard_map.58 = bf16[16,2048]{1,0:T(8,128)(2,1)} custom-call(f32[4,16,640]{2,1,0:T(8,128)S(1)} %all_to_all.10.held, f32[16,128]{1,0:T(8,128)S(1)} %broadcast_in_dim.2.bias), custom_call_target="tpu_custom_call" | custom-call | tf_op jit(solution)/shard_map/pallas_call | solution.py:205
  (17 shorter events, 0.1 us)
Async XLA Ops:
  0.0 21.3 %copy-start = (bf16[3,3,3,128,128]{4,3,2,1,0:T(8,128)(2,1)S(1)}, bf16[3,3,3,128,128]{4,3,2,1,0:T(8,128)(2,1)}, u32[]{:S(2)}) copy-start(bf16[3,3,3,128,128]{4,3,2,1,0:T(8,128)(2,1)} %w.3) | copy-start | bytes 2654212
  1.1 14.3 %collective-permute-start = (bf16[4,128,128]{2,1,0:T(8,128)(2,1)S(1)}, bf16[4,128,128]{2,1,0:T(8,128)(2,1)S(1)}, u32[]{:S(2)}, u32[]{:S(2)}) collective-permute-start(bf16[4,128,128]{2,1,0:T(8,128)(2,1)S(1)} %get-tuple-element.10), channel_id=1, source_target_pairs={{0,0},{16,32},{32,16},{48,64},{64,48},{80,96},{96,80},{112,128},{1... | collective-permute-start | bytes 393224 | tf_op jit(solution)/shard_map/ppermute | solution.py:222
  3.3 12.1 %collective-permute-start.1 = (bf16[4,128,128]{2,1,0:T(8,128)(2,1)S(1)}, bf16[4,128,128]{2,1,0:T(8,128)(2,1)S(1)}, u32[]{:S(2)}, u32[]{:S(2)}) collective-permute-start(bf16[4,128,128]{2,1,0:T(8,128)(2,1)S(1)} %get-tuple-element.9), channel_id=1, source_target_pairs={{0,16},{16,0},{32,48},{48,32},{64,80},{80,64},{96,112},{112,96},{1... | collective-permute-start | bytes 393224 | tf_op jit(solution)/shard_map/ppermute | solution.py:223
  11.2 10.2 %copy-start.1 = (bf16[2,4,128,128]{3,2,1,0:T(8,128)(2,1)S(1)}, bf16[2,4,128,128]{3,2,1,0:T(8,128)(2,1)}, u32[]{:S(2)}) copy-start(bf16[2,4,128,128]{3,2,1,0:T(8,128)(2,1)} %vol.1) | copy-start | bytes 786436
  11.2 10.1 %collective-permute-start.2 = (bf16[2,128,128]{2,1,0:T(8,128)(2,1)S(1)}, bf16[2,128,128]{2,1,0:T(8,128)(2,1)S(1)}, u32[]{:S(2)}, u32[]{:S(2)}) collective-permute-start(bf16[2,128,128]{2,1,0:T(8,128)(2,1)S(1)} %get-tuple-element.8), channel_id=1, source_target_pairs={{0,0},{1,2},{2,1},{3,4},{4,3},{5,6},{6,5},{7,8},{8,7},{9,10},{10,9... | collective-permute-start | bytes 196616 | tf_op jit(solution)/shard_map/ppermute | solution.py:224
  12.0 9.3 %collective-permute-start.3 = (bf16[2,128,128]{2,1,0:T(8,128)(2,1)S(1)}, bf16[2,128,128]{2,1,0:T(8,128)(2,1)S(1)}, u32[]{:S(2)}, u32[]{:S(2)}) collective-permute-start(bf16[2,128,128]{2,1,0:T(8,128)(2,1)S(1)} %get-tuple-element.7), channel_id=1, source_target_pairs={{0,1},{1,0},{2,3},{3,2},{4,5},{5,4},{6,7},{7,6},{8,9},{9,8},{10,11... | collective-permute-start | bytes 196616 | tf_op jit(solution)/shard_map/ppermute | solution.py:225
  15.4 7.5 %collective-permute-start.4 = (bf16[2,128,128]{2,1,0:T(8,128)(2,1)S(1)}, bf16[2,128,128]{2,1,0:T(8,128)(2,1)S(1)}, u32[]{:S(2)}, u32[]{:S(2)}) collective-permute-start(bf16[2,128,128]{2,1,0:T(8,128)(2,1)S(1)} %get-tuple-element.6), channel_id=1, source_target_pairs={{0,0},{1,2},{2,1},{3,4},{4,3},{5,6},{6,5},{7,8},{8,7},{9,10},{10,9... | collective-permute-start | bytes 196616 | tf_op jit(solution)/shard_map/ppermute | solution.py:227
  16.1 7.7 %collective-permute-start.5 = (bf16[2,128,128]{2,1,0:T(8,128)(2,1)S(1)}, bf16[2,128,128]{2,1,0:T(8,128)(2,1)S(1)}, u32[]{:S(2)}, u32[]{:S(2)}) collective-permute-start(bf16[2,128,128]{2,1,0:T(8,128)(2,1)S(1)} %get-tuple-element.5), channel_id=1, source_target_pairs={{0,1},{1,0},{2,3},{3,2},{4,5},{5,4},{6,7},{7,6},{8,9},{9,8},{10,11... | collective-permute-start | bytes 196616 | tf_op jit(solution)/shard_map/ppermute | solution.py:228
  22.8 0.9 %copy-start.2 = (f32[128]{0:T(128)S(1)}, f32[128]{0:T(128)}, u32[]{:S(2)}) copy-start(f32[128]{0:T(128)} %param.7) | copy-start | bytes 1540
  24.8 6.2 %copy-start.3 = (bf16[3,3,3,128,16]{3,4,2,1,0:T(8,128)(2,1)S(1)}, bf16[3,3,3,128,16]{3,4,2,1,0:T(8,128)(2,1)}, u32[]{:S(2)}) copy-start(bf16[3,3,3,128,16]{3,4,2,1,0:T(8,128)(2,1)} %param.8) | copy-start | bytes 331780
  24.8 15.0 %all-to-all-start = ((bf16[8,2,64,128]{3,2,1,0:T(8,128)(2,1)}), bf16[8,2,64,128]{3,2,1,0:T(8,128)(2,1)S(1)}, u32[]{:S(2)}, u32[]{:S(2)}) async-start(bf16[8,2,64,128]{3,2,1,0:T(8,128)(2,1)} %shard_map.56), calls=%async_computation | async-start | bytes 524288 | tf_op jit(solution)/shard_map/all_to_all | solution.py:239
  31.0 5.9 %collective-permute-start.7 = (bf16[27,16,128]{2,1,0:T(8,128)(2,1)S(1)}, bf16[27,16,128]{2,1,0:T(8,128)(2,1)S(1)}, u32[]{:S(2)}, u32[]{:S(2)}) collective-permute-start(bf16[27,16,128]{2,1,0:T(8,128)(2,1)S(1)} %bitcast.30), channel_id=1, source_target_pairs={{0,4},{1,5},{2,6},{3,7},{4,0},{5,1},{6,2},{7,3},{8,12},{9,13},{10,... | collective-permute-start | bytes 331784 | tf_op jit(solution)/shard_map/ppermute | solution.py:234
  36.9 9.0 %collective-permute-start.8 = (bf16[2,27,16,128]{3,2,1,0:T(8,128)(2,1)S(1)}, bf16[2,27,16,128]{3,2,1,0:T(8,128)(2,1)S(1)}, u32[]{:S(2)}, u32[]{:S(2)}) collective-permute-start(bf16[2,27,16,128]{3,2,1,0:T(8,128)(2,1)S(1)} %pad_maximum_fusion.pair), channel_id=1, source_target_pairs={{0,8},{1,9},{2,10},{3,11},{4,12},{5,13},{6,14},{7,15},{8,0},{9,1},... | collective-permute-start | bytes 663560 | tf_op jit(solution)/shard_map/ppermute | solution.py:235
  39.8 6.2 %collective-permute-start.6 = (bf16[4,2,64,128]{3,2,1,0:T(8,128)(2,1)S(1)}, bf16[4,2,64,128]{3,2,1,0:T(8,128)(2,1)S(1)}, u32[]{:S(2)}, u32[]{:S(2)}) collective-permute-start(bf16[4,2,64,128]{3,2,1,0:T(8,128)(2,1)S(1)} %dynamic-slice_bitcast_fusion), channel_id=1, source_target_pairs={{0,16},{16,0},{32,48},{48,32},{64,80},{80,64},{96,112},{112,96},{1... | collective-permute-start | bytes 393224 | tf_op jit(solution)/shard_map/ppermute | solution.py:242
  46.7 10.2 %copy-start.4 = (f32[16]{0:T(128)S(1)}, f32[16]{0:T(128)}, u32[]{:S(2)}) copy-start(f32[16]{0:T(128)} %param.9) | copy-start | bytes 196

commit v8 on v7

--- a/solution.py
+++ b/solution.py
@@ -33,7 +33,7 @@
     return line[:, 128:256] + left + right
 
 
-def fine_kernel(vol, x2, x1, r2, r1, w, out, cells):
+def fine_kernel(vol, x2, x1, r2, r1, w, bias, ends, best, corner_w, cells):
     pd = lax.rem(lax.axis_index("depth"), 2)
     pr = lax.rem(lax.axis_index("rows"), 2)
     inner_d = inner("depth")
@@ -74,63 +74,65 @@
             )
             term = jnp.dot(lhs, rhs, preferred_element_type=F32)
             total = term if total is None else total + term
-        for t in range(4):
-            out[s, t] = spread(total[t * 128 : (t + 1) * 128], col)
-
-
-def fine_level(vol, x2, x1, r2, r1, w):
+        for q in range(2):
+            ends[s, q] = spread(total[3 * q * 128 : (3 * q + 1) * 128], col) + bias[...]
+            middle = spread(total[(q + 1) * 128 : (q + 2) * 128], col) + bias[...]
+            best[q] = middle if s == 0 else jnp.maximum(best[q], middle)
+            a, b = 2 * s, 2 * q
+            for c in range(3):
+                corner_w[s, q, :, 128 * c : 128 * c + 128] = w[a + pd * (2 - 2 * a), b + pr * (2 - 2 * b), c]
+
+
+def fine_level(vol, x2, x1, r2, r1, w, bias):
     vmem = pl.BlockSpec(memory_space=pltpu.VMEM)
     return pl.pallas_call(
         fine_kernel,
-        out_shape=jax.ShapeDtypeStruct((2, 4, 128, 128), F32),
-        in_specs=[vmem] * 6,
-        out_specs=vmem,
+        out_shape=[
+            jax.ShapeDtypeStruct((2, 2, 128, 128), F32),
+            jax.ShapeDtypeStruct((2, 128, 128), F32),
+            jax.ShapeDtypeStruct((2, 2, 128, 384), BF16),
+        ],
+        in_specs=[vmem] * 7,
+        out_specs=[vmem] * 3,
         scratch_shapes=[pltpu.VMEM((4, 6, 128, 128), BF16)],
         compiler_params=pltpu.CompilerParams(vmem_limit_bytes=32 * 1024 * 1024),
         cost_estimate=pl.CostEstimate(flops=20_000_000_000, bytes_accessed=0, transcendentals=0),
-    )(vol, x2, x1, r2, r1, w)
-
-
-def finish_kernel(sums, c2, c1, w, bias, out, peak):
-    pd = lax.rem(lax.axis_index("depth"), 2)
+    )(vol, x2, x1, r2, r1, w, bias)
+
+
+def finish_kernel(ends, best, corner_w, c2, c1, other, out, peak):
     pr = lax.rem(lax.axis_index("rows"), 2)
     inner_d = inner("depth")
     inner_r = inner("rows")
     zero = jnp.zeros((128, 128), BF16)
     col = lax.broadcasted_iota(jnp.int32, (128, 128), 0)
     for q in range(2):
-        edge = 2 * q
-        best = None
+        value = best[q]
         for s in range(2):
-            side = 2 * s
             piece = (c2, c1)[q][s]
             if q == 0:
                 piece = jnp.where(inner_r, piece, zero)
             if s == 0:
                 piece = jnp.where(inner_d, piece, zero)
-            rhs = jnp.concatenate(
-                [w[side + pd * (2 - 2 * side), edge + pr * (2 - 2 * edge), c] for c in range(3)], axis=1
-            )
-            corner = spread(jnp.dot(piece, rhs, preferred_element_type=F32), col)
-            value = jnp.maximum(sums[s, 3 * q] + corner, sums[s, q + 1])
-            best = value if best is None else jnp.maximum(best, value)
-        peak[...] = best
+            corner = jnp.dot(piece, corner_w[s, q], preferred_element_type=F32)
+            value = jnp.maximum(value, ends[s, q] + spread(corner, col))
+        peak[...] = value
         pooled = jnp.maximum(peak[pl.ds(0, 64, stride=2), :], peak[pl.ds(1, 64, stride=2), :])
-        pooled = jnp.maximum(pooled + bias[...], 0.0).astype(BF16)
+        pooled = jnp.maximum(pooled, 0.0).astype(BF16)
         for k in range(8):
             out[k, q + pr * (1 - 2 * q)] = pooled
 
 
-def finish(sums, c2, c1, w, bias):
+def finish(main, c2, c1, other):
     vmem = pl.BlockSpec(memory_space=pltpu.VMEM)
     return pl.pallas_call(
         finish_kernel,
         out_shape=jax.ShapeDtypeStruct((8, 2, 64, 128), BF16),
-        in_specs=[vmem] * 5,
+        in_specs=[vmem] * 5 + [pl.BlockSpec(memory_space=pl.ANY)],
         out_specs=vmem,
         scratch_shapes=[pltpu.VMEM((128, 128), F32)],
         compiler_params=pltpu.CompilerParams(vmem_limit_bytes=32 * 1024 * 1024),
-    )(sums, c2, c1, w, bias)
+    )(*main, c2, c1, other)
 
 
 def coarse_kernel(both, near, pair, other, out, cells):
@@ -233,8 +235,8 @@
     w = jnp.transpose(coarse_filters, (0, 1, 2, 4, 3)).reshape(27, 16, 128)
     pair = jnp.stack([w, lax.ppermute(w, "rows", along_y(1))])
     other = lax.ppermute(pair, "rows", along_y(2))
-    main = fine_level(volume, x2, x1, r2, r1, fine_filters)
-    pooled = finish(main, c2, c1, fine_filters, fine_bias.reshape(1, 128))
+    main = fine_level(volume, x2, x1, r2, r1, fine_filters, fine_bias.reshape(1, 128))
+    pooled = finish(main, c2, c1, other)
 
     both = lax.all_to_all(
         pooled, ("depth", "rows"), 0, 0, axis_index_groups=far_and_z(), tiled=True

time: 58.1 us -> 55.4 us (0.954)
  blocking collectives: 10.2 us -> 23.7 us
  waiting for transfers between devices: 9.23 us -> 1.69 us
  starting transfers between devices: 32.1 us -> 25.2 us
  local copies, waits for them, and re-layouts: 2.05 us -> 1.2 us
  Pallas kernels: 3.93 us -> 3.24 us
    all_to_all x0 -> x1, blocking collectives: none -> 13 us  [body(): lax.all_to_all(pooled, ('depth', 'rows'), 0, 0, axis_index_groups=far_and...]
    all_to_all x1 -> x0, starting transfers between devices: 6.18 us -> none  [body(): lax.all_to_all(pooled, ('depth', 'rows'), 0, 0, axis_index_groups=far_and...]
    ppermute x1, waiting for transfers between devices: 4.37 us -> 0.01 us  [body(): pair = jnp.stack([w, lax.ppermute(w, 'rows', along_y(1))])]
    ppermute x1, waiting for transfers between devices: 3.94 us -> 0.01 us  [body(): other = lax.ppermute(pair, 'rows', along_y(2))]
    ppermute x1, waiting for transfers between devices: 0.01 us -> 0.99 us  [body(): lax.ppermute(lax.dynamic_index_in_dim(both, 1 - pd, 0, False), 'depth', d...]
    squeeze x1, local copies, waits for them, and re-layouts: 0.88 us -> 0.01 us  [body(): lax.dynamic_index_in_dim(volume, 3 - 3 * pr, 1, False)]
    ppermute x1, starting transfers between devices: 5.26 us -> 4.42 us  [body(): lax.ppermute(lax.dynamic_index_in_dim(sides, 3 - 3 * pr, 1, False), 'rows...]
    pallas_call x1, Pallas kernels: 0.99 us -> 0.28 us  [finish(): pl.pallas_call(finish_kernel, out_shape=jax.ShapeDtypeStruct((8, 2, 64, 1...]
  transfers between devices with their start and end apart: 10 -> 9, of which waited for: 3 -> 2; matrix products, arithmetic and copies ran while one was open for 2% -> 0% of each run, Pallas kernels for 3% -> 3%
where the time goes in v8:
time: 55.4 us; the launch traced here: 55.2 us
  starting transfers between devices  25.2 us (45%)
  blocking collectives  23.7 us (43%)
  Pallas kernels  3.24 us (6%)
  waiting for transfers between devices  1.69 us (3%)
  local copies, waits for them, and re-layouts  1.2 us (2%)
    all_to_all x1, blocking collectives, body(): lax.all_to_all(pooled, ('depth', 'rows'), 0, 0, axis_index_groups=far_and...  13 us
    all_to_all x1, blocking collectives, body(): lax.all_to_all(sums, 'rows', 0, 0, axis_index_groups=[[4 * y + z for y in...  10.7 us
    ppermute x1, starting transfers between devices, body(): lax.ppermute(lax.dynamic_index_in_dim(volume, 1 - pd, 0, False), 'depth',...  7.04 us
    ppermute x1, starting transfers between devices, body(): lax.ppermute(lax.dynamic_index_in_dim(sides, 3 - 3 * pr, 1, False), 'rows...  4.42 us
    ppermute x1, starting transfers between devices, body(): lax.ppermute(lax.dynamic_index_in_dim(volume, 3 - 3 * pr, 1, False), 'row...  3.37 us
    ppermute x1, starting transfers between devices, body(): other = lax.ppermute(pair, 'rows', along_y(2))  2.99 us
    ppermute x1, starting transfers between devices, body(): lax.ppermute(lax.dynamic_index_in_dim(both, 1 - pd, 0, False), 'depth', d...  2.26 us
    ppermute x1, starting transfers between devices, body(): lax.ppermute(lax.dynamic_index_in_dim(volume, pd, 0, False), 'depth', dep...  2.18 us
  transfers between devices with their start and end apart: 9, of which 2 were waited for; matrix products, arithmetic and copies ran while one was open for 0% of the time, Pallas kernels for 3%

profile of v8, /device:TPU:6, one launch (start us, length us, event | category | flops | bytes accessed | tf_op | source)
XLA Modules:
  0.0 55.2 jit_solution(11514931343263080550)
XLA Ops:
  0.0 1.1 %dynamic-slice_bitcast_fusion.1 = (bf16[4,128,128]{2,1,0:T(8,128)(2,1)S(1)}, bf16[4,128,128]{2,1,0:T(8,128)(2,1)S(1)}) fusion(bf16[2,4,128,128]{3,2,1,0:T(8,128)(2,1)} %vol.1, s32[]{:T(128)S(6)} %select_n.19, s32[]{:T(128)S(6)} %select_n.18), kind=kLoop, calls=%fused_computation.6 | loop fusion | bytes 524296 | tf_op jit(solution)/shard_map/jit(dynamic_index_in_dim)/squeeze | solution.py:225
  1.1 2.2 %collective-permute-start = (bf16[4,128,128]{2,1,0:T(8,128)(2,1)S(1)}, bf16[4,128,128]{2,1,0:T(8,128)(2,1)S(1)}, u32[]{:S(2)}, u32[]{:S(2)}) collective-permute-start(bf16[4,128,128]{2,1,0:T(8,128)(2,1)S(1)} %get-tuple-element.16), channel_id=1, source_target_pairs={{0,0},{16,32},{32,16},{48,64},{64,48},{80,96},{96,80},{112,128},{1... | collective-permute-start | bytes 393224 | tf_op jit(solution)/shard_map/ppermute | solution.py:224
  3.3 7.0 %collective-permute-start.1 = (bf16[4,128,128]{2,1,0:T(8,128)(2,1)S(1)}, bf16[4,128,128]{2,1,0:T(8,128)(2,1)S(1)}, u32[]{:S(2)}, u32[]{:S(2)}) collective-permute-start(bf16[4,128,128]{2,1,0:T(8,128)(2,1)S(1)} %get-tuple-element.15), channel_id=1, source_target_pairs={{0,16},{16,0},{32,48},{48,32},{64,80},{80,64},{96,112},{112,96},{1... | collective-permute-start | bytes 393224 | tf_op jit(solution)/shard_map/ppermute | solution.py:225
  10.3 1.6 %collective-permute-start.6 = (bf16[27,16,128]{2,1,0:T(8,128)(2,1)S(1)}, bf16[27,16,128]{2,1,0:T(8,128)(2,1)S(1)}, u32[]{:S(2)}, u32[]{:S(2)}) collective-permute-start(bf16[27,16,128]{2,1,0:T(8,128)(2,1)S(1)} %bitcast.30), channel_id=1, source_target_pairs={{0,4},{1,5},{2,6},{3,7},{4,0},{5,1},{6,2},{7,3},{8,12},{9,13},{10,... | collective-permute-start | bytes 331784 | tf_op jit(solution)/shard_map/ppermute | solution.py:236
  11.9 0.7 %collective-permute-start.2 = (bf16[2,128,128]{2,1,0:T(8,128)(2,1)S(1)}, bf16[2,128,128]{2,1,0:T(8,128)(2,1)S(1)}, u32[]{:S(2)}, u32[]{:S(2)}) collective-permute-start(bf16[2,128,128]{2,1,0:T(8,128)(2,1)S(1)} %get-tuple-element.14), channel_id=1, source_target_pairs={{0,0},{1,2},{2,1},{3,4},{4,3},{5,6},{6,5},{7,8},{8,7},{9,10},{10,9... | collective-permute-start | bytes 196616 | tf_op jit(solution)/shard_map/ppermute | solution.py:226
  12.6 3.4 %collective-permute-start.3 = (bf16[2,128,128]{2,1,0:T(8,128)(2,1)S(1)}, bf16[2,128,128]{2,1,0:T(8,128)(2,1)S(1)}, u32[]{:S(2)}, u32[]{:S(2)}) collective-permute-start(bf16[2,128,128]{2,1,0:T(8,128)(2,1)S(1)} %get-tuple-element.13), channel_id=1, source_target_pairs={{0,1},{1,0},{2,3},{3,2},{4,5},{5,4},{6,7},{7,6},{8,9},{9,8},{10,11... | collective-permute-start | bytes 196616 | tf_op jit(solution)/shard_map/ppermute | solution.py:227
  16.0 0.0 collective-permute-done.6
  16.0 3.0 %collective-permute-start.7 = (bf16[2,27,16,128]{3,2,1,0:T(8,128)(2,1)S(1)}, bf16[2,27,16,128]{3,2,1,0:T(8,128)(2,1)S(1)}, u32[]{:S(2)}, u32[]{:S(2)}) collective-permute-start(bf16[2,27,16,128]{3,2,1,0:T(8,128)(2,1)S(1)} %pad_maximum_fusion.pair), channel_id=1, source_target_pairs={{0,8},{1,9},{2,10},{3,11},{4,12},{5,13},{6,14},{7,15},{8,0},{9,1},... | collective-permute-start | bytes 663560 | tf_op jit(solution)/shard_map/ppermute | solution.py:237
  19.0 0.0 collective-permute-done.x2
  19.0 0.0 collective-permute-done.1.x1
  19.0 0.7 %collective-permute-start.4 = (bf16[2,128,128]{2,1,0:T(8,128)(2,1)S(1)}, bf16[2,128,128]{2,1,0:T(8,128)(2,1)S(1)}, u32[]{:S(2)}, u32[]{:S(2)}) collective-permute-start(bf16[2,128,128]{2,1,0:T(8,128)(2,1)S(1)} %get-tuple-element.12), channel_id=1, source_target_pairs={{0,0},{1,2},{2,1},{3,4},{4,3},{5,6},{6,5},{7,8},{8,7},{9,10},{10,9... | collective-permute-start | bytes 196616 | tf_op jit(solution)/shard_map/ppermute | solution.py:229
  19.7 0.0 copy-start.2
  19.7 4.4 %collective-permute-start.5 = (bf16[2,128,128]{2,1,0:T(8,128)(2,1)S(1)}, bf16[2,128,128]{2,1,0:T(8,128)(2,1)S(1)}, u32[]{:S(2)}, u32[]{:S(2)}) collective-permute-start(bf16[2,128,128]{2,1,0:T(8,128)(2,1)S(1)} %get-tuple-element.11), channel_id=1, source_target_pairs={{0,1},{1,0},{2,3},{3,2},{4,5},{5,4},{6,7},{7,6},{8,9},{9,8},{10,11... | collective-permute-start | bytes 196616 | tf_op jit(solution)/shard_map/ppermute | solution.py:230
  24.1 1.5 %shard_map.55 = (f32[2,2,128,128]{3,2,1,0:T(8,128)S(1)}, f32[2,128,128]{2,1,0:T(8,128)S(1)}, bf16[2,2,128,384]{3,2,1,0:T(8,128)(2,1)S(1)}) custom-call(bf16[2,4,128,128]{3,2,1,0:T(8,128)(2,1)S(1)} %copy-done, bf16[4,128,128]{2,1,0:T(8,128)(2,1)S(1)} %collective-permute-done.x2, bf16[4,128,128]{2,1,0:T(8,128)(2,1)S(1)} %collective-permute-done.1.x1, ...), custom_call_target="tpu_custom_call" | custom-call | flops 20000000000 | tf_op jit(solution)/shard_map/pallas_call | solution.py:88
  25.7 0.7 %collective-permute-done.5.c1 = bf16[2,128,128]{2,1,0:T(8,128)(2,1)S(1)} collective-permute-done((bf16[2,128,128]{2,1,0:T(8,128)(2,1)S(1)}, bf16[2,128,128]{2,1,0:T(8,128)(2,1)S(1)}, u32[]{:S(2)}, u32[]{:S(2)}) %collective-permute-start.5) | collective-permute-done | bytes 65568 | tf_op jit(solution)/shard_map/ppermute | solution.py:230
  26.4 0.3 shard_map.56
  26.6 13.0 %all_to_all.10 = bf16[8,2,64,128]{3,2,1,0:T(8,128)(2,1)S(1)} all-to-all(bf16[8,2,64,128]{3,2,1,0:T(8,128)(2,1)S(1)} %shard_map.56), channel_id=1, replica_groups={{16,17,18,19,32,33,34,35},{20,21,22,23,36,37,38,39},{24,25,26,27,40,41,..., dimensions={0} | all-to-all | bytes 524288 | tf_op jit(solution)/shard_map/all_to_all | solution.py:241
  39.7 2.3 %collective-permute-start.8 = (bf16[4,2,64,128]{3,2,1,0:T(8,128)(2,1)S(1)}, bf16[4,2,64,128]{3,2,1,0:T(8,128)(2,1)S(1)}, u32[]{:S(2)}, u32[]{:S(2)}) collective-permute-start(bf16[4,2,64,128]{3,2,1,0:T(8,128)(2,1)S(1)} %dynamic-slice_bitcast_fusion), channel_id=1, source_target_pairs={{0,16},{16,0},{32,48},{48,32},{64,80},{80,64},{96,112},{112,96},{1... | collective-permute-start | bytes 393224 | tf_op jit(solution)/shard_map/ppermute | solution.py:244
  42.0 1.0 %collective-permute-done.8.near = bf16[4,2,64,128]{3,2,1,0:T(8,128)(2,1)S(1)} collective-permute-done((bf16[4,2,64,128]{3,2,1,0:T(8,128)(2,1)S(1)}, bf16[4,2,64,128]{3,2,1,0:T(8,128)(2,1)S(1)}, u32[]{:S(2)}, u32[]{:S(2)}) %collective-permute-start.8) | collective-permute-done | bytes 131104 | tf_op jit(solution)/shard_map/ppermute | solution.py:244
  42.9 0.8 %shard_map.57 = f32[4,16,640]{2,1,0:T(8,128)S(1)} custom-call(bf16[2,4,2,64,128]{4,3,2,1,0:T(8,128)(2,1)S(1)} %bitcast.26, bf16[4,2,64,128]{3,2,1,0:T(8,128)(2,1)S(1)} %collective-permute-done.8.near, bf16[2,27,16,128]{3,2,1,0:T(8,128)(2,1)S(1)} %pad_maximum_fusion.pair, bf16[2,27,16,128]{3,2,1,0:T(8,128)(2,1)S(1)} %collective-permute-done.7.other), custom_call_target="tpu_custom_call" | custom-call | tf_op jit(solution)/shard_map/pallas_call | solution.py:182
  43.7 0.0 copy-start.4
  43.7 10.7 %all_to_all.11.held = f32[4,16,640]{2,1,0:T(8,128)S(1)} all-to-all(f32[4,16,640]{2,1,0:T(8,128)S(1)} %shard_map.57), channel_id=1, replica_groups={{0,4,8,12},{1,5,9,13},{2,6,10,14},{3,7,11,15},{16,20,24,28},{17,21,25,2..., dimensions={0} | all-to-all | bytes 327680 | tf_op jit(solution)/shard_map/all_to_all | solution.py:246
  54.4 0.1 broadcast_in_dim.2.bias
  54.5 0.7 %shard_map.58 = bf16[16,2048]{1,0:T(8,128)(2,1)} custom-call(f32[4,16,640]{2,1,0:T(8,128)S(1)} %all_to_all.11.held, f32[16,128]{1,0:T(8,128)S(1)} %broadcast_in_dim.2.bias), custom_call_target="tpu_custom_call" | custom-call | tf_op jit(solution)/shard_map/pallas_call | solution.py:207
  (16 shorter events, 0.1 us)
Async XLA Ops:
  0.0 10.3 %copy-start.3 = (bf16[3,3,3,128,16]{3,4,2,1,0:T(8,128)(2,1)S(1)}, bf16[3,3,3,128,16]{3,4,2,1,0:T(8,128)(2,1)}, u32[]{:S(2)}) copy-start(bf16[3,3,3,128,16]{3,4,2,1,0:T(8,128)(2,1)} %param.8) | copy-start | bytes 331780
  0.0 11.9 %copy-start = (bf16[2,4,128,128]{3,2,1,0:T(8,128)(2,1)S(1)}, bf16[2,4,128,128]{3,2,1,0:T(8,128)(2,1)}, u32[]{:S(2)}) copy-start(bf16[2,4,128,128]{3,2,1,0:T(8,128)(2,1)} %vol.1) | copy-start | bytes 786436
  0.0 24.1 %copy-start.1 = (bf16[3,3,3,128,128]{4,3,2,1,0:T(8,128)(2,1)S(1)}, bf16[3,3,3,128,128]{4,3,2,1,0:T(8,128)(2,1)}, u32[]{:S(2)}) copy-start(bf16[3,3,3,128,128]{4,3,2,1,0:T(8,128)(2,1)} %w.1) | copy-start | bytes 2654212
  1.1 17.9 %collective-permute-start = (bf16[4,128,128]{2,1,0:T(8,128)(2,1)S(1)}, bf16[4,128,128]{2,1,0:T(8,128)(2,1)S(1)}, u32[]{:S(2)}, u32[]{:S(2)}) collective-permute-start(bf16[4,128,128]{2,1,0:T(8,128)(2,1)S(1)} %get-tuple-element.16), channel_id=1, source_target_pairs={{0,0},{16,32},{32,16},{48,64},{64,48},{80,96},{96,80},{112,128},{1... | collective-permute-start | bytes 393224 | tf_op jit(solution)/shard_map/ppermute | solution.py:224
  3.3 15.7 %collective-permute-start.1 = (bf16[4,128,128]{2,1,0:T(8,128)(2,1)S(1)}, bf16[4,128,128]{2,1,0:T(8,128)(2,1)S(1)}, u32[]{:S(2)}, u32[]{:S(2)}) collective-permute-start(bf16[4,128,128]{2,1,0:T(8,128)(2,1)S(1)} %get-tuple-element.15), channel_id=1, source_target_pairs={{0,16},{16,0},{32,48},{48,32},{64,80},{80,64},{96,112},{112,96},{1... | collective-permute-start | bytes 393224 | tf_op jit(solution)/shard_map/ppermute | solution.py:225
  10.3 5.6 %collective-permute-start.6 = (bf16[27,16,128]{2,1,0:T(8,128)(2,1)S(1)}, bf16[27,16,128]{2,1,0:T(8,128)(2,1)S(1)}, u32[]{:S(2)}, u32[]{:S(2)}) collective-permute-start(bf16[27,16,128]{2,1,0:T(8,128)(2,1)S(1)} %bitcast.30), channel_id=1, source_target_pairs={{0,4},{1,5},{2,6},{3,7},{4,0},{5,1},{6,2},{7,3},{8,12},{9,13},{10,... | collective-permute-start | bytes 331784 | tf_op jit(solution)/shard_map/ppermute | solution.py:236
  11.9 12.2 %collective-permute-start.2 = (bf16[2,128,128]{2,1,0:T(8,128)(2,1)S(1)}, bf16[2,128,128]{2,1,0:T(8,128)(2,1)S(1)}, u32[]{:S(2)}, u32[]{:S(2)}) collective-permute-start(bf16[2,128,128]{2,1,0:T(8,128)(2,1)S(1)} %get-tuple-element.14), channel_id=1, source_target_pairs={{0,0},{1,2},{2,1},{3,4},{4,3},{5,6},{6,5},{7,8},{8,7},{9,10},{10,9... | collective-permute-start | bytes 196616 | tf_op jit(solution)/shard_map/ppermute | solution.py:226
  12.6 11.5 %collective-permute-start.3 = (bf16[2,128,128]{2,1,0:T(8,128)(2,1)S(1)}, bf16[2,128,128]{2,1,0:T(8,128)(2,1)S(1)}, u32[]{:S(2)}, u32[]{:S(2)}) collective-permute-start(bf16[2,128,128]{2,1,0:T(8,128)(2,1)S(1)} %get-tuple-element.13), channel_id=1, source_target_pairs={{0,1},{1,0},{2,3},{3,2},{4,5},{5,4},{6,7},{7,6},{8,9},{9,8},{10,11... | collective-permute-start | bytes 196616 | tf_op jit(solution)/shard_map/ppermute | solution.py:227
  16.0 10.4 %collective-permute-start.7 = (bf16[2,27,16,128]{3,2,1,0:T(8,128)(2,1)S(1)}, bf16[2,27,16,128]{3,2,1,0:T(8,128)(2,1)S(1)}, u32[]{:S(2)}, u32[]{:S(2)}) collective-permute-start(bf16[2,27,16,128]{3,2,1,0:T(8,128)(2,1)S(1)} %pad_maximum_fusion.pair), channel_id=1, source_target_pairs={{0,8},{1,9},{2,10},{3,11},{4,12},{5,13},{6,14},{7,15},{8,0},{9,1},... | collective-permute-start | bytes 663560 | tf_op jit(solution)/shard_map/ppermute | solution.py:237
  19.0 6.7 %collective-permute-start.4 = (bf16[2,128,128]{2,1,0:T(8,128)(2,1)S(1)}, bf16[2,128,128]{2,1,0:T(8,128)(2,1)S(1)}, u32[]{:S(2)}, u32[]{:S(2)}) collective-permute-start(bf16[2,128,128]{2,1,0:T(8,128)(2,1)S(1)} %get-tuple-element.12), channel_id=1, source_target_pairs={{0,0},{1,2},{2,1},{3,4},{4,3},{5,6},{6,5},{7,8},{8,7},{9,10},{10,9... | collective-permute-start | bytes 196616 | tf_op jit(solution)/shard_map/ppermute | solution.py:229
  19.7 4.5 %copy-start.2 = (f32[128]{0:T(128)S(1)}, f32[128]{0:T(128)}, u32[]{:S(2)}) copy-start(f32[128]{0:T(128)} %param.7) | copy-start | bytes 1540
  19.7 6.7 %collective-permute-start.5 = (bf16[2,128,128]{2,1,0:T(8,128)(2,1)S(1)}, bf16[2,128,128]{2,1,0:T(8,128)(2,1)S(1)}, u32[]{:S(2)}, u32[]{:S(2)}) collective-permute-start(bf16[2,128,128]{2,1,0:T(8,128)(2,1)S(1)} %get-tuple-element.11), channel_id=1, source_target_pairs={{0,1},{1,0},{2,3},{3,2},{4,5},{5,4},{6,7},{7,6},{8,9},{9,8},{10,11... | collective-permute-start | bytes 196616 | tf_op jit(solution)/shard_map/ppermute | solution.py:230
  39.7 3.2 %collective-permute-start.8 = (bf16[4,2,64,128]{3,2,1,0:T(8,128)(2,1)S(1)}, bf16[4,2,64,128]{3,2,1,0:T(8,128)(2,1)S(1)}, u32[]{:S(2)}, u32[]{:S(2)}) collective-permute-start(bf16[4,2,64,128]{3,2,1,0:T(8,128)(2,1)S(1)} %dynamic-slice_bitcast_fusion), channel_id=1, source_target_pairs={{0,16},{16,0},{32,48},{48,32},{64,80},{80,64},{96,112},{112,96},{1... | collective-permute-start | bytes 393224 | tf_op jit(solution)/shard_map/ppermute | solution.py:244
  43.7 10.7 %copy-start.4 = (f32[16]{0:T(128)S(1)}, f32[16]{0:T(128)}, u32[]{:S(2)}) copy-start(f32[16]{0:T(128)} %param.9) | copy-start | bytes 196

commit v9 on v8

v9 whole, which is shorter than its diff:
```python
import jax
import jax.numpy as jnp
from jax import lax
from jax.experimental import pallas as pl
from jax.experimental.pallas import tpu as pltpu
from jax.sharding import PartitionSpec as P

BF16 = jnp.bfloat16
F32 = jnp.float32


def near_pairs(count):
    return [(i, i ^ 1) for i in range(count)]


def far_pairs(count):
    return [(i, min(max(((i - 1) ^ 1) + 1, 0), count - 1)) for i in range(count)]


def far_and_z():
    pairs = [(d, d + 1) for d in range(1, 15, 2)] + [(15, 0)]
    return [[d * 16 + 4 * y + z for d in pair for z in range(4)] for pair in pairs for y in range(4)]


def inner(axis):
    i = lax.axis_index(axis)
    return (i > 0) & (i < 15)


def spread(line, col):
    left = jnp.where(col == 0, 0.0, pltpu.roll(line[:, :128], 1, 0))
    right = jnp.where(col == 127, 0.0, pltpu.roll(line[:, 256:], 127, 0))
    return line[:, 128:256] + left + right


def fine_kernel(vol, x2, x1, w, bias, ends, best, edge_w, cells):
    pd = lax.rem(lax.axis_index("depth"), 2)
    pr = lax.rem(lax.axis_index("rows"), 2)
    inner_d = inner("depth")
    zero = jnp.zeros((128, 128), BF16)
    for j in range(4):
        for i in range(6):
            row = (i - 1) + pr * (5 - 2 * i)
            if i in (0, 5):
                piece = zero
            elif j == 0:
                piece = jnp.where(inner_d, x2[row], zero)
            elif j == 3:
                piece = x1[row]
            else:
                piece = vol[(j - 1) + pd * (3 - 2 * j), row]
            cells[j, i] = piece
    taps = [(a, b) for a in range(3) for b in range(3)]
    groups = [taps[i : i + 2] for i in range(0, 9, 2)]
    col = lax.broadcasted_iota(jnp.int32, (128, 128), 0)
    for s in range(2):
        total = None
        for group in groups:
            lhs = jnp.concatenate(
                [cells[s + a, b : b + 4].reshape(512, 128) for a, b in group], axis=1
            )
            rhs = jnp.concatenate(
                [
                    jnp.concatenate(
                        [w[a + pd * (2 - 2 * a), b + pr * (2 - 2 * b), c] for c in range(3)], axis=1
                    )
                    for a, b in group
                ],
                axis=0,
            )
            term = jnp.dot(lhs, rhs, preferred_element_type=F32)
            total = term if total is None else total + term
        for q in range(2):
            ends[s, q] = spread(total[3 * q * 128 : (3 * q + 1) * 128], col) + bias[...]
            middle = spread(total[(q + 1) * 128 : (q + 2) * 128], col) + bias[...]
            best[q] = middle if s == 0 else jnp.maximum(best[q], middle)
    for q in range(2):
        b = 2 * q
        for a in range(3):
            for c in range(3):
                edge_w[q, 128 * a : 128 * a + 128, 128 * c : 128 * c + 128] = w[
                    a + pd * (2 - 2 * a), b + pr * (2 - 2 * b), c
                ]


def fine_level(vol, x2, x1, w, bias):
    vmem = pl.BlockSpec(memory_space=pltpu.VMEM)
    return pl.pallas_call(
        fine_kernel,
        out_shape=[
            jax.ShapeDtypeStruct((2, 2, 128, 128), F32),
            jax.ShapeDtypeStruct((2, 128, 128), F32),
            jax.ShapeDtypeStruct((2, 384, 384), BF16),
        ],
        in_specs=[vmem] * 5,
        out_specs=[vmem] * 3,
        scratch_shapes=[pltpu.VMEM((4, 6, 128, 128), BF16)],
        compiler_params=pltpu.CompilerParams(vmem_limit_bytes=32 * 1024 * 1024),
        cost_estimate=pl.CostEstimate(flops=400_000_000_000, bytes_accessed=0, transcendentals=0),
    )(vol, x2, x1, w, bias)


def finish_kernel(ends, best, edge_w, c2, c1, other, out, peak):
    pd = lax.rem(lax.axis_index("depth"), 2)
    pr = lax.rem(lax.axis_index("rows"), 2)
    inner_d = inner("depth")
    inner_r = inner("rows")
    zero = jnp.zeros((128, 128), BF16)
    col = lax.broadcasted_iota(jnp.int32, (128, 128), 0)
    for q in range(2):
        rows = []
        for j in range(4):
            plane = j if j in (0, 3) else j + pd * (3 - 2 * j)
            piece = (c2, c1)[q][plane]
            if q == 0:
                piece = jnp.where(inner_r, piece, zero)
            if j == 0:
                piece = jnp.where(inner_d, piece, zero)
            rows.append(piece)
        lhs = jnp.concatenate([jnp.concatenate(rows[s : s + 3], axis=1) for s in range(2)], axis=0)
        edge = jnp.dot(lhs, edge_w[q], preferred_element_type=F32)
        value = best[q]
        for s in range(2):
            value = jnp.maximum(value, ends[s, q] + spread(edge[128 * s : 128 * s + 128], col))
        peak[...] = value
        pooled = jnp.maximum(peak[pl.ds(0, 64, stride=2), :], peak[pl.ds(1, 64, stride=2), :])
        pooled = jnp.maximum(pooled, 0.0).astype(BF16)
        for k in range(8):
            out[k, q + pr * (1 - 2 * q)] = pooled


def finish(main, c2, c1, other):
    vmem = pl.BlockSpec(memory_space=pltpu.VMEM)
    return pl.pallas_call(
        finish_kernel,
        out_shape=jax.ShapeDtypeStruct((8, 2, 64, 128), BF16),
        in_specs=[vmem] * 5 + [pl.BlockSpec(memory_space=pl.ANY)],
        out_specs=vmem,
        scratch_shapes=[pltpu.VMEM((128, 128), F32)],
        compiler_params=pltpu.CompilerParams(vmem_limit_bytes=32 * 1024 * 1024),
    )(*main, c2, c1, other)


def coarse_sums(cells, taps, pair, other, add):
    lhs = jnp.concatenate(
        [
            jnp.concatenate([w[m, 9 * a + 3 * b + c] for a in taps for b in range(3)], axis=1)
            for c in range(3)
            for w, m in ((pair, 0), (pair, 1), (other, 0), (other, 1))
        ],
        axis=0,
    )
    count = len(taps)
    for start, size in ((0, 256), (256, 256), (512, 128)):
        if start < 512:
            first = start // 64 + 1
            blocks = [
                cells[i, first + b : first + b + 4].reshape(256, 128) for i in range(count) for b in range(3)
            ]
        else:
            blocks = [
                jnp.concatenate([cells[i, 9 + b], cells[i, b]], axis=0) for i in range(count) for b in range(3)
            ]
        rhs = jnp.concatenate(blocks, axis=1)
        term = lax.dot_general(lhs, rhs, (((1,), (1,)), ((), ())), preferred_element_type=F32)
        lane = lax.rem(lax.broadcasted_iota(jnp.int32, (64, size), 1), 64)
        left = jnp.where(lane == 0, 0.0, pltpu.roll(term[:64], 1, 1))
        right = jnp.where(lane == 63, 0.0, pltpu.roll(term[128:], size - 1, 1))
        add(start, size, term[64:128] + left + right)


def coarse_kernel(both, pair, other, out, cells):
    pd = lax.rem(lax.axis_index("depth"), 2)
    inner_d = inner("depth")
    for a in range(2):
        for i in (0, 1, 10, 11):
            cells[a, i] = jnp.zeros((64, 128), BF16)
    for k in range(4):
        far = both[pd, k]
        cells[0, 2 + 2 * k : 4 + 2 * k] = jnp.where(inner_d, far, jnp.zeros_like(far))
        cells[1, 2 + 2 * k : 4 + 2 * k] = both[1 - pd, k]

    def put(start, size, value):
        out[:, start : start + size] = value

    coarse_sums(cells, (2 * pd, 1), pair, other, put)


def coarse_level(both, pair, other):
    vmem = pl.BlockSpec(memory_space=pltpu.VMEM)
    return pl.pallas_call(
        coarse_kernel,
        out_shape=jax.ShapeDtypeStruct((64, 640), F32),
        in_specs=[vmem] * 3,
        out_specs=vmem,
        scratch_shapes=[pltpu.VMEM((2, 12, 64, 128), BF16)],
        compiler_params=pltpu.CompilerParams(vmem_limit_bytes=32 * 1024 * 1024),
        cost_estimate=pl.CostEstimate(flops=1_000_000_000, bytes_accessed=0, transcendentals=0),
    )(both, pair, other)


def near_kernel(near, sums, pair, other, out, cells):
    pd = lax.rem(lax.axis_index("depth"), 2)
    y = lax.div(lax.axis_index("rows"), 4)
    for i in (0, 1, 10, 11):
        cells[0, i] = jnp.zeros((64, 128), BF16)
    for k in range(4):
        cells[0, 2 + 2 * k : 4 + 2 * k] = near[k]

    def put(start, size, value):
        value = value + sums[:, start : start + size]
        for k in range(4):
            out[y ^ k, :, start : start + size] = value[16 * k : 16 * k + 16]

    coarse_sums(cells, (2 - 2 * pd,), pair, other, put)


def near_level(near, sums, pair, other):
    vmem = pl.BlockSpec(memory_space=pltpu.VMEM)
    return pl.pallas_call(
        near_kernel,
        out_shape=jax.ShapeDtypeStruct((4, 16, 640), F32),
        in_specs=[vmem] * 4,
        out_specs=vmem,
        scratch_shapes=[pltpu.VMEM((1, 12, 64, 128), BF16)],
        compiler_params=pltpu.CompilerParams(vmem_limit_bytes=32 * 1024 * 1024),
    )(near, sums, pair, other)


def join_kernel(held, bias, out):
    low = lax.broadcasted_iota(jnp.int32, (16, 128), 1) < 64
    for m in range(4):
        tiles = [held[m, :, 128 * i : 128 * i + 128] for i in range(4)]
        if m > 0:
            tiles[0] = tiles[0] + jnp.where(low, held[m - 1, :, 512:], 0.0)
        if m < 3:
            tiles[3] = tiles[3] + jnp.where(low, 0.0, held[m + 1, :, 512:])
        for i in range(4):
            value = jnp.maximum(tiles[i] + bias[...], 0.0).astype(BF16)
            out[:, 512 * m + 128 * i : 512 * m + 128 * i + 128] = value


def join(parts, bias):
    vmem = pl.BlockSpec(memory_space=pltpu.VMEM)
    return pl.pallas_call(
        join_kernel,
        out_shape=jax.ShapeDtypeStruct((16, 2048), BF16),
        in_specs=[vmem] * 2,
        out_specs=vmem,
        compiler_params=pltpu.CompilerParams(vmem_limit_bytes=32 * 1024 * 1024),
    )(parts, bias)


def body(volume, fine_filters, fine_bias, coarse_filters, coarse_bias):
    d = lax.axis_index("depth")
    r = lax.axis_index("rows")
    pd = lax.rem(d, 2)
    pr = lax.rem(r, 2)
    depth_near, depth_far = near_pairs(16), far_pairs(16)
    rows_near, rows_far = near_pairs(16), far_pairs(16)

    far_plane = lax.dynamic_index_in_dim(volume, pd, 0, False)
    x2 = lax.ppermute(far_plane, "depth", depth_far)
    x1 = lax.ppermute(lax.dynamic_index_in_dim(volume, 1 - pd, 0, False), "depth", depth_near)
    def row_of(k):
        return jnp.stack(
            [lax.dynamic_index_in_dim(p, k, 0, False) for p in (x2, volume[0], volume[1], x1)]
        )

    c2 = lax.ppermute(row_of(3 * pr), "rows", rows_far)
    c1 = lax.ppermute(row_of(3 - 3 * pr), "rows", rows_near)

    def along_y(k):
        return [(i, i ^ (4 * k)) for i in range(16)]

    w = jnp.transpose(coarse_filters, (0, 1, 2, 4, 3)).reshape(27, 16, 128)
    w = w + far_plane[0, 0, 0] * jnp.bfloat16(0)
    pair = jnp.stack([w, lax.ppermute(w, "rows", along_y(1))])
    other = lax.ppermute(pair, "rows", along_y(2))
    main = fine_level(volume, x2, x1, fine_filters, fine_bias.reshape(1, 128))
    pooled = finish(main, c2, c1, other)

    both = lax.all_to_all(
        pooled, ("depth", "rows"), 0, 0, axis_index_groups=far_and_z(), tiled=True
    ).reshape(2, 4, 2, 64, 128)
    near = lax.ppermute(lax.dynamic_index_in_dim(both, 1 - pd, 0, False), "depth", depth_near)
    sums = near_level(near, coarse_level(both, pair, other), pair, other)
    parts = lax.all_to_all(
        sums, "rows", 0, 0, axis_index_groups=[[4 * y + z for y in range(4)] for z in range(4)], tiled=True
    )
    result = join(parts, jnp.broadcast_to(coarse_bias[:, None], (16, 128)))
    return result.reshape(16, 1, 2048)


def solution(mesh):
    placed = (
        P("depth", "rows", None, None),
        P(),
        P(),
        P(None, None, None, None, "rows"),
        P("rows"),
    )
    return jax.shard_map(
        body, mesh=mesh, in_specs=placed, out_specs=P("rows", "depth", None), check_vma=False
    )
```

time: 55.4 us -> 62.1 us (1.12)
  waiting for transfers between devices: 1.69 us -> 7.44 us
  starting transfers between devices: 25.2 us -> 20.5 us
  Pallas kernels: 3.24 us -> 6.7 us
  other arithmetic: 0.03 us -> 2.06 us
  blocking collectives: 23.7 us -> 22.5 us
  between operations: 0.12 us -> 0.79 us
    ppermute x5 -> x3, starting transfers between devices: 11.3 us -> 6.12 us  [the longest x1 2.18 us: body(): x2 = lax.ppermute(far_plane, 'depth', depth_far)]
    ppermute x1, waiting for transfers between devices: 0.01 us -> 3.39 us  [body(): pair = jnp.stack([w, lax.ppermute(w, 'rows', along_y(1))])]
    ppermute x5 -> x3, waiting for transfers between devices: 0.7 us -> 4.04 us  [the longest x1 4.04 us: body(): c1 = lax.ppermute(row_of(3 - 3 * pr), 'rows', rows_near)]
    pallas_call x1 -> x2, Pallas kernels: 0.79 us -> 3.1 us  [the longest x1 1.63 us: coarse_level(): pl.pallas_call(coarse_kernel, out_shape=jax.ShapeDtypeStruct((64, 640), F...]
    slice x0 -> x2, local copies, waits for them, and re-layouts: none -> 1.68 us  [the longest x1 1.16 us: row_of(): volume[0]]
    another operation x0 -> x2, other arithmetic: none -> 1.34 us  [row_of(): jnp.stack([lax.dynamic_index_in_dim(p, k, 0, False) for p in (x2, volume[...]
    pallas_call x1, Pallas kernels: 0.28 us -> 1.38 us  [finish(): pl.pallas_call(finish_kernel, out_shape=jax.ShapeDtypeStruct((8, 2, 64, 1...]
    squeeze x2 -> x0, local copies, waits for them, and re-layouts: 1.1 us -> none  [the longest x1 1.09 us: body(): lax.dynamic_index_in_dim(volume, 1 - pd, 0, False)]
  transfers between devices with their start and end apart: 9 -> 7, of which waited for: 2 -> 2; matrix products, arithmetic and copies ran while one was open for 0% -> 4% of each run, Pallas kernels for 3% -> 5%
where the time goes in v9:
time: 62.1 us; the launch traced here: 61.8 us
  blocking collectives  22.5 us (36%)
  starting transfers between devices  20.5 us (33%)
  waiting for transfers between devices  7.44 us (12%)
  Pallas kernels  6.7 us (11%)
  other arithmetic  2.06 us (3%)
  local copies, waits for them, and re-layouts  1.81 us (3%)
  between operations  0.79 us (1%)
    all_to_all x1, blocking collectives, body(): lax.all_to_all(pooled, ('depth', 'rows'), 0, 0, axis_index_groups=far_and...  12.5 us
    all_to_all x1, blocking collectives, body(): lax.all_to_all(sums, 'rows', 0, 0, axis_index_groups=[[4 * y + z for y in...  10 us
    ppermute x1, starting transfers between devices, body(): lax.ppermute(lax.dynamic_index_in_dim(volume, 1 - pd, 0, False), 'depth',...  7.04 us
    ppermute x1, waiting for transfers between devices, body(): c1 = lax.ppermute(row_of(3 - 3 * pr), 'rows', rows_near)  4.04 us
    ppermute x1, waiting for transfers between devices, body(): pair = jnp.stack([w, lax.ppermute(w, 'rows', along_y(1))])  3.39 us
    ppermute x1, starting transfers between devices, body(): other = lax.ppermute(pair, 'rows', along_y(2))  3.19 us
    ppermute x1, starting transfers between devices, body(): lax.ppermute(lax.dynamic_index_in_dim(both, 1 - pd, 0, False), 'depth', d...  2.44 us
    ppermute x1, starting transfers between devices, body(): x2 = lax.ppermute(far_plane, 'depth', depth_far)  2.18 us
  transfers between devices with their start and end apart: 7, of which 2 were waited for; matrix products, arithmetic and copies ran while one was open for 4% of the time, Pallas kernels for 5%

profile of v9, /device:TPU:6, one launch (start us, length us, event | category | flops | bytes accessed | tf_op | source)
XLA Modules:
  0.0 61.8 jit_solution(10500643036107714641)
XLA Ops:
  0.0 1.2 %fusion = (bf16[1,4,128,128]{3,2,1,0:T(8,128)(2,1)S(1)}, bf16[4,128,128]{2,1,0:T(8,128)(2,1)S(1)}, bf16[4,128,128]{2,1,0:T(8,128)(2,1)S(1)}, bf16[1,4,128,128]{3,2,1,0:T(8,128)(2,1)S(1)}) fusion(bf16[2,4,128,128]{3,2,1,0:T(8,128)(2,1)} %vol.1, s32[]{:T(128)S(6)} %select_n.23, s32[]{:T(128)S(6)} %select_n.22), kind=kLoop, calls=%fused_computation.15 | loop fusion | bytes 1048584 | tf_op jit(solution)/shard_map/slice | solution.py:267
  1.2 2.2 %collective-permute-start = (bf16[4,128,128]{2,1,0:T(8,128)(2,1)S(1)}, bf16[4,128,128]{2,1,0:T(8,128)(2,1)S(1)}, u32[]{:S(2)}, u32[]{:S(2)}) collective-permute-start(bf16[4,128,128]{2,1,0:T(8,128)(2,1)S(1)} %get-tuple-element.13), channel_id=1, source_target_pairs={{0,0},{16,32},{32,16},{48,64},{64,48},{80,96},{96,80},{112,128},{1... | collective-permute-start | bytes 393224 | tf_op jit(solution)/shard_map/ppermute | solution.py:263
  3.4 7.0 %collective-permute-start.1 = (bf16[4,128,128]{2,1,0:T(8,128)(2,1)S(1)}, bf16[4,128,128]{2,1,0:T(8,128)(2,1)S(1)}, u32[]{:S(2)}, u32[]{:S(2)}) collective-permute-start(bf16[4,128,128]{2,1,0:T(8,128)(2,1)S(1)} %get-tuple-element.12), channel_id=1, source_target_pairs={{0,16},{16,0},{32,48},{48,32},{64,80},{80,64},{96,112},{112,96},{1... | collective-permute-start | bytes 393224 | tf_op jit(solution)/shard_map/ppermute | solution.py:264
  10.4 0.5 slice.14
  11.6 0.0 copy-start.1
  11.6 1.7 %collective-permute-start.4 = (bf16[27,16,128]{2,1,0:T(8,128)(2,1)S(1)}, bf16[27,16,128]{2,1,0:T(8,128)(2,1)S(1)}, u32[]{:S(2)}, u32[]{:S(2)}) collective-permute-start(bf16[27,16,128]{2,1,0:T(8,128)(2,1)S(1)} %bitcast.27), channel_id=1, source_target_pairs={{0,4},{1,5},{2,6},{3,7},{4,0},{5,1},{6,2},{7,3},{8,12},{9,13},{10,... | collective-permute-start | bytes 331784 | tf_op jit(solution)/shard_map/ppermute | solution.py:278
  13.3 3.4 %collective-permute-done.4 = bf16[27,16,128]{2,1,0:T(8,128)(2,1)S(1)} collective-permute-done((bf16[27,16,128]{2,1,0:T(8,128)(2,1)S(1)}, bf16[27,16,128]{2,1,0:T(8,128)(2,1)S(1)}, u32[]{:S(2)}, u32[]{:S(2)}) %collective-permute-start.4) | collective-permute-done | bytes 110624 | tf_op jit(solution)/shard_map/ppermute | solution.py:278
  16.7 0.7 %pad_maximum_fusion.pair = bf16[2,27,16,128]{3,2,1,0:T(8,128)(2,1)} fusion(bf16[1,27,16,128]{3,2,1,0:T(8,128)(2,1)S(1)} %bitcast.29, bf16[1,27,16,128]{3,2,1,0:T(8,128)(2,1)S(1)} %bitcast.28), kind=kLoop, calls=%fused_computation | loop fusion | flops 110592 | bytes 442368 | tf_op jit(solution)/shard_map/stack | solution.py:278
  17.4 3.2 %collective-permute-start.5 = (bf16[2,27,16,128]{3,2,1,0:T(8,128)(2,1)}, bf16[2,27,16,128]{3,2,1,0:T(8,128)(2,1)}, u32[]{:S(2)}, u32[]{:S(2)}) collective-permute-start(bf16[2,27,16,128]{3,2,1,0:T(8,128)(2,1)} %pad_maximum_fusion.pair), channel_id=1, source_target_pairs={{0,8},{1,9},{2,10},{3,11},{4,12},{5,13},{6,14},{7,15},{8,0},{9,1},... | collective-permute-start | bytes 663560 | tf_op jit(solution)/shard_map/ppermute | solution.py:279
  20.6 0.0 copy-start
  20.6 0.7 %pad_maximum_fusion.1 = bf16[4,128,128]{2,1,0:T(8,128)(2,1)} fusion(bf16[1,128,128]{2,1,0:T(8,128)(2,1)S(1)} %get-tuple-element.22, bf16[1,128,128]{2,1,0:T(8,128)(2,1)S(1)} %get-tuple-element.20, bf16[1,128,128]{2,1,0:T(8,128)(2,1)S(1)} %get-tuple-element.23, bf16[1,128,128]{2,1,0:T(8,128)(2,1)S(1)} %get-tuple-element.16), kind=kLoop, calls=%fused_computation.1 | loop fusion | flops 196608 | bytes 262144 | tf_op jit(solution)/shard_map/stack | solution.py:266
  21.3 2.2 %collective-permute-start.2 = (bf16[4,128,128]{2,1,0:T(8,128)(2,1)}, bf16[4,128,128]{2,1,0:T(8,128)(2,1)}, u32[]{:S(2)}, u32[]{:S(2)}) collective-permute-start(bf16[4,128,128]{2,1,0:T(8,128)(2,1)} %pad_maximum_fusion.1), channel_id=1, source_target_pairs={{0,0},{1,2},{2,1},{3,4},{4,3},{5,6},{6,5},{7,8},{8,7},{9,10},{10,9... | collective-permute-start | bytes 393224 | tf_op jit(solution)/shard_map/ppermute | solution.py:270
  23.5 0.7 %pad_maximum_fusion.2 = bf16[4,128,128]{2,1,0:T(8,128)(2,1)} fusion(bf16[1,128,128]{2,1,0:T(8,128)(2,1)S(1)} %get-tuple-element.21, bf16[1,128,128]{2,1,0:T(8,128)(2,1)S(1)} %get-tuple-element.19, bf16[1,128,128]{2,1,0:T(8,128)(2,1)S(1)} %get-tuple-element.24, bf16[1,128,128]{2,1,0:T(8,128)(2,1)S(1)} %get-tuple-element.15), kind=kLoop, calls=%fused_computation.2 | loop fusion | flops 196608 | bytes 262144 | tf_op jit(solution)/shard_map/stack | solution.py:266
  24.1 1.8 %collective-permute-start.3 = (bf16[4,128,128]{2,1,0:T(8,128)(2,1)}, bf16[4,128,128]{2,1,0:T(8,128)(2,1)}, u32[]{:S(2)}, u32[]{:S(2)}) collective-permute-start(bf16[4,128,128]{2,1,0:T(8,128)(2,1)} %pad_maximum_fusion.2), channel_id=1, source_target_pairs={{0,1},{1,0},{2,3},{3,2},{4,5},{5,4},{6,7},{7,6},{8,9},{9,8},{10,11... | collective-permute-start | bytes 393224 | tf_op jit(solution)/shard_map/ppermute | solution.py:271
  25.9 1.6 %shard_map.55 = (f32[2,2,128,128]{3,2,1,0:T(8,128)S(1)}, f32[2,128,128]{2,1,0:T(8,128)S(1)}, bf16[2,384,384]{2,1,0:T(8,128)(2,1)S(1)}) custom-call(bf16[2,4,128,128]{3,2,1,0:T(8,128)(2,1)S(1)} %copy-done, bf16[4,128,128]{2,1,0:T(8,128)(2,1)S(1)} %collective-permute-done.x2, bf16[4,128,128]{2,1,0:T(8,128)(2,1)S(1)} %collective-permute-done.1.x1, ...), custom_call_target="tpu_custom_call" | custom-call | flops 399999991808 | tf_op jit(solution)/shard_map/pallas_call | solution.py:88
  27.5 4.0 %collective-permute-done.3.c1 = bf16[4,128,128]{2,1,0:T(8,128)(2,1)} collective-permute-done((bf16[4,128,128]{2,1,0:T(8,128)(2,1)}, bf16[4,128,128]{2,1,0:T(8,128)(2,1)}, u32[]{:S(2)}, u32[]{:S(2)}) %collective-permute-start.3) | collective-permute-done | bytes 131104 | tf_op jit(solution)/shard_map/ppermute | solution.py:271
  31.6 1.4 %shard_map.56 = bf16[8,2,64,128]{3,2,1,0:T(8,128)(2,1)S(1)} custom-call(f32[2,2,128,128]{3,2,1,0:T(8,128)S(1)} %get-tuple-element.8.ends, f32[2,128,128]{2,1,0:T(8,128)S(1)} %get-tuple-element.9.best, bf16[2,384,384]{2,1,0:T(8,128)(2,1)S(1)} %get-tuple-element.10.edge_w, bf16[4,128,128]{2,1,0:T(8,128)(2,1)} %collective-permute-done.2.c2, ...), custom_call_target="tpu_custom_call" | custom-call | tf_op jit(solution)/shard_map/pallas_call | solution.py:134
  32.9 12.5 %all_to_all.10 = bf16[8,2,64,128]{3,2,1,0:T(8,128)(2,1)S(1)} all-to-all(bf16[8,2,64,128]{3,2,1,0:T(8,128)(2,1)S(1)} %shard_map.56), channel_id=1, replica_groups={{16,17,18,19,32,33,34,35},{20,21,22,23,36,37,38,39},{24,25,26,27,40,41,..., dimensions={0} | all-to-all | bytes 524288 | tf_op jit(solution)/shard_map/all_to_all | solution.py:283
  45.4 2.4 %collective-permute-start.6 = (bf16[4,2,64,128]{3,2,1,0:T(8,128)(2,1)S(1)}, bf16[4,2,64,128]{3,2,1,0:T(8,128)(2,1)S(1)}, u32[]{:S(2)}, u32[]{:S(2)}) collective-permute-start(bf16[4,2,64,128]{3,2,1,0:T(8,128)(2,1)S(1)} %dynamic-slice_bitcast_fusion), channel_id=1, source_target_pairs={{0,16},{16,0},{32,48},{48,32},{64,80},{80,64},{96,112},{112,96},{1... | collective-permute-start | bytes 393224 | tf_op jit(solution)/shard_map/ppermute | solution.py:286
  47.9 1.6 %shard_map.57.sums = f32[64,640]{1,0:T(8,128)S(1)} custom-call(bf16[2,4,2,64,128]{4,3,2,1,0:T(8,128)(2,1)S(1)} %bitcast.25, bf16[2,27,16,128]{3,2,1,0:T(8,128)(2,1)} %pad_maximum_fusion.pair, bf16[2,27,16,128]{3,2,1,0:T(8,128)(2,1)} %collective-permute-done.5.other), custom_call_target="tpu_custom_call" | custom-call | flops 1000000000 | tf_op jit(solution)/shard_map/pallas_call | solution.py:191
  49.5 1.5 %shard_map.58 = f32[4,16,640]{2,1,0:T(8,128)S(1)} custom-call(bf16[4,2,64,128]{3,2,1,0:T(8,128)(2,1)S(1)} %collective-permute-done.6.near, f32[64,640]{1,0:T(8,128)S(1)} %shard_map.57.sums, bf16[2,27,16,128]{3,2,1,0:T(8,128)(2,1)} %pad_maximum_fusion.pair, bf16[2,27,16,128]{3,2,1,0:T(8,128)(2,1)} %collective-permute-done.5.other), custom_call_target="tpu_custom_call" | custom-call | tf_op jit(solution)/shard_map/pallas_call | solution.py:220
  51.0 10.0 %all_to_all.11.held = f32[4,16,640]{2,1,0:T(8,128)S(1)} all-to-all(f32[4,16,640]{2,1,0:T(8,128)S(1)} %shard_map.58), channel_id=1, replica_groups={{0,4,8,12},{1,5,9,13},{2,6,10,14},{3,7,11,15},{16,20,24,28},{17,21,25,2..., dimensions={0} | all-to-all | bytes 327680 | tf_op jit(solution)/shard_map/all_to_all | solution.py:288
  61.1 0.1 broadcast_in_dim.2.bias
  61.1 0.7 %shard_map.59 = bf16[16,2048]{1,0:T(8,128)(2,1)} custom-call(f32[4,16,640]{2,1,0:T(8,128)S(1)} %all_to_all.11.held, f32[16,128]{1,0:T(8,128)S(1)} %broadcast_in_dim.2.bias), custom_call_target="tpu_custom_call" | custom-call | tf_op jit(solution)/shard_map/pallas_call | solution.py:245
  (18 shorter events, 0.1 us)
Async XLA Ops:
  0.0 11.6 %copy-start.3 = (bf16[3,3,3,128,16]{3,4,2,1,0:T(8,128)(2,1)S(1)}, bf16[3,3,3,128,16]{3,4,2,1,0:T(8,128)(2,1)}, u32[]{:S(2)}) copy-start(bf16[3,3,3,128,16]{3,4,2,1,0:T(8,128)(2,1)} %param.8) | copy-start | bytes 331780
  1.2 19.4 %collective-permute-start = (bf16[4,128,128]{2,1,0:T(8,128)(2,1)S(1)}, bf16[4,128,128]{2,1,0:T(8,128)(2,1)S(1)}, u32[]{:S(2)}, u32[]{:S(2)}) collective-permute-start(bf16[4,128,128]{2,1,0:T(8,128)(2,1)S(1)} %get-tuple-element.13), channel_id=1, source_target_pairs={{0,0},{16,32},{32,16},{48,64},{64,48},{80,96},{96,80},{112,128},{1... | collective-permute-start | bytes 393224 | tf_op jit(solution)/shard_map/ppermute | solution.py:263
  3.4 17.2 %collective-permute-start.1 = (bf16[4,128,128]{2,1,0:T(8,128)(2,1)S(1)}, bf16[4,128,128]{2,1,0:T(8,128)(2,1)S(1)}, u32[]{:S(2)}, u32[]{:S(2)}) collective-permute-start(bf16[4,128,128]{2,1,0:T(8,128)(2,1)S(1)} %get-tuple-element.12), channel_id=1, source_target_pairs={{0,16},{16,0},{32,48},{48,32},{64,80},{80,64},{96,112},{112,96},{1... | collective-permute-start | bytes 393224 | tf_op jit(solution)/shard_map/ppermute | solution.py:264
  11.6 14.4 %copy-start.1 = (bf16[3,3,3,128,128]{4,3,2,1,0:T(8,128)(2,1)S(1)}, bf16[3,3,3,128,128]{4,3,2,1,0:T(8,128)(2,1)}, u32[]{:S(2)}) copy-start(bf16[3,3,3,128,128]{4,3,2,1,0:T(8,128)(2,1)} %w.1) | copy-start | bytes 2654212
  11.6 5.1 %collective-permute-start.4 = (bf16[27,16,128]{2,1,0:T(8,128)(2,1)S(1)}, bf16[27,16,128]{2,1,0:T(8,128)(2,1)S(1)}, u32[]{:S(2)}, u32[]{:S(2)}) collective-permute-start(bf16[27,16,128]{2,1,0:T(8,128)(2,1)S(1)} %bitcast.27), channel_id=1, source_target_pairs={{0,4},{1,5},{2,6},{3,7},{4,0},{5,1},{6,2},{7,3},{8,12},{9,13},{10,... | collective-permute-start | bytes 331784 | tf_op jit(solution)/shard_map/ppermute | solution.py:278
  17.4 14.2 %collective-permute-start.5 = (bf16[2,27,16,128]{3,2,1,0:T(8,128)(2,1)}, bf16[2,27,16,128]{3,2,1,0:T(8,128)(2,1)}, u32[]{:S(2)}, u32[]{:S(2)}) collective-permute-start(bf16[2,27,16,128]{3,2,1,0:T(8,128)(2,1)} %pad_maximum_fusion.pair), channel_id=1, source_target_pairs={{0,8},{1,9},{2,10},{3,11},{4,12},{5,13},{6,14},{7,15},{8,0},{9,1},... | collective-permute-start | bytes 663560 | tf_op jit(solution)/shard_map/ppermute | solution.py:279
  20.6 5.3 %copy-start = (bf16[2,4,128,128]{3,2,1,0:T(8,128)(2,1)S(1)}, bf16[2,4,128,128]{3,2,1,0:T(8,128)(2,1)}, u32[]{:S(2)}) copy-start(bf16[2,4,128,128]{3,2,1,0:T(8,128)(2,1)} %vol.1) | copy-start | bytes 786436
  21.3 6.2 %collective-permute-start.2 = (bf16[4,128,128]{2,1,0:T(8,128)(2,1)}, bf16[4,128,128]{2,1,0:T(8,128)(2,1)}, u32[]{:S(2)}, u32[]{:S(2)}) collective-permute-start(bf16[4,128,128]{2,1,0:T(8,128)(2,1)} %pad_maximum_fusion.1), channel_id=1, source_target_pairs={{0,0},{1,2},{2,1},{3,4},{4,3},{5,6},{6,5},{7,8},{8,7},{9,10},{10,9... | collective-permute-start | bytes 393224 | tf_op jit(solution)/shard_map/ppermute | solution.py:270
  24.1 1.8 %copy-start.2 = (f32[128]{0:T(128)S(1)}, f32[128]{0:T(128)}, u32[]{:S(2)}) copy-start(f32[128]{0:T(128)} %param.7) | copy-start | bytes 1540
  24.1 7.4 %collective-permute-start.3 = (bf16[4,128,128]{2,1,0:T(8,128)(2,1)}, bf16[4,128,128]{2,1,0:T(8,128)(2,1)}, u32[]{:S(2)}, u32[]{:S(2)}) collective-permute-start(bf16[4,128,128]{2,1,0:T(8,128)(2,1)} %pad_maximum_fusion.2), channel_id=1, source_target_pairs={{0,1},{1,0},{2,3},{3,2},{4,5},{5,4},{6,7},{7,6},{8,9},{9,8},{10,11... | collective-permute-start | bytes 393224 | tf_op jit(solution)/shard_map/ppermute | solution.py:271
  45.4 4.1 %collective-permute-start.6 = (bf16[4,2,64,128]{3,2,1,0:T(8,128)(2,1)S(1)}, bf16[4,2,64,128]{3,2,1,0:T(8,128)(2,1)S(1)}, u32[]{:S(2)}, u32[]{:S(2)}) collective-permute-start(bf16[4,2,64,128]{3,2,1,0:T(8,128)(2,1)S(1)} %dynamic-slice_bitcast_fusion), channel_id=1, source_target_pairs={{0,16},{16,0},{32,48},{48,32},{64,80},{80,64},{96,112},{112,96},{1... | collective-permute-start | bytes 393224 | tf_op jit(solution)/shard_map/ppermute | solution.py:286
  51.0 10.1 %copy-start.4 = (f32[16]{0:T(128)S(1)}, f32[16]{0:T(128)}, u32[]{:S(2)}) copy-start(f32[16]{0:T(128)} %param.9) | copy-start | bytes 196

commit v10 on v8

--- a/solution.py
+++ b/solution.py
@@ -95,7 +95,7 @@
         in_specs=[vmem] * 7,
         out_specs=[vmem] * 3,
         scratch_shapes=[pltpu.VMEM((4, 6, 128, 128), BF16)],
-        compiler_params=pltpu.CompilerParams(vmem_limit_bytes=32 * 1024 * 1024),
+        compiler_params=pltpu.CompilerParams(vmem_limit_bytes=12 * 1024 * 1024),
         cost_estimate=pl.CostEstimate(flops=20_000_000_000, bytes_accessed=0, transcendentals=0),
     )(vol, x2, x1, r2, r1, w, bias)
 
@@ -131,7 +131,7 @@
         in_specs=[vmem] * 5 + [pl.BlockSpec(memory_space=pl.ANY)],
         out_specs=vmem,
         scratch_shapes=[pltpu.VMEM((128, 128), F32)],
-        compiler_params=pltpu.CompilerParams(vmem_limit_bytes=32 * 1024 * 1024),
+        compiler_params=pltpu.CompilerParams(vmem_limit_bytes=6 * 1024 * 1024),
     )(*main, c2, c1, other)
 
 
@@ -153,7 +153,7 @@
                 [w[m, 9 * (a + pd * (2 - 2 * a)) + 3 * b + c] for a in range(3) for b in range(3)], axis=1
             )
             for c in range(3)
-            for w, m in ((pair, 0), (pair, 1), (other, 0), (other, 1))
+            for w, m in ((pair, 0), (pair, 1), (other, 1), (other, 0))
         ],
         axis=0,
     )
@@ -185,7 +185,7 @@
         in_specs=[vmem] * 4,
         out_specs=vmem,
         scratch_shapes=[pltpu.VMEM((3, 12, 64, 128), BF16)],
-        compiler_params=pltpu.CompilerParams(vmem_limit_bytes=32 * 1024 * 1024),
+        compiler_params=pltpu.CompilerParams(vmem_limit_bytes=8 * 1024 * 1024),
     )(both, near, pair, other)
 
 
@@ -209,7 +209,7 @@
         out_shape=jax.ShapeDtypeStruct((16, 2048), BF16),
         in_specs=[vmem] * 2,
         out_specs=vmem,
-        compiler_params=pltpu.CompilerParams(vmem_limit_bytes=32 * 1024 * 1024),
+        compiler_params=pltpu.CompilerParams(vmem_limit_bytes=4 * 1024 * 1024),
     )(parts, bias)
 
 
@@ -234,7 +234,7 @@
 
     w = jnp.transpose(coarse_filters, (0, 1, 2, 4, 3)).reshape(27, 16, 128)
     pair = jnp.stack([w, lax.ppermute(w, "rows", along_y(1))])
-    other = lax.ppermute(pair, "rows", along_y(2))
+    other = lax.ppermute(pair, "rows", along_y(3))
     main = fine_level(volume, x2, x1, r2, r1, fine_filters, fine_bias.reshape(1, 128))
     pooled = finish(main, c2, c1, other)
 

time: 55.4 us -> 55 us (level)
  starting transfers between devices: 25.2 us -> 24 us
  blocking collectives: 23.7 us -> 24.4 us
    ppermute x1, starting transfers between devices: 4.42 us -> 3.34 us  [body(): lax.ppermute(lax.dynamic_index_in_dim(sides, 3 - 3 * pr, 1, False), 'rows...]
    all_to_all x1, blocking collectives: 13 us -> 14 us  [body(): lax.all_to_all(pooled, ('depth', 'rows'), 0, 0, axis_index_groups=far_and...]
where the time goes in v10:
time: 55 us; the launch traced here: 54.7 us
  blocking collectives  24.4 us (44%)
  starting transfers between devices  24 us (44%)
  Pallas kernels  3.23 us (6%)
  waiting for transfers between devices  1.7 us (3%)
  local copies, waits for them, and re-layouts  1.2 us (2%)
    all_to_all x1, blocking collectives, body(): lax.all_to_all(pooled, ('depth', 'rows'), 0, 0, axis_index_groups=far_and...  14 us
    all_to_all x1, blocking collectives, body(): lax.all_to_all(sums, 'rows', 0, 0, axis_index_groups=[[4 * y + z for y in...  10.4 us
    ppermute x1, starting transfers between devices, body(): lax.ppermute(lax.dynamic_index_in_dim(volume, 1 - pd, 0, False), 'depth',...  7.04 us
    ppermute x1, starting transfers between devices, body(): lax.ppermute(lax.dynamic_index_in_dim(volume, 3 - 3 * pr, 1, False), 'row...  3.37 us
    ppermute x1, starting transfers between devices, body(): lax.ppermute(lax.dynamic_index_in_dim(sides, 3 - 3 * pr, 1, False), 'rows...  3.34 us
    ppermute x1, starting transfers between devices, body(): other = lax.ppermute(pair, 'rows', along_y(3))  2.9 us
    ppermute x1, starting transfers between devices, body(): lax.ppermute(lax.dynamic_index_in_dim(both, 1 - pd, 0, False), 'depth', d...  2.29 us
    ppermute x1, starting transfers between devices, body(): lax.ppermute(lax.dynamic_index_in_dim(volume, pd, 0, False), 'depth', dep...  2.18 us
  transfers between devices with their start and end apart: 9, of which 2 were waited for; matrix products, arithmetic and copies ran while one was open for 0% of the time, Pallas kernels for 3%

profile of v10, /device:TPU:6, one launch (start us, length us, event | category | flops | bytes accessed | tf_op | source)
XLA Modules:
  0.0 54.7 jit_solution(6929600540357959572)
XLA Ops:
  0.0 1.1 %dynamic-slice_bitcast_fusion.1 = (bf16[4,128,128]{2,1,0:T(8,128)(2,1)S(1)}, bf16[4,128,128]{2,1,0:T(8,128)(2,1)S(1)}) fusion(bf16[2,4,128,128]{3,2,1,0:T(8,128)(2,1)} %vol.1, s32[]{:T(128)S(6)} %select_n.19, s32[]{:T(128)S(6)} %select_n.18), kind=kLoop, calls=%fused_computation.6 | loop fusion | bytes 524296 | tf_op jit(solution)/shard_map/jit(dynamic_index_in_dim)/squeeze | solution.py:225
  1.1 2.2 %collective-permute-start = (bf16[4,128,128]{2,1,0:T(8,128)(2,1)S(1)}, bf16[4,128,128]{2,1,0:T(8,128)(2,1)S(1)}, u32[]{:S(2)}, u32[]{:S(2)}) collective-permute-start(bf16[4,128,128]{2,1,0:T(8,128)(2,1)S(1)} %get-tuple-element.16), channel_id=1, source_target_pairs={{0,0},{16,32},{32,16},{48,64},{64,48},{80,96},{96,80},{112,128},{1... | collective-permute-start | bytes 393224 | tf_op jit(solution)/shard_map/ppermute | solution.py:224
  3.3 7.0 %collective-permute-start.1 = (bf16[4,128,128]{2,1,0:T(8,128)(2,1)S(1)}, bf16[4,128,128]{2,1,0:T(8,128)(2,1)S(1)}, u32[]{:S(2)}, u32[]{:S(2)}) collective-permute-start(bf16[4,128,128]{2,1,0:T(8,128)(2,1)S(1)} %get-tuple-element.15), channel_id=1, source_target_pairs={{0,16},{16,0},{32,48},{48,32},{64,80},{80,64},{96,112},{112,96},{1... | collective-permute-start | bytes 393224 | tf_op jit(solution)/shard_map/ppermute | solution.py:225
  10.3 1.6 %collective-permute-start.6 = (bf16[27,16,128]{2,1,0:T(8,128)(2,1)S(1)}, bf16[27,16,128]{2,1,0:T(8,128)(2,1)S(1)}, u32[]{:S(2)}, u32[]{:S(2)}) collective-permute-start(bf16[27,16,128]{2,1,0:T(8,128)(2,1)S(1)} %bitcast.30), channel_id=1, source_target_pairs={{0,4},{1,5},{2,6},{3,7},{4,0},{5,1},{6,2},{7,3},{8,12},{9,13},{10,... | collective-permute-start | bytes 331784 | tf_op jit(solution)/shard_map/ppermute | solution.py:236
  11.9 0.7 %collective-permute-start.2 = (bf16[2,128,128]{2,1,0:T(8,128)(2,1)S(1)}, bf16[2,128,128]{2,1,0:T(8,128)(2,1)S(1)}, u32[]{:S(2)}, u32[]{:S(2)}) collective-permute-start(bf16[2,128,128]{2,1,0:T(8,128)(2,1)S(1)} %get-tuple-element.14), channel_id=1, source_target_pairs={{0,0},{1,2},{2,1},{3,4},{4,3},{5,6},{6,5},{7,8},{8,7},{9,10},{10,9... | collective-permute-start | bytes 196616 | tf_op jit(solution)/shard_map/ppermute | solution.py:226
  12.6 3.4 %collective-permute-start.3 = (bf16[2,128,128]{2,1,0:T(8,128)(2,1)S(1)}, bf16[2,128,128]{2,1,0:T(8,128)(2,1)S(1)}, u32[]{:S(2)}, u32[]{:S(2)}) collective-permute-start(bf16[2,128,128]{2,1,0:T(8,128)(2,1)S(1)} %get-tuple-element.13), channel_id=1, source_target_pairs={{0,1},{1,0},{2,3},{3,2},{4,5},{5,4},{6,7},{7,6},{8,9},{9,8},{10,11... | collective-permute-start | bytes 196616 | tf_op jit(solution)/shard_map/ppermute | solution.py:227
  16.0 0.0 collective-permute-done.6
  16.0 2.9 %collective-permute-start.7 = (bf16[2,27,16,128]{3,2,1,0:T(8,128)(2,1)S(1)}, bf16[2,27,16,128]{3,2,1,0:T(8,128)(2,1)S(1)}, u32[]{:S(2)}, u32[]{:S(2)}) collective-permute-start(bf16[2,27,16,128]{3,2,1,0:T(8,128)(2,1)S(1)} %pad_maximum_fusion.pair), channel_id=1, source_target_pairs={{0,12},{1,13},{2,14},{3,15},{4,8},{5,9},{6,10},{7,11},{8,4},{9,5},... | collective-permute-start | bytes 663560 | tf_op jit(solution)/shard_map/ppermute | solution.py:237
  18.9 0.0 collective-permute-done.x2
  18.9 0.0 collective-permute-done.1.x1
  18.9 0.7 %collective-permute-start.4 = (bf16[2,128,128]{2,1,0:T(8,128)(2,1)S(1)}, bf16[2,128,128]{2,1,0:T(8,128)(2,1)S(1)}, u32[]{:S(2)}, u32[]{:S(2)}) collective-permute-start(bf16[2,128,128]{2,1,0:T(8,128)(2,1)S(1)} %get-tuple-element.12), channel_id=1, source_target_pairs={{0,0},{1,2},{2,1},{3,4},{4,3},{5,6},{6,5},{7,8},{8,7},{9,10},{10,9... | collective-permute-start | bytes 196616 | tf_op jit(solution)/shard_map/ppermute | solution.py:229
  19.6 0.0 copy-start.2
  19.6 3.3 %collective-permute-start.5 = (bf16[2,128,128]{2,1,0:T(8,128)(2,1)S(1)}, bf16[2,128,128]{2,1,0:T(8,128)(2,1)S(1)}, u32[]{:S(2)}, u32[]{:S(2)}) collective-permute-start(bf16[2,128,128]{2,1,0:T(8,128)(2,1)S(1)} %get-tuple-element.11), channel_id=1, source_target_pairs={{0,1},{1,0},{2,3},{3,2},{4,5},{5,4},{6,7},{7,6},{8,9},{9,8},{10,11... | collective-permute-start | bytes 196616 | tf_op jit(solution)/shard_map/ppermute | solution.py:230
  23.0 1.5 %shard_map.55 = (f32[2,2,128,128]{3,2,1,0:T(8,128)S(1)}, f32[2,128,128]{2,1,0:T(8,128)S(1)}, bf16[2,2,128,384]{3,2,1,0:T(8,128)(2,1)S(1)}) custom-call(bf16[2,4,128,128]{3,2,1,0:T(8,128)(2,1)S(1)} %copy-done, bf16[4,128,128]{2,1,0:T(8,128)(2,1)S(1)} %collective-permute-done.x2, bf16[4,128,128]{2,1,0:T(8,128)(2,1)S(1)} %collective-permute-done.1.x1, ...), custom_call_target="tpu_custom_call" | custom-call | flops 20000000000 | tf_op jit(solution)/shard_map/pallas_call | solution.py:88
  24.5 0.7 %collective-permute-done.5.c1 = bf16[2,128,128]{2,1,0:T(8,128)(2,1)S(1)} collective-permute-done((bf16[2,128,128]{2,1,0:T(8,128)(2,1)S(1)}, bf16[2,128,128]{2,1,0:T(8,128)(2,1)S(1)}, u32[]{:S(2)}, u32[]{:S(2)}) %collective-permute-start.5) | collective-permute-done | bytes 65568 | tf_op jit(solution)/shard_map/ppermute | solution.py:230
  25.2 0.3 shard_map.56
  25.5 14.0 %all_to_all.10 = bf16[8,2,64,128]{3,2,1,0:T(8,128)(2,1)S(1)} all-to-all(bf16[8,2,64,128]{3,2,1,0:T(8,128)(2,1)S(1)} %shard_map.56), channel_id=1, replica_groups={{16,17,18,19,32,33,34,35},{20,21,22,23,36,37,38,39},{24,25,26,27,40,41,..., dimensions={0} | all-to-all | bytes 524288 | tf_op jit(solution)/shard_map/all_to_all | solution.py:241
  39.5 2.3 %collective-permute-start.8 = (bf16[4,2,64,128]{3,2,1,0:T(8,128)(2,1)S(1)}, bf16[4,2,64,128]{3,2,1,0:T(8,128)(2,1)S(1)}, u32[]{:S(2)}, u32[]{:S(2)}) collective-permute-start(bf16[4,2,64,128]{3,2,1,0:T(8,128)(2,1)S(1)} %dynamic-slice_bitcast_fusion), channel_id=1, source_target_pairs={{0,16},{16,0},{32,48},{48,32},{64,80},{80,64},{96,112},{112,96},{1... | collective-permute-start | bytes 393224 | tf_op jit(solution)/shard_map/ppermute | solution.py:244
  41.8 1.0 %collective-permute-done.8.near = bf16[4,2,64,128]{3,2,1,0:T(8,128)(2,1)S(1)} collective-permute-done((bf16[4,2,64,128]{3,2,1,0:T(8,128)(2,1)S(1)}, bf16[4,2,64,128]{3,2,1,0:T(8,128)(2,1)S(1)}, u32[]{:S(2)}, u32[]{:S(2)}) %collective-permute-start.8) | collective-permute-done | bytes 131104 | tf_op jit(solution)/shard_map/ppermute | solution.py:244
  42.8 0.8 %shard_map.57 = f32[4,16,640]{2,1,0:T(8,128)S(1)} custom-call(bf16[2,4,2,64,128]{4,3,2,1,0:T(8,128)(2,1)S(1)} %bitcast.26, bf16[4,2,64,128]{3,2,1,0:T(8,128)(2,1)S(1)} %collective-permute-done.8.near, bf16[2,27,16,128]{3,2,1,0:T(8,128)(2,1)S(1)} %pad_maximum_fusion.pair, bf16[2,27,16,128]{3,2,1,0:T(8,128)(2,1)S(1)} %collective-permute-done.7.other), custom_call_target="tpu_custom_call" | custom-call | tf_op jit(solution)/shard_map/pallas_call | solution.py:182
  43.6 0.0 copy-start.4
  43.6 10.4 %all_to_all.11.held = f32[4,16,640]{2,1,0:T(8,128)S(1)} all-to-all(f32[4,16,640]{2,1,0:T(8,128)S(1)} %shard_map.57), channel_id=1, replica_groups={{0,4,8,12},{1,5,9,13},{2,6,10,14},{3,7,11,15},{16,20,24,28},{17,21,25,2..., dimensions={0} | all-to-all | bytes 327680 | tf_op jit(solution)/shard_map/all_to_all | solution.py:246
  53.9 0.1 broadcast_in_dim.2.bias
  54.0 0.7 %shard_map.58 = bf16[16,2048]{1,0:T(8,128)(2,1)} custom-call(f32[4,16,640]{2,1,0:T(8,128)S(1)} %all_to_all.11.held, f32[16,128]{1,0:T(8,128)S(1)} %broadcast_in_dim.2.bias), custom_call_target="tpu_custom_call" | custom-call | tf_op jit(solution)/shard_map/pallas_call | solution.py:207
  (16 shorter events, 0.1 us)
Async XLA Ops:
  0.0 10.3 %copy-start.3 = (bf16[3,3,3,128,16]{3,4,2,1,0:T(8,128)(2,1)S(1)}, bf16[3,3,3,128,16]{3,4,2,1,0:T(8,128)(2,1)}, u32[]{:S(2)}) copy-start(bf16[3,3,3,128,16]{3,4,2,1,0:T(8,128)(2,1)} %param.8) | copy-start | bytes 331780
  0.0 11.9 %copy-start = (bf16[2,4,128,128]{3,2,1,0:T(8,128)(2,1)S(1)}, bf16[2,4,128,128]{3,2,1,0:T(8,128)(2,1)}, u32[]{:S(2)}) copy-start(bf16[2,4,128,128]{3,2,1,0:T(8,128)(2,1)} %vol.1) | copy-start | bytes 786436
  0.0 23.0 %copy-start.1 = (bf16[3,3,3,128,128]{4,3,2,1,0:T(8,128)(2,1)S(1)}, bf16[3,3,3,128,128]{4,3,2,1,0:T(8,128)(2,1)}, u32[]{:S(2)}) copy-start(bf16[3,3,3,128,128]{4,3,2,1,0:T(8,128)(2,1)} %w.1) | copy-start | bytes 2654212
  1.1 17.8 %collective-permute-start = (bf16[4,128,128]{2,1,0:T(8,128)(2,1)S(1)}, bf16[4,128,128]{2,1,0:T(8,128)(2,1)S(1)}, u32[]{:S(2)}, u32[]{:S(2)}) collective-permute-start(bf16[4,128,128]{2,1,0:T(8,128)(2,1)S(1)} %get-tuple-element.16), channel_id=1, source_target_pairs={{0,0},{16,32},{32,16},{48,64},{64,48},{80,96},{96,80},{112,128},{1... | collective-permute-start | bytes 393224 | tf_op jit(solution)/shard_map/ppermute | solution.py:224
  3.3 15.6 %collective-permute-start.1 = (bf16[4,128,128]{2,1,0:T(8,128)(2,1)S(1)}, bf16[4,128,128]{2,1,0:T(8,128)(2,1)S(1)}, u32[]{:S(2)}, u32[]{:S(2)}) collective-permute-start(bf16[4,128,128]{2,1,0:T(8,128)(2,1)S(1)} %get-tuple-element.15), channel_id=1, source_target_pairs={{0,16},{16,0},{32,48},{48,32},{64,80},{80,64},{96,112},{112,96},{1... | collective-permute-start | bytes 393224 | tf_op jit(solution)/shard_map/ppermute | solution.py:225
  10.3 5.6 %collective-permute-start.6 = (bf16[27,16,128]{2,1,0:T(8,128)(2,1)S(1)}, bf16[27,16,128]{2,1,0:T(8,128)(2,1)S(1)}, u32[]{:S(2)}, u32[]{:S(2)}) collective-permute-start(bf16[27,16,128]{2,1,0:T(8,128)(2,1)S(1)} %bitcast.30), channel_id=1, source_target_pairs={{0,4},{1,5},{2,6},{3,7},{4,0},{5,1},{6,2},{7,3},{8,12},{9,13},{10,... | collective-permute-start | bytes 331784 | tf_op jit(solution)/shard_map/ppermute | solution.py:236
  11.9 11.0 %collective-permute-start.2 = (bf16[2,128,128]{2,1,0:T(8,128)(2,1)S(1)}, bf16[2,128,128]{2,1,0:T(8,128)(2,1)S(1)}, u32[]{:S(2)}, u32[]{:S(2)}) collective-permute-start(bf16[2,128,128]{2,1,0:T(8,128)(2,1)S(1)} %get-tuple-element.14), channel_id=1, source_target_pairs={{0,0},{1,2},{2,1},{3,4},{4,3},{5,6},{6,5},{7,8},{8,7},{9,10},{10,9... | collective-permute-start | bytes 196616 | tf_op jit(solution)/shard_map/ppermute | solution.py:226
  12.6 10.4 %collective-permute-start.3 = (bf16[2,128,128]{2,1,0:T(8,128)(2,1)S(1)}, bf16[2,128,128]{2,1,0:T(8,128)(2,1)S(1)}, u32[]{:S(2)}, u32[]{:S(2)}) collective-permute-start(bf16[2,128,128]{2,1,0:T(8,128)(2,1)S(1)} %get-tuple-element.13), channel_id=1, source_target_pairs={{0,1},{1,0},{2,3},{3,2},{4,5},{5,4},{6,7},{7,6},{8,9},{9,8},{10,11... | collective-permute-start | bytes 196616 | tf_op jit(solution)/shard_map/ppermute | solution.py:227
  16.0 9.2 %collective-permute-start.7 = (bf16[2,27,16,128]{3,2,1,0:T(8,128)(2,1)S(1)}, bf16[2,27,16,128]{3,2,1,0:T(8,128)(2,1)S(1)}, u32[]{:S(2)}, u32[]{:S(2)}) collective-permute-start(bf16[2,27,16,128]{3,2,1,0:T(8,128)(2,1)S(1)} %pad_maximum_fusion.pair), channel_id=1, source_target_pairs={{0,12},{1,13},{2,14},{3,15},{4,8},{5,9},{6,10},{7,11},{8,4},{9,5},... | collective-permute-start | bytes 663560 | tf_op jit(solution)/shard_map/ppermute | solution.py:237
  18.9 5.6 %collective-permute-start.4 = (bf16[2,128,128]{2,1,0:T(8,128)(2,1)S(1)}, bf16[2,128,128]{2,1,0:T(8,128)(2,1)S(1)}, u32[]{:S(2)}, u32[]{:S(2)}) collective-permute-start(bf16[2,128,128]{2,1,0:T(8,128)(2,1)S(1)} %get-tuple-element.12), channel_id=1, source_target_pairs={{0,0},{1,2},{2,1},{3,4},{4,3},{5,6},{6,5},{7,8},{8,7},{9,10},{10,9... | collective-permute-start | bytes 196616 | tf_op jit(solution)/shard_map/ppermute | solution.py:229
  19.6 3.4 %copy-start.2 = (f32[128]{0:T(128)S(1)}, f32[128]{0:T(128)}, u32[]{:S(2)}) copy-start(f32[128]{0:T(128)} %param.7) | copy-start | bytes 1540
  19.6 5.6 %collective-permute-start.5 = (bf16[2,128,128]{2,1,0:T(8,128)(2,1)S(1)}, bf16[2,128,128]{2,1,0:T(8,128)(2,1)S(1)}, u32[]{:S(2)}, u32[]{:S(2)}) collective-permute-start(bf16[2,128,128]{2,1,0:T(8,128)(2,1)S(1)} %get-tuple-element.11), channel_id=1, source_target_pairs={{0,1},{1,0},{2,3},{3,2},{4,5},{5,4},{6,7},{7,6},{8,9},{9,8},{10,11... | collective-permute-start | bytes 196616 | tf_op jit(solution)/shard_map/ppermute | solution.py:230
  39.5 3.3 %collective-permute-start.8 = (bf16[4,2,64,128]{3,2,1,0:T(8,128)(2,1)S(1)}, bf16[4,2,64,128]{3,2,1,0:T(8,128)(2,1)S(1)}, u32[]{:S(2)}, u32[]{:S(2)}) collective-permute-start(bf16[4,2,64,128]{3,2,1,0:T(8,128)(2,1)S(1)} %dynamic-slice_bitcast_fusion), channel_id=1, source_target_pairs={{0,16},{16,0},{32,48},{48,32},{64,80},{80,64},{96,112},{112,96},{1... | collective-permute-start | bytes 393224 | tf_op jit(solution)/shard_map/ppermute | solution.py:244
  43.6 10.4 %copy-start.4 = (f32[16]{0:T(128)S(1)}, f32[16]{0:T(128)}, u32[]{:S(2)}) copy-start(f32[16]{0:T(128)} %param.9) | copy-start | bytes 196

commit v11 on v10

--- a/solution.py
+++ b/solution.py
@@ -33,26 +33,22 @@
     return line[:, 128:256] + left + right
 
 
-def fine_kernel(vol, x2, x1, r2, r1, w, bias, ends, best, corner_w, cells):
+def fine_kernel(vol, x2, x1, w, bias, ends, best, edge_w, cells):
     pd = lax.rem(lax.axis_index("depth"), 2)
     pr = lax.rem(lax.axis_index("rows"), 2)
     inner_d = inner("depth")
-    inner_r = inner("rows")
     zero = jnp.zeros((128, 128), BF16)
     for j in range(4):
         for i in range(6):
             row = (i - 1) + pr * (5 - 2 * i)
-            if j in (1, 2):
-                plane = (j - 1) + pd * (3 - 2 * j)
-                piece = r2[plane] if i == 0 else r1[plane] if i == 5 else vol[plane, row]
-            elif i in (0, 5):
+            if i in (0, 5):
                 piece = zero
+            elif j == 0:
+                piece = jnp.where(inner_d, x2[row], zero)
+            elif j == 3:
+                piece = x1[row]
             else:
-                piece = (x2 if j == 0 else x1)[row]
-            if i == 0:
-                piece = jnp.where(inner_r, piece, zero)
-            if j == 0:
-                piece = jnp.where(inner_d, piece, zero)
+                piece = vol[(j - 1) + pd * (3 - 2 * j), row]
             cells[j, i] = piece
     taps = [(a, b) for a in range(3) for b in range(3)]
     groups = [taps[i : i + 2] for i in range(0, 9, 2)]
@@ -78,44 +74,54 @@
             ends[s, q] = spread(total[3 * q * 128 : (3 * q + 1) * 128], col) + bias[...]
             middle = spread(total[(q + 1) * 128 : (q + 2) * 128], col) + bias[...]
             best[q] = middle if s == 0 else jnp.maximum(best[q], middle)
-            a, b = 2 * s, 2 * q
+    for q in range(2):
+        b = 2 * q
+        for a in range(3):
             for c in range(3):
-                corner_w[s, q, :, 128 * c : 128 * c + 128] = w[a + pd * (2 - 2 * a), b + pr * (2 - 2 * b), c]
-
-
-def fine_level(vol, x2, x1, r2, r1, w, bias):
+                edge_w[q, 128 * a : 128 * a + 128, 128 * c : 128 * c + 128] = w[
+                    a + pd * (2 - 2 * a), b + pr * (2 - 2 * b), c
+                ]
+
+
+def fine_level(vol, x2, x1, w, bias):
     vmem = pl.BlockSpec(memory_space=pltpu.VMEM)
     return pl.pallas_call(
         fine_kernel,
         out_shape=[
             jax.ShapeDtypeStruct((2, 2, 128, 128), F32),
             jax.ShapeDtypeStruct((2, 128, 128), F32),
-            jax.ShapeDtypeStruct((2, 2, 128, 384), BF16),
+            jax.ShapeDtypeStruct((2, 384, 384), BF16),
         ],
-        in_specs=[vmem] * 7,
+        in_specs=[vmem] * 5,
         out_specs=[vmem] * 3,
         scratch_shapes=[pltpu.VMEM((4, 6, 128, 128), BF16)],
         compiler_params=pltpu.CompilerParams(vmem_limit_bytes=12 * 1024 * 1024),
         cost_estimate=pl.CostEstimate(flops=20_000_000_000, bytes_accessed=0, transcendentals=0),
-    )(vol, x2, x1, r2, r1, w, bias)
-
-
-def finish_kernel(ends, best, corner_w, c2, c1, other, out, peak):
+    )(vol, x2, x1, w, bias)
+
+
+def finish_kernel(ends, best, edge_w, c1, c2, w2, w1, w3, out, peak):
+    pd = lax.rem(lax.axis_index("depth"), 2)
     pr = lax.rem(lax.axis_index("rows"), 2)
     inner_d = inner("depth")
     inner_r = inner("rows")
     zero = jnp.zeros((128, 128), BF16)
     col = lax.broadcasted_iota(jnp.int32, (128, 128), 0)
     for q in range(2):
+        rows = []
+        for j in range(4):
+            plane = j if j in (0, 3) else j + pd * (3 - 2 * j)
+            piece = (c2, c1)[q][plane]
+            if q == 0:
+                piece = jnp.where(inner_r, piece, zero)
+            if j == 0:
+                piece = jnp.where(inner_d, piece, zero)
+            rows.append(piece)
+        lhs = jnp.concatenate([jnp.concatenate(rows[s : s + 3], axis=1) for s in range(2)], axis=0)
+        edge = jnp.dot(lhs, edge_w[q], preferred_element_type=F32)
         value = best[q]
         for s in range(2):
-            piece = (c2, c1)[q][s]
-            if q == 0:
-                piece = jnp.where(inner_r, piece, zero)
-            if s == 0:
-                piece = jnp.where(inner_d, piece, zero)
-            corner = jnp.dot(piece, corner_w[s, q], preferred_element_type=F32)
-            value = jnp.maximum(value, ends[s, q] + spread(corner, col))
+            value = jnp.maximum(value, ends[s, q] + spread(edge[128 * s : 128 * s + 128], col))
         peak[...] = value
         pooled = jnp.maximum(peak[pl.ds(0, 64, stride=2), :], peak[pl.ds(1, 64, stride=2), :])
         pooled = jnp.maximum(pooled, 0.0).astype(BF16)
@@ -123,19 +129,19 @@
             out[k, q + pr * (1 - 2 * q)] = pooled
 
 
-def finish(main, c2, c1, other):
+def finish(main, c2, c1, weights):
     vmem = pl.BlockSpec(memory_space=pltpu.VMEM)
     return pl.pallas_call(
         finish_kernel,
         out_shape=jax.ShapeDtypeStruct((8, 2, 64, 128), BF16),
-        in_specs=[vmem] * 5 + [pl.BlockSpec(memory_space=pl.ANY)],
+        in_specs=[vmem] * 5 + [pl.BlockSpec(memory_space=pl.ANY)] * 3,
         out_specs=vmem,
         scratch_shapes=[pltpu.VMEM((128, 128), F32)],
         compiler_params=pltpu.CompilerParams(vmem_limit_bytes=6 * 1024 * 1024),
-    )(*main, c2, c1, other)
-
-
-def coarse_kernel(both, near, pair, other, out, cells):
+    )(*main, c1, c2, *weights)
+
+
+def coarse_kernel(both, near, w0, w1, w2, w3, out, cells):
     pd = lax.rem(lax.axis_index("depth"), 2)
     y = lax.div(lax.axis_index("rows"), 4)
     inner_d = inner("depth")
@@ -150,10 +156,10 @@
     lhs = jnp.concatenate(
         [
             jnp.concatenate(
-                [w[m, 9 * (a + pd * (2 - 2 * a)) + 3 * b + c] for a in range(3) for b in range(3)], axis=1
+                [w[9 * (a + pd * (2 - 2 * a)) + 3 * b + c] for a in range(3) for b in range(3)], axis=1
             )
             for c in range(3)
-            for w, m in ((pair, 0), (pair, 1), (other, 1), (other, 0))
+            for w in (w0, w1, w2, w3)
         ],
         axis=0,
     )
@@ -177,16 +183,16 @@
             out[y ^ k, :, start : start + size] = value[16 * k : 16 * k + 16]
 
 
-def coarse_level(both, near, pair, other):
+def coarse_level(both, near, weights):
     vmem = pl.BlockSpec(memory_space=pltpu.VMEM)
     return pl.pallas_call(
         coarse_kernel,
         out_shape=jax.ShapeDtypeStruct((4, 16, 640), F32),
-        in_specs=[vmem] * 4,
+        in_specs=[vmem] * 6,
         out_specs=vmem,
         scratch_shapes=[pltpu.VMEM((3, 12, 64, 128), BF16)],
         compiler_params=pltpu.CompilerParams(vmem_limit_bytes=8 * 1024 * 1024),
-    )(both, near, pair, other)
+    )(both, near, *weights)
 
 
 def join_kernel(held, bias, out):
@@ -221,28 +227,31 @@
     depth_near, depth_far = near_pairs(16), far_pairs(16)
     rows_near, rows_far = near_pairs(16), far_pairs(16)
 
-    x2 = lax.ppermute(lax.dynamic_index_in_dim(volume, pd, 0, False), "depth", depth_far)
+    far_plane = lax.dynamic_index_in_dim(volume, pd, 0, False)
+    x2 = lax.ppermute(far_plane, "depth", depth_far)
     x1 = lax.ppermute(lax.dynamic_index_in_dim(volume, 1 - pd, 0, False), "depth", depth_near)
-    r2 = lax.ppermute(lax.dynamic_index_in_dim(volume, 3 * pr, 1, False), "rows", rows_far)
-    r1 = lax.ppermute(lax.dynamic_index_in_dim(volume, 3 - 3 * pr, 1, False), "rows", rows_near)
-    sides = jnp.stack([x2, x1])
-    c2 = lax.ppermute(lax.dynamic_index_in_dim(sides, 3 * pr, 1, False), "rows", rows_far)
-    c1 = lax.ppermute(lax.dynamic_index_in_dim(sides, 3 - 3 * pr, 1, False), "rows", rows_near)
+
+    def row_of(k):
+        return jnp.stack(
+            [lax.dynamic_index_in_dim(p, k, 0, False) for p in (x2, volume[0], volume[1], x1)]
+        )
+
+    c2 = lax.ppermute(row_of(3 * pr), "rows", rows_far)
+    c1 = lax.ppermute(row_of(3 - 3 * pr), "rows", rows_near)
 
     def along_y(k):
         return [(i, i ^ (4 * k)) for i in range(16)]
 
     w = jnp.transpose(coarse_filters, (0, 1, 2, 4, 3)).reshape(27, 16, 128)
-    pair = jnp.stack([w, lax.ppermute(w, "rows", along_y(1))])
-    other = lax.ppermute(pair, "rows", along_y(3))
-    main = fine_level(volume, x2, x1, r2, r1, fine_filters, fine_bias.reshape(1, 128))
-    pooled = finish(main, c2, c1, other)
+    w2, w1, w3 = [lax.ppermute(w, "rows", along_y(k)) for k in (2, 1, 3)]
+    main = fine_level(volume, x2, x1, fine_filters, fine_bias.reshape(1, 128))
+    pooled = finish(main, c2, c1, (w2, w1, w3))
 
     both = lax.all_to_all(
         pooled, ("depth", "rows"), 0, 0, axis_index_groups=far_and_z(), tiled=True
     ).reshape(2, 4, 2, 64, 128)
     near = lax.ppermute(lax.dynamic_index_in_dim(both, 1 - pd, 0, False), "depth", depth_near)
-    sums = coarse_level(both, near, pair, other)
+    sums = coarse_level(both, near, (w, w1, w2, w3))
     parts = lax.all_to_all(
         sums, "rows", 0, 0, axis_index_groups=[[4 * y + z for y in range(4)] for z in range(4)], tiled=True
     )

time: 55 us -> 56.7 us (1.031)
  waiting for transfers between devices: 1.7 us -> 7.08 us
  starting transfers between devices: 24 us -> 19.6 us
    ppermute x7 -> x6, waiting for transfers between devices: 0.71 us -> 5.15 us  [the longest x1 5.13 us: body(): c1 = lax.ppermute(row_of(3 - 3 * pr), 'rows', rows_near)]
    ppermute x7 -> x6, starting transfers between devices: 14.7 us -> 10.7 us  [the longest x3 4.34 us: body(): w2, w1, w3 = [lax.ppermute(w, 'rows', along_y(k)) for k in (2, 1, 3)]]
    slice x0 -> x1, local copies, waits for them, and re-layouts: none -> 1.22 us  [row_of(): volume[0]]
    squeeze x2 -> x0, local copies, waits for them, and re-layouts: 1.1 us -> none  [the longest x1 1.09 us: body(): lax.dynamic_index_in_dim(volume, 1 - pd, 0, False)]
    all_to_all x1, blocking collectives: 10.4 us -> 11.3 us  [body(): lax.all_to_all(sums, 'rows', 0, 0, axis_index_groups=[[4 * y + z for y in...]
    ppermute x1, waiting for transfers between devices: 0.01 us -> 0.94 us  [body(): lax.ppermute(lax.dynamic_index_in_dim(volume, 1 - pd, 0, False), 'depth',...]
    ppermute x1, starting transfers between devices: 7.04 us -> 6.39 us  [body(): lax.ppermute(lax.dynamic_index_in_dim(volume, 1 - pd, 0, False), 'depth',...]
  transfers between devices with their start and end apart: 9 -> 8, of which waited for: 2 -> 3; matrix products, arithmetic and copies ran while one was open for 0% -> 0% of each run, Pallas kernels for 3% -> 3%
where the time goes in v11:
time: 56.7 us; the launch traced here: 56.4 us
  blocking collectives  24.9 us (44%)
  starting transfers between devices  19.6 us (35%)
  waiting for transfers between devices  7.08 us (12%)
  Pallas kernels  3.41 us (6%)
  local copies, waits for them, and re-layouts  1.35 us (2%)
    all_to_all x1, blocking collectives, body(): lax.all_to_all(pooled, ('depth', 'rows'), 0, 0, axis_index_groups=far_and...  13.5 us
    all_to_all x1, blocking collectives, body(): lax.all_to_all(sums, 'rows', 0, 0, axis_index_groups=[[4 * y + z for y in...  11.3 us
    ppermute x1, starting transfers between devices, body(): lax.ppermute(lax.dynamic_index_in_dim(volume, 1 - pd, 0, False), 'depth',...  6.39 us
    ppermute x1, waiting for transfers between devices, body(): c1 = lax.ppermute(row_of(3 - 3 * pr), 'rows', rows_near)  5.13 us
    ppermute x3, starting transfers between devices, body(): w2, w1, w3 = [lax.ppermute(w, 'rows', along_y(k)) for k in (2, 1, 3)]  4.34 us
    ppermute x1, starting transfers between devices, body(): c1 = lax.ppermute(row_of(3 - 3 * pr), 'rows', rows_near)  3.36 us
    ppermute x1, starting transfers between devices, body(): lax.ppermute(lax.dynamic_index_in_dim(both, 1 - pd, 0, False), 'depth', d...  2.5 us
    ppermute x1, starting transfers between devices, body(): x2 = lax.ppermute(far_plane, 'depth', depth_far)  2.18 us
  transfers between devices with their start and end apart: 8, of which 3 were waited for; matrix products, arithmetic and copies ran while one was open for 0% of the time, Pallas kernels for 3%

profile of v11, /device:TPU:6, one launch (start us, length us, event | category | flops | bytes accessed | tf_op | source)
XLA Modules:
  0.0 56.4 jit_solution(6128755099437979026)
XLA Ops:
  0.0 1.2 %fusion = (bf16[1,4,128,128]{3,2,1,0:T(8,128)(2,1)S(1)}, bf16[4,128,128]{2,1,0:T(8,128)(2,1)S(1)}, bf16[4,128,128]{2,1,0:T(8,128)(2,1)S(1)}, bf16[1,4,128,128]{3,2,1,0:T(8,128)(2,1)S(1)}) fusion(bf16[2,4,128,128]{3,2,1,0:T(8,128)(2,1)} %vol.1, s32[]{:T(128)S(6)} %select_n.23, s32[]{:T(128)S(6)} %select_n.22), kind=kLoop, calls=%fused_computation.13 | loop fusion | bytes 1048584 | tf_op jit(solution)/shard_map/slice | solution.py:236
  1.2 2.2 %collective-permute-start = (bf16[4,128,128]{2,1,0:T(8,128)(2,1)S(1)}, bf16[4,128,128]{2,1,0:T(8,128)(2,1)S(1)}, u32[]{:S(2)}, u32[]{:S(2)}) collective-permute-start(bf16[4,128,128]{2,1,0:T(8,128)(2,1)S(1)} %get-tuple-element.13), channel_id=1, source_target_pairs={{0,0},{16,32},{32,16},{48,64},{64,48},{80,96},{96,80},{112,128},{1... | collective-permute-start | bytes 393224 | tf_op jit(solution)/shard_map/ppermute | solution.py:231
  3.4 3.3 %collective-permute-start.4 = (bf16[27,16,128]{2,1,0:T(8,128)(2,1)S(1)}, bf16[27,16,128]{2,1,0:T(8,128)(2,1)S(1)}, u32[]{:S(2)}, u32[]{:S(2)}) collective-permute-start(bf16[27,16,128]{2,1,0:T(8,128)(2,1)S(1)} %bitcast.22), channel_id=1, source_target_pairs={{0,8},{1,9},{2,10},{3,11},{4,12},{5,13},{6,14},{7,15},{8,0},{9,1},... | collective-permute-start | bytes 331784 | tf_op jit(solution)/shard_map/ppermute | solution.py:246
  6.7 0.7 %collective-permute-start.5 = (bf16[27,16,128]{2,1,0:T(8,128)(2,1)S(1)}, bf16[27,16,128]{2,1,0:T(8,128)(2,1)S(1)}, u32[]{:S(2)}, u32[]{:S(2)}) collective-permute-start(bf16[27,16,128]{2,1,0:T(8,128)(2,1)S(1)} %bitcast.23), channel_id=1, source_target_pairs={{0,4},{1,5},{2,6},{3,7},{4,0},{5,1},{6,2},{7,3},{8,12},{9,13},{10,... | collective-permute-start | bytes 331784 | tf_op jit(solution)/shard_map/ppermute | solution.py:246
  7.4 0.4 collective-permute-start.6
  7.8 6.4 %collective-permute-start.1 = (bf16[4,128,128]{2,1,0:T(8,128)(2,1)S(1)}, bf16[4,128,128]{2,1,0:T(8,128)(2,1)S(1)}, u32[]{:S(2)}, u32[]{:S(2)}) collective-permute-start(bf16[4,128,128]{2,1,0:T(8,128)(2,1)S(1)} %get-tuple-element.12), channel_id=1, source_target_pairs={{0,16},{16,0},{32,48},{48,32},{64,80},{80,64},{96,112},{112,96},{1... | collective-permute-start | bytes 393224 | tf_op jit(solution)/shard_map/ppermute | solution.py:232
  14.2 0.9 %collective-permute-done.1.x1 = bf16[4,128,128]{2,1,0:T(8,128)(2,1)S(1)} collective-permute-done((bf16[4,128,128]{2,1,0:T(8,128)(2,1)S(1)}, bf16[4,128,128]{2,1,0:T(8,128)(2,1)S(1)}, u32[]{:S(2)}, u32[]{:S(2)}) %collective-permute-start.1) | collective-permute-done | bytes 131104 | tf_op jit(solution)/shard_map/ppermute | solution.py:232
  15.2 0.8 %collective-permute-start.3 = (bf16[4,128,128]{2,1,0:T(8,128)(2,1)S(1)}, bf16[4,128,128]{2,1,0:T(8,128)(2,1)S(1)}, u32[]{:S(2)}, u32[]{:S(2)}) collective-permute-start(bf16[4,128,128]{2,1,0:T(8,128)(2,1)S(1)} %pad_maximum_fusion.1), channel_id=1, source_target_pairs={{0,0},{1,2},{2,1},{3,4},{4,3},{5,6},{6,5},{7,8},{8,7},{9,10},{10,9... | collective-permute-start | bytes 393224 | tf_op jit(solution)/shard_map/ppermute | solution.py:239
  16.0 0.0 copy-start.3
  16.0 3.4 %collective-permute-start.2 = (bf16[4,128,128]{2,1,0:T(8,128)(2,1)S(1)}, bf16[4,128,128]{2,1,0:T(8,128)(2,1)S(1)}, u32[]{:S(2)}, u32[]{:S(2)}) collective-permute-start(bf16[4,128,128]{2,1,0:T(8,128)(2,1)S(1)} %pad_maximum_fusion), channel_id=1, source_target_pairs={{0,1},{1,0},{2,3},{3,2},{4,5},{5,4},{6,7},{7,6},{8,9},{9,8},{10,11... | collective-permute-start | bytes 393224 | tf_op jit(solution)/shard_map/ppermute | solution.py:240
  19.4 1.6 %shard_map.55 = (f32[2,2,128,128]{3,2,1,0:T(8,128)S(1)}, f32[2,128,128]{2,1,0:T(8,128)S(1)}, bf16[2,384,384]{2,1,0:T(8,128)(2,1)S(1)}) custom-call(bf16[2,4,128,128]{3,2,1,0:T(8,128)(2,1)S(1)} %copy-done, bf16[4,128,128]{2,1,0:T(8,128)(2,1)S(1)} %collective-permute-done.x2, bf16[4,128,128]{2,1,0:T(8,128)(2,1)S(1)} %collective-permute-done.1.x1, ...), custom_call_target="tpu_custom_call" | custom-call | flops 20000000000 | tf_op jit(solution)/shard_map/pallas_call | solution.py:88
  21.0 0.0 collective-permute-done.4.w2
  21.0 0.0 collective-permute-done.5.w1
  21.0 0.0 collective-permute-done.3.c2
  21.0 5.1 %collective-permute-done.2.c1 = bf16[4,128,128]{2,1,0:T(8,128)(2,1)S(1)} collective-permute-done((bf16[4,128,128]{2,1,0:T(8,128)(2,1)S(1)}, bf16[4,128,128]{2,1,0:T(8,128)(2,1)S(1)}, u32[]{:S(2)}, u32[]{:S(2)}) %collective-permute-start.2) | collective-permute-done | bytes 131104 | tf_op jit(solution)/shard_map/ppermute | solution.py:240
  26.1 0.4 shard_map.56
  26.6 13.5 %all_to_all.10 = bf16[8,2,64,128]{3,2,1,0:T(8,128)(2,1)S(1)} all-to-all(bf16[8,2,64,128]{3,2,1,0:T(8,128)(2,1)S(1)} %shard_map.56), channel_id=1, replica_groups={{16,17,18,19,32,33,34,35},{20,21,22,23,36,37,38,39},{24,25,26,27,40,41,..., dimensions={0} | all-to-all | bytes 524288 | tf_op jit(solution)/shard_map/all_to_all | solution.py:250
  40.1 2.5 %collective-permute-start.7 = (bf16[4,2,64,128]{3,2,1,0:T(8,128)(2,1)S(1)}, bf16[4,2,64,128]{3,2,1,0:T(8,128)(2,1)S(1)}, u32[]{:S(2)}, u32[]{:S(2)}) collective-permute-start(bf16[4,2,64,128]{3,2,1,0:T(8,128)(2,1)S(1)} %dynamic-slice_bitcast_fusion), channel_id=1, source_target_pairs={{0,16},{16,0},{32,48},{48,32},{64,80},{80,64},{96,112},{112,96},{1... | collective-permute-start | bytes 393224 | tf_op jit(solution)/shard_map/ppermute | solution.py:253
  42.6 1.0 %collective-permute-done.7.near = bf16[4,2,64,128]{3,2,1,0:T(8,128)(2,1)S(1)} collective-permute-done((bf16[4,2,64,128]{3,2,1,0:T(8,128)(2,1)S(1)}, bf16[4,2,64,128]{3,2,1,0:T(8,128)(2,1)S(1)}, u32[]{:S(2)}, u32[]{:S(2)}) %collective-permute-start.7) | collective-permute-done | bytes 131104 | tf_op jit(solution)/shard_map/ppermute | solution.py:253
  43.6 0.8 %shard_map.57 = f32[4,16,640]{2,1,0:T(8,128)S(1)} custom-call(bf16[2,4,2,64,128]{4,3,2,1,0:T(8,128)(2,1)S(1)} %bitcast.21, bf16[4,2,64,128]{3,2,1,0:T(8,128)(2,1)S(1)} %collective-permute-done.7.near, bf16[27,16,128]{2,1,0:T(8,128)(2,1)S(1)} %bitcast.25, bf16[27,16,128]{2,1,0:T(8,128)(2,1)S(1)} %collective-permute-done.5.w1, ...), custom_call_target="tpu_custom_call" | custom-call | tf_op jit(solution)/shard_map/pallas_call | solution.py:188
  44.4 0.0 copy-start.4
  44.4 11.3 %all_to_all.11.held = f32[4,16,640]{2,1,0:T(8,128)S(1)} all-to-all(f32[4,16,640]{2,1,0:T(8,128)S(1)} %shard_map.57), channel_id=1, replica_groups={{0,4,8,12},{1,5,9,13},{2,6,10,14},{3,7,11,15},{16,20,24,28},{17,21,25,2..., dimensions={0} | all-to-all | bytes 327680 | tf_op jit(solution)/shard_map/all_to_all | solution.py:255
  55.7 0.1 broadcast_in_dim.2.bias
  55.8 0.7 %shard_map.58 = bf16[16,2048]{1,0:T(8,128)(2,1)} custom-call(f32[4,16,640]{2,1,0:T(8,128)S(1)} %all_to_all.11.held, f32[16,128]{1,0:T(8,128)S(1)} %broadcast_in_dim.2.bias), custom_call_target="tpu_custom_call" | custom-call | tf_op jit(solution)/shard_map/pallas_call | solution.py:213
  (16 shorter events, 0.1 us)
Async XLA Ops:
  0.0 3.4 %copy-start.1 = (bf16[3,3,3,128,16]{3,4,2,1,0:T(8,128)(2,1)S(1)}, bf16[3,3,3,128,16]{3,4,2,1,0:T(8,128)(2,1)}, u32[]{:S(2)}) copy-start(bf16[3,3,3,128,16]{3,4,2,1,0:T(8,128)(2,1)} %param.8) | copy-start | bytes 331780
  0.0 19.4 %copy-start.2 = (bf16[3,3,3,128,128]{4,3,2,1,0:T(8,128)(2,1)S(1)}, bf16[3,3,3,128,128]{4,3,2,1,0:T(8,128)(2,1)}, u32[]{:S(2)}) copy-start(bf16[3,3,3,128,128]{4,3,2,1,0:T(8,128)(2,1)} %w.1) | copy-start | bytes 2654212
  1.2 12.9 %collective-permute-start = (bf16[4,128,128]{2,1,0:T(8,128)(2,1)S(1)}, bf16[4,128,128]{2,1,0:T(8,128)(2,1)S(1)}, u32[]{:S(2)}, u32[]{:S(2)}) collective-permute-start(bf16[4,128,128]{2,1,0:T(8,128)(2,1)S(1)} %get-tuple-element.13), channel_id=1, source_target_pairs={{0,0},{16,32},{32,16},{48,64},{64,48},{80,96},{96,80},{112,128},{1... | collective-permute-start | bytes 393224 | tf_op jit(solution)/shard_map/ppermute | solution.py:231
  3.4 17.5 %collective-permute-start.4 = (bf16[27,16,128]{2,1,0:T(8,128)(2,1)S(1)}, bf16[27,16,128]{2,1,0:T(8,128)(2,1)S(1)}, u32[]{:S(2)}, u32[]{:S(2)}) collective-permute-start(bf16[27,16,128]{2,1,0:T(8,128)(2,1)S(1)} %bitcast.22), channel_id=1, source_target_pairs={{0,8},{1,9},{2,10},{3,11},{4,12},{5,13},{6,14},{7,15},{8,0},{9,1},... | collective-permute-start | bytes 331784 | tf_op jit(solution)/shard_map/ppermute | solution.py:246
  6.7 14.3 %collective-permute-start.5 = (bf16[27,16,128]{2,1,0:T(8,128)(2,1)S(1)}, bf16[27,16,128]{2,1,0:T(8,128)(2,1)S(1)}, u32[]{:S(2)}, u32[]{:S(2)}) collective-permute-start(bf16[27,16,128]{2,1,0:T(8,128)(2,1)S(1)} %bitcast.23), channel_id=1, source_target_pairs={{0,4},{1,5},{2,6},{3,7},{4,0},{5,1},{6,2},{7,3},{8,12},{9,13},{10,... | collective-permute-start | bytes 331784 | tf_op jit(solution)/shard_map/ppermute | solution.py:246
  7.4 13.6 %collective-permute-start.6 = (bf16[27,16,128]{2,1,0:T(8,128)(2,1)S(1)}, bf16[27,16,128]{2,1,0:T(8,128)(2,1)S(1)}, u32[]{:S(2)}, u32[]{:S(2)}) collective-permute-start(bf16[27,16,128]{2,1,0:T(8,128)(2,1)S(1)} %bitcast.24), channel_id=1, source_target_pairs={{0,12},{1,13},{2,14},{3,15},{4,8},{5,9},{6,10},{7,11},{8,4},{9,5},... | collective-permute-start | bytes 331784 | tf_op jit(solution)/shard_map/ppermute | solution.py:246
  7.8 7.4 %collective-permute-start.1 = (bf16[4,128,128]{2,1,0:T(8,128)(2,1)S(1)}, bf16[4,128,128]{2,1,0:T(8,128)(2,1)S(1)}, u32[]{:S(2)}, u32[]{:S(2)}) collective-permute-start(bf16[4,128,128]{2,1,0:T(8,128)(2,1)S(1)} %get-tuple-element.12), channel_id=1, source_target_pairs={{0,16},{16,0},{32,48},{48,32},{64,80},{80,64},{96,112},{112,96},{1... | collective-permute-start | bytes 393224 | tf_op jit(solution)/shard_map/ppermute | solution.py:232
  15.2 4.2 %copy-start = (bf16[2,4,128,128]{3,2,1,0:T(8,128)(2,1)S(1)}, bf16[2,4,128,128]{3,2,1,0:T(8,128)(2,1)}, u32[]{:S(2)}) copy-start(bf16[2,4,128,128]{3,2,1,0:T(8,128)(2,1)} %vol.1) | copy-start | bytes 786436
  15.2 5.8 %collective-permute-start.3 = (bf16[4,128,128]{2,1,0:T(8,128)(2,1)S(1)}, bf16[4,128,128]{2,1,0:T(8,128)(2,1)S(1)}, u32[]{:S(2)}, u32[]{:S(2)}) collective-permute-start(bf16[4,128,128]{2,1,0:T(8,128)(2,1)S(1)} %pad_maximum_fusion.1), channel_id=1, source_target_pairs={{0,0},{1,2},{2,1},{3,4},{4,3},{5,6},{6,5},{7,8},{8,7},{9,10},{10,9... | collective-permute-start | bytes 393224 | tf_op jit(solution)/shard_map/ppermute | solution.py:239
  16.0 3.4 %copy-start.3 = (f32[128]{0:T(128)S(1)}, f32[128]{0:T(128)}, u32[]{:S(2)}) copy-start(f32[128]{0:T(128)} %param.7) | copy-start | bytes 1540
  16.0 10.1 %collective-permute-start.2 = (bf16[4,128,128]{2,1,0:T(8,128)(2,1)S(1)}, bf16[4,128,128]{2,1,0:T(8,128)(2,1)S(1)}, u32[]{:S(2)}, u32[]{:S(2)}) collective-permute-start(bf16[4,128,128]{2,1,0:T(8,128)(2,1)S(1)} %pad_maximum_fusion), channel_id=1, source_target_pairs={{0,1},{1,0},{2,3},{3,2},{4,5},{5,4},{6,7},{7,6},{8,9},{9,8},{10,11... | collective-permute-start | bytes 393224 | tf_op jit(solution)/shard_map/ppermute | solution.py:240
  40.1 3.5 %collective-permute-start.7 = (bf16[4,2,64,128]{3,2,1,0:T(8,128)(2,1)S(1)}, bf16[4,2,64,128]{3,2,1,0:T(8,128)(2,1)S(1)}, u32[]{:S(2)}, u32[]{:S(2)}) collective-permute-start(bf16[4,2,64,128]{3,2,1,0:T(8,128)(2,1)S(1)} %dynamic-slice_bitcast_fusion), channel_id=1, source_target_pairs={{0,16},{16,0},{32,48},{48,32},{64,80},{80,64},{96,112},{112,96},{1... | collective-permute-start | bytes 393224 | tf_op jit(solution)/shard_map/ppermute | solution.py:253
  44.4 11.4 %copy-start.4 = (f32[16]{0:T(128)S(1)}, f32[16]{0:T(128)}, u32[]{:S(2)}) copy-start(f32[16]{0:T(128)} %param.9) | copy-start | bytes 196

commit v12 on v10

--- a/solution.py
+++ b/solution.py
@@ -135,61 +135,95 @@
     )(*main, c2, c1, other)
 
 
-def coarse_kernel(both, near, pair, other, out, cells):
+def coarse_sums(cells, taps, pair, other, add):
+    lhs = jnp.concatenate(
+        [
+            jnp.concatenate([w[m, 9 * a + 3 * b + c] for a in taps for b in range(3)], axis=1)
+            for c in range(3)
+            for w, m in ((pair, 0), (pair, 1), (other, 1), (other, 0))
+        ],
+        axis=0,
+    )
+    count = len(taps)
+    for start, size in ((0, 256), (256, 256), (512, 128)):
+        if start < 512:
+            first = start // 64 + 1
+            blocks = [
+                cells[i, first + b : first + b + 4].reshape(256, 128) for i in range(count) for b in range(3)
+            ]
+        else:
+            blocks = [
+                jnp.concatenate([cells[i, 9 + b], cells[i, b]], axis=0) for i in range(count) for b in range(3)
+            ]
+        rhs = jnp.concatenate(blocks, axis=1)
+        term = lax.dot_general(lhs, rhs, (((1,), (1,)), ((), ())), preferred_element_type=F32)
+        lane = lax.rem(lax.broadcasted_iota(jnp.int32, (64, size), 1), 64)
+        left = jnp.where(lane == 0, 0.0, pltpu.roll(term[:64], 1, 1))
+        right = jnp.where(lane == 63, 0.0, pltpu.roll(term[128:], size - 1, 1))
+        add(start, size, term[64:128] + left + right)
+
+
+def coarse_kernel(both, pair, other, out, cells):
     pd = lax.rem(lax.axis_index("depth"), 2)
-    y = lax.div(lax.axis_index("rows"), 4)
     inner_d = inner("depth")
-    for a in range(3):
+    for a in range(2):
         for i in (0, 1, 10, 11):
             cells[a, i] = jnp.zeros((64, 128), BF16)
     for k in range(4):
         far = both[pd, k]
         cells[0, 2 + 2 * k : 4 + 2 * k] = jnp.where(inner_d, far, jnp.zeros_like(far))
         cells[1, 2 + 2 * k : 4 + 2 * k] = both[1 - pd, k]
-        cells[2, 2 + 2 * k : 4 + 2 * k] = near[k]
-    lhs = jnp.concatenate(
-        [
-            jnp.concatenate(
-                [w[m, 9 * (a + pd * (2 - 2 * a)) + 3 * b + c] for a in range(3) for b in range(3)], axis=1
-            )
-            for c in range(3)
-            for w, m in ((pair, 0), (pair, 1), (other, 1), (other, 0))
-        ],
-        axis=0,
-    )
-    for start, size in ((0, 256), (256, 256), (512, 128)):
-        if start < 512:
-            first = start // 64 + 1
-            blocks = [
-                cells[a, first + b : first + b + 4].reshape(256, 128) for a in range(3) for b in range(3)
-            ]
-        else:
-            blocks = [
-                jnp.concatenate([cells[a, 9 + b], cells[a, b]], axis=0) for a in range(3) for b in range(3)
-            ]
-        rhs = jnp.concatenate(blocks, axis=1)
-        term = lax.dot_general(lhs, rhs, (((1,), (1,)), ((), ())), preferred_element_type=F32)
-        lane = lax.rem(lax.broadcasted_iota(jnp.int32, (64, size), 1), 64)
-        left = jnp.where(lane == 0, 0.0, pltpu.roll(term[:64], 1, 1))
-        right = jnp.where(lane == 63, 0.0, pltpu.roll(term[128:], size - 1, 1))
-        value = term[64:128] + left + right
-        for k in range(4):
-            out[y ^ k, :, start : start + size] = value[16 * k : 16 * k + 16]
-
-
-def coarse_level(both, near, pair, other):
+
+    def put(start, size, value):
+        out[:, start : start + size] = value
+
+    coarse_sums(cells, (2 * pd, 1), pair, other, put)
+
+
+def coarse_level(both, pair, other):
     vmem = pl.BlockSpec(memory_space=pltpu.VMEM)
     return pl.pallas_call(
         coarse_kernel,
-        out_shape=jax.ShapeDtypeStruct((4, 16, 640), F32),
+        out_shape=jax.ShapeDtypeStruct((64, 640), F32),
+        in_specs=[vmem] * 3,
+        out_specs=vmem,
+        scratch_shapes=[pltpu.VMEM((2, 12, 64, 128), BF16)],
+        compiler_params=pltpu.CompilerParams(vmem_limit_bytes=6 * 1024 * 1024),
+        cost_estimate=pl.CostEstimate(flops=150_000_000, bytes_accessed=0, transcendentals=0),
+    )(both, pair, other)
+
+
+def near_kernel(near, sums, pair, other, o0, o1, o2, o3, cells):
+    pd = lax.rem(lax.axis_index("depth"), 2)
+    for i in (0, 1, 10, 11):
+        cells[0, i] = jnp.zeros((64, 128), BF16)
+    for k in range(4):
+        cells[0, 2 + 2 * k : 4 + 2 * k] = near[k]
+
+    def put(start, size, value):
+        value = value + sums[:, start : start + size]
+        for k, out in enumerate((o0, o1, o2, o3)):
+            out[:, start : start + size] = value[16 * k : 16 * k + 16]
+
+    coarse_sums(cells, (2 - 2 * pd,), pair, other, put)
+
+
+def near_level(near, sums, pair, other):
+    vmem = pl.BlockSpec(memory_space=pltpu.VMEM)
+    return pl.pallas_call(
+        near_kernel,
+        out_shape=[jax.ShapeDtypeStruct((16, 640), F32)] * 4,
         in_specs=[vmem] * 4,
-        out_specs=vmem,
-        scratch_shapes=[pltpu.VMEM((3, 12, 64, 128), BF16)],
-        compiler_params=pltpu.CompilerParams(vmem_limit_bytes=8 * 1024 * 1024),
-    )(both, near, pair, other)
-
-
-def join_kernel(held, bias, out):
+        out_specs=[vmem] * 4,
+        scratch_shapes=[pltpu.VMEM((1, 12, 64, 128), BF16)],
+        compiler_params=pltpu.CompilerParams(vmem_limit_bytes=6 * 1024 * 1024),
+    )(near, sums, pair, other)
+
+
+def join_kernel(s0, s1, s2, s3, bias, out, held):
+    y = lax.div(lax.axis_index("rows"), 4)
+    for k, part in enumerate((s0, s1, s2, s3)):
+        held[y ^ k] = part[...]
     low = lax.broadcasted_iota(jnp.int32, (16, 128), 1) < 64
     for m in range(4):
         tiles = [held[m, :, 128 * i : 128 * i + 128] for i in range(4)]
@@ -207,10 +241,11 @@
     return pl.pallas_call(
         join_kernel,
         out_shape=jax.ShapeDtypeStruct((16, 2048), BF16),
-        in_specs=[vmem] * 2,
+        in_specs=[vmem] * 5,
         out_specs=vmem,
+        scratch_shapes=[pltpu.VMEM((4, 16, 640), F32)],
         compiler_params=pltpu.CompilerParams(vmem_limit_bytes=4 * 1024 * 1024),
-    )(parts, bias)
+    )(*parts, bias)
 
 
 def body(volume, fine_filters, fine_bias, coarse_filters, coarse_bias):
@@ -242,10 +277,8 @@
         pooled, ("depth", "rows"), 0, 0, axis_index_groups=far_and_z(), tiled=True
     ).reshape(2, 4, 2, 64, 128)
     near = lax.ppermute(lax.dynamic_index_in_dim(both, 1 - pd, 0, False), "depth", depth_near)
-    sums = coarse_level(both, near, pair, other)
-    parts = lax.all_to_all(
-        sums, "rows", 0, 0, axis_index_groups=[[4 * y + z for y in range(4)] for z in range(4)], tiled=True
-    )
+    sums = near_level(near, coarse_level(both, pair, other), pair, other)
+    parts = [sums[0]] + [lax.ppermute(sums[k], "rows", along_y(k)) for k in (1, 2, 3)]
     result = join(parts, jnp.broadcast_to(coarse_bias[:, None], (16, 128)))
     return result.reshape(16, 1, 2048)
 

time: 55 us -> 53.3 us (0.969)
  blocking collectives: 24.4 us -> 14 us
  starting transfers between devices: 24 us -> 29.1 us
  waiting for transfers between devices: 1.7 us -> 5.11 us
    all_to_all x1 -> x0, blocking collectives: 10.4 us -> none  [body(): lax.all_to_all(sums, 'rows', 0, 0, axis_index_groups=[[4 * y + z for y in...]
    ppermute x0 -> x3, starting transfers between devices: none -> 5.09 us  [body(): lax.ppermute(sums[k], 'rows', along_y(k))]
    ppermute x0 -> x3, waiting for transfers between devices: none -> 4 us  [body(): lax.ppermute(sums[k], 'rows', along_y(k))]
    ppermute x1, waiting for transfers between devices: 0.99 us -> 0.4 us  [body(): lax.ppermute(lax.dynamic_index_in_dim(both, 1 - pd, 0, False), 'depth', d...]
  transfers between devices with their start and end apart: 9 -> 12, of which waited for: 2 -> 5; matrix products, arithmetic and copies ran while one was open for 0% -> 0% of each run, Pallas kernels for 3% -> 4%
where the time goes in v12:
time: 53.3 us; the launch traced here: 53 us
  starting transfers between devices  29.1 us (55%)
  blocking collectives  14 us (26%)
  waiting for transfers between devices  5.11 us (10%)
  Pallas kernels  3.48 us (7%)
  local copies, waits for them, and re-layouts  1.2 us (2%)
    all_to_all x1, blocking collectives, body(): lax.all_to_all(pooled, ('depth', 'rows'), 0, 0, axis_index_groups=far_and...  14 us
    ppermute x1, starting transfers between devices, body(): lax.ppermute(lax.dynamic_index_in_dim(volume, 1 - pd, 0, False), 'depth',...  7.04 us
    ppermute x3, starting transfers between devices, body(): lax.ppermute(sums[k], 'rows', along_y(k))  5.09 us
    ppermute x3, waiting for transfers between devices, body(): lax.ppermute(sums[k], 'rows', along_y(k))  4 us
    ppermute x1, starting transfers between devices, body(): lax.ppermute(lax.dynamic_index_in_dim(volume, 3 - 3 * pr, 1, False), 'row...  3.37 us
    ppermute x1, starting transfers between devices, body(): lax.ppermute(lax.dynamic_index_in_dim(sides, 3 - 3 * pr, 1, False), 'rows...  3.34 us
    ppermute x1, starting transfers between devices, body(): other = lax.ppermute(pair, 'rows', along_y(3))  2.9 us
    ppermute x1, starting transfers between devices, body(): lax.ppermute(lax.dynamic_index_in_dim(both, 1 - pd, 0, False), 'depth', d...  2.29 us
  transfers between devices with their start and end apart: 12, of which 5 were waited for; matrix products, arithmetic and copies ran while one was open for 0% of the time, Pallas kernels for 4%

profile of v12, /device:TPU:6, one launch (start us, length us, event | category | flops | bytes accessed | tf_op | source)
XLA Modules:
  0.0 53.0 jit_solution(8999371709243367129)
XLA Ops:
  0.0 1.1 %dynamic-slice_bitcast_fusion.1 = (bf16[4,128,128]{2,1,0:T(8,128)(2,1)S(1)}, bf16[4,128,128]{2,1,0:T(8,128)(2,1)S(1)}) fusion(bf16[2,4,128,128]{3,2,1,0:T(8,128)(2,1)} %vol.1, s32[]{:T(128)S(6)} %select_n.19, s32[]{:T(128)S(6)} %select_n.18), kind=kLoop, calls=%fused_computation.6 | loop fusion | bytes 524296 | tf_op jit(solution)/shard_map/jit(dynamic_index_in_dim)/squeeze | solution.py:260
  1.1 2.2 %collective-permute-start = (bf16[4,128,128]{2,1,0:T(8,128)(2,1)S(1)}, bf16[4,128,128]{2,1,0:T(8,128)(2,1)S(1)}, u32[]{:S(2)}, u32[]{:S(2)}) collective-permute-start(bf16[4,128,128]{2,1,0:T(8,128)(2,1)S(1)} %get-tuple-element.24), channel_id=1, source_target_pairs={{0,0},{16,32},{32,16},{48,64},{64,48},{80,96},{96,80},{112,128},{1... | collective-permute-start | bytes 393224 | tf_op jit(solution)/shard_map/ppermute | solution.py:259
  3.3 7.0 %collective-permute-start.1 = (bf16[4,128,128]{2,1,0:T(8,128)(2,1)S(1)}, bf16[4,128,128]{2,1,0:T(8,128)(2,1)S(1)}, u32[]{:S(2)}, u32[]{:S(2)}) collective-permute-start(bf16[4,128,128]{2,1,0:T(8,128)(2,1)S(1)} %get-tuple-element.23), channel_id=1, source_target_pairs={{0,16},{16,0},{32,48},{48,32},{64,80},{80,64},{96,112},{112,96},{1... | collective-permute-start | bytes 393224 | tf_op jit(solution)/shard_map/ppermute | solution.py:260
  10.3 1.6 %collective-permute-start.6 = (bf16[27,16,128]{2,1,0:T(8,128)(2,1)S(1)}, bf16[27,16,128]{2,1,0:T(8,128)(2,1)S(1)}, u32[]{:S(2)}, u32[]{:S(2)}) collective-permute-start(bf16[27,16,128]{2,1,0:T(8,128)(2,1)S(1)} %bitcast.30), channel_id=1, source_target_pairs={{0,4},{1,5},{2,6},{3,7},{4,0},{5,1},{6,2},{7,3},{8,12},{9,13},{10,... | collective-permute-start | bytes 331784 | tf_op jit(solution)/shard_map/ppermute | solution.py:271
  11.9 0.7 %collective-permute-start.2 = (bf16[2,128,128]{2,1,0:T(8,128)(2,1)S(1)}, bf16[2,128,128]{2,1,0:T(8,128)(2,1)S(1)}, u32[]{:S(2)}, u32[]{:S(2)}) collective-permute-start(bf16[2,128,128]{2,1,0:T(8,128)(2,1)S(1)} %get-tuple-element.22), channel_id=1, source_target_pairs={{0,0},{1,2},{2,1},{3,4},{4,3},{5,6},{6,5},{7,8},{8,7},{9,10},{10,9... | collective-permute-start | bytes 196616 | tf_op jit(solution)/shard_map/ppermute | solution.py:261
  12.6 3.4 %collective-permute-start.3 = (bf16[2,128,128]{2,1,0:T(8,128)(2,1)S(1)}, bf16[2,128,128]{2,1,0:T(8,128)(2,1)S(1)}, u32[]{:S(2)}, u32[]{:S(2)}) collective-permute-start(bf16[2,128,128]{2,1,0:T(8,128)(2,1)S(1)} %get-tuple-element.21), channel_id=1, source_target_pairs={{0,1},{1,0},{2,3},{3,2},{4,5},{5,4},{6,7},{7,6},{8,9},{9,8},{10,11... | collective-permute-start | bytes 196616 | tf_op jit(solution)/shard_map/ppermute | solution.py:262
  16.0 2.9 %collective-permute-start.7 = (bf16[2,27,16,128]{3,2,1,0:T(8,128)(2,1)S(1)}, bf16[2,27,16,128]{3,2,1,0:T(8,128)(2,1)S(1)}, u32[]{:S(2)}, u32[]{:S(2)}) collective-permute-start(bf16[2,27,16,128]{3,2,1,0:T(8,128)(2,1)S(1)} %pad_maximum_fusion.pair), channel_id=1, source_target_pairs={{0,12},{1,13},{2,14},{3,15},{4,8},{5,9},{6,10},{7,11},{8,4},{9,5},... | collective-permute-start | bytes 663560 | tf_op jit(solution)/shard_map/ppermute | solution.py:272
  18.9 0.7 %collective-permute-start.4 = (bf16[2,128,128]{2,1,0:T(8,128)(2,1)S(1)}, bf16[2,128,128]{2,1,0:T(8,128)(2,1)S(1)}, u32[]{:S(2)}, u32[]{:S(2)}) collective-permute-start(bf16[2,128,128]{2,1,0:T(8,128)(2,1)S(1)} %get-tuple-element.20), channel_id=1, source_target_pairs={{0,0},{1,2},{2,1},{3,4},{4,3},{5,6},{6,5},{7,8},{8,7},{9,10},{10,9... | collective-permute-start | bytes 196616 | tf_op jit(solution)/shard_map/ppermute | solution.py:264
  19.6 3.3 %collective-permute-start.5 = (bf16[2,128,128]{2,1,0:T(8,128)(2,1)S(1)}, bf16[2,128,128]{2,1,0:T(8,128)(2,1)S(1)}, u32[]{:S(2)}, u32[]{:S(2)}) collective-permute-start(bf16[2,128,128]{2,1,0:T(8,128)(2,1)S(1)} %get-tuple-element.19), channel_id=1, source_target_pairs={{0,1},{1,0},{2,3},{3,2},{4,5},{5,4},{6,7},{7,6},{8,9},{9,8},{10,11... | collective-permute-start | bytes 196616 | tf_op jit(solution)/shard_map/ppermute | solution.py:265
  23.0 1.5 %shard_map.55 = (f32[2,2,128,128]{3,2,1,0:T(8,128)S(1)}, f32[2,128,128]{2,1,0:T(8,128)S(1)}, bf16[2,2,128,384]{3,2,1,0:T(8,128)(2,1)S(1)}) custom-call(bf16[2,4,128,128]{3,2,1,0:T(8,128)(2,1)S(1)} %copy-done, bf16[4,128,128]{2,1,0:T(8,128)(2,1)S(1)} %collective-permute-done.x2, bf16[4,128,128]{2,1,0:T(8,128)(2,1)S(1)} %collective-permute-done.1.x1, ...), custom_call_target="tpu_custom_call" | custom-call | flops 20000000000 | tf_op jit(solution)/shard_map/pallas_call | solution.py:88
  24.5 0.7 %collective-permute-done.5.c1 = bf16[2,128,128]{2,1,0:T(8,128)(2,1)S(1)} collective-permute-done((bf16[2,128,128]{2,1,0:T(8,128)(2,1)S(1)}, bf16[2,128,128]{2,1,0:T(8,128)(2,1)S(1)}, u32[]{:S(2)}, u32[]{:S(2)}) %collective-permute-start.5) | collective-permute-done | bytes 65568 | tf_op jit(solution)/shard_map/ppermute | solution.py:265
  25.2 0.3 shard_map.56
  25.5 14.0 %all_to_all.5 = bf16[8,2,64,128]{3,2,1,0:T(8,128)(2,1)S(1)} all-to-all(bf16[8,2,64,128]{3,2,1,0:T(8,128)(2,1)S(1)} %shard_map.56), channel_id=1, replica_groups={{16,17,18,19,32,33,34,35},{20,21,22,23,36,37,38,39},{24,25,26,27,40,41,..., dimensions={0} | all-to-all | bytes 524288 | tf_op jit(solution)/shard_map/all_to_all | solution.py:276
  39.5 2.3 %collective-permute-start.8 = (bf16[4,2,64,128]{3,2,1,0:T(8,128)(2,1)S(1)}, bf16[4,2,64,128]{3,2,1,0:T(8,128)(2,1)S(1)}, u32[]{:S(2)}, u32[]{:S(2)}) collective-permute-start(bf16[4,2,64,128]{3,2,1,0:T(8,128)(2,1)S(1)} %dynamic-slice_bitcast_fusion), channel_id=1, source_target_pairs={{0,16},{16,0},{32,48},{48,32},{64,80},{80,64},{96,112},{112,96},{1... | collective-permute-start | bytes 393224 | tf_op jit(solution)/shard_map/ppermute | solution.py:279
  41.8 0.6 %shard_map.57.sums = f32[64,640]{1,0:T(8,128)S(1)} custom-call(bf16[2,4,2,64,128]{4,3,2,1,0:T(8,128)(2,1)S(1)} %bitcast.26, bf16[2,27,16,128]{3,2,1,0:T(8,128)(2,1)S(1)} %pad_maximum_fusion.pair, bf16[2,27,16,128]{3,2,1,0:T(8,128)(2,1)S(1)} %collective-permute-done.7.other), custom_call_target="tpu_custom_call" | custom-call | flops 150000000 | tf_op jit(solution)/shard_map/pallas_call | solution.py:185
  42.4 0.4 collective-permute-done.8.near
  42.8 0.4 shard_map.58
  43.2 3.2 %collective-permute-start.10 = (f32[16,640]{1,0:T(8,128)S(1)}, f32[16,640]{1,0:T(8,128)S(1)}, u32[]{:S(2)}, u32[]{:S(2)}) collective-permute-start(f32[16,640]{1,0:T(8,128)S(1)} %get-tuple-element.17), channel_id=1, source_target_pairs={{0,8},{1,9},{2,10},{3,11},{4,12},{5,13},{6,14},{7,15},{8,0},{9,1},... | collective-permute-start | bytes 122888 | tf_op jit(solution)/shard_map/ppermute | solution.py:281
  46.4 1.8 %collective-permute-start.11 = (f32[16,640]{1,0:T(8,128)S(1)}, f32[16,640]{1,0:T(8,128)S(1)}, u32[]{:S(2)}, u32[]{:S(2)}) collective-permute-start(f32[16,640]{1,0:T(8,128)S(1)} %get-tuple-element.18), channel_id=1, source_target_pairs={{0,12},{1,13},{2,14},{3,15},{4,8},{5,9},{6,10},{7,11},{8,4},{9,5},... | collective-permute-start | bytes 122888 | tf_op jit(solution)/shard_map/ppermute | solution.py:281
  48.3 0.5 collective-permute-done.10.s2
  48.8 2.8 %collective-permute-done.11.s3 = f32[16,640]{1,0:T(8,128)S(1)} collective-permute-done((f32[16,640]{1,0:T(8,128)S(1)}, f32[16,640]{1,0:T(8,128)S(1)}, u32[]{:S(2)}, u32[]{:S(2)}) %collective-permute-start.11) | collective-permute-done | bytes 40992 | tf_op jit(solution)/shard_map/ppermute | solution.py:281
  51.6 0.6 %collective-permute-done.9.s1 = f32[16,640]{1,0:T(8,128)S(1)} collective-permute-done((f32[16,640]{1,0:T(8,128)S(1)}, f32[16,640]{1,0:T(8,128)S(1)}, u32[]{:S(2)}, u32[]{:S(2)}) %collective-permute-start.9) | collective-permute-done | bytes 40992 | tf_op jit(solution)/shard_map/ppermute | solution.py:281
  52.3 0.1 broadcast_in_dim.2.bias
  52.4 0.7 %shard_map.59 = bf16[16,2048]{1,0:T(8,128)(2,1)} custom-call(f32[16,640]{1,0:T(8,128)S(1)} %get-tuple-element.15.s0, f32[16,640]{1,0:T(8,128)S(1)} %collective-permute-done.9.s1, f32[16,640]{1,0:T(8,128)S(1)} %collective-permute-done.10.s2, f32[16,640]{1,0:T(8,128)S(1)} %collective-permute-done.11.s3, f32[16,128]{1,0:T(8,128)S(1)} %broadcast_in_dim.2.bias), custom_call_target="tpu_custom_call" | custom-call | tf_op jit(solution)/shard_map/pallas_call | solution.py:241
  (22 shorter events, 0.1 us)
Async XLA Ops:
  0.0 10.3 %copy-start.3 = (bf16[3,3,3,128,16]{3,4,2,1,0:T(8,128)(2,1)S(1)}, bf16[3,3,3,128,16]{3,4,2,1,0:T(8,128)(2,1)}, u32[]{:S(2)}) copy-start(bf16[3,3,3,128,16]{3,4,2,1,0:T(8,128)(2,1)} %param.8) | copy-start | bytes 331780
  0.0 11.9 %copy-start = (bf16[2,4,128,128]{3,2,1,0:T(8,128)(2,1)S(1)}, bf16[2,4,128,128]{3,2,1,0:T(8,128)(2,1)}, u32[]{:S(2)}) copy-start(bf16[2,4,128,128]{3,2,1,0:T(8,128)(2,1)} %vol.1) | copy-start | bytes 786436
  0.0 23.0 %copy-start.1 = (bf16[3,3,3,128,128]{4,3,2,1,0:T(8,128)(2,1)S(1)}, bf16[3,3,3,128,128]{4,3,2,1,0:T(8,128)(2,1)}, u32[]{:S(2)}) copy-start(bf16[3,3,3,128,128]{4,3,2,1,0:T(8,128)(2,1)} %w.1) | copy-start | bytes 2654212
  1.1 17.8 %collective-permute-start = (bf16[4,128,128]{2,1,0:T(8,128)(2,1)S(1)}, bf16[4,128,128]{2,1,0:T(8,128)(2,1)S(1)}, u32[]{:S(2)}, u32[]{:S(2)}) collective-permute-start(bf16[4,128,128]{2,1,0:T(8,128)(2,1)S(1)} %get-tuple-element.24), channel_id=1, source_target_pairs={{0,0},{16,32},{32,16},{48,64},{64,48},{80,96},{96,80},{112,128},{1... | collective-permute-start | bytes 393224 | tf_op jit(solution)/shard_map/ppermute | solution.py:259
  3.3 15.6 %collective-permute-start.1 = (bf16[4,128,128]{2,1,0:T(8,128)(2,1)S(1)}, bf16[4,128,128]{2,1,0:T(8,128)(2,1)S(1)}, u32[]{:S(2)}, u32[]{:S(2)}) collective-permute-start(bf16[4,128,128]{2,1,0:T(8,128)(2,1)S(1)} %get-tuple-element.23), channel_id=1, source_target_pairs={{0,16},{16,0},{32,48},{48,32},{64,80},{80,64},{96,112},{112,96},{1... | collective-permute-start | bytes 393224 | tf_op jit(solution)/shard_map/ppermute | solution.py:260
  10.3 5.6 %collective-permute-start.6 = (bf16[27,16,128]{2,1,0:T(8,128)(2,1)S(1)}, bf16[27,16,128]{2,1,0:T(8,128)(2,1)S(1)}, u32[]{:S(2)}, u32[]{:S(2)}) collective-permute-start(bf16[27,16,128]{2,1,0:T(8,128)(2,1)S(1)} %bitcast.30), channel_id=1, source_target_pairs={{0,4},{1,5},{2,6},{3,7},{4,0},{5,1},{6,2},{7,3},{8,12},{9,13},{10,... | collective-permute-start | bytes 331784 | tf_op jit(solution)/shard_map/ppermute | solution.py:271
  11.9 11.0 %collective-permute-start.2 = (bf16[2,128,128]{2,1,0:T(8,128)(2,1)S(1)}, bf16[2,128,128]{2,1,0:T(8,128)(2,1)S(1)}, u32[]{:S(2)}, u32[]{:S(2)}) collective-permute-start(bf16[2,128,128]{2,1,0:T(8,128)(2,1)S(1)} %get-tuple-element.22), channel_id=1, source_target_pairs={{0,0},{1,2},{2,1},{3,4},{4,3},{5,6},{6,5},{7,8},{8,7},{9,10},{10,9... | collective-permute-start | bytes 196616 | tf_op jit(solution)/shard_map/ppermute | solution.py:261
  12.6 10.4 %collective-permute-start.3 = (bf16[2,128,128]{2,1,0:T(8,128)(2,1)S(1)}, bf16[2,128,128]{2,1,0:T(8,128)(2,1)S(1)}, u32[]{:S(2)}, u32[]{:S(2)}) collective-permute-start(bf16[2,128,128]{2,1,0:T(8,128)(2,1)S(1)} %get-tuple-element.21), channel_id=1, source_target_pairs={{0,1},{1,0},{2,3},{3,2},{4,5},{5,4},{6,7},{7,6},{8,9},{9,8},{10,11... | collective-permute-start | bytes 196616 | tf_op jit(solution)/shard_map/ppermute | solution.py:262
  16.0 9.2 %collective-permute-start.7 = (bf16[2,27,16,128]{3,2,1,0:T(8,128)(2,1)S(1)}, bf16[2,27,16,128]{3,2,1,0:T(8,128)(2,1)S(1)}, u32[]{:S(2)}, u32[]{:S(2)}) collective-permute-start(bf16[2,27,16,128]{3,2,1,0:T(8,128)(2,1)S(1)} %pad_maximum_fusion.pair), channel_id=1, source_target_pairs={{0,12},{1,13},{2,14},{3,15},{4,8},{5,9},{6,10},{7,11},{8,4},{9,5},... | collective-permute-start | bytes 663560 | tf_op jit(solution)/shard_map/ppermute | solution.py:272
  18.9 5.6 %collective-permute-start.4 = (bf16[2,128,128]{2,1,0:T(8,128)(2,1)S(1)}, bf16[2,128,128]{2,1,0:T(8,128)(2,1)S(1)}, u32[]{:S(2)}, u32[]{:S(2)}) collective-permute-start(bf16[2,128,128]{2,1,0:T(8,128)(2,1)S(1)} %get-tuple-element.20), channel_id=1, source_target_pairs={{0,0},{1,2},{2,1},{3,4},{4,3},{5,6},{6,5},{7,8},{8,7},{9,10},{10,9... | collective-permute-start | bytes 196616 | tf_op jit(solution)/shard_map/ppermute | solution.py:264
  19.6 3.4 %copy-start.2 = (f32[128]{0:T(128)S(1)}, f32[128]{0:T(128)}, u32[]{:S(2)}) copy-start(f32[128]{0:T(128)} %param.7) | copy-start | bytes 1540
  19.6 5.6 %collective-permute-start.5 = (bf16[2,128,128]{2,1,0:T(8,128)(2,1)S(1)}, bf16[2,128,128]{2,1,0:T(8,128)(2,1)S(1)}, u32[]{:S(2)}, u32[]{:S(2)}) collective-permute-start(bf16[2,128,128]{2,1,0:T(8,128)(2,1)S(1)} %get-tuple-element.19), channel_id=1, source_target_pairs={{0,1},{1,0},{2,3},{3,2},{4,5},{5,4},{6,7},{7,6},{8,9},{9,8},{10,11... | collective-permute-start | bytes 196616 | tf_op jit(solution)/shard_map/ppermute | solution.py:265
  39.5 3.3 %collective-permute-start.8 = (bf16[4,2,64,128]{3,2,1,0:T(8,128)(2,1)S(1)}, bf16[4,2,64,128]{3,2,1,0:T(8,128)(2,1)S(1)}, u32[]{:S(2)}, u32[]{:S(2)}) collective-permute-start(bf16[4,2,64,128]{3,2,1,0:T(8,128)(2,1)S(1)} %dynamic-slice_bitcast_fusion), channel_id=1, source_target_pairs={{0,16},{16,0},{32,48},{48,32},{64,80},{80,64},{96,112},{112,96},{1... | collective-permute-start | bytes 393224 | tf_op jit(solution)/shard_map/ppermute | solution.py:279
  43.2 5.6 %collective-permute-start.10 = (f32[16,640]{1,0:T(8,128)S(1)}, f32[16,640]{1,0:T(8,128)S(1)}, u32[]{:S(2)}, u32[]{:S(2)}) collective-permute-start(f32[16,640]{1,0:T(8,128)S(1)} %get-tuple-element.17), channel_id=1, source_target_pairs={{0,8},{1,9},{2,10},{3,11},{4,12},{5,13},{6,14},{7,15},{8,0},{9,1},... | collective-permute-start | bytes 122888 | tf_op jit(solution)/shard_map/ppermute | solution.py:281
  46.4 5.2 %collective-permute-start.11 = (f32[16,640]{1,0:T(8,128)S(1)}, f32[16,640]{1,0:T(8,128)S(1)}, u32[]{:S(2)}, u32[]{:S(2)}) collective-permute-start(f32[16,640]{1,0:T(8,128)S(1)} %get-tuple-element.18), channel_id=1, source_target_pairs={{0,12},{1,13},{2,14},{3,15},{4,8},{5,9},{6,10},{7,11},{8,4},{9,5},... | collective-permute-start | bytes 122888 | tf_op jit(solution)/shard_map/ppermute | solution.py:281
  48.3 4.0 %copy-start.4 = (f32[16]{0:T(128)S(1)}, f32[16]{0:T(128)}, u32[]{:S(2)}) copy-start(f32[16]{0:T(128)} %param.9) | copy-start | bytes 196
  48.3 4.0 %collective-permute-start.9 = (f32[16,640]{1,0:T(8,128)S(1)}, f32[16,640]{1,0:T(8,128)S(1)}, u32[]{:S(2)}, u32[]{:S(2)}) collective-permute-start(f32[16,640]{1,0:T(8,128)S(1)} %get-tuple-element.16), channel_id=1, source_target_pairs={{0,4},{1,5},{2,6},{3,7},{4,0},{5,1},{6,2},{7,3},{8,12},{9,13},{10,... | collective-permute-start | bytes 122888 | tf_op jit(solution)/shard_map/ppermute | solution.py:281

commit v13 on v12

--- a/solution.py
+++ b/solution.py
@@ -18,8 +18,16 @@
 
 
 def far_and_z():
-    pairs = [(d, d + 1) for d in range(1, 15, 2)] + [(15, 0)]
-    return [[d * 16 + 4 * y + z for d in pair for z in range(4)] for pair in pairs for y in range(4)]
+    groups = [
+        [d * 16 + 4 * y + z for d in (k, k + 1) for z in range(4)] for k in range(1, 15, 2) for y in range(4)
+    ]
+    groups += [[d * 16 + 4 * y + z for y in (k, k + 1) for z in range(4)] for d in (0, 15) for k in (0, 2)]
+    return groups
+
+
+def own_half():
+    y = lax.div(lax.axis_index("rows"), 4)
+    return jnp.where(inner("depth"), 1 - lax.rem(lax.axis_index("depth"), 2), lax.rem(y, 2))
 
 
 def inner(axis):
@@ -169,10 +177,11 @@
     for a in range(2):
         for i in (0, 1, 10, 11):
             cells[a, i] = jnp.zeros((64, 128), BF16)
+    own = own_half()
     for k in range(4):
-        far = both[pd, k]
+        far = both[1 - own, k]
         cells[0, 2 + 2 * k : 4 + 2 * k] = jnp.where(inner_d, far, jnp.zeros_like(far))
-        cells[1, 2 + 2 * k : 4 + 2 * k] = both[1 - pd, k]
+        cells[1, 2 + 2 * k : 4 + 2 * k] = both[own, k]
 
     def put(start, size, value):
         out[:, start : start + size] = value
@@ -276,7 +285,7 @@
     both = lax.all_to_all(
         pooled, ("depth", "rows"), 0, 0, axis_index_groups=far_and_z(), tiled=True
     ).reshape(2, 4, 2, 64, 128)
-    near = lax.ppermute(lax.dynamic_index_in_dim(both, 1 - pd, 0, False), "depth", depth_near)
+    near = lax.ppermute(lax.dynamic_index_in_dim(both, own_half(), 0, False), "depth", depth_near)
     sums = near_level(near, coarse_level(both, pair, other), pair, other)
     parts = [sums[0]] + [lax.ppermute(sums[k], "rows", along_y(k)) for k in (1, 2, 3)]
     result = join(parts, jnp.broadcast_to(coarse_bias[:, None], (16, 128)))

time: 53.3 us -> 54.2 us (1.017)
  blocking collectives: 14 us -> 0 us
  waiting for transfers between devices: 5.11 us -> 12.7 us
  starting transfers between devices: 29.1 us -> 35.7 us
  Pallas kernels: 3.48 us -> 4.18 us
    all_to_all x1 -> x0, blocking collectives: 14 us -> none  [body(): lax.all_to_all(pooled, ('depth', 'rows'), 0, 0, axis_index_groups=far_and...]
    all_to_all x0 -> x1, waiting for transfers between devices: none -> 7.59 us  [body(): lax.all_to_all(pooled, ('depth', 'rows'), 0, 0, axis_index_groups=far_and...]
    all_to_all x0 -> x1, starting transfers between devices: none -> 6.6 us  [body(): lax.all_to_all(pooled, ('depth', 'rows'), 0, 0, axis_index_groups=far_and...]
    pallas_call x1, Pallas kernels: 0.28 us -> 0.98 us  [finish(): pl.pallas_call(finish_kernel, out_shape=jax.ShapeDtypeStruct((8, 2, 64, 1...]
  transfers between devices with their start and end apart: 12 -> 13, of which waited for: 5 -> 6; matrix products, arithmetic and copies ran while one was open for 0% -> 0% of each run, Pallas kernels for 4% -> 4%
where the time goes in v13:
time: 54.2 us; the launch traced here: 53.9 us
  starting transfers between devices  35.7 us (66%)
  waiting for transfers between devices  12.7 us (23%)
  Pallas kernels  4.18 us (8%)
  local copies, waits for them, and re-layouts  1.2 us (2%)
    all_to_all x1, waiting for transfers between devices, body(): lax.all_to_all(pooled, ('depth', 'rows'), 0, 0, axis_index_groups=far_and...  7.59 us
    ppermute x1, starting transfers between devices, body(): lax.ppermute(lax.dynamic_index_in_dim(volume, 1 - pd, 0, False), 'depth',...  7.04 us
    all_to_all x1, starting transfers between devices, body(): lax.all_to_all(pooled, ('depth', 'rows'), 0, 0, axis_index_groups=far_and...  6.6 us
    ppermute x3, starting transfers between devices, body(): lax.ppermute(sums[k], 'rows', along_y(k))  5.12 us
    ppermute x3, waiting for transfers between devices, body(): lax.ppermute(sums[k], 'rows', along_y(k))  4 us
    ppermute x1, starting transfers between devices, body(): lax.ppermute(lax.dynamic_index_in_dim(volume, 3 - 3 * pr, 1, False), 'row...  3.37 us
    ppermute x1, starting transfers between devices, body(): lax.ppermute(lax.dynamic_index_in_dim(sides, 3 - 3 * pr, 1, False), 'rows...  3.34 us
    ppermute x1, starting transfers between devices, body(): other = lax.ppermute(pair, 'rows', along_y(3))  2.9 us
  transfers between devices with their start and end apart: 13, of which 6 were waited for; matrix products, arithmetic and copies ran while one was open for 0% of the time, Pallas kernels for 4%

profile of v13, /device:TPU:6, one launch (start us, length us, event | category | flops | bytes accessed | tf_op | source)
XLA Modules:
  0.0 53.9 jit_solution(8498266766189722854)
XLA Ops:
  0.0 1.1 %dynamic-slice_bitcast_fusion.1 = (bf16[4,128,128]{2,1,0:T(8,128)(2,1)S(1)}, bf16[4,128,128]{2,1,0:T(8,128)(2,1)S(1)}) fusion(bf16[2,4,128,128]{3,2,1,0:T(8,128)(2,1)} %vol.1, s32[]{:T(128)S(6)} %select_n.25, s32[]{:T(128)S(6)} %select_n.24), kind=kLoop, calls=%fused_computation.6 | loop fusion | bytes 524296 | tf_op jit(solution)/shard_map/jit(dynamic_index_in_dim)/squeeze | solution.py:269
  1.1 2.2 %collective-permute-start = (bf16[4,128,128]{2,1,0:T(8,128)(2,1)S(1)}, bf16[4,128,128]{2,1,0:T(8,128)(2,1)S(1)}, u32[]{:S(2)}, u32[]{:S(2)}) collective-permute-start(bf16[4,128,128]{2,1,0:T(8,128)(2,1)S(1)} %get-tuple-element.24), channel_id=1, source_target_pairs={{0,0},{16,32},{32,16},{48,64},{64,48},{80,96},{96,80},{112,128},{1... | collective-permute-start | bytes 393224 | tf_op jit(solution)/shard_map/ppermute | solution.py:268
  3.3 7.0 %collective-permute-start.1 = (bf16[4,128,128]{2,1,0:T(8,128)(2,1)S(1)}, bf16[4,128,128]{2,1,0:T(8,128)(2,1)S(1)}, u32[]{:S(2)}, u32[]{:S(2)}) collective-permute-start(bf16[4,128,128]{2,1,0:T(8,128)(2,1)S(1)} %get-tuple-element.23), channel_id=1, source_target_pairs={{0,16},{16,0},{32,48},{48,32},{64,80},{80,64},{96,112},{112,96},{1... | collective-permute-start | bytes 393224 | tf_op jit(solution)/shard_map/ppermute | solution.py:269
  10.3 1.6 %collective-permute-start.6 = (bf16[27,16,128]{2,1,0:T(8,128)(2,1)S(1)}, bf16[27,16,128]{2,1,0:T(8,128)(2,1)S(1)}, u32[]{:S(2)}, u32[]{:S(2)}) collective-permute-start(bf16[27,16,128]{2,1,0:T(8,128)(2,1)S(1)} %bitcast.30), channel_id=1, source_target_pairs={{0,4},{1,5},{2,6},{3,7},{4,0},{5,1},{6,2},{7,3},{8,12},{9,13},{10,... | collective-permute-start | bytes 331784 | tf_op jit(solution)/shard_map/ppermute | solution.py:280
  11.9 0.7 %collective-permute-start.2 = (bf16[2,128,128]{2,1,0:T(8,128)(2,1)S(1)}, bf16[2,128,128]{2,1,0:T(8,128)(2,1)S(1)}, u32[]{:S(2)}, u32[]{:S(2)}) collective-permute-start(bf16[2,128,128]{2,1,0:T(8,128)(2,1)S(1)} %get-tuple-element.22), channel_id=1, source_target_pairs={{0,0},{1,2},{2,1},{3,4},{4,3},{5,6},{6,5},{7,8},{8,7},{9,10},{10,9... | collective-permute-start | bytes 196616 | tf_op jit(solution)/shard_map/ppermute | solution.py:270
  12.6 3.4 %collective-permute-start.3 = (bf16[2,128,128]{2,1,0:T(8,128)(2,1)S(1)}, bf16[2,128,128]{2,1,0:T(8,128)(2,1)S(1)}, u32[]{:S(2)}, u32[]{:S(2)}) collective-permute-start(bf16[2,128,128]{2,1,0:T(8,128)(2,1)S(1)} %get-tuple-element.21), channel_id=1, source_target_pairs={{0,1},{1,0},{2,3},{3,2},{4,5},{5,4},{6,7},{7,6},{8,9},{9,8},{10,11... | collective-permute-start | bytes 196616 | tf_op jit(solution)/shard_map/ppermute | solution.py:271
  16.0 2.9 %collective-permute-start.7 = (bf16[2,27,16,128]{3,2,1,0:T(8,128)(2,1)S(1)}, bf16[2,27,16,128]{3,2,1,0:T(8,128)(2,1)S(1)}, u32[]{:S(2)}, u32[]{:S(2)}) collective-permute-start(bf16[2,27,16,128]{3,2,1,0:T(8,128)(2,1)S(1)} %pad_maximum_fusion.pair), channel_id=1, source_target_pairs={{0,12},{1,13},{2,14},{3,15},{4,8},{5,9},{6,10},{7,11},{8,4},{9,5},... | collective-permute-start | bytes 663560 | tf_op jit(solution)/shard_map/ppermute | solution.py:281
  18.9 0.7 %collective-permute-start.4 = (bf16[2,128,128]{2,1,0:T(8,128)(2,1)S(1)}, bf16[2,128,128]{2,1,0:T(8,128)(2,1)S(1)}, u32[]{:S(2)}, u32[]{:S(2)}) collective-permute-start(bf16[2,128,128]{2,1,0:T(8,128)(2,1)S(1)} %get-tuple-element.20), channel_id=1, source_target_pairs={{0,0},{1,2},{2,1},{3,4},{4,3},{5,6},{6,5},{7,8},{8,7},{9,10},{10,9... | collective-permute-start | bytes 196616 | tf_op jit(solution)/shard_map/ppermute | solution.py:273
  19.6 3.3 %collective-permute-start.5 = (bf16[2,128,128]{2,1,0:T(8,128)(2,1)S(1)}, bf16[2,128,128]{2,1,0:T(8,128)(2,1)S(1)}, u32[]{:S(2)}, u32[]{:S(2)}) collective-permute-start(bf16[2,128,128]{2,1,0:T(8,128)(2,1)S(1)} %get-tuple-element.19), channel_id=1, source_target_pairs={{0,1},{1,0},{2,3},{3,2},{4,5},{5,4},{6,7},{7,6},{8,9},{9,8},{10,11... | collective-permute-start | bytes 196616 | tf_op jit(solution)/shard_map/ppermute | solution.py:274
  23.0 1.5 %shard_map.55 = (f32[2,2,128,128]{3,2,1,0:T(8,128)S(1)}, f32[2,128,128]{2,1,0:T(8,128)S(1)}, bf16[2,2,128,384]{3,2,1,0:T(8,128)(2,1)S(1)}) custom-call(bf16[2,4,128,128]{3,2,1,0:T(8,128)(2,1)S(1)} %copy-done, bf16[4,128,128]{2,1,0:T(8,128)(2,1)S(1)} %collective-permute-done.x2, bf16[4,128,128]{2,1,0:T(8,128)(2,1)S(1)} %collective-permute-done.1.x1, ...), custom_call_target="tpu_custom_call" | custom-call | flops 20000000000 | tf_op jit(solution)/shard_map/pallas_call | solution.py:96
  24.5 0.7 %collective-permute-done.5.c1 = bf16[2,128,128]{2,1,0:T(8,128)(2,1)S(1)} collective-permute-done((bf16[2,128,128]{2,1,0:T(8,128)(2,1)S(1)}, bf16[2,128,128]{2,1,0:T(8,128)(2,1)S(1)}, u32[]{:S(2)}, u32[]{:S(2)}) %collective-permute-start.5) | collective-permute-done | bytes 65568 | tf_op jit(solution)/shard_map/ppermute | solution.py:274
  25.2 1.0 %shard_map.56 = bf16[8,2,64,128]{3,2,1,0:T(8,128)(2,1)} custom-call(f32[2,2,128,128]{3,2,1,0:T(8,128)S(1)} %get-tuple-element.12.ends, f32[2,128,128]{2,1,0:T(8,128)S(1)} %get-tuple-element.13.best, bf16[2,2,128,384]{3,2,1,0:T(8,128)(2,1)S(1)} %get-tuple-element.14.corner_w, bf16[2,128,128]{2,1,0:T(8,128)(2,1)S(1)} %collective-permute-done.4.c2, ...), custom_call_target="tpu_custom_call" | custom-call | tf_op jit(solution)/shard_map/pallas_call | solution.py:136
  26.2 6.6 %all-to-all-start = ((bf16[8,2,64,128]{3,2,1,0:T(8,128)(2,1)}), bf16[8,2,64,128]{3,2,1,0:T(8,128)(2,1)S(1)}, u32[]{:S(2)}, u32[]{:S(2)}) async-start(bf16[8,2,64,128]{3,2,1,0:T(8,128)(2,1)} %shard_map.56), calls=%async_computation | async-start | bytes 524288 | tf_op jit(solution)/shard_map/all_to_all | solution.py:285
  32.8 7.6 %all-to-all-done = bf16[8,2,64,128]{3,2,1,0:T(8,128)(2,1)S(1)} async-done(((bf16[8,2,64,128]{3,2,1,0:T(8,128)(2,1)}), bf16[8,2,64,128]{3,2,1,0:T(8,128)(2,1)S(1)}, u32[]{:S(2)}, u32[]{:S(2)}) %all-to-all-start) | async-done | bytes 262176 | tf_op jit(solution)/shard_map/all_to_all | solution.py:285
  40.4 2.2 %collective-permute-start.8 = (bf16[4,2,64,128]{3,2,1,0:T(8,128)(2,1)S(1)}, bf16[4,2,64,128]{3,2,1,0:T(8,128)(2,1)S(1)}, u32[]{:S(2)}, u32[]{:S(2)}) collective-permute-start(bf16[4,2,64,128]{3,2,1,0:T(8,128)(2,1)S(1)} %dynamic-slice_bitcast_fusion), channel_id=1, source_target_pairs={{0,16},{16,0},{32,48},{48,32},{64,80},{80,64},{96,112},{112,96},{1... | collective-permute-start | bytes 393224 | tf_op jit(solution)/shard_map/ppermute | solution.py:288
  42.6 0.6 %shard_map.57.sums = f32[64,640]{1,0:T(8,128)S(1)} custom-call(bf16[2,4,2,64,128]{4,3,2,1,0:T(8,128)(2,1)S(1)} %bitcast.26, bf16[2,27,16,128]{3,2,1,0:T(8,128)(2,1)S(1)} %pad_maximum_fusion.pair, bf16[2,27,16,128]{3,2,1,0:T(8,128)(2,1)S(1)} %collective-permute-done.7.other), custom_call_target="tpu_custom_call" | custom-call | flops 150000000 | tf_op jit(solution)/shard_map/pallas_call | solution.py:194
  43.2 0.4 collective-permute-done.8.near
  43.6 0.4 shard_map.58
  44.1 3.3 %collective-permute-start.10 = (f32[16,640]{1,0:T(8,128)S(1)}, f32[16,640]{1,0:T(8,128)S(1)}, u32[]{:S(2)}, u32[]{:S(2)}) collective-permute-start(f32[16,640]{1,0:T(8,128)S(1)} %get-tuple-element.17), channel_id=1, source_target_pairs={{0,8},{1,9},{2,10},{3,11},{4,12},{5,13},{6,14},{7,15},{8,0},{9,1},... | collective-permute-start | bytes 122888 | tf_op jit(solution)/shard_map/ppermute | solution.py:290
  47.3 1.8 %collective-permute-start.11 = (f32[16,640]{1,0:T(8,128)S(1)}, f32[16,640]{1,0:T(8,128)S(1)}, u32[]{:S(2)}, u32[]{:S(2)}) collective-permute-start(f32[16,640]{1,0:T(8,128)S(1)} %get-tuple-element.18), channel_id=1, source_target_pairs={{0,12},{1,13},{2,14},{3,15},{4,8},{5,9},{6,10},{7,11},{8,4},{9,5},... | collective-permute-start | bytes 122888 | tf_op jit(solution)/shard_map/ppermute | solution.py:290
  49.2 0.5 collective-permute-done.10.s2
  49.7 2.9 %collective-permute-done.11.s3 = f32[16,640]{1,0:T(8,128)S(1)} collective-permute-done((f32[16,640]{1,0:T(8,128)S(1)}, f32[16,640]{1,0:T(8,128)S(1)}, u32[]{:S(2)}, u32[]{:S(2)}) %collective-permute-start.11) | collective-permute-done | bytes 40992 | tf_op jit(solution)/shard_map/ppermute | solution.py:290
  52.5 0.6 %collective-permute-done.9.s1 = f32[16,640]{1,0:T(8,128)S(1)} collective-permute-done((f32[16,640]{1,0:T(8,128)S(1)}, f32[16,640]{1,0:T(8,128)S(1)}, u32[]{:S(2)}, u32[]{:S(2)}) %collective-permute-start.9) | collective-permute-done | bytes 40992 | tf_op jit(solution)/shard_map/ppermute | solution.py:290
  53.2 0.7 %shard_map.59 = bf16[16,2048]{1,0:T(8,128)(2,1)} custom-call(f32[16,640]{1,0:T(8,128)S(1)} %get-tuple-element.15.s0, f32[16,640]{1,0:T(8,128)S(1)} %collective-permute-done.9.s1, f32[16,640]{1,0:T(8,128)S(1)} %collective-permute-done.10.s2, f32[16,640]{1,0:T(8,128)S(1)} %collective-permute-done.11.s3, f32[16,128]{1,0:T(8,128)S(1)} %broadcast_in_dim.2.bias), custom_call_target="tpu_custom_call" | custom-call | tf_op jit(solution)/shard_map/pallas_call | solution.py:250
  (23 shorter events, 0.2 us)
Async XLA Ops:
  0.0 10.3 %copy-start.3 = (bf16[3,3,3,128,16]{3,4,2,1,0:T(8,128)(2,1)S(1)}, bf16[3,3,3,128,16]{3,4,2,1,0:T(8,128)(2,1)}, u32[]{:S(2)}) copy-start(bf16[3,3,3,128,16]{3,4,2,1,0:T(8,128)(2,1)} %param.8) | copy-start | bytes 331780
  0.0 11.9 %copy-start = (bf16[2,4,128,128]{3,2,1,0:T(8,128)(2,1)S(1)}, bf16[2,4,128,128]{3,2,1,0:T(8,128)(2,1)}, u32[]{:S(2)}) copy-start(bf16[2,4,128,128]{3,2,1,0:T(8,128)(2,1)} %vol.1) | copy-start | bytes 786436
  0.0 23.0 %copy-start.1 = (bf16[3,3,3,128,128]{4,3,2,1,0:T(8,128)(2,1)S(1)}, bf16[3,3,3,128,128]{4,3,2,1,0:T(8,128)(2,1)}, u32[]{:S(2)}) copy-start(bf16[3,3,3,128,128]{4,3,2,1,0:T(8,128)(2,1)} %w.1) | copy-start | bytes 2654212
  1.1 17.8 %collective-permute-start = (bf16[4,128,128]{2,1,0:T(8,128)(2,1)S(1)}, bf16[4,128,128]{2,1,0:T(8,128)(2,1)S(1)}, u32[]{:S(2)}, u32[]{:S(2)}) collective-permute-start(bf16[4,128,128]{2,1,0:T(8,128)(2,1)S(1)} %get-tuple-element.24), channel_id=1, source_target_pairs={{0,0},{16,32},{32,16},{48,64},{64,48},{80,96},{96,80},{112,128},{1... | collective-permute-start | bytes 393224 | tf_op jit(solution)/shard_map/ppermute | solution.py:268
  3.3 15.6 %collective-permute-start.1 = (bf16[4,128,128]{2,1,0:T(8,128)(2,1)S(1)}, bf16[4,128,128]{2,1,0:T(8,128)(2,1)S(1)}, u32[]{:S(2)}, u32[]{:S(2)}) collective-permute-start(bf16[4,128,128]{2,1,0:T(8,128)(2,1)S(1)} %get-tuple-element.23), channel_id=1, source_target_pairs={{0,16},{16,0},{32,48},{48,32},{64,80},{80,64},{96,112},{112,96},{1... | collective-permute-start | bytes 393224 | tf_op jit(solution)/shard_map/ppermute | solution.py:269
  10.3 5.6 %collective-permute-start.6 = (bf16[27,16,128]{2,1,0:T(8,128)(2,1)S(1)}, bf16[27,16,128]{2,1,0:T(8,128)(2,1)S(1)}, u32[]{:S(2)}, u32[]{:S(2)}) collective-permute-start(bf16[27,16,128]{2,1,0:T(8,128)(2,1)S(1)} %bitcast.30), channel_id=1, source_target_pairs={{0,4},{1,5},{2,6},{3,7},{4,0},{5,1},{6,2},{7,3},{8,12},{9,13},{10,... | collective-permute-start | bytes 331784 | tf_op jit(solution)/shard_map/ppermute | solution.py:280
  11.9 11.0 %collective-permute-start.2 = (bf16[2,128,128]{2,1,0:T(8,128)(2,1)S(1)}, bf16[2,128,128]{2,1,0:T(8,128)(2,1)S(1)}, u32[]{:S(2)}, u32[]{:S(2)}) collective-permute-start(bf16[2,128,128]{2,1,0:T(8,128)(2,1)S(1)} %get-tuple-element.22), channel_id=1, source_target_pairs={{0,0},{1,2},{2,1},{3,4},{4,3},{5,6},{6,5},{7,8},{8,7},{9,10},{10,9... | collective-permute-start | bytes 196616 | tf_op jit(solution)/shard_map/ppermute | solution.py:270
  12.6 10.4 %collective-permute-start.3 = (bf16[2,128,128]{2,1,0:T(8,128)(2,1)S(1)}, bf16[2,128,128]{2,1,0:T(8,128)(2,1)S(1)}, u32[]{:S(2)}, u32[]{:S(2)}) collective-permute-start(bf16[2,128,128]{2,1,0:T(8,128)(2,1)S(1)} %get-tuple-element.21), channel_id=1, source_target_pairs={{0,1},{1,0},{2,3},{3,2},{4,5},{5,4},{6,7},{7,6},{8,9},{9,8},{10,11... | collective-permute-start | bytes 196616 | tf_op jit(solution)/shard_map/ppermute | solution.py:271
  16.0 9.2 %collective-permute-start.7 = (bf16[2,27,16,128]{3,2,1,0:T(8,128)(2,1)S(1)}, bf16[2,27,16,128]{3,2,1,0:T(8,128)(2,1)S(1)}, u32[]{:S(2)}, u32[]{:S(2)}) collective-permute-start(bf16[2,27,16,128]{3,2,1,0:T(8,128)(2,1)S(1)} %pad_maximum_fusion.pair), channel_id=1, source_target_pairs={{0,12},{1,13},{2,14},{3,15},{4,8},{5,9},{6,10},{7,11},{8,4},{9,5},... | collective-permute-start | bytes 663560 | tf_op jit(solution)/shard_map/ppermute | solution.py:281
  18.9 5.6 %collective-permute-start.4 = (bf16[2,128,128]{2,1,0:T(8,128)(2,1)S(1)}, bf16[2,128,128]{2,1,0:T(8,128)(2,1)S(1)}, u32[]{:S(2)}, u32[]{:S(2)}) collective-permute-start(bf16[2,128,128]{2,1,0:T(8,128)(2,1)S(1)} %get-tuple-element.20), channel_id=1, source_target_pairs={{0,0},{1,2},{2,1},{3,4},{4,3},{5,6},{6,5},{7,8},{8,7},{9,10},{10,9... | collective-permute-start | bytes 196616 | tf_op jit(solution)/shard_map/ppermute | solution.py:273
  19.6 3.4 %copy-start.2 = (f32[128]{0:T(128)S(1)}, f32[128]{0:T(128)}, u32[]{:S(2)}) copy-start(f32[128]{0:T(128)} %param.7) | copy-start | bytes 1540
  19.6 5.6 %collective-permute-start.5 = (bf16[2,128,128]{2,1,0:T(8,128)(2,1)S(1)}, bf16[2,128,128]{2,1,0:T(8,128)(2,1)S(1)}, u32[]{:S(2)}, u32[]{:S(2)}) collective-permute-start(bf16[2,128,128]{2,1,0:T(8,128)(2,1)S(1)} %get-tuple-element.19), channel_id=1, source_target_pairs={{0,1},{1,0},{2,3},{3,2},{4,5},{5,4},{6,7},{7,6},{8,9},{9,8},{10,11... | collective-permute-start | bytes 196616 | tf_op jit(solution)/shard_map/ppermute | solution.py:274
  26.2 14.2 %all-to-all-start = ((bf16[8,2,64,128]{3,2,1,0:T(8,128)(2,1)}), bf16[8,2,64,128]{3,2,1,0:T(8,128)(2,1)S(1)}, u32[]{:S(2)}, u32[]{:S(2)}) async-start(bf16[8,2,64,128]{3,2,1,0:T(8,128)(2,1)} %shard_map.56), calls=%async_computation | async-start | bytes 524288 | tf_op jit(solution)/shard_map/all_to_all | solution.py:285
  40.4 3.2 %collective-permute-start.8 = (bf16[4,2,64,128]{3,2,1,0:T(8,128)(2,1)S(1)}, bf16[4,2,64,128]{3,2,1,0:T(8,128)(2,1)S(1)}, u32[]{:S(2)}, u32[]{:S(2)}) collective-permute-start(bf16[4,2,64,128]{3,2,1,0:T(8,128)(2,1)S(1)} %dynamic-slice_bitcast_fusion), channel_id=1, source_target_pairs={{0,16},{16,0},{32,48},{48,32},{64,80},{80,64},{96,112},{112,96},{1... | collective-permute-start | bytes 393224 | tf_op jit(solution)/shard_map/ppermute | solution.py:288
  44.1 5.6 %collective-permute-start.10 = (f32[16,640]{1,0:T(8,128)S(1)}, f32[16,640]{1,0:T(8,128)S(1)}, u32[]{:S(2)}, u32[]{:S(2)}) collective-permute-start(f32[16,640]{1,0:T(8,128)S(1)} %get-tuple-element.17), channel_id=1, source_target_pairs={{0,8},{1,9},{2,10},{3,11},{4,12},{5,13},{6,14},{7,15},{8,0},{9,1},... | collective-permute-start | bytes 122888 | tf_op jit(solution)/shard_map/ppermute | solution.py:290
  47.3 5.2 %collective-permute-start.11 = (f32[16,640]{1,0:T(8,128)S(1)}, f32[16,640]{1,0:T(8,128)S(1)}, u32[]{:S(2)}, u32[]{:S(2)}) collective-permute-start(f32[16,640]{1,0:T(8,128)S(1)} %get-tuple-element.18), channel_id=1, source_target_pairs={{0,12},{1,13},{2,14},{3,15},{4,8},{5,9},{6,10},{7,11},{8,4},{9,5},... | collective-permute-start | bytes 122888 | tf_op jit(solution)/shard_map/ppermute | solution.py:290
  49.2 4.0 %copy-start.4 = (f32[16]{0:T(128)S(1)}, f32[16]{0:T(128)}, u32[]{:S(2)}) copy-start(f32[16]{0:T(128)} %param.9) | copy-start | bytes 196
  49.2 4.0 %collective-permute-start.9 = (f32[16,640]{1,0:T(8,128)S(1)}, f32[16,640]{1,0:T(8,128)S(1)}, u32[]{:S(2)}, u32[]{:S(2)}) collective-permute-start(f32[16,640]{1,0:T(8,128)S(1)} %get-tuple-element.16), channel_id=1, source_target_pairs={{0,4},{1,5},{2,6},{3,7},{4,0},{5,1},{6,2},{7,3},{8,12},{9,13},{10,... | collective-permute-start | bytes 122888 | tf_op jit(solution)/shard_map/ppermute | solution.py:290

commit v14 on v12

--- a/solution.py
+++ b/solution.py
@@ -100,7 +100,24 @@
     )(vol, x2, x1, r2, r1, w, bias)
 
 
-def finish_kernel(ends, best, corner_w, c2, c1, other, out, peak):
+def outer_kernel(far_row, near_row, r2, r1, out):
+    pd = lax.rem(lax.axis_index("depth"), 2)
+    out[0] = r2[1 - pd]
+    out[1] = r1[1 - pd]
+
+
+def outer_rows(far_row, near_row, r2, r1):
+    vmem = pl.BlockSpec(memory_space=pltpu.VMEM)
+    return pl.pallas_call(
+        outer_kernel,
+        out_shape=jax.ShapeDtypeStruct((2, 128, 128), BF16),
+        in_specs=[pl.BlockSpec(memory_space=pl.ANY)] * 2 + [vmem] * 2,
+        out_specs=vmem,
+        compiler_params=pltpu.CompilerParams(vmem_limit_bytes=2 * 1024 * 1024),
+    )(far_row, near_row, r2, r1)
+
+
+def finish_kernel(ends, best, corner_w, c2, c1, e, other, out, peak):
     pr = lax.rem(lax.axis_index("rows"), 2)
     inner_d = inner("depth")
     inner_r = inner("rows")
@@ -109,7 +126,7 @@
     for q in range(2):
         value = best[q]
         for s in range(2):
-            piece = (c2, c1)[q][s]
+            piece = e[q] if s == 1 else (c2, c1)[q][...]
             if q == 0:
                 piece = jnp.where(inner_r, piece, zero)
             if s == 0:
@@ -123,16 +140,16 @@
             out[k, q + pr * (1 - 2 * q)] = pooled
 
 
-def finish(main, c2, c1, other):
+def finish(main, c2, c1, e, other):
     vmem = pl.BlockSpec(memory_space=pltpu.VMEM)
     return pl.pallas_call(
         finish_kernel,
         out_shape=jax.ShapeDtypeStruct((8, 2, 64, 128), BF16),
-        in_specs=[vmem] * 5 + [pl.BlockSpec(memory_space=pl.ANY)],
+        in_specs=[vmem] * 6 + [pl.BlockSpec(memory_space=pl.ANY)],
         out_specs=vmem,
         scratch_shapes=[pltpu.VMEM((128, 128), F32)],
         compiler_params=pltpu.CompilerParams(vmem_limit_bytes=6 * 1024 * 1024),
-    )(*main, c2, c1, other)
+    )(*main, c2, c1, e, other)
 
 
 def coarse_sums(cells, taps, pair, other, add):
@@ -260,9 +277,11 @@
     x1 = lax.ppermute(lax.dynamic_index_in_dim(volume, 1 - pd, 0, False), "depth", depth_near)
     r2 = lax.ppermute(lax.dynamic_index_in_dim(volume, 3 * pr, 1, False), "rows", rows_far)
     r1 = lax.ppermute(lax.dynamic_index_in_dim(volume, 3 - 3 * pr, 1, False), "rows", rows_near)
-    sides = jnp.stack([x2, x1])
-    c2 = lax.ppermute(lax.dynamic_index_in_dim(sides, 3 * pr, 1, False), "rows", rows_far)
-    c1 = lax.ppermute(lax.dynamic_index_in_dim(sides, 3 - 3 * pr, 1, False), "rows", rows_near)
+    far_row = lax.dynamic_index_in_dim(x2, 3 * pr, 0, False)
+    near_row = lax.dynamic_index_in_dim(x2, 3 - 3 * pr, 0, False)
+    c2 = lax.ppermute(far_row, "rows", rows_far)
+    c1 = lax.ppermute(near_row, "rows", rows_near)
+    e = lax.ppermute(outer_rows(far_row, near_row, r2, r1), "depth", depth_near)
 
     def along_y(k):
         return [(i, i ^ (4 * k)) for i in range(16)]
@@ -271,7 +290,7 @@
     pair = jnp.stack([w, lax.ppermute(w, "rows", along_y(1))])
     other = lax.ppermute(pair, "rows", along_y(3))
     main = fine_level(volume, x2, x1, r2, r1, fine_filters, fine_bias.reshape(1, 128))
-    pooled = finish(main, c2, c1, other)
+    pooled = finish(main, c2, c1, e, other)
 
     both = lax.all_to_all(
         pooled, ("depth", "rows"), 0, 0, axis_index_groups=far_and_z(), tiled=True

time: 53.3 us -> 54.1 us (1.015)
  starting transfers between devices: 29.1 us -> 28.4 us
    ppermute x1, starting transfers between devices: 7.04 us -> 4.31 us  [body(): lax.ppermute(lax.dynamic_index_in_dim(volume, 1 - pd, 0, False), 'depth',...]
    ppermute x1, starting transfers between devices: 3.37 us -> 5.17 us  [body(): lax.ppermute(lax.dynamic_index_in_dim(volume, 3 - 3 * pr, 1, False), 'row...]
    ppermute x3, waiting for transfers between devices: 4 us -> 5.21 us  [body(): lax.ppermute(sums[k], 'rows', along_y(k))]
    ppermute x2 -> x3, waiting for transfers between devices: 0.69 us -> 0.01 us  [the longest x1 0.01 us: body(): c1 = lax.ppermute(near_row, 'rows', rows_near)]
    ppermute x2 -> x3, starting transfers between devices: 4.01 us -> 3.75 us  [the longest x1 2.99 us: body(): c1 = lax.ppermute(near_row, 'rows', rows_near)]
  transfers between devices with their start and end apart: 12 -> 13, of which waited for: 5 -> 3; matrix products, arithmetic and copies ran while one was open for 0% -> 0% of each run, Pallas kernels for 4% -> 4%
where the time goes in v14:
time: 54.1 us; the launch traced here: 53.9 us
  starting transfers between devices  28.4 us (52%)
  blocking collectives  14.5 us (27%)
  waiting for transfers between devices  5.63 us (10%)
  Pallas kernels  3.49 us (6%)
  local copies, waits for them, and re-layouts  1.73 us (3%)
    all_to_all x1, blocking collectives, body(): lax.all_to_all(pooled, ('depth', 'rows'), 0, 0, axis_index_groups=far_and...  14.5 us
    ppermute x3, waiting for transfers between devices, body(): lax.ppermute(sums[k], 'rows', along_y(k))  5.21 us
    ppermute x1, starting transfers between devices, body(): lax.ppermute(lax.dynamic_index_in_dim(volume, 3 - 3 * pr, 1, False), 'row...  5.17 us
    ppermute x3, starting transfers between devices, body(): lax.ppermute(sums[k], 'rows', along_y(k))  4.93 us
    ppermute x1, starting transfers between devices, body(): lax.ppermute(lax.dynamic_index_in_dim(volume, 1 - pd, 0, False), 'depth',...  4.31 us
    ppermute x1, starting transfers between devices, body(): other = lax.ppermute(pair, 'rows', along_y(3))  3.26 us
    ppermute x1, starting transfers between devices, body(): c1 = lax.ppermute(near_row, 'rows', rows_near)  2.99 us
    ppermute x1, starting transfers between devices, body(): lax.ppermute(lax.dynamic_index_in_dim(both, 1 - pd, 0, False), 'depth', d...  2.44 us
  transfers between devices with their start and end apart: 13, of which 3 were waited for; matrix products, arithmetic and copies ran while one was open for 0% of the time, Pallas kernels for 4%

profile of v14, /device:TPU:6, one launch (start us, length us, event | category | flops | bytes accessed | tf_op | source)
XLA Modules:
  0.0 53.9 jit_solution(13965399931499507904)
XLA Ops:
  0.0 1.1 %dynamic-slice_bitcast_fusion.1 = (bf16[4,128,128]{2,1,0:T(8,128)(2,1)S(1)}, bf16[4,128,128]{2,1,0:T(8,128)(2,1)S(1)}) fusion(bf16[2,4,128,128]{3,2,1,0:T(8,128)(2,1)} %vol.1, s32[]{:T(128)S(6)} %select_n.20, s32[]{:T(128)S(6)} %select_n.19), kind=kLoop, calls=%fused_computation.2 | loop fusion | bytes 524296 | tf_op jit(solution)/shard_map/jit(dynamic_index_in_dim)/squeeze | solution.py:277
  1.1 2.2 %collective-permute-start = (bf16[4,128,128]{2,1,0:T(8,128)(2,1)S(1)}, bf16[4,128,128]{2,1,0:T(8,128)(2,1)S(1)}, u32[]{:S(2)}, u32[]{:S(2)}) collective-permute-start(bf16[4,128,128]{2,1,0:T(8,128)(2,1)S(1)} %get-tuple-element.22), channel_id=1, source_target_pairs={{0,0},{16,32},{32,16},{48,64},{64,48},{80,96},{96,80},{112,128},{1... | collective-permute-start | bytes 393224 | tf_op jit(solution)/shard_map/ppermute | solution.py:276
  3.3 1.7 %collective-permute-start.7 = (bf16[27,16,128]{2,1,0:T(8,128)(2,1)S(1)}, bf16[27,16,128]{2,1,0:T(8,128)(2,1)S(1)}, u32[]{:S(2)}, u32[]{:S(2)}) collective-permute-start(bf16[27,16,128]{2,1,0:T(8,128)(2,1)S(1)} %bitcast.26), channel_id=1, source_target_pairs={{0,4},{1,5},{2,6},{3,7},{4,0},{5,1},{6,2},{7,3},{8,12},{9,13},{10,... | collective-permute-start | bytes 331784 | tf_op jit(solution)/shard_map/ppermute | solution.py:290
  5.0 0.7 %collective-permute-start.2 = (bf16[2,128,128]{2,1,0:T(8,128)(2,1)S(1)}, bf16[2,128,128]{2,1,0:T(8,128)(2,1)S(1)}, u32[]{:S(2)}, u32[]{:S(2)}) collective-permute-start(bf16[2,128,128]{2,1,0:T(8,128)(2,1)S(1)} %get-tuple-element.20), channel_id=1, source_target_pairs={{0,0},{1,2},{2,1},{3,4},{4,3},{5,6},{6,5},{7,8},{8,7},{9,10},{10,9... | collective-permute-start | bytes 196616 | tf_op jit(solution)/shard_map/ppermute | solution.py:278
  5.6 5.2 %collective-permute-start.3 = (bf16[2,128,128]{2,1,0:T(8,128)(2,1)S(1)}, bf16[2,128,128]{2,1,0:T(8,128)(2,1)S(1)}, u32[]{:S(2)}, u32[]{:S(2)}) collective-permute-start(bf16[2,128,128]{2,1,0:T(8,128)(2,1)S(1)} %get-tuple-element.19), channel_id=1, source_target_pairs={{0,1},{1,0},{2,3},{3,2},{4,5},{5,4},{6,7},{7,6},{8,9},{9,8},{10,11... | collective-permute-start | bytes 196616 | tf_op jit(solution)/shard_map/ppermute | solution.py:279
  10.8 4.3 %collective-permute-start.1 = (bf16[4,128,128]{2,1,0:T(8,128)(2,1)S(1)}, bf16[4,128,128]{2,1,0:T(8,128)(2,1)S(1)}, u32[]{:S(2)}, u32[]{:S(2)}) collective-permute-start(bf16[4,128,128]{2,1,0:T(8,128)(2,1)S(1)} %get-tuple-element.21), channel_id=1, source_target_pairs={{0,16},{16,0},{32,48},{48,32},{64,80},{80,64},{96,112},{112,96},{1... | collective-permute-start | bytes 393224 | tf_op jit(solution)/shard_map/ppermute | solution.py:277
  15.2 3.3 %collective-permute-start.8 = (bf16[2,27,16,128]{3,2,1,0:T(8,128)(2,1)S(1)}, bf16[2,27,16,128]{3,2,1,0:T(8,128)(2,1)S(1)}, u32[]{:S(2)}, u32[]{:S(2)}) collective-permute-start(bf16[2,27,16,128]{3,2,1,0:T(8,128)(2,1)S(1)} %pad_maximum_fusion.pair), channel_id=1, source_target_pairs={{0,12},{1,13},{2,14},{3,15},{4,8},{5,9},{6,10},{7,11},{8,4},{9,5},... | collective-permute-start | bytes 663560 | tf_op jit(solution)/shard_map/ppermute | solution.py:291
  18.4 0.7 %collective-permute-start.4 = (bf16[128,128]{1,0:T(8,128)(2,1)S(1)}, bf16[128,128]{1,0:T(8,128)(2,1)S(1)}, u32[]{:S(2)}, u32[]{:S(2)}) collective-permute-start(bf16[128,128]{1,0:T(8,128)(2,1)S(1)} %get-tuple-element.24.far_row), channel_id=1, source_target_pairs={{0,0},{1,2},{2,1},{3,4},{4,3},{5,6},{6,5},{7,8},{8,7},{9,10},{10,9... | collective-permute-start | bytes 98312 | tf_op jit(solution)/shard_map/ppermute | solution.py:282
  19.1 3.0 %collective-permute-start.5 = (bf16[128,128]{1,0:T(8,128)(2,1)S(1)}, bf16[128,128]{1,0:T(8,128)(2,1)S(1)}, u32[]{:S(2)}, u32[]{:S(2)}) collective-permute-start(bf16[128,128]{1,0:T(8,128)(2,1)S(1)} %get-tuple-element.23.near_row), channel_id=1, source_target_pairs={{0,1},{1,0},{2,3},{3,2},{4,5},{5,4},{6,7},{7,6},{8,9},{9,8},{10,11... | collective-permute-start | bytes 98312 | tf_op jit(solution)/shard_map/ppermute | solution.py:283
  22.1 0.1 collective-permute-start.6
  22.2 0.5 copy-done.2
  22.8 1.5 %shard_map.55 = (f32[2,2,128,128]{3,2,1,0:T(8,128)S(1)}, f32[2,128,128]{2,1,0:T(8,128)S(1)}, bf16[2,2,128,384]{3,2,1,0:T(8,128)(2,1)S(1)}) custom-call(bf16[2,4,128,128]{3,2,1,0:T(8,128)(2,1)S(1)} %copy-done, bf16[4,128,128]{2,1,0:T(8,128)(2,1)S(1)} %collective-permute-done.x2, bf16[4,128,128]{2,1,0:T(8,128)(2,1)S(1)} %collective-permute-done.1.x1, ...), custom_call_target="tpu_custom_call" | custom-call | flops 20000000000 | tf_op jit(solution)/shard_map/pallas_call | solution.py:88
  24.3 0.3 shard_map.57
  24.6 14.5 %all_to_all.5 = bf16[8,2,64,128]{3,2,1,0:T(8,128)(2,1)S(1)} all-to-all(bf16[8,2,64,128]{3,2,1,0:T(8,128)(2,1)S(1)} %shard_map.57), channel_id=1, replica_groups={{16,17,18,19,32,33,34,35},{20,21,22,23,36,37,38,39},{24,25,26,27,40,41,..., dimensions={0} | all-to-all | bytes 524288 | tf_op jit(solution)/shard_map/all_to_all | solution.py:295
  39.1 2.4 %collective-permute-start.9 = (bf16[4,2,64,128]{3,2,1,0:T(8,128)(2,1)S(1)}, bf16[4,2,64,128]{3,2,1,0:T(8,128)(2,1)S(1)}, u32[]{:S(2)}, u32[]{:S(2)}) collective-permute-start(bf16[4,2,64,128]{3,2,1,0:T(8,128)(2,1)S(1)} %dynamic-slice_bitcast_fusion), channel_id=1, source_target_pairs={{0,16},{16,0},{32,48},{48,32},{64,80},{80,64},{96,112},{112,96},{1... | collective-permute-start | bytes 393224 | tf_op jit(solution)/shard_map/ppermute | solution.py:298
  41.6 0.6 %shard_map.58.sums = f32[64,640]{1,0:T(8,128)S(1)} custom-call(bf16[2,4,2,64,128]{4,3,2,1,0:T(8,128)(2,1)S(1)} %bitcast.24, bf16[2,27,16,128]{3,2,1,0:T(8,128)(2,1)S(1)} %pad_maximum_fusion.pair, bf16[2,27,16,128]{3,2,1,0:T(8,128)(2,1)S(1)} %collective-permute-done.8.other), custom_call_target="tpu_custom_call" | custom-call | flops 150000000 | tf_op jit(solution)/shard_map/pallas_call | solution.py:202
  42.1 0.4 collective-permute-done.9.near
  42.5 0.4 shard_map.59
  43.0 1.9 %collective-permute-start.10 = (f32[16,640]{1,0:T(8,128)S(1)}, f32[16,640]{1,0:T(8,128)S(1)}, u32[]{:S(2)}, u32[]{:S(2)}) collective-permute-start(f32[16,640]{1,0:T(8,128)S(1)} %get-tuple-element.16), channel_id=1, source_target_pairs={{0,4},{1,5},{2,6},{3,7},{4,0},{5,1},{6,2},{7,3},{8,12},{9,13},{10,... | collective-permute-start | bytes 122888 | tf_op jit(solution)/shard_map/ppermute | solution.py:300
  44.9 3.0 %collective-permute-start.11 = (f32[16,640]{1,0:T(8,128)S(1)}, f32[16,640]{1,0:T(8,128)S(1)}, u32[]{:S(2)}, u32[]{:S(2)}) collective-permute-start(f32[16,640]{1,0:T(8,128)S(1)} %get-tuple-element.17), channel_id=1, source_target_pairs={{0,8},{1,9},{2,10},{3,11},{4,12},{5,13},{6,14},{7,15},{8,0},{9,1},... | collective-permute-start | bytes 122888 | tf_op jit(solution)/shard_map/ppermute | solution.py:300
  47.9 2.7 %collective-permute-done.11.s2 = f32[16,640]{1,0:T(8,128)S(1)} collective-permute-done((f32[16,640]{1,0:T(8,128)S(1)}, f32[16,640]{1,0:T(8,128)S(1)}, u32[]{:S(2)}, u32[]{:S(2)}) %collective-permute-start.11) | collective-permute-done | bytes 40992 | tf_op jit(solution)/shard_map/ppermute | solution.py:300
  50.6 2.5 %collective-permute-done.12.s3 = f32[16,640]{1,0:T(8,128)S(1)} collective-permute-done((f32[16,640]{1,0:T(8,128)S(1)}, f32[16,640]{1,0:T(8,128)S(1)}, u32[]{:S(2)}, u32[]{:S(2)}) %collective-permute-start.12) | collective-permute-done | bytes 40992 | tf_op jit(solution)/shard_map/ppermute | solution.py:300
  53.1 0.1 broadcast_in_dim.2.bias
  53.2 0.7 %shard_map.60 = bf16[16,2048]{1,0:T(8,128)(2,1)} custom-call(f32[16,640]{1,0:T(8,128)S(1)} %get-tuple-element.15.s0, f32[16,640]{1,0:T(8,128)S(1)} %collective-permute-done.10.s1, f32[16,640]{1,0:T(8,128)S(1)} %collective-permute-done.11.s2, f32[16,640]{1,0:T(8,128)S(1)} %collective-permute-done.12.s3, f32[16,128]{1,0:T(8,128)S(1)} %broadcast_in_dim.2.bias), custom_call_target="tpu_custom_call" | custom-call | tf_op jit(solution)/shard_map/pallas_call | solution.py:258
  (25 shorter events, 0.1 us)
Async XLA Ops:
  0.0 3.3 %copy-start.3 = (bf16[3,3,3,128,16]{3,4,2,1,0:T(8,128)(2,1)S(1)}, bf16[3,3,3,128,16]{3,4,2,1,0:T(8,128)(2,1)}, u32[]{:S(2)}) copy-start(bf16[3,3,3,128,16]{3,4,2,1,0:T(8,128)(2,1)} %param.8) | copy-start | bytes 331780
  0.0 5.0 %copy-start = (bf16[2,4,128,128]{3,2,1,0:T(8,128)(2,1)S(1)}, bf16[2,4,128,128]{3,2,1,0:T(8,128)(2,1)}, u32[]{:S(2)}) copy-start(bf16[2,4,128,128]{3,2,1,0:T(8,128)(2,1)} %vol.1) | copy-start | bytes 786436
  0.0 22.2 %copy-start.1 = (bf16[3,3,3,128,128]{4,3,2,1,0:T(8,128)(2,1)S(1)}, bf16[3,3,3,128,128]{4,3,2,1,0:T(8,128)(2,1)}, u32[]{:S(2)}) copy-start(bf16[3,3,3,128,128]{4,3,2,1,0:T(8,128)(2,1)} %w.1) | copy-start | bytes 2654212
  1.1 17.3 %collective-permute-start = (bf16[4,128,128]{2,1,0:T(8,128)(2,1)S(1)}, bf16[4,128,128]{2,1,0:T(8,128)(2,1)S(1)}, u32[]{:S(2)}, u32[]{:S(2)}) collective-permute-start(bf16[4,128,128]{2,1,0:T(8,128)(2,1)S(1)} %get-tuple-element.22), channel_id=1, source_target_pairs={{0,0},{16,32},{32,16},{48,64},{64,48},{80,96},{96,80},{112,128},{1... | collective-permute-start | bytes 393224 | tf_op jit(solution)/shard_map/ppermute | solution.py:276
  3.3 11.8 %collective-permute-start.7 = (bf16[27,16,128]{2,1,0:T(8,128)(2,1)S(1)}, bf16[27,16,128]{2,1,0:T(8,128)(2,1)S(1)}, u32[]{:S(2)}, u32[]{:S(2)}) collective-permute-start(bf16[27,16,128]{2,1,0:T(8,128)(2,1)S(1)} %bitcast.26), channel_id=1, source_target_pairs={{0,4},{1,5},{2,6},{3,7},{4,0},{5,1},{6,2},{7,3},{8,12},{9,13},{10,... | collective-permute-start | bytes 331784 | tf_op jit(solution)/shard_map/ppermute | solution.py:290
  5.0 14.1 %collective-permute-start.2 = (bf16[2,128,128]{2,1,0:T(8,128)(2,1)S(1)}, bf16[2,128,128]{2,1,0:T(8,128)(2,1)S(1)}, u32[]{:S(2)}, u32[]{:S(2)}) collective-permute-start(bf16[2,128,128]{2,1,0:T(8,128)(2,1)S(1)} %get-tuple-element.20), channel_id=1, source_target_pairs={{0,0},{1,2},{2,1},{3,4},{4,3},{5,6},{6,5},{7,8},{8,7},{9,10},{10,9... | collective-permute-start | bytes 196616 | tf_op jit(solution)/shard_map/ppermute | solution.py:278
  5.6 16.5 %collective-permute-start.3 = (bf16[2,128,128]{2,1,0:T(8,128)(2,1)S(1)}, bf16[2,128,128]{2,1,0:T(8,128)(2,1)S(1)}, u32[]{:S(2)}, u32[]{:S(2)}) collective-permute-start(bf16[2,128,128]{2,1,0:T(8,128)(2,1)S(1)} %get-tuple-element.19), channel_id=1, source_target_pairs={{0,1},{1,0},{2,3},{3,2},{4,5},{5,4},{6,7},{7,6},{8,9},{9,8},{10,11... | collective-permute-start | bytes 196616 | tf_op jit(solution)/shard_map/ppermute | solution.py:279
  10.8 11.4 %collective-permute-start.1 = (bf16[4,128,128]{2,1,0:T(8,128)(2,1)S(1)}, bf16[4,128,128]{2,1,0:T(8,128)(2,1)S(1)}, u32[]{:S(2)}, u32[]{:S(2)}) collective-permute-start(bf16[4,128,128]{2,1,0:T(8,128)(2,1)S(1)} %get-tuple-element.21), channel_id=1, source_target_pairs={{0,16},{16,0},{32,48},{48,32},{64,80},{80,64},{96,112},{112,96},{1... | collective-permute-start | bytes 393224 | tf_op jit(solution)/shard_map/ppermute | solution.py:277
  15.2 9.2 %collective-permute-start.8 = (bf16[2,27,16,128]{3,2,1,0:T(8,128)(2,1)S(1)}, bf16[2,27,16,128]{3,2,1,0:T(8,128)(2,1)S(1)}, u32[]{:S(2)}, u32[]{:S(2)}) collective-permute-start(bf16[2,27,16,128]{3,2,1,0:T(8,128)(2,1)S(1)} %pad_maximum_fusion.pair), channel_id=1, source_target_pairs={{0,12},{1,13},{2,14},{3,15},{4,8},{5,9},{6,10},{7,11},{8,4},{9,5},... | collective-permute-start | bytes 663560 | tf_op jit(solution)/shard_map/ppermute | solution.py:291
  18.4 5.9 %collective-permute-start.4 = (bf16[128,128]{1,0:T(8,128)(2,1)S(1)}, bf16[128,128]{1,0:T(8,128)(2,1)S(1)}, u32[]{:S(2)}, u32[]{:S(2)}) collective-permute-start(bf16[128,128]{1,0:T(8,128)(2,1)S(1)} %get-tuple-element.24.far_row), channel_id=1, source_target_pairs={{0,0},{1,2},{2,1},{3,4},{4,3},{5,6},{6,5},{7,8},{8,7},{9,10},{10,9... | collective-permute-start | bytes 98312 | tf_op jit(solution)/shard_map/ppermute | solution.py:282
  19.1 5.2 %collective-permute-start.5 = (bf16[128,128]{1,0:T(8,128)(2,1)S(1)}, bf16[128,128]{1,0:T(8,128)(2,1)S(1)}, u32[]{:S(2)}, u32[]{:S(2)}) collective-permute-start(bf16[128,128]{1,0:T(8,128)(2,1)S(1)} %get-tuple-element.23.near_row), channel_id=1, source_target_pairs={{0,1},{1,0},{2,3},{3,2},{4,5},{5,4},{6,7},{7,6},{8,9},{9,8},{10,11... | collective-permute-start | bytes 98312 | tf_op jit(solution)/shard_map/ppermute | solution.py:283
  22.1 0.7 %copy-start.2 = (f32[128]{0:T(128)S(1)}, f32[128]{0:T(128)}, u32[]{:S(2)}) copy-start(f32[128]{0:T(128)} %param.7) | copy-start | bytes 1540
  22.1 2.2 %collective-permute-start.6 = (bf16[2,128,128]{2,1,0:T(8,128)(2,1)S(1)}, bf16[2,128,128]{2,1,0:T(8,128)(2,1)S(1)}, u32[]{:S(2)}, u32[]{:S(2)}) collective-permute-start(bf16[2,128,128]{2,1,0:T(8,128)(2,1)S(1)} %shard_map.56), channel_id=1, source_target_pairs={{0,16},{16,0},{32,48},{48,32},{64,80},{80,64},{96,112},{112,96},{1... | collective-permute-start | bytes 196616 | tf_op jit(solution)/shard_map/ppermute | solution.py:284
  39.1 3.4 %collective-permute-start.9 = (bf16[4,2,64,128]{3,2,1,0:T(8,128)(2,1)S(1)}, bf16[4,2,64,128]{3,2,1,0:T(8,128)(2,1)S(1)}, u32[]{:S(2)}, u32[]{:S(2)}) collective-permute-start(bf16[4,2,64,128]{3,2,1,0:T(8,128)(2,1)S(1)} %dynamic-slice_bitcast_fusion), channel_id=1, source_target_pairs={{0,16},{16,0},{32,48},{48,32},{64,80},{80,64},{96,112},{112,96},{1... | collective-permute-start | bytes 393224 | tf_op jit(solution)/shard_map/ppermute | solution.py:298
  43.0 4.9 %collective-permute-start.10 = (f32[16,640]{1,0:T(8,128)S(1)}, f32[16,640]{1,0:T(8,128)S(1)}, u32[]{:S(2)}, u32[]{:S(2)}) collective-permute-start(f32[16,640]{1,0:T(8,128)S(1)} %get-tuple-element.16), channel_id=1, source_target_pairs={{0,4},{1,5},{2,6},{3,7},{4,0},{5,1},{6,2},{7,3},{8,12},{9,13},{10,... | collective-permute-start | bytes 122888 | tf_op jit(solution)/shard_map/ppermute | solution.py:300
  44.9 5.7 %collective-permute-start.11 = (f32[16,640]{1,0:T(8,128)S(1)}, f32[16,640]{1,0:T(8,128)S(1)}, u32[]{:S(2)}, u32[]{:S(2)}) collective-permute-start(f32[16,640]{1,0:T(8,128)S(1)} %get-tuple-element.17), channel_id=1, source_target_pairs={{0,8},{1,9},{2,10},{3,11},{4,12},{5,13},{6,14},{7,15},{8,0},{9,1},... | collective-permute-start | bytes 122888 | tf_op jit(solution)/shard_map/ppermute | solution.py:300
  47.9 5.2 %copy-start.4 = (f32[16]{0:T(128)S(1)}, f32[16]{0:T(128)}, u32[]{:S(2)}) copy-start(f32[16]{0:T(128)} %param.9) | copy-start | bytes 196
  47.9 5.2 %collective-permute-start.12 = (f32[16,640]{1,0:T(8,128)S(1)}, f32[16,640]{1,0:T(8,128)S(1)}, u32[]{:S(2)}, u32[]{:S(2)}) collective-permute-start(f32[16,640]{1,0:T(8,128)S(1)} %get-tuple-element.18), channel_id=1, source_target_pairs={{0,12},{1,13},{2,14},{3,15},{4,8},{5,9},{6,10},{7,11},{8,4},{9,5},... | collective-permute-start | bytes 122888 | tf_op jit(solution)/shard_map/ppermute | solution.py:300

commit v15 on v14

--- a/solution.py
+++ b/solution.py
@@ -237,7 +237,7 @@
     )(near, sums, pair, other)
 
 
-def join_kernel(s0, s1, s2, s3, bias, out, held):
+def join_kernel(s0, s2, s3, s1, bias, out, held):
     y = lax.div(lax.axis_index("rows"), 4)
     for k, part in enumerate((s0, s1, s2, s3)):
         held[y ^ k] = part[...]
@@ -297,7 +297,7 @@
     ).reshape(2, 4, 2, 64, 128)
     near = lax.ppermute(lax.dynamic_index_in_dim(both, 1 - pd, 0, False), "depth", depth_near)
     sums = near_level(near, coarse_level(both, pair, other), pair, other)
-    parts = [sums[0]] + [lax.ppermute(sums[k], "rows", along_y(k)) for k in (1, 2, 3)]
+    parts = [sums[0]] + [lax.ppermute(sums[k], "rows", along_y(k)) for k in (2, 3, 1)]
     result = join(parts, jnp.broadcast_to(coarse_bias[:, None], (16, 128)))
     return result.reshape(16, 1, 2048)
 

time: 54.1 us -> 53 us (0.980)
  waiting for transfers between devices: 5.63 us -> 4.81 us
    ppermute x3, waiting for transfers between devices: 5.21 us -> 4.39 us  [body(): lax.ppermute(sums[k], 'rows', along_y(k))]
where the time goes in v15:
time: 53 us; the launch traced here: 52.7 us
  starting transfers between devices  28 us (53%)
  blocking collectives  14.5 us (27%)
  waiting for transfers between devices  4.81 us (9%)
  Pallas kernels  3.49 us (7%)
  local copies, waits for them, and re-layouts  1.73 us (3%)
    all_to_all x1, blocking collectives, body(): lax.all_to_all(pooled, ('depth', 'rows'), 0, 0, axis_index_groups=far_and...  14.5 us
    ppermute x1, starting transfers between devices, body(): lax.ppermute(lax.dynamic_index_in_dim(volume, 3 - 3 * pr, 1, False), 'row...  5.17 us
    ppermute x3, starting transfers between devices, body(): lax.ppermute(sums[k], 'rows', along_y(k))  4.6 us
    ppermute x3, waiting for transfers between devices, body(): lax.ppermute(sums[k], 'rows', along_y(k))  4.39 us
    ppermute x1, starting transfers between devices, body(): lax.ppermute(lax.dynamic_index_in_dim(volume, 1 - pd, 0, False), 'depth',...  4.31 us
    ppermute x1, starting transfers between devices, body(): other = lax.ppermute(pair, 'rows', along_y(3))  3.26 us
    ppermute x1, starting transfers between devices, body(): c1 = lax.ppermute(near_row, 'rows', rows_near)  2.99 us
    ppermute x1, starting transfers between devices, body(): lax.ppermute(lax.dynamic_index_in_dim(both, 1 - pd, 0, False), 'depth', d...  2.44 us
  transfers between devices with their start and end apart: 13, of which 3 were waited for; matrix products, arithmetic and copies ran while one was open for 0% of the time, Pallas kernels for 4%

profile of v15, /device:TPU:6, one launch (start us, length us, event | category | flops | bytes accessed | tf_op | source)
XLA Modules:
  0.0 52.7 jit_solution(11494244750193573681)
XLA Ops:
  0.0 1.1 %dynamic-slice_bitcast_fusion.1 = (bf16[4,128,128]{2,1,0:T(8,128)(2,1)S(1)}, bf16[4,128,128]{2,1,0:T(8,128)(2,1)S(1)}) fusion(bf16[2,4,128,128]{3,2,1,0:T(8,128)(2,1)} %vol.1, s32[]{:T(128)S(6)} %select_n.20, s32[]{:T(128)S(6)} %select_n.19), kind=kLoop, calls=%fused_computation.2 | loop fusion | bytes 524296 | tf_op jit(solution)/shard_map/jit(dynamic_index_in_dim)/squeeze | solution.py:277
  1.1 2.2 %collective-permute-start = (bf16[4,128,128]{2,1,0:T(8,128)(2,1)S(1)}, bf16[4,128,128]{2,1,0:T(8,128)(2,1)S(1)}, u32[]{:S(2)}, u32[]{:S(2)}) collective-permute-start(bf16[4,128,128]{2,1,0:T(8,128)(2,1)S(1)} %get-tuple-element.22), channel_id=1, source_target_pairs={{0,0},{16,32},{32,16},{48,64},{64,48},{80,96},{96,80},{112,128},{1... | collective-permute-start | bytes 393224 | tf_op jit(solution)/shard_map/ppermute | solution.py:276
  3.3 1.7 %collective-permute-start.7 = (bf16[27,16,128]{2,1,0:T(8,128)(2,1)S(1)}, bf16[27,16,128]{2,1,0:T(8,128)(2,1)S(1)}, u32[]{:S(2)}, u32[]{:S(2)}) collective-permute-start(bf16[27,16,128]{2,1,0:T(8,128)(2,1)S(1)} %bitcast.26), channel_id=1, source_target_pairs={{0,4},{1,5},{2,6},{3,7},{4,0},{5,1},{6,2},{7,3},{8,12},{9,13},{10,... | collective-permute-start | bytes 331784 | tf_op jit(solution)/shard_map/ppermute | solution.py:290
  5.0 0.7 %collective-permute-start.2 = (bf16[2,128,128]{2,1,0:T(8,128)(2,1)S(1)}, bf16[2,128,128]{2,1,0:T(8,128)(2,1)S(1)}, u32[]{:S(2)}, u32[]{:S(2)}) collective-permute-start(bf16[2,128,128]{2,1,0:T(8,128)(2,1)S(1)} %get-tuple-element.20), channel_id=1, source_target_pairs={{0,0},{1,2},{2,1},{3,4},{4,3},{5,6},{6,5},{7,8},{8,7},{9,10},{10,9... | collective-permute-start | bytes 196616 | tf_op jit(solution)/shard_map/ppermute | solution.py:278
  5.6 5.2 %collective-permute-start.3 = (bf16[2,128,128]{2,1,0:T(8,128)(2,1)S(1)}, bf16[2,128,128]{2,1,0:T(8,128)(2,1)S(1)}, u32[]{:S(2)}, u32[]{:S(2)}) collective-permute-start(bf16[2,128,128]{2,1,0:T(8,128)(2,1)S(1)} %get-tuple-element.19), channel_id=1, source_target_pairs={{0,1},{1,0},{2,3},{3,2},{4,5},{5,4},{6,7},{7,6},{8,9},{9,8},{10,11... | collective-permute-start | bytes 196616 | tf_op jit(solution)/shard_map/ppermute | solution.py:279
  10.8 4.3 %collective-permute-start.1 = (bf16[4,128,128]{2,1,0:T(8,128)(2,1)S(1)}, bf16[4,128,128]{2,1,0:T(8,128)(2,1)S(1)}, u32[]{:S(2)}, u32[]{:S(2)}) collective-permute-start(bf16[4,128,128]{2,1,0:T(8,128)(2,1)S(1)} %get-tuple-element.21), channel_id=1, source_target_pairs={{0,16},{16,0},{32,48},{48,32},{64,80},{80,64},{96,112},{112,96},{1... | collective-permute-start | bytes 393224 | tf_op jit(solution)/shard_map/ppermute | solution.py:277
  15.2 3.3 %collective-permute-start.8 = (bf16[2,27,16,128]{3,2,1,0:T(8,128)(2,1)S(1)}, bf16[2,27,16,128]{3,2,1,0:T(8,128)(2,1)S(1)}, u32[]{:S(2)}, u32[]{:S(2)}) collective-permute-start(bf16[2,27,16,128]{3,2,1,0:T(8,128)(2,1)S(1)} %pad_maximum_fusion.pair), channel_id=1, source_target_pairs={{0,12},{1,13},{2,14},{3,15},{4,8},{5,9},{6,10},{7,11},{8,4},{9,5},... | collective-permute-start | bytes 663560 | tf_op jit(solution)/shard_map/ppermute | solution.py:291
  18.4 0.7 %collective-permute-start.4 = (bf16[128,128]{1,0:T(8,128)(2,1)S(1)}, bf16[128,128]{1,0:T(8,128)(2,1)S(1)}, u32[]{:S(2)}, u32[]{:S(2)}) collective-permute-start(bf16[128,128]{1,0:T(8,128)(2,1)S(1)} %get-tuple-element.24.far_row), channel_id=1, source_target_pairs={{0,0},{1,2},{2,1},{3,4},{4,3},{5,6},{6,5},{7,8},{8,7},{9,10},{10,9... | collective-permute-start | bytes 98312 | tf_op jit(solution)/shard_map/ppermute | solution.py:282
  19.1 3.0 %collective-permute-start.5 = (bf16[128,128]{1,0:T(8,128)(2,1)S(1)}, bf16[128,128]{1,0:T(8,128)(2,1)S(1)}, u32[]{:S(2)}, u32[]{:S(2)}) collective-permute-start(bf16[128,128]{1,0:T(8,128)(2,1)S(1)} %get-tuple-element.23.near_row), channel_id=1, source_target_pairs={{0,1},{1,0},{2,3},{3,2},{4,5},{5,4},{6,7},{7,6},{8,9},{9,8},{10,11... | collective-permute-start | bytes 98312 | tf_op jit(solution)/shard_map/ppermute | solution.py:283
  22.1 0.1 collective-permute-start.6
  22.2 0.5 copy-done.2
  22.8 1.5 %shard_map.55 = (f32[2,2,128,128]{3,2,1,0:T(8,128)S(1)}, f32[2,128,128]{2,1,0:T(8,128)S(1)}, bf16[2,2,128,384]{3,2,1,0:T(8,128)(2,1)S(1)}) custom-call(bf16[2,4,128,128]{3,2,1,0:T(8,128)(2,1)S(1)} %copy-done, bf16[4,128,128]{2,1,0:T(8,128)(2,1)S(1)} %collective-permute-done.x2, bf16[4,128,128]{2,1,0:T(8,128)(2,1)S(1)} %collective-permute-done.1.x1, ...), custom_call_target="tpu_custom_call" | custom-call | flops 20000000000 | tf_op jit(solution)/shard_map/pallas_call | solution.py:88
  24.3 0.3 shard_map.57
  24.6 14.5 %all_to_all.5 = bf16[8,2,64,128]{3,2,1,0:T(8,128)(2,1)S(1)} all-to-all(bf16[8,2,64,128]{3,2,1,0:T(8,128)(2,1)S(1)} %shard_map.57), channel_id=1, replica_groups={{16,17,18,19,32,33,34,35},{20,21,22,23,36,37,38,39},{24,25,26,27,40,41,..., dimensions={0} | all-to-all | bytes 524288 | tf_op jit(solution)/shard_map/all_to_all | solution.py:295
  39.1 2.4 %collective-permute-start.9 = (bf16[4,2,64,128]{3,2,1,0:T(8,128)(2,1)S(1)}, bf16[4,2,64,128]{3,2,1,0:T(8,128)(2,1)S(1)}, u32[]{:S(2)}, u32[]{:S(2)}) collective-permute-start(bf16[4,2,64,128]{3,2,1,0:T(8,128)(2,1)S(1)} %dynamic-slice_bitcast_fusion), channel_id=1, source_target_pairs={{0,16},{16,0},{32,48},{48,32},{64,80},{80,64},{96,112},{112,96},{1... | collective-permute-start | bytes 393224 | tf_op jit(solution)/shard_map/ppermute | solution.py:298
  41.6 0.6 %shard_map.58.sums = f32[64,640]{1,0:T(8,128)S(1)} custom-call(bf16[2,4,2,64,128]{4,3,2,1,0:T(8,128)(2,1)S(1)} %bitcast.24, bf16[2,27,16,128]{3,2,1,0:T(8,128)(2,1)S(1)} %pad_maximum_fusion.pair, bf16[2,27,16,128]{3,2,1,0:T(8,128)(2,1)S(1)} %collective-permute-done.8.other), custom_call_target="tpu_custom_call" | custom-call | flops 150000000 | tf_op jit(solution)/shard_map/pallas_call | solution.py:202
  42.1 0.4 collective-permute-done.9.near
  42.5 0.4 shard_map.59
  43.0 3.8 %collective-permute-start.10 = (f32[16,640]{1,0:T(8,128)S(1)}, f32[16,640]{1,0:T(8,128)S(1)}, u32[]{:S(2)}, u32[]{:S(2)}) collective-permute-start(f32[16,640]{1,0:T(8,128)S(1)} %get-tuple-element.16), channel_id=1, source_target_pairs={{0,8},{1,9},{2,10},{3,11},{4,12},{5,13},{6,14},{7,15},{8,0},{9,1},... | collective-permute-start | bytes 122888 | tf_op jit(solution)/shard_map/ppermute | solution.py:300
  46.8 0.8 %collective-permute-start.11 = (f32[16,640]{1,0:T(8,128)S(1)}, f32[16,640]{1,0:T(8,128)S(1)}, u32[]{:S(2)}, u32[]{:S(2)}) collective-permute-start(f32[16,640]{1,0:T(8,128)S(1)} %get-tuple-element.17), channel_id=1, source_target_pairs={{0,12},{1,13},{2,14},{3,15},{4,8},{5,9},{6,10},{7,11},{8,4},{9,5},... | collective-permute-start | bytes 122888 | tf_op jit(solution)/shard_map/ppermute | solution.py:300
  47.6 1.3 %collective-permute-done.10.s2 = f32[16,640]{1,0:T(8,128)S(1)} collective-permute-done((f32[16,640]{1,0:T(8,128)S(1)}, f32[16,640]{1,0:T(8,128)S(1)}, u32[]{:S(2)}, u32[]{:S(2)}) %collective-permute-start.10) | collective-permute-done | bytes 40992 | tf_op jit(solution)/shard_map/ppermute | solution.py:300
  48.8 3.1 %collective-permute-done.11.s3 = f32[16,640]{1,0:T(8,128)S(1)} collective-permute-done((f32[16,640]{1,0:T(8,128)S(1)}, f32[16,640]{1,0:T(8,128)S(1)}, u32[]{:S(2)}, u32[]{:S(2)}) %collective-permute-start.11) | collective-permute-done | bytes 40992 | tf_op jit(solution)/shard_map/ppermute | solution.py:300
  52.0 0.1 broadcast_in_dim.2.bias
  52.1 0.7 %shard_map.60 = bf16[16,2048]{1,0:T(8,128)(2,1)} custom-call(f32[16,640]{1,0:T(8,128)S(1)} %get-tuple-element.15.s0, f32[16,640]{1,0:T(8,128)S(1)} %collective-permute-done.10.s2, f32[16,640]{1,0:T(8,128)S(1)} %collective-permute-done.11.s3, f32[16,640]{1,0:T(8,128)S(1)} %collective-permute-done.12.s1, f32[16,128]{1,0:T(8,128)S(1)} %broadcast_in_dim.2.bias), custom_call_target="tpu_custom_call" | custom-call | tf_op jit(solution)/shard_map/pallas_call | solution.py:258
  (25 shorter events, 0.1 us)
Async XLA Ops:
  0.0 3.3 %copy-start.3 = (bf16[3,3,3,128,16]{3,4,2,1,0:T(8,128)(2,1)S(1)}, bf16[3,3,3,128,16]{3,4,2,1,0:T(8,128)(2,1)}, u32[]{:S(2)}) copy-start(bf16[3,3,3,128,16]{3,4,2,1,0:T(8,128)(2,1)} %param.8) | copy-start | bytes 331780
  0.0 5.0 %copy-start = (bf16[2,4,128,128]{3,2,1,0:T(8,128)(2,1)S(1)}, bf16[2,4,128,128]{3,2,1,0:T(8,128)(2,1)}, u32[]{:S(2)}) copy-start(bf16[2,4,128,128]{3,2,1,0:T(8,128)(2,1)} %vol.1) | copy-start | bytes 786436
  0.0 22.2 %copy-start.1 = (bf16[3,3,3,128,128]{4,3,2,1,0:T(8,128)(2,1)S(1)}, bf16[3,3,3,128,128]{4,3,2,1,0:T(8,128)(2,1)}, u32[]{:S(2)}) copy-start(bf16[3,3,3,128,128]{4,3,2,1,0:T(8,128)(2,1)} %w.1) | copy-start | bytes 2654212
  1.1 17.3 %collective-permute-start = (bf16[4,128,128]{2,1,0:T(8,128)(2,1)S(1)}, bf16[4,128,128]{2,1,0:T(8,128)(2,1)S(1)}, u32[]{:S(2)}, u32[]{:S(2)}) collective-permute-start(bf16[4,128,128]{2,1,0:T(8,128)(2,1)S(1)} %get-tuple-element.22), channel_id=1, source_target_pairs={{0,0},{16,32},{32,16},{48,64},{64,48},{80,96},{96,80},{112,128},{1... | collective-permute-start | bytes 393224 | tf_op jit(solution)/shard_map/ppermute | solution.py:276
  3.3 11.8 %collective-permute-start.7 = (bf16[27,16,128]{2,1,0:T(8,128)(2,1)S(1)}, bf16[27,16,128]{2,1,0:T(8,128)(2,1)S(1)}, u32[]{:S(2)}, u32[]{:S(2)}) collective-permute-start(bf16[27,16,128]{2,1,0:T(8,128)(2,1)S(1)} %bitcast.26), channel_id=1, source_target_pairs={{0,4},{1,5},{2,6},{3,7},{4,0},{5,1},{6,2},{7,3},{8,12},{9,13},{10,... | collective-permute-start | bytes 331784 | tf_op jit(solution)/shard_map/ppermute | solution.py:290
  5.0 14.1 %collective-permute-start.2 = (bf16[2,128,128]{2,1,0:T(8,128)(2,1)S(1)}, bf16[2,128,128]{2,1,0:T(8,128)(2,1)S(1)}, u32[]{:S(2)}, u32[]{:S(2)}) collective-permute-start(bf16[2,128,128]{2,1,0:T(8,128)(2,1)S(1)} %get-tuple-element.20), channel_id=1, source_target_pairs={{0,0},{1,2},{2,1},{3,4},{4,3},{5,6},{6,5},{7,8},{8,7},{9,10},{10,9... | collective-permute-start | bytes 196616 | tf_op jit(solution)/shard_map/ppermute | solution.py:278
  5.6 16.5 %collective-permute-start.3 = (bf16[2,128,128]{2,1,0:T(8,128)(2,1)S(1)}, bf16[2,128,128]{2,1,0:T(8,128)(2,1)S(1)}, u32[]{:S(2)}, u32[]{:S(2)}) collective-permute-start(bf16[2,128,128]{2,1,0:T(8,128)(2,1)S(1)} %get-tuple-element.19), channel_id=1, source_target_pairs={{0,1},{1,0},{2,3},{3,2},{4,5},{5,4},{6,7},{7,6},{8,9},{9,8},{10,11... | collective-permute-start | bytes 196616 | tf_op jit(solution)/shard_map/ppermute | solution.py:279
  10.8 11.4 %collective-permute-start.1 = (bf16[4,128,128]{2,1,0:T(8,128)(2,1)S(1)}, bf16[4,128,128]{2,1,0:T(8,128)(2,1)S(1)}, u32[]{:S(2)}, u32[]{:S(2)}) collective-permute-start(bf16[4,128,128]{2,1,0:T(8,128)(2,1)S(1)} %get-tuple-element.21), channel_id=1, source_target_pairs={{0,16},{16,0},{32,48},{48,32},{64,80},{80,64},{96,112},{112,96},{1... | collective-permute-start | bytes 393224 | tf_op jit(solution)/shard_map/ppermute | solution.py:277
  15.2 9.2 %collective-permute-start.8 = (bf16[2,27,16,128]{3,2,1,0:T(8,128)(2,1)S(1)}, bf16[2,27,16,128]{3,2,1,0:T(8,128)(2,1)S(1)}, u32[]{:S(2)}, u32[]{:S(2)}) collective-permute-start(bf16[2,27,16,128]{3,2,1,0:T(8,128)(2,1)S(1)} %pad_maximum_fusion.pair), channel_id=1, source_target_pairs={{0,12},{1,13},{2,14},{3,15},{4,8},{5,9},{6,10},{7,11},{8,4},{9,5},... | collective-permute-start | bytes 663560 | tf_op jit(solution)/shard_map/ppermute | solution.py:291
  18.4 5.9 %collective-permute-start.4 = (bf16[128,128]{1,0:T(8,128)(2,1)S(1)}, bf16[128,128]{1,0:T(8,128)(2,1)S(1)}, u32[]{:S(2)}, u32[]{:S(2)}) collective-permute-start(bf16[128,128]{1,0:T(8,128)(2,1)S(1)} %get-tuple-element.24.far_row), channel_id=1, source_target_pairs={{0,0},{1,2},{2,1},{3,4},{4,3},{5,6},{6,5},{7,8},{8,7},{9,10},{10,9... | collective-permute-start | bytes 98312 | tf_op jit(solution)/shard_map/ppermute | solution.py:282
  19.1 5.2 %collective-permute-start.5 = (bf16[128,128]{1,0:T(8,128)(2,1)S(1)}, bf16[128,128]{1,0:T(8,128)(2,1)S(1)}, u32[]{:S(2)}, u32[]{:S(2)}) collective-permute-start(bf16[128,128]{1,0:T(8,128)(2,1)S(1)} %get-tuple-element.23.near_row), channel_id=1, source_target_pairs={{0,1},{1,0},{2,3},{3,2},{4,5},{5,4},{6,7},{7,6},{8,9},{9,8},{10,11... | collective-permute-start | bytes 98312 | tf_op jit(solution)/shard_map/ppermute | solution.py:283
  22.1 0.7 %copy-start.2 = (f32[128]{0:T(128)S(1)}, f32[128]{0:T(128)}, u32[]{:S(2)}) copy-start(f32[128]{0:T(128)} %param.7) | copy-start | bytes 1540
  22.1 2.2 %collective-permute-start.6 = (bf16[2,128,128]{2,1,0:T(8,128)(2,1)S(1)}, bf16[2,128,128]{2,1,0:T(8,128)(2,1)S(1)}, u32[]{:S(2)}, u32[]{:S(2)}) collective-permute-start(bf16[2,128,128]{2,1,0:T(8,128)(2,1)S(1)} %shard_map.56), channel_id=1, source_target_pairs={{0,16},{16,0},{32,48},{48,32},{64,80},{80,64},{96,112},{112,96},{1... | collective-permute-start | bytes 196616 | tf_op jit(solution)/shard_map/ppermute | solution.py:284
  39.1 3.4 %collective-permute-start.9 = (bf16[4,2,64,128]{3,2,1,0:T(8,128)(2,1)S(1)}, bf16[4,2,64,128]{3,2,1,0:T(8,128)(2,1)S(1)}, u32[]{:S(2)}, u32[]{:S(2)}) collective-permute-start(bf16[4,2,64,128]{3,2,1,0:T(8,128)(2,1)S(1)} %dynamic-slice_bitcast_fusion), channel_id=1, source_target_pairs={{0,16},{16,0},{32,48},{48,32},{64,80},{80,64},{96,112},{112,96},{1... | collective-permute-start | bytes 393224 | tf_op jit(solution)/shard_map/ppermute | solution.py:298
  43.0 5.9 %collective-permute-start.10 = (f32[16,640]{1,0:T(8,128)S(1)}, f32[16,640]{1,0:T(8,128)S(1)}, u32[]{:S(2)}, u32[]{:S(2)}) collective-permute-start(f32[16,640]{1,0:T(8,128)S(1)} %get-tuple-element.16), channel_id=1, source_target_pairs={{0,8},{1,9},{2,10},{3,11},{4,12},{5,13},{6,14},{7,15},{8,0},{9,1},... | collective-permute-start | bytes 122888 | tf_op jit(solution)/shard_map/ppermute | solution.py:300
  46.8 5.2 %collective-permute-start.11 = (f32[16,640]{1,0:T(8,128)S(1)}, f32[16,640]{1,0:T(8,128)S(1)}, u32[]{:S(2)}, u32[]{:S(2)}) collective-permute-start(f32[16,640]{1,0:T(8,128)S(1)} %get-tuple-element.17), channel_id=1, source_target_pairs={{0,12},{1,13},{2,14},{3,15},{4,8},{5,9},{6,10},{7,11},{8,4},{9,5},... | collective-permute-start | bytes 122888 | tf_op jit(solution)/shard_map/ppermute | solution.py:300
  47.6 4.4 %copy-start.4 = (f32[16]{0:T(128)S(1)}, f32[16]{0:T(128)}, u32[]{:S(2)}) copy-start(f32[16]{0:T(128)} %param.9) | copy-start | bytes 196
  47.6 4.4 %collective-permute-start.12 = (f32[16,640]{1,0:T(8,128)S(1)}, f32[16,640]{1,0:T(8,128)S(1)}, u32[]{:S(2)}, u32[]{:S(2)}) collective-permute-start(f32[16,640]{1,0:T(8,128)S(1)} %get-tuple-element.18), channel_id=1, source_target_pairs={{0,4},{1,5},{2,6},{3,7},{4,0},{5,1},{6,2},{7,3},{8,12},{9,13},{10,... | collective-permute-start | bytes 122888 | tf_op jit(solution)/shard_map/ppermute | solution.py:300

commit v16 on v15

--- a/solution.py
+++ b/solution.py
@@ -25,6 +25,20 @@
 def inner(axis):
     i = lax.axis_index(axis)
     return (i > 0) & (i < 15)
+
+
+def far_plane_kernel(vol, out):
+    out[...] = vol[lax.rem(lax.axis_index("depth"), 2)]
+
+
+def far_plane(vol):
+    return pl.pallas_call(
+        far_plane_kernel,
+        out_shape=jax.ShapeDtypeStruct(vol.shape[1:], BF16),
+        in_specs=[pl.BlockSpec(memory_space=pltpu.VMEM)],
+        out_specs=pl.BlockSpec(memory_space=pltpu.VMEM),
+        compiler_params=pltpu.CompilerParams(vmem_limit_bytes=2 * 1024 * 1024),
+    )(vol)
 
 
 def spread(line, col):
@@ -273,7 +287,7 @@
     depth_near, depth_far = near_pairs(16), far_pairs(16)
     rows_near, rows_far = near_pairs(16), far_pairs(16)
 
-    x2 = lax.ppermute(lax.dynamic_index_in_dim(volume, pd, 0, False), "depth", depth_far)
+    x2 = lax.ppermute(far_plane(volume), "depth", depth_far)
     x1 = lax.ppermute(lax.dynamic_index_in_dim(volume, 1 - pd, 0, False), "depth", depth_near)
     r2 = lax.ppermute(lax.dynamic_index_in_dim(volume, 3 * pr, 1, False), "rows", rows_far)
     r1 = lax.ppermute(lax.dynamic_index_in_dim(volume, 3 - 3 * pr, 1, False), "rows", rows_near)

time: 53 us -> 57 us (1.075); the launches traced: 52.7 us -> 56 us
  starting transfers between devices: 28 us -> 31.9 us
  other arithmetic: 0.02 us -> 0.92 us
  local copies, waits for them, and re-layouts: 1.73 us -> 1.08 us
  blocking collectives: 14.5 us -> 13.9 us
    ppermute x1, starting transfers between devices: 2.44 us -> 4.25 us  [body(): lax.ppermute(lax.dynamic_index_in_dim(both, 1 - pd, 0, False), 'depth', d...]
    ppermute x1, starting transfers between devices: 0.09 us -> 1.49 us  [body(): e = lax.ppermute(outer_rows(far_row, near_row, r2, r1), 'depth', depth_near)]
    ppermute x1, starting transfers between devices: 2.99 us -> 4.1 us  [body(): c1 = lax.ppermute(near_row, 'rows', rows_near)]
    squeeze x1, local copies, waits for them, and re-layouts: 1.09 us -> 0.01 us  [body(): lax.dynamic_index_in_dim(volume, 1 - pd, 0, False)]
    another operation x1, other arithmetic: 0.02 us -> 0.92 us  [body(): pair = jnp.stack([w, lax.ppermute(w, 'rows', along_y(1))])]
    ppermute x1, starting transfers between devices: 1.66 us -> 2.35 us  [body(): pair = jnp.stack([w, lax.ppermute(w, 'rows', along_y(1))])]
  transfers between devices with their start and end apart: 13 -> 13, of which waited for: 3 -> 3; matrix products, arithmetic and copies ran while one was open for 0% -> 2% of each run, Pallas kernels for 4% -> 4%
where the time goes in v16:
time: 57 us; the launch traced here: 56 us
  starting transfers between devices  31.9 us (56%)
  blocking collectives  13.9 us (24%)
  waiting for transfers between devices  4.44 us (8%)
  Pallas kernels  3.51 us (6%)
  local copies, waits for them, and re-layouts  1.08 us (2%)
  other arithmetic  0.92 us (2%)
    all_to_all x1, blocking collectives, body(): lax.all_to_all(pooled, ('depth', 'rows'), 0, 0, axis_index_groups=far_and...  13.9 us
    ppermute x1, starting transfers between devices, body(): lax.ppermute(lax.dynamic_index_in_dim(volume, 3 - 3 * pr, 1, False), 'row...  5.17 us
    ppermute x1, starting transfers between devices, body(): lax.ppermute(lax.dynamic_index_in_dim(both, 1 - pd, 0, False), 'depth', d...  4.25 us
    ppermute x3, starting transfers between devices, body(): lax.ppermute(sums[k], 'rows', along_y(k))  4.18 us
    ppermute x1, starting transfers between devices, body(): c1 = lax.ppermute(near_row, 'rows', rows_near)  4.1 us
    ppermute x3, waiting for transfers between devices, body(): lax.ppermute(sums[k], 'rows', along_y(k))  4.02 us
    ppermute x1, starting transfers between devices, body(): lax.ppermute(lax.dynamic_index_in_dim(volume, 1 - pd, 0, False), 'depth',...  3.78 us
    ppermute x1, starting transfers between devices, body(): other = lax.ppermute(pair, 'rows', along_y(3))  2.98 us
  transfers between devices with their start and end apart: 13, of which 3 were waited for; matrix products, arithmetic and copies ran while one was open for 2% of the time, Pallas kernels for 4%

profile of v16, /device:TPU:6, one launch (start us, length us, event | category | flops | bytes accessed | tf_op | source)
XLA Modules:
  0.0 56.0 jit_solution(4648967629218781809)
XLA Ops:
  0.0 0.9 %copy-done = bf16[2,4,128,128]{3,2,1,0:T(8,128)(2,1)S(1)} copy-done((bf16[2,4,128,128]{3,2,1,0:T(8,128)(2,1)S(1)}, bf16[2,4,128,128]{3,2,1,0:T(8,128)(2,1)}, u32[]{:S(2)}) %copy-start) | copy-done | bytes 262168
  1.0 2.3 %collective-permute-start = (bf16[4,128,128]{2,1,0:T(8,128)(2,1)S(1)}, bf16[4,128,128]{2,1,0:T(8,128)(2,1)S(1)}, u32[]{:S(2)}, u32[]{:S(2)}) collective-permute-start(bf16[4,128,128]{2,1,0:T(8,128)(2,1)S(1)} %shard_map.55), channel_id=1, source_target_pairs={{0,0},{16,32},{32,16},{48,64},{64,48},{80,96},{96,80},{112,128},{1... | collective-permute-start | bytes 393224 | tf_op jit(solution)/shard_map/ppermute | solution.py:290
  3.3 0.7 %collective-permute-start.2 = (bf16[2,128,128]{2,1,0:T(8,128)(2,1)S(1)}, bf16[2,128,128]{2,1,0:T(8,128)(2,1)S(1)}, u32[]{:S(2)}, u32[]{:S(2)}) collective-permute-start(bf16[2,128,128]{2,1,0:T(8,128)(2,1)S(1)} %get-tuple-element.20), channel_id=1, source_target_pairs={{0,0},{1,2},{2,1},{3,4},{4,3},{5,6},{6,5},{7,8},{8,7},{9,10},{10,9... | collective-permute-start | bytes 196616 | tf_op jit(solution)/shard_map/ppermute | solution.py:292
  4.0 5.2 %collective-permute-start.3 = (bf16[2,128,128]{2,1,0:T(8,128)(2,1)S(1)}, bf16[2,128,128]{2,1,0:T(8,128)(2,1)S(1)}, u32[]{:S(2)}, u32[]{:S(2)}) collective-permute-start(bf16[2,128,128]{2,1,0:T(8,128)(2,1)S(1)} %get-tuple-element.19), channel_id=1, source_target_pairs={{0,1},{1,0},{2,3},{3,2},{4,5},{5,4},{6,7},{7,6},{8,9},{9,8},{10,11... | collective-permute-start | bytes 196616 | tf_op jit(solution)/shard_map/ppermute | solution.py:293
  9.2 2.4 %collective-permute-start.7 = (bf16[27,16,128]{2,1,0:T(8,128)(2,1)}, bf16[27,16,128]{2,1,0:T(8,128)(2,1)S(1)}, u32[]{:S(2)}, u32[]{:S(2)}) collective-permute-start(bf16[27,16,128]{2,1,0:T(8,128)(2,1)} %bitcast.24), channel_id=1, source_target_pairs={{0,4},{1,5},{2,6},{3,7},{4,0},{5,1},{6,2},{7,3},{8,12},{9,13},{10,... | collective-permute-start | bytes 331784 | tf_op jit(solution)/shard_map/ppermute | solution.py:304
  11.5 3.8 %collective-permute-start.1 = (bf16[4,128,128]{2,1,0:T(8,128)(2,1)S(1)}, bf16[4,128,128]{2,1,0:T(8,128)(2,1)S(1)}, u32[]{:S(2)}, u32[]{:S(2)}) collective-permute-start(bf16[4,128,128]{2,1,0:T(8,128)(2,1)S(1)} %dynamic-slice_bitcast_fusion.1), channel_id=1, source_target_pairs={{0,16},{16,0},{32,48},{48,32},{64,80},{80,64},{96,112},{112,96},{1... | collective-permute-start | bytes 393224 | tf_op jit(solution)/shard_map/ppermute | solution.py:291
  15.3 0.9 %pad_maximum_fusion.pair = bf16[2,27,16,128]{3,2,1,0:T(8,128)(2,1)S(1)} fusion(bf16[1,27,16,128]{3,2,1,0:T(8,128)(2,1)S(1)} %bitcast.26, bf16[1,27,16,128]{3,2,1,0:T(8,128)(2,1)} %bitcast.25), kind=kLoop, calls=%fused_computation | loop fusion | flops 110592 | bytes 442368 | tf_op jit(solution)/shard_map/stack | solution.py:304
  16.2 3.0 %collective-permute-start.8 = (bf16[2,27,16,128]{3,2,1,0:T(8,128)(2,1)S(1)}, bf16[2,27,16,128]{3,2,1,0:T(8,128)(2,1)S(1)}, u32[]{:S(2)}, u32[]{:S(2)}) collective-permute-start(bf16[2,27,16,128]{3,2,1,0:T(8,128)(2,1)S(1)} %pad_maximum_fusion.pair), channel_id=1, source_target_pairs={{0,12},{1,13},{2,14},{3,15},{4,8},{5,9},{6,10},{7,11},{8,4},{9,5},... | collective-permute-start | bytes 663560 | tf_op jit(solution)/shard_map/ppermute | solution.py:305
  19.2 0.7 %collective-permute-start.4 = (bf16[128,128]{1,0:T(8,128)(2,1)S(1)}, bf16[128,128]{1,0:T(8,128)(2,1)S(1)}, u32[]{:S(2)}, u32[]{:S(2)}) collective-permute-start(bf16[128,128]{1,0:T(8,128)(2,1)S(1)} %get-tuple-element.22.far_row), channel_id=1, source_target_pairs={{0,0},{1,2},{2,1},{3,4},{4,3},{5,6},{6,5},{7,8},{8,7},{9,10},{10,9... | collective-permute-start | bytes 98312 | tf_op jit(solution)/shard_map/ppermute | solution.py:296
  19.9 4.1 %collective-permute-start.5 = (bf16[128,128]{1,0:T(8,128)(2,1)S(1)}, bf16[128,128]{1,0:T(8,128)(2,1)S(1)}, u32[]{:S(2)}, u32[]{:S(2)}) collective-permute-start(bf16[128,128]{1,0:T(8,128)(2,1)S(1)} %get-tuple-element.21.near_row), channel_id=1, source_target_pairs={{0,1},{1,0},{2,3},{3,2},{4,5},{5,4},{6,7},{7,6},{8,9},{9,8},{10,11... | collective-permute-start | bytes 98312 | tf_op jit(solution)/shard_map/ppermute | solution.py:297
  24.0 1.5 %collective-permute-start.6 = (bf16[2,128,128]{2,1,0:T(8,128)(2,1)S(1)}, bf16[2,128,128]{2,1,0:T(8,128)(2,1)S(1)}, u32[]{:S(2)}, u32[]{:S(2)}) collective-permute-start(bf16[2,128,128]{2,1,0:T(8,128)(2,1)S(1)} %shard_map.57), channel_id=1, source_target_pairs={{0,16},{16,0},{32,48},{48,32},{64,80},{80,64},{96,112},{112,96},{1... | collective-permute-start | bytes 196616 | tf_op jit(solution)/shard_map/ppermute | solution.py:298
  25.5 1.5 %shard_map.56 = (f32[2,2,128,128]{3,2,1,0:T(8,128)S(1)}, f32[2,128,128]{2,1,0:T(8,128)S(1)}, bf16[2,2,128,384]{3,2,1,0:T(8,128)(2,1)S(1)}) custom-call(bf16[2,4,128,128]{3,2,1,0:T(8,128)(2,1)S(1)} %copy-done.1, bf16[4,128,128]{2,1,0:T(8,128)(2,1)S(1)} %collective-permute-done.x2, bf16[4,128,128]{2,1,0:T(8,128)(2,1)S(1)} %collective-permute-done.1.x1, ...), custom_call_target="tpu_custom_call" | custom-call | flops 20000000000 | tf_op jit(solution)/shard_map/pallas_call | solution.py:102
  27.1 0.3 shard_map.58
  27.4 13.9 %all_to_all.5 = bf16[8,2,64,128]{3,2,1,0:T(8,128)(2,1)S(1)} all-to-all(bf16[8,2,64,128]{3,2,1,0:T(8,128)(2,1)S(1)} %shard_map.58), channel_id=1, replica_groups={{16,17,18,19,32,33,34,35},{20,21,22,23,36,37,38,39},{24,25,26,27,40,41,..., dimensions={0} | all-to-all | bytes 524288 | tf_op jit(solution)/shard_map/all_to_all | solution.py:309
  41.4 4.2 %collective-permute-start.9 = (bf16[4,2,64,128]{3,2,1,0:T(8,128)(2,1)S(1)}, bf16[4,2,64,128]{3,2,1,0:T(8,128)(2,1)S(1)}, u32[]{:S(2)}, u32[]{:S(2)}) collective-permute-start(bf16[4,2,64,128]{3,2,1,0:T(8,128)(2,1)S(1)} %dynamic-slice_bitcast_fusion), channel_id=1, source_target_pairs={{0,16},{16,0},{32,48},{48,32},{64,80},{80,64},{96,112},{112,96},{1... | collective-permute-start | bytes 393224 | tf_op jit(solution)/shard_map/ppermute | solution.py:312
  45.6 0.6 %shard_map.59.sums = f32[64,640]{1,0:T(8,128)S(1)} custom-call(bf16[2,4,2,64,128]{4,3,2,1,0:T(8,128)(2,1)S(1)} %bitcast.22, bf16[2,27,16,128]{3,2,1,0:T(8,128)(2,1)S(1)} %pad_maximum_fusion.pair, bf16[2,27,16,128]{3,2,1,0:T(8,128)(2,1)S(1)} %collective-permute-done.8.other), custom_call_target="tpu_custom_call" | custom-call | flops 150000000 | tf_op jit(solution)/shard_map/pallas_call | solution.py:216
  46.2 0.4 collective-permute-done.9.near
  46.6 0.4 shard_map.60
  47.0 3.0 %collective-permute-start.10 = (f32[16,640]{1,0:T(8,128)S(1)}, f32[16,640]{1,0:T(8,128)S(1)}, u32[]{:S(2)}, u32[]{:S(2)}) collective-permute-start(f32[16,640]{1,0:T(8,128)S(1)} %get-tuple-element.16), channel_id=1, source_target_pairs={{0,8},{1,9},{2,10},{3,11},{4,12},{5,13},{6,14},{7,15},{8,0},{9,1},... | collective-permute-start | bytes 122888 | tf_op jit(solution)/shard_map/ppermute | solution.py:314
  50.0 1.2 %collective-permute-start.11 = (f32[16,640]{1,0:T(8,128)S(1)}, f32[16,640]{1,0:T(8,128)S(1)}, u32[]{:S(2)}, u32[]{:S(2)}) collective-permute-start(f32[16,640]{1,0:T(8,128)S(1)} %get-tuple-element.17), channel_id=1, source_target_pairs={{0,12},{1,13},{2,14},{3,15},{4,8},{5,9},{6,10},{7,11},{8,4},{9,5},... | collective-permute-start | bytes 122888 | tf_op jit(solution)/shard_map/ppermute | solution.py:314
  51.2 1.4 %collective-permute-done.10.s2 = f32[16,640]{1,0:T(8,128)S(1)} collective-permute-done((f32[16,640]{1,0:T(8,128)S(1)}, f32[16,640]{1,0:T(8,128)S(1)}, u32[]{:S(2)}, u32[]{:S(2)}) %collective-permute-start.10) | collective-permute-done | bytes 40992 | tf_op jit(solution)/shard_map/ppermute | solution.py:314
  52.6 2.6 %collective-permute-done.11.s3 = f32[16,640]{1,0:T(8,128)S(1)} collective-permute-done((f32[16,640]{1,0:T(8,128)S(1)}, f32[16,640]{1,0:T(8,128)S(1)}, u32[]{:S(2)}, u32[]{:S(2)}) %collective-permute-start.11) | collective-permute-done | bytes 40992 | tf_op jit(solution)/shard_map/ppermute | solution.py:314
  55.2 0.1 broadcast_in_dim.2.bias
  55.3 0.7 %shard_map.61 = bf16[16,2048]{1,0:T(8,128)(2,1)} custom-call(f32[16,640]{1,0:T(8,128)S(1)} %get-tuple-element.15.s0, f32[16,640]{1,0:T(8,128)S(1)} %collective-permute-done.10.s2, f32[16,640]{1,0:T(8,128)S(1)} %collective-permute-done.11.s3, f32[16,640]{1,0:T(8,128)S(1)} %collective-permute-done.12.s1, f32[16,128]{1,0:T(8,128)S(1)} %broadcast_in_dim.2.bias), custom_call_target="tpu_custom_call" | custom-call | tf_op jit(solution)/shard_map/pallas_call | solution.py:272
  (26 shorter events, 0.1 us)
Async XLA Ops:
  0.0 0.9 %copy-start = (bf16[2,4,128,128]{3,2,1,0:T(8,128)(2,1)S(1)}, bf16[2,4,128,128]{3,2,1,0:T(8,128)(2,1)}, u32[]{:S(2)}) copy-start(bf16[2,4,128,128]{3,2,1,0:T(8,128)(2,1)} %vol.3) | copy-start | bytes 786436
  1.0 2.3 %copy-start.1 = (bf16[2,4,128,128]{3,2,1,0:T(8,128)(2,1)S(1)}, bf16[2,4,128,128]{3,2,1,0:T(8,128)(2,1)}, u32[]{:S(2)}) copy-start(bf16[2,4,128,128]{3,2,1,0:T(8,128)(2,1)} %vol.3) | copy-start | bytes 786436
  1.0 24.6 %copy-start.2 = (bf16[3,3,3,128,128]{4,3,2,1,0:T(8,128)(2,1)S(1)}, bf16[3,3,3,128,128]{4,3,2,1,0:T(8,128)(2,1)}, u32[]{:S(2)}) copy-start(bf16[3,3,3,128,128]{4,3,2,1,0:T(8,128)(2,1)} %w.1) | copy-start | bytes 2654212
  1.0 18.3 %collective-permute-start = (bf16[4,128,128]{2,1,0:T(8,128)(2,1)S(1)}, bf16[4,128,128]{2,1,0:T(8,128)(2,1)S(1)}, u32[]{:S(2)}, u32[]{:S(2)}) collective-permute-start(bf16[4,128,128]{2,1,0:T(8,128)(2,1)S(1)} %shard_map.55), channel_id=1, source_target_pairs={{0,0},{16,32},{32,16},{48,64},{64,48},{80,96},{96,80},{112,128},{1... | collective-permute-start | bytes 393224 | tf_op jit(solution)/shard_map/ppermute | solution.py:290
  3.3 16.6 %collective-permute-start.2 = (bf16[2,128,128]{2,1,0:T(8,128)(2,1)S(1)}, bf16[2,128,128]{2,1,0:T(8,128)(2,1)S(1)}, u32[]{:S(2)}, u32[]{:S(2)}) collective-permute-start(bf16[2,128,128]{2,1,0:T(8,128)(2,1)S(1)} %get-tuple-element.20), channel_id=1, source_target_pairs={{0,0},{1,2},{2,1},{3,4},{4,3},{5,6},{6,5},{7,8},{8,7},{9,10},{10,9... | collective-permute-start | bytes 196616 | tf_op jit(solution)/shard_map/ppermute | solution.py:292
  4.0 20.0 %collective-permute-start.3 = (bf16[2,128,128]{2,1,0:T(8,128)(2,1)S(1)}, bf16[2,128,128]{2,1,0:T(8,128)(2,1)S(1)}, u32[]{:S(2)}, u32[]{:S(2)}) collective-permute-start(bf16[2,128,128]{2,1,0:T(8,128)(2,1)S(1)} %get-tuple-element.19), channel_id=1, source_target_pairs={{0,1},{1,0},{2,3},{3,2},{4,5},{5,4},{6,7},{7,6},{8,9},{9,8},{10,11... | collective-permute-start | bytes 196616 | tf_op jit(solution)/shard_map/ppermute | solution.py:293
  9.2 6.2 %collective-permute-start.7 = (bf16[27,16,128]{2,1,0:T(8,128)(2,1)}, bf16[27,16,128]{2,1,0:T(8,128)(2,1)S(1)}, u32[]{:S(2)}, u32[]{:S(2)}) collective-permute-start(bf16[27,16,128]{2,1,0:T(8,128)(2,1)} %bitcast.24), channel_id=1, source_target_pairs={{0,4},{1,5},{2,6},{3,7},{4,0},{5,1},{6,2},{7,3},{8,12},{9,13},{10,... | collective-permute-start | bytes 331784 | tf_op jit(solution)/shard_map/ppermute | solution.py:304
  11.5 14.0 %collective-permute-start.1 = (bf16[4,128,128]{2,1,0:T(8,128)(2,1)S(1)}, bf16[4,128,128]{2,1,0:T(8,128)(2,1)S(1)}, u32[]{:S(2)}, u32[]{:S(2)}) collective-permute-start(bf16[4,128,128]{2,1,0:T(8,128)(2,1)S(1)} %dynamic-slice_bitcast_fusion.1), channel_id=1, source_target_pairs={{0,16},{16,0},{32,48},{48,32},{64,80},{80,64},{96,112},{112,96},{1... | collective-permute-start | bytes 393224 | tf_op jit(solution)/shard_map/ppermute | solution.py:291
  16.2 10.9 %collective-permute-start.8 = (bf16[2,27,16,128]{3,2,1,0:T(8,128)(2,1)S(1)}, bf16[2,27,16,128]{3,2,1,0:T(8,128)(2,1)S(1)}, u32[]{:S(2)}, u32[]{:S(2)}) collective-permute-start(bf16[2,27,16,128]{3,2,1,0:T(8,128)(2,1)S(1)} %pad_maximum_fusion.pair), channel_id=1, source_target_pairs={{0,12},{1,13},{2,14},{3,15},{4,8},{5,9},{6,10},{7,11},{8,4},{9,5},... | collective-permute-start | bytes 663560 | tf_op jit(solution)/shard_map/ppermute | solution.py:305
  19.2 7.8 %collective-permute-start.4 = (bf16[128,128]{1,0:T(8,128)(2,1)S(1)}, bf16[128,128]{1,0:T(8,128)(2,1)S(1)}, u32[]{:S(2)}, u32[]{:S(2)}) collective-permute-start(bf16[128,128]{1,0:T(8,128)(2,1)S(1)} %get-tuple-element.22.far_row), channel_id=1, source_target_pairs={{0,0},{1,2},{2,1},{3,4},{4,3},{5,6},{6,5},{7,8},{8,7},{9,10},{10,9... | collective-permute-start | bytes 98312 | tf_op jit(solution)/shard_map/ppermute | solution.py:296
  19.9 7.2 %collective-permute-start.5 = (bf16[128,128]{1,0:T(8,128)(2,1)S(1)}, bf16[128,128]{1,0:T(8,128)(2,1)S(1)}, u32[]{:S(2)}, u32[]{:S(2)}) collective-permute-start(bf16[128,128]{1,0:T(8,128)(2,1)S(1)} %get-tuple-element.21.near_row), channel_id=1, source_target_pairs={{0,1},{1,0},{2,3},{3,2},{4,5},{5,4},{6,7},{7,6},{8,9},{9,8},{10,11... | collective-permute-start | bytes 98312 | tf_op jit(solution)/shard_map/ppermute | solution.py:297
  24.0 1.5 %copy-start.3 = (f32[128]{0:T(128)S(1)}, f32[128]{0:T(128)}, u32[]{:S(2)}) copy-start(f32[128]{0:T(128)} %param.7) | copy-start | bytes 1540
  24.0 3.0 %collective-permute-start.6 = (bf16[2,128,128]{2,1,0:T(8,128)(2,1)S(1)}, bf16[2,128,128]{2,1,0:T(8,128)(2,1)S(1)}, u32[]{:S(2)}, u32[]{:S(2)}) collective-permute-start(bf16[2,128,128]{2,1,0:T(8,128)(2,1)S(1)} %shard_map.57), channel_id=1, source_target_pairs={{0,16},{16,0},{32,48},{48,32},{64,80},{80,64},{96,112},{112,96},{1... | collective-permute-start | bytes 196616 | tf_op jit(solution)/shard_map/ppermute | solution.py:298
  41.4 5.2 %collective-permute-start.9 = (bf16[4,2,64,128]{3,2,1,0:T(8,128)(2,1)S(1)}, bf16[4,2,64,128]{3,2,1,0:T(8,128)(2,1)S(1)}, u32[]{:S(2)}, u32[]{:S(2)}) collective-permute-start(bf16[4,2,64,128]{3,2,1,0:T(8,128)(2,1)S(1)} %dynamic-slice_bitcast_fusion), channel_id=1, source_target_pairs={{0,16},{16,0},{32,48},{48,32},{64,80},{80,64},{96,112},{112,96},{1... | collective-permute-start | bytes 393224 | tf_op jit(solution)/shard_map/ppermute | solution.py:312
  47.0 5.6 %collective-permute-start.10 = (f32[16,640]{1,0:T(8,128)S(1)}, f32[16,640]{1,0:T(8,128)S(1)}, u32[]{:S(2)}, u32[]{:S(2)}) collective-permute-start(f32[16,640]{1,0:T(8,128)S(1)} %get-tuple-element.16), channel_id=1, source_target_pairs={{0,8},{1,9},{2,10},{3,11},{4,12},{5,13},{6,14},{7,15},{8,0},{9,1},... | collective-permute-start | bytes 122888 | tf_op jit(solution)/shard_map/ppermute | solution.py:314
  50.0 5.2 %collective-permute-start.11 = (f32[16,640]{1,0:T(8,128)S(1)}, f32[16,640]{1,0:T(8,128)S(1)}, u32[]{:S(2)}, u32[]{:S(2)}) collective-permute-start(f32[16,640]{1,0:T(8,128)S(1)} %get-tuple-element.17), channel_id=1, source_target_pairs={{0,12},{1,13},{2,14},{3,15},{4,8},{5,9},{6,10},{7,11},{8,4},{9,5},... | collective-permute-start | bytes 122888 | tf_op jit(solution)/shard_map/ppermute | solution.py:314
  51.2 4.0 %copy-start.4 = (f32[16]{0:T(128)S(1)}, f32[16]{0:T(128)}, u32[]{:S(2)}) copy-start(f32[16]{0:T(128)} %param.9) | copy-start | bytes 196
  51.2 4.0 %collective-permute-start.12 = (f32[16,640]{1,0:T(8,128)S(1)}, f32[16,640]{1,0:T(8,128)S(1)}, u32[]{:S(2)}, u32[]{:S(2)}) collective-permute-start(f32[16,640]{1,0:T(8,128)S(1)} %get-tuple-element.18), channel_id=1, source_target_pairs={{0,4},{1,5},{2,6},{3,7},{4,0},{5,1},{6,2},{7,3},{8,12},{9,13},{10,... | collective-permute-start | bytes 122888 | tf_op jit(solution)/shard_map/ppermute | solution.py:314

commit v17 on v15

--- a/solution.py
+++ b/solution.py
@@ -277,8 +277,9 @@
     x1 = lax.ppermute(lax.dynamic_index_in_dim(volume, 1 - pd, 0, False), "depth", depth_near)
     r2 = lax.ppermute(lax.dynamic_index_in_dim(volume, 3 * pr, 1, False), "rows", rows_far)
     r1 = lax.ppermute(lax.dynamic_index_in_dim(volume, 3 - 3 * pr, 1, False), "rows", rows_near)
-    far_row = lax.dynamic_index_in_dim(x2, 3 * pr, 0, False)
-    near_row = lax.dynamic_index_in_dim(x2, 3 - 3 * pr, 0, False)
+    sides = jnp.stack([x2, x1])
+    far_row = lax.dynamic_index_in_dim(sides, 3 * pr, 1, False)[0]
+    near_row = lax.dynamic_index_in_dim(sides, 3 - 3 * pr, 1, False)[0]
     c2 = lax.ppermute(far_row, "rows", rows_far)
     c1 = lax.ppermute(near_row, "rows", rows_near)
     e = lax.ppermute(outer_rows(far_row, near_row, r2, r1), "depth", depth_near)

time: 53 us -> 52.6 us (level)
  starting transfers between devices: 28 us -> 29 us
  blocking collectives: 14.5 us -> 13.6 us
    ppermute x1, starting transfers between devices: 4.31 us -> 7.04 us  [body(): lax.ppermute(lax.dynamic_index_in_dim(volume, 1 - pd, 0, False), 'depth',...]
    ppermute x1, starting transfers between devices: 5.17 us -> 3.37 us  [body(): lax.ppermute(lax.dynamic_index_in_dim(volume, 3 - 3 * pr, 1, False), 'row...]
    all_to_all x1, blocking collectives: 14.5 us -> 13.6 us  [body(): lax.all_to_all(pooled, ('depth', 'rows'), 0, 0, axis_index_groups=far_and...]
  transfers between devices with their start and end apart: 13 -> 13, of which waited for: 3 -> 4; matrix products, arithmetic and copies ran while one was open for 0% -> 0% of each run, Pallas kernels for 4% -> 4%
where the time goes in v17:
time: 52.6 us; the launch traced here: 52.4 us
  starting transfers between devices  29 us (55%)
  blocking collectives  13.6 us (26%)
  waiting for transfers between devices  4.42 us (8%)
  Pallas kernels  3.48 us (7%)
  local copies, waits for them, and re-layouts  1.73 us (3%)
    all_to_all x1, blocking collectives, body(): lax.all_to_all(pooled, ('depth', 'rows'), 0, 0, axis_index_groups=far_and...  13.6 us
    ppermute x1, starting transfers between devices, body(): lax.ppermute(lax.dynamic_index_in_dim(volume, 1 - pd, 0, False), 'depth',...  7.04 us
    ppermute x3, starting transfers between devices, body(): lax.ppermute(sums[k], 'rows', along_y(k))  4.85 us
    ppermute x3, waiting for transfers between devices, body(): lax.ppermute(sums[k], 'rows', along_y(k))  4 us
    ppermute x1, starting transfers between devices, body(): lax.ppermute(lax.dynamic_index_in_dim(volume, 3 - 3 * pr, 1, False), 'row...  3.37 us
    ppermute x1, starting transfers between devices, body(): c1 = lax.ppermute(near_row, 'rows', rows_near)  3.34 us
    ppermute x1, starting transfers between devices, body(): other = lax.ppermute(pair, 'rows', along_y(3))  2.9 us
    ppermute x1, starting transfers between devices, body(): lax.ppermute(lax.dynamic_index_in_dim(both, 1 - pd, 0, False), 'depth', d...  2.28 us
  transfers between devices with their start and end apart: 13, of which 4 were waited for; matrix products, arithmetic and copies ran while one was open for 0% of the time, Pallas kernels for 4%

profile of v17, /device:TPU:6, one launch (start us, length us, event | category | flops | bytes accessed | tf_op | source)
XLA Modules:
  0.0 52.4 jit_solution(12587256094252155323)
XLA Ops:
  0.0 1.1 %dynamic-slice_bitcast_fusion.1 = (bf16[4,128,128]{2,1,0:T(8,128)(2,1)S(1)}, bf16[4,128,128]{2,1,0:T(8,128)(2,1)S(1)}) fusion(bf16[2,4,128,128]{3,2,1,0:T(8,128)(2,1)} %vol.1, s32[]{:T(128)S(6)} %select_n.19, s32[]{:T(128)S(6)} %select_n.18), kind=kLoop, calls=%fused_computation.6 | loop fusion | bytes 524296 | tf_op jit(solution)/shard_map/jit(dynamic_index_in_dim)/squeeze | solution.py:277
  1.1 2.2 %collective-permute-start = (bf16[4,128,128]{2,1,0:T(8,128)(2,1)S(1)}, bf16[4,128,128]{2,1,0:T(8,128)(2,1)S(1)}, u32[]{:S(2)}, u32[]{:S(2)}) collective-permute-start(bf16[4,128,128]{2,1,0:T(8,128)(2,1)S(1)} %get-tuple-element.24), channel_id=1, source_target_pairs={{0,0},{16,32},{32,16},{48,64},{64,48},{80,96},{96,80},{112,128},{1... | collective-permute-start | bytes 393224 | tf_op jit(solution)/shard_map/ppermute | solution.py:276
  3.3 7.0 %collective-permute-start.1 = (bf16[4,128,128]{2,1,0:T(8,128)(2,1)S(1)}, bf16[4,128,128]{2,1,0:T(8,128)(2,1)S(1)}, u32[]{:S(2)}, u32[]{:S(2)}) collective-permute-start(bf16[4,128,128]{2,1,0:T(8,128)(2,1)S(1)} %get-tuple-element.23), channel_id=1, source_target_pairs={{0,16},{16,0},{32,48},{48,32},{64,80},{80,64},{96,112},{112,96},{1... | collective-permute-start | bytes 393224 | tf_op jit(solution)/shard_map/ppermute | solution.py:277
  10.3 1.6 %collective-permute-start.7 = (bf16[27,16,128]{2,1,0:T(8,128)(2,1)S(1)}, bf16[27,16,128]{2,1,0:T(8,128)(2,1)S(1)}, u32[]{:S(2)}, u32[]{:S(2)}) collective-permute-start(bf16[27,16,128]{2,1,0:T(8,128)(2,1)S(1)} %bitcast.30), channel_id=1, source_target_pairs={{0,4},{1,5},{2,6},{3,7},{4,0},{5,1},{6,2},{7,3},{8,12},{9,13},{10,... | collective-permute-start | bytes 331784 | tf_op jit(solution)/shard_map/ppermute | solution.py:291
  11.9 0.7 %collective-permute-start.2 = (bf16[2,128,128]{2,1,0:T(8,128)(2,1)S(1)}, bf16[2,128,128]{2,1,0:T(8,128)(2,1)S(1)}, u32[]{:S(2)}, u32[]{:S(2)}) collective-permute-start(bf16[2,128,128]{2,1,0:T(8,128)(2,1)S(1)} %get-tuple-element.22), channel_id=1, source_target_pairs={{0,0},{1,2},{2,1},{3,4},{4,3},{5,6},{6,5},{7,8},{8,7},{9,10},{10,9... | collective-permute-start | bytes 196616 | tf_op jit(solution)/shard_map/ppermute | solution.py:278
  12.6 3.4 %collective-permute-start.3 = (bf16[2,128,128]{2,1,0:T(8,128)(2,1)S(1)}, bf16[2,128,128]{2,1,0:T(8,128)(2,1)S(1)}, u32[]{:S(2)}, u32[]{:S(2)}) collective-permute-start(bf16[2,128,128]{2,1,0:T(8,128)(2,1)S(1)} %get-tuple-element.21), channel_id=1, source_target_pairs={{0,1},{1,0},{2,3},{3,2},{4,5},{5,4},{6,7},{7,6},{8,9},{9,8},{10,11... | collective-permute-start | bytes 196616 | tf_op jit(solution)/shard_map/ppermute | solution.py:279
  16.0 2.9 %collective-permute-start.8 = (bf16[2,27,16,128]{3,2,1,0:T(8,128)(2,1)S(1)}, bf16[2,27,16,128]{3,2,1,0:T(8,128)(2,1)S(1)}, u32[]{:S(2)}, u32[]{:S(2)}) collective-permute-start(bf16[2,27,16,128]{3,2,1,0:T(8,128)(2,1)S(1)} %pad_maximum_fusion.pair), channel_id=1, source_target_pairs={{0,12},{1,13},{2,14},{3,15},{4,8},{5,9},{6,10},{7,11},{8,4},{9,5},... | collective-permute-start | bytes 663560 | tf_op jit(solution)/shard_map/ppermute | solution.py:292
  18.9 0.7 %collective-permute-start.4 = (bf16[128,128]{1,0:T(8,128)(2,1)S(1)}, bf16[128,128]{1,0:T(8,128)(2,1)S(1)}, u32[]{:S(2)}, u32[]{:S(2)}) collective-permute-start(bf16[128,128]{1,0:T(8,128)(2,1)S(1)} %get-tuple-element.20.far_row), channel_id=1, source_target_pairs={{0,0},{1,2},{2,1},{3,4},{4,3},{5,6},{6,5},{7,8},{8,7},{9,10},{10,9... | collective-permute-start | bytes 98312 | tf_op jit(solution)/shard_map/ppermute | solution.py:283
  19.6 3.3 %collective-permute-start.5 = (bf16[128,128]{1,0:T(8,128)(2,1)S(1)}, bf16[128,128]{1,0:T(8,128)(2,1)S(1)}, u32[]{:S(2)}, u32[]{:S(2)}) collective-permute-start(bf16[128,128]{1,0:T(8,128)(2,1)S(1)} %get-tuple-element.19.near_row), channel_id=1, source_target_pairs={{0,1},{1,0},{2,3},{3,2},{4,5},{5,4},{6,7},{7,6},{8,9},{9,8},{10,11... | collective-permute-start | bytes 98312 | tf_op jit(solution)/shard_map/ppermute | solution.py:284
  23.0 0.1 collective-permute-start.6
  23.1 0.5 %copy-done.2 = f32[128]{0:T(128)S(1)} copy-done((f32[128]{0:T(128)S(1)}, f32[128]{0:T(128)}, u32[]{:S(2)}) %copy-start.2) | copy-done | bytes 536
  23.6 1.5 %shard_map.55 = (f32[2,2,128,128]{3,2,1,0:T(8,128)S(1)}, f32[2,128,128]{2,1,0:T(8,128)S(1)}, bf16[2,2,128,384]{3,2,1,0:T(8,128)(2,1)S(1)}) custom-call(bf16[2,4,128,128]{3,2,1,0:T(8,128)(2,1)S(1)} %copy-done, bf16[4,128,128]{2,1,0:T(8,128)(2,1)S(1)} %collective-permute-done.x2, bf16[4,128,128]{2,1,0:T(8,128)(2,1)S(1)} %collective-permute-done.1.x1, ...), custom_call_target="tpu_custom_call" | custom-call | flops 20000000000 | tf_op jit(solution)/shard_map/pallas_call | solution.py:88
  25.2 0.3 shard_map.57
  25.4 13.6 %all_to_all.5 = bf16[8,2,64,128]{3,2,1,0:T(8,128)(2,1)S(1)} all-to-all(bf16[8,2,64,128]{3,2,1,0:T(8,128)(2,1)S(1)} %shard_map.57), channel_id=1, replica_groups={{16,17,18,19,32,33,34,35},{20,21,22,23,36,37,38,39},{24,25,26,27,40,41,..., dimensions={0} | all-to-all | bytes 524288 | tf_op jit(solution)/shard_map/all_to_all | solution.py:296
  39.1 2.3 %collective-permute-start.9 = (bf16[4,2,64,128]{3,2,1,0:T(8,128)(2,1)S(1)}, bf16[4,2,64,128]{3,2,1,0:T(8,128)(2,1)S(1)}, u32[]{:S(2)}, u32[]{:S(2)}) collective-permute-start(bf16[4,2,64,128]{3,2,1,0:T(8,128)(2,1)S(1)} %dynamic-slice_bitcast_fusion), channel_id=1, source_target_pairs={{0,16},{16,0},{32,48},{48,32},{64,80},{80,64},{96,112},{112,96},{1... | collective-permute-start | bytes 393224 | tf_op jit(solution)/shard_map/ppermute | solution.py:299
  41.4 0.6 %shard_map.58.sums = f32[64,640]{1,0:T(8,128)S(1)} custom-call(bf16[2,4,2,64,128]{4,3,2,1,0:T(8,128)(2,1)S(1)} %bitcast.26, bf16[2,27,16,128]{3,2,1,0:T(8,128)(2,1)S(1)} %pad_maximum_fusion.pair, bf16[2,27,16,128]{3,2,1,0:T(8,128)(2,1)S(1)} %collective-permute-done.8.other), custom_call_target="tpu_custom_call" | custom-call | flops 150000000 | tf_op jit(solution)/shard_map/pallas_call | solution.py:202
  42.0 0.4 collective-permute-done.9.near
  42.4 0.4 shard_map.59
  42.8 3.2 %collective-permute-start.10 = (f32[16,640]{1,0:T(8,128)S(1)}, f32[16,640]{1,0:T(8,128)S(1)}, u32[]{:S(2)}, u32[]{:S(2)}) collective-permute-start(f32[16,640]{1,0:T(8,128)S(1)} %get-tuple-element.16), channel_id=1, source_target_pairs={{0,8},{1,9},{2,10},{3,11},{4,12},{5,13},{6,14},{7,15},{8,0},{9,1},... | collective-permute-start | bytes 122888 | tf_op jit(solution)/shard_map/ppermute | solution.py:301
  46.1 1.6 %collective-permute-start.11 = (f32[16,640]{1,0:T(8,128)S(1)}, f32[16,640]{1,0:T(8,128)S(1)}, u32[]{:S(2)}, u32[]{:S(2)}) collective-permute-start(f32[16,640]{1,0:T(8,128)S(1)} %get-tuple-element.17), channel_id=1, source_target_pairs={{0,12},{1,13},{2,14},{3,15},{4,8},{5,9},{6,10},{7,11},{8,4},{9,5},... | collective-permute-start | bytes 122888 | tf_op jit(solution)/shard_map/ppermute | solution.py:301
  47.7 0.8 %collective-permute-done.10.s2 = f32[16,640]{1,0:T(8,128)S(1)} collective-permute-done((f32[16,640]{1,0:T(8,128)S(1)}, f32[16,640]{1,0:T(8,128)S(1)}, u32[]{:S(2)}, u32[]{:S(2)}) %collective-permute-start.10) | collective-permute-done | bytes 40992 | tf_op jit(solution)/shard_map/ppermute | solution.py:301
  48.4 2.9 %collective-permute-done.11.s3 = f32[16,640]{1,0:T(8,128)S(1)} collective-permute-done((f32[16,640]{1,0:T(8,128)S(1)}, f32[16,640]{1,0:T(8,128)S(1)}, u32[]{:S(2)}, u32[]{:S(2)}) %collective-permute-start.11) | collective-permute-done | bytes 40992 | tf_op jit(solution)/shard_map/ppermute | solution.py:301
  51.3 0.4 collective-permute-done.12.s1
  51.7 0.7 %shard_map.60 = bf16[16,2048]{1,0:T(8,128)(2,1)} custom-call(f32[16,640]{1,0:T(8,128)S(1)} %get-tuple-element.15.s0, f32[16,640]{1,0:T(8,128)S(1)} %collective-permute-done.10.s2, f32[16,640]{1,0:T(8,128)S(1)} %collective-permute-done.11.s3, f32[16,640]{1,0:T(8,128)S(1)} %collective-permute-done.12.s1, f32[16,128]{1,0:T(8,128)S(1)} %broadcast_in_dim.2.bias), custom_call_target="tpu_custom_call" | custom-call | tf_op jit(solution)/shard_map/pallas_call | solution.py:258
  (25 shorter events, 0.2 us)
Async XLA Ops:
  0.0 10.3 %copy-start.3 = (bf16[3,3,3,128,16]{3,4,2,1,0:T(8,128)(2,1)S(1)}, bf16[3,3,3,128,16]{3,4,2,1,0:T(8,128)(2,1)}, u32[]{:S(2)}) copy-start(bf16[3,3,3,128,16]{3,4,2,1,0:T(8,128)(2,1)} %param.8) | copy-start | bytes 331780
  0.0 11.9 %copy-start = (bf16[2,4,128,128]{3,2,1,0:T(8,128)(2,1)S(1)}, bf16[2,4,128,128]{3,2,1,0:T(8,128)(2,1)}, u32[]{:S(2)}) copy-start(bf16[2,4,128,128]{3,2,1,0:T(8,128)(2,1)} %vol.1) | copy-start | bytes 786436
  0.0 23.1 %copy-start.1 = (bf16[3,3,3,128,128]{4,3,2,1,0:T(8,128)(2,1)S(1)}, bf16[3,3,3,128,128]{4,3,2,1,0:T(8,128)(2,1)}, u32[]{:S(2)}) copy-start(bf16[3,3,3,128,128]{4,3,2,1,0:T(8,128)(2,1)} %w.1) | copy-start | bytes 2654212
  1.1 17.8 %collective-permute-start = (bf16[4,128,128]{2,1,0:T(8,128)(2,1)S(1)}, bf16[4,128,128]{2,1,0:T(8,128)(2,1)S(1)}, u32[]{:S(2)}, u32[]{:S(2)}) collective-permute-start(bf16[4,128,128]{2,1,0:T(8,128)(2,1)S(1)} %get-tuple-element.24), channel_id=1, source_target_pairs={{0,0},{16,32},{32,16},{48,64},{64,48},{80,96},{96,80},{112,128},{1... | collective-permute-start | bytes 393224 | tf_op jit(solution)/shard_map/ppermute | solution.py:276
  3.3 15.6 %collective-permute-start.1 = (bf16[4,128,128]{2,1,0:T(8,128)(2,1)S(1)}, bf16[4,128,128]{2,1,0:T(8,128)(2,1)S(1)}, u32[]{:S(2)}, u32[]{:S(2)}) collective-permute-start(bf16[4,128,128]{2,1,0:T(8,128)(2,1)S(1)} %get-tuple-element.23), channel_id=1, source_target_pairs={{0,16},{16,0},{32,48},{48,32},{64,80},{80,64},{96,112},{112,96},{1... | collective-permute-start | bytes 393224 | tf_op jit(solution)/shard_map/ppermute | solution.py:277
  10.3 5.6 %collective-permute-start.7 = (bf16[27,16,128]{2,1,0:T(8,128)(2,1)S(1)}, bf16[27,16,128]{2,1,0:T(8,128)(2,1)S(1)}, u32[]{:S(2)}, u32[]{:S(2)}) collective-permute-start(bf16[27,16,128]{2,1,0:T(8,128)(2,1)S(1)} %bitcast.30), channel_id=1, source_target_pairs={{0,4},{1,5},{2,6},{3,7},{4,0},{5,1},{6,2},{7,3},{8,12},{9,13},{10,... | collective-permute-start | bytes 331784 | tf_op jit(solution)/shard_map/ppermute | solution.py:291
  11.9 11.0 %collective-permute-start.2 = (bf16[2,128,128]{2,1,0:T(8,128)(2,1)S(1)}, bf16[2,128,128]{2,1,0:T(8,128)(2,1)S(1)}, u32[]{:S(2)}, u32[]{:S(2)}) collective-permute-start(bf16[2,128,128]{2,1,0:T(8,128)(2,1)S(1)} %get-tuple-element.22), channel_id=1, source_target_pairs={{0,0},{1,2},{2,1},{3,4},{4,3},{5,6},{6,5},{7,8},{8,7},{9,10},{10,9... | collective-permute-start | bytes 196616 | tf_op jit(solution)/shard_map/ppermute | solution.py:278
  12.6 10.3 %collective-permute-start.3 = (bf16[2,128,128]{2,1,0:T(8,128)(2,1)S(1)}, bf16[2,128,128]{2,1,0:T(8,128)(2,1)S(1)}, u32[]{:S(2)}, u32[]{:S(2)}) collective-permute-start(bf16[2,128,128]{2,1,0:T(8,128)(2,1)S(1)} %get-tuple-element.21), channel_id=1, source_target_pairs={{0,1},{1,0},{2,3},{3,2},{4,5},{5,4},{6,7},{7,6},{8,9},{9,8},{10,11... | collective-permute-start | bytes 196616 | tf_op jit(solution)/shard_map/ppermute | solution.py:279
  16.0 9.2 %collective-permute-start.8 = (bf16[2,27,16,128]{3,2,1,0:T(8,128)(2,1)S(1)}, bf16[2,27,16,128]{3,2,1,0:T(8,128)(2,1)S(1)}, u32[]{:S(2)}, u32[]{:S(2)}) collective-permute-start(bf16[2,27,16,128]{3,2,1,0:T(8,128)(2,1)S(1)} %pad_maximum_fusion.pair), channel_id=1, source_target_pairs={{0,12},{1,13},{2,14},{3,15},{4,8},{5,9},{6,10},{7,11},{8,4},{9,5},... | collective-permute-start | bytes 663560 | tf_op jit(solution)/shard_map/ppermute | solution.py:292
  18.9 6.2 %collective-permute-start.4 = (bf16[128,128]{1,0:T(8,128)(2,1)S(1)}, bf16[128,128]{1,0:T(8,128)(2,1)S(1)}, u32[]{:S(2)}, u32[]{:S(2)}) collective-permute-start(bf16[128,128]{1,0:T(8,128)(2,1)S(1)} %get-tuple-element.20.far_row), channel_id=1, source_target_pairs={{0,0},{1,2},{2,1},{3,4},{4,3},{5,6},{6,5},{7,8},{8,7},{9,10},{10,9... | collective-permute-start | bytes 98312 | tf_op jit(solution)/shard_map/ppermute | solution.py:283
  19.6 5.6 %collective-permute-start.5 = (bf16[128,128]{1,0:T(8,128)(2,1)S(1)}, bf16[128,128]{1,0:T(8,128)(2,1)S(1)}, u32[]{:S(2)}, u32[]{:S(2)}) collective-permute-start(bf16[128,128]{1,0:T(8,128)(2,1)S(1)} %get-tuple-element.19.near_row), channel_id=1, source_target_pairs={{0,1},{1,0},{2,3},{3,2},{4,5},{5,4},{6,7},{7,6},{8,9},{9,8},{10,11... | collective-permute-start | bytes 98312 | tf_op jit(solution)/shard_map/ppermute | solution.py:284
  22.9 0.7 %copy-start.2 = (f32[128]{0:T(128)S(1)}, f32[128]{0:T(128)}, u32[]{:S(2)}) copy-start(f32[128]{0:T(128)} %param.7) | copy-start | bytes 1540
  23.0 2.2 %collective-permute-start.6 = (bf16[2,128,128]{2,1,0:T(8,128)(2,1)S(1)}, bf16[2,128,128]{2,1,0:T(8,128)(2,1)S(1)}, u32[]{:S(2)}, u32[]{:S(2)}) collective-permute-start(bf16[2,128,128]{2,1,0:T(8,128)(2,1)S(1)} %shard_map.56), channel_id=1, source_target_pairs={{0,16},{16,0},{32,48},{48,32},{64,80},{80,64},{96,112},{112,96},{1... | collective-permute-start | bytes 196616 | tf_op jit(solution)/shard_map/ppermute | solution.py:285
  39.1 3.3 %collective-permute-start.9 = (bf16[4,2,64,128]{3,2,1,0:T(8,128)(2,1)S(1)}, bf16[4,2,64,128]{3,2,1,0:T(8,128)(2,1)S(1)}, u32[]{:S(2)}, u32[]{:S(2)}) collective-permute-start(bf16[4,2,64,128]{3,2,1,0:T(8,128)(2,1)S(1)} %dynamic-slice_bitcast_fusion), channel_id=1, source_target_pairs={{0,16},{16,0},{32,48},{48,32},{64,80},{80,64},{96,112},{112,96},{1... | collective-permute-start | bytes 393224 | tf_op jit(solution)/shard_map/ppermute | solution.py:299
  42.8 5.6 %collective-permute-start.10 = (f32[16,640]{1,0:T(8,128)S(1)}, f32[16,640]{1,0:T(8,128)S(1)}, u32[]{:S(2)}, u32[]{:S(2)}) collective-permute-start(f32[16,640]{1,0:T(8,128)S(1)} %get-tuple-element.16), channel_id=1, source_target_pairs={{0,8},{1,9},{2,10},{3,11},{4,12},{5,13},{6,14},{7,15},{8,0},{9,1},... | collective-permute-start | bytes 122888 | tf_op jit(solution)/shard_map/ppermute | solution.py:301
  46.1 5.2 %collective-permute-start.11 = (f32[16,640]{1,0:T(8,128)S(1)}, f32[16,640]{1,0:T(8,128)S(1)}, u32[]{:S(2)}, u32[]{:S(2)}) collective-permute-start(f32[16,640]{1,0:T(8,128)S(1)} %get-tuple-element.17), channel_id=1, source_target_pairs={{0,12},{1,13},{2,14},{3,15},{4,8},{5,9},{6,10},{7,11},{8,4},{9,5},... | collective-permute-start | bytes 122888 | tf_op jit(solution)/shard_map/ppermute | solution.py:301
  47.7 4.0 %copy-start.4 = (f32[16]{0:T(128)S(1)}, f32[16]{0:T(128)}, u32[]{:S(2)}) copy-start(f32[16]{0:T(128)} %param.9) | copy-start | bytes 196
  47.7 4.0 %collective-permute-start.12 = (f32[16,640]{1,0:T(8,128)S(1)}, f32[16,640]{1,0:T(8,128)S(1)}, u32[]{:S(2)}, u32[]{:S(2)}) collective-permute-start(f32[16,640]{1,0:T(8,128)S(1)} %get-tuple-element.18), channel_id=1, source_target_pairs={{0,4},{1,5},{2,6},{3,7},{4,0},{5,1},{6,2},{7,3},{8,12},{9,13},{10,... | collective-permute-start | bytes 122888 | tf_op jit(solution)/shard_map/ppermute | solution.py:301

commit v18 on v17

--- a/solution.py
+++ b/solution.py
@@ -75,8 +75,8 @@
             term = jnp.dot(lhs, rhs, preferred_element_type=F32)
             total = term if total is None else total + term
         for q in range(2):
-            ends[s, q] = spread(total[3 * q * 128 : (3 * q + 1) * 128], col) + bias[...]
-            middle = spread(total[(q + 1) * 128 : (q + 2) * 128], col) + bias[...]
+            ends[s, q] = spread(total[3 * q * 128 : (3 * q + 1) * 128], col) + bias[:1]
+            middle = spread(total[(q + 1) * 128 : (q + 2) * 128], col) + bias[:1]
             best[q] = middle if s == 0 else jnp.maximum(best[q], middle)
             a, b = 2 * s, 2 * q
             for c in range(3):
@@ -290,7 +290,7 @@
     w = jnp.transpose(coarse_filters, (0, 1, 2, 4, 3)).reshape(27, 16, 128)
     pair = jnp.stack([w, lax.ppermute(w, "rows", along_y(1))])
     other = lax.ppermute(pair, "rows", along_y(3))
-    main = fine_level(volume, x2, x1, r2, r1, fine_filters, fine_bias.reshape(1, 128))
+    main = fine_level(volume, x2, x1, r2, r1, fine_filters, jnp.broadcast_to(fine_bias, (8, 128)))
     pooled = finish(main, c2, c1, e, other)
 
     both = lax.all_to_all(

time: 52.6 us -> 52.6 us (level)
  local copies, waits for them, and re-layouts: 1.73 us -> 1.2 us
    unnamed x10, local copies, waits for them, and re-layouts: 0.55 us -> 0.02 us
  transfers between devices with their start and end apart: 13 -> 13, of which waited for: 4 -> 5; matrix products, arithmetic and copies ran while one was open for 0% -> 0% of each run, Pallas kernels for 4% -> 4%
where the time goes in v18:
time: 52.6 us; the launch traced here: 52.4 us
  starting transfers between devices  29 us (55%)
  blocking collectives  14 us (27%)
  waiting for transfers between devices  4.63 us (9%)
  Pallas kernels  3.49 us (7%)
  local copies, waits for them, and re-layouts  1.2 us (2%)
    all_to_all x1, blocking collectives, body(): lax.all_to_all(pooled, ('depth', 'rows'), 0, 0, axis_index_groups=far_and...  14 us
    ppermute x1, starting transfers between devices, body(): lax.ppermute(lax.dynamic_index_in_dim(volume, 1 - pd, 0, False), 'depth',...  7.04 us
    ppermute x3, starting transfers between devices, body(): lax.ppermute(sums[k], 'rows', along_y(k))  4.86 us
    ppermute x3, waiting for transfers between devices, body(): lax.ppermute(sums[k], 'rows', along_y(k))  4 us
    ppermute x1, starting transfers between devices, body(): lax.ppermute(lax.dynamic_index_in_dim(volume, 3 - 3 * pr, 1, False), 'row...  3.37 us
    ppermute x1, starting transfers between devices, body(): c1 = lax.ppermute(near_row, 'rows', rows_near)  3.34 us
    ppermute x1, starting transfers between devices, body(): other = lax.ppermute(pair, 'rows', along_y(3))  2.9 us
    ppermute x1, starting transfers between devices, body(): lax.ppermute(lax.dynamic_index_in_dim(both, 1 - pd, 0, False), 'depth', d...  2.28 us
  transfers between devices with their start and end apart: 13, of which 5 were waited for; matrix products, arithmetic and copies ran while one was open for 0% of the time, Pallas kernels for 4%

profile of v18, /device:TPU:6, one launch (start us, length us, event | category | flops | bytes accessed | tf_op | source)
XLA Modules:
  0.0 52.4 jit_solution(16779766041448308076)
XLA Ops:
  0.0 1.1 %dynamic-slice_bitcast_fusion.1 = (bf16[4,128,128]{2,1,0:T(8,128)(2,1)S(1)}, bf16[4,128,128]{2,1,0:T(8,128)(2,1)S(1)}) fusion(bf16[2,4,128,128]{3,2,1,0:T(8,128)(2,1)} %vol.1, s32[]{:T(128)S(6)} %select_n.19, s32[]{:T(128)S(6)} %select_n.18), kind=kLoop, calls=%fused_computation.6 | loop fusion | bytes 524296 | tf_op jit(solution)/shard_map/jit(dynamic_index_in_dim)/squeeze | solution.py:277
  1.1 2.2 %collective-permute-start = (bf16[4,128,128]{2,1,0:T(8,128)(2,1)S(1)}, bf16[4,128,128]{2,1,0:T(8,128)(2,1)S(1)}, u32[]{:S(2)}, u32[]{:S(2)}) collective-permute-start(bf16[4,128,128]{2,1,0:T(8,128)(2,1)S(1)} %get-tuple-element.24), channel_id=1, source_target_pairs={{0,0},{16,32},{32,16},{48,64},{64,48},{80,96},{96,80},{112,128},{1... | collective-permute-start | bytes 393224 | tf_op jit(solution)/shard_map/ppermute | solution.py:276
  3.3 7.0 %collective-permute-start.1 = (bf16[4,128,128]{2,1,0:T(8,128)(2,1)S(1)}, bf16[4,128,128]{2,1,0:T(8,128)(2,1)S(1)}, u32[]{:S(2)}, u32[]{:S(2)}) collective-permute-start(bf16[4,128,128]{2,1,0:T(8,128)(2,1)S(1)} %get-tuple-element.23), channel_id=1, source_target_pairs={{0,16},{16,0},{32,48},{48,32},{64,80},{80,64},{96,112},{112,96},{1... | collective-permute-start | bytes 393224 | tf_op jit(solution)/shard_map/ppermute | solution.py:277
  10.3 1.6 %collective-permute-start.7 = (bf16[27,16,128]{2,1,0:T(8,128)(2,1)S(1)}, bf16[27,16,128]{2,1,0:T(8,128)(2,1)S(1)}, u32[]{:S(2)}, u32[]{:S(2)}) collective-permute-start(bf16[27,16,128]{2,1,0:T(8,128)(2,1)S(1)} %bitcast.28), channel_id=1, source_target_pairs={{0,4},{1,5},{2,6},{3,7},{4,0},{5,1},{6,2},{7,3},{8,12},{9,13},{10,... | collective-permute-start | bytes 331784 | tf_op jit(solution)/shard_map/ppermute | solution.py:291
  11.9 0.7 %collective-permute-start.2 = (bf16[2,128,128]{2,1,0:T(8,128)(2,1)S(1)}, bf16[2,128,128]{2,1,0:T(8,128)(2,1)S(1)}, u32[]{:S(2)}, u32[]{:S(2)}) collective-permute-start(bf16[2,128,128]{2,1,0:T(8,128)(2,1)S(1)} %get-tuple-element.22), channel_id=1, source_target_pairs={{0,0},{1,2},{2,1},{3,4},{4,3},{5,6},{6,5},{7,8},{8,7},{9,10},{10,9... | collective-permute-start | bytes 196616 | tf_op jit(solution)/shard_map/ppermute | solution.py:278
  12.6 3.4 %collective-permute-start.3 = (bf16[2,128,128]{2,1,0:T(8,128)(2,1)S(1)}, bf16[2,128,128]{2,1,0:T(8,128)(2,1)S(1)}, u32[]{:S(2)}, u32[]{:S(2)}) collective-permute-start(bf16[2,128,128]{2,1,0:T(8,128)(2,1)S(1)} %get-tuple-element.21), channel_id=1, source_target_pairs={{0,1},{1,0},{2,3},{3,2},{4,5},{5,4},{6,7},{7,6},{8,9},{9,8},{10,11... | collective-permute-start | bytes 196616 | tf_op jit(solution)/shard_map/ppermute | solution.py:279
  16.0 2.9 %collective-permute-start.8 = (bf16[2,27,16,128]{3,2,1,0:T(8,128)(2,1)S(1)}, bf16[2,27,16,128]{3,2,1,0:T(8,128)(2,1)S(1)}, u32[]{:S(2)}, u32[]{:S(2)}) collective-permute-start(bf16[2,27,16,128]{3,2,1,0:T(8,128)(2,1)S(1)} %pad_maximum_fusion.pair), channel_id=1, source_target_pairs={{0,12},{1,13},{2,14},{3,15},{4,8},{5,9},{6,10},{7,11},{8,4},{9,5},... | collective-permute-start | bytes 663560 | tf_op jit(solution)/shard_map/ppermute | solution.py:292
  18.9 0.7 %collective-permute-start.4 = (bf16[128,128]{1,0:T(8,128)(2,1)S(1)}, bf16[128,128]{1,0:T(8,128)(2,1)S(1)}, u32[]{:S(2)}, u32[]{:S(2)}) collective-permute-start(bf16[128,128]{1,0:T(8,128)(2,1)S(1)} %get-tuple-element.20.far_row), channel_id=1, source_target_pairs={{0,0},{1,2},{2,1},{3,4},{4,3},{5,6},{6,5},{7,8},{8,7},{9,10},{10,9... | collective-permute-start | bytes 98312 | tf_op jit(solution)/shard_map/ppermute | solution.py:283
  19.6 3.3 %collective-permute-start.5 = (bf16[128,128]{1,0:T(8,128)(2,1)S(1)}, bf16[128,128]{1,0:T(8,128)(2,1)S(1)}, u32[]{:S(2)}, u32[]{:S(2)}) collective-permute-start(bf16[128,128]{1,0:T(8,128)(2,1)S(1)} %get-tuple-element.19.near_row), channel_id=1, source_target_pairs={{0,1},{1,0},{2,3},{3,2},{4,5},{5,4},{6,7},{7,6},{8,9},{9,8},{10,11... | collective-permute-start | bytes 98312 | tf_op jit(solution)/shard_map/ppermute | solution.py:284
  23.0 0.1 collective-permute-start.6
  23.1 1.5 %shard_map.55 = (f32[2,2,128,128]{3,2,1,0:T(8,128)S(1)}, f32[2,128,128]{2,1,0:T(8,128)S(1)}, bf16[2,2,128,384]{3,2,1,0:T(8,128)(2,1)S(1)}) custom-call(bf16[2,4,128,128]{3,2,1,0:T(8,128)(2,1)S(1)} %copy-done, bf16[4,128,128]{2,1,0:T(8,128)(2,1)S(1)} %collective-permute-done.x2, bf16[4,128,128]{2,1,0:T(8,128)(2,1)S(1)} %collective-permute-done.1.x1, ...), custom_call_target="tpu_custom_call" | custom-call | flops 20000000000 | tf_op jit(solution)/shard_map/pallas_call | solution.py:88
  24.6 0.2 collective-permute-done.5.c1
  24.8 0.3 shard_map.57
  25.1 14.0 %all_to_all.5 = bf16[8,2,64,128]{3,2,1,0:T(8,128)(2,1)S(1)} all-to-all(bf16[8,2,64,128]{3,2,1,0:T(8,128)(2,1)S(1)} %shard_map.57), channel_id=1, replica_groups={{16,17,18,19,32,33,34,35},{20,21,22,23,36,37,38,39},{24,25,26,27,40,41,..., dimensions={0} | all-to-all | bytes 524288 | tf_op jit(solution)/shard_map/all_to_all | solution.py:296
  39.1 2.3 %collective-permute-start.9 = (bf16[4,2,64,128]{3,2,1,0:T(8,128)(2,1)S(1)}, bf16[4,2,64,128]{3,2,1,0:T(8,128)(2,1)S(1)}, u32[]{:S(2)}, u32[]{:S(2)}) collective-permute-start(bf16[4,2,64,128]{3,2,1,0:T(8,128)(2,1)S(1)} %dynamic-slice_bitcast_fusion), channel_id=1, source_target_pairs={{0,16},{16,0},{32,48},{48,32},{64,80},{80,64},{96,112},{112,96},{1... | collective-permute-start | bytes 393224 | tf_op jit(solution)/shard_map/ppermute | solution.py:299
  41.4 0.6 %shard_map.58.sums = f32[64,640]{1,0:T(8,128)S(1)} custom-call(bf16[2,4,2,64,128]{4,3,2,1,0:T(8,128)(2,1)S(1)} %bitcast.25, bf16[2,27,16,128]{3,2,1,0:T(8,128)(2,1)S(1)} %pad_maximum_fusion.pair, bf16[2,27,16,128]{3,2,1,0:T(8,128)(2,1)S(1)} %collective-permute-done.8.other), custom_call_target="tpu_custom_call" | custom-call | flops 150000000 | tf_op jit(solution)/shard_map/pallas_call | solution.py:202
  42.0 0.4 collective-permute-done.9.near
  42.4 0.4 shard_map.59
  42.8 3.2 %collective-permute-start.10 = (f32[16,640]{1,0:T(8,128)S(1)}, f32[16,640]{1,0:T(8,128)S(1)}, u32[]{:S(2)}, u32[]{:S(2)}) collective-permute-start(f32[16,640]{1,0:T(8,128)S(1)} %get-tuple-element.16), channel_id=1, source_target_pairs={{0,8},{1,9},{2,10},{3,11},{4,12},{5,13},{6,14},{7,15},{8,0},{9,1},... | collective-permute-start | bytes 122888 | tf_op jit(solution)/shard_map/ppermute | solution.py:301
  46.1 1.6 %collective-permute-start.11 = (f32[16,640]{1,0:T(8,128)S(1)}, f32[16,640]{1,0:T(8,128)S(1)}, u32[]{:S(2)}, u32[]{:S(2)}) collective-permute-start(f32[16,640]{1,0:T(8,128)S(1)} %get-tuple-element.17), channel_id=1, source_target_pairs={{0,12},{1,13},{2,14},{3,15},{4,8},{5,9},{6,10},{7,11},{8,4},{9,5},... | collective-permute-start | bytes 122888 | tf_op jit(solution)/shard_map/ppermute | solution.py:301
  47.7 0.7 %collective-permute-done.10.s2 = f32[16,640]{1,0:T(8,128)S(1)} collective-permute-done((f32[16,640]{1,0:T(8,128)S(1)}, f32[16,640]{1,0:T(8,128)S(1)}, u32[]{:S(2)}, u32[]{:S(2)}) %collective-permute-start.10) | collective-permute-done | bytes 40992 | tf_op jit(solution)/shard_map/ppermute | solution.py:301
  48.4 2.9 %collective-permute-done.11.s3 = f32[16,640]{1,0:T(8,128)S(1)} collective-permute-done((f32[16,640]{1,0:T(8,128)S(1)}, f32[16,640]{1,0:T(8,128)S(1)}, u32[]{:S(2)}, u32[]{:S(2)}) %collective-permute-start.11) | collective-permute-done | bytes 40992 | tf_op jit(solution)/shard_map/ppermute | solution.py:301
  51.3 0.4 collective-permute-done.12.s1
  51.7 0.7 %shard_map.60 = bf16[16,2048]{1,0:T(8,128)(2,1)} custom-call(f32[16,640]{1,0:T(8,128)S(1)} %get-tuple-element.15.s0, f32[16,640]{1,0:T(8,128)S(1)} %collective-permute-done.10.s2, f32[16,640]{1,0:T(8,128)S(1)} %collective-permute-done.11.s3, f32[16,640]{1,0:T(8,128)S(1)} %collective-permute-done.12.s1, f32[16,128]{1,0:T(8,128)S(1)} %broadcast_in_dim.10.bias), custom_call_target="tpu_custom_call" | custom-call | tf_op jit(solution)/shard_map/pallas_call | solution.py:258
  (26 shorter events, 0.2 us)
Async XLA Ops:
  0.0 10.3 %copy-start.2 = (bf16[3,3,3,128,16]{3,4,2,1,0:T(8,128)(2,1)S(1)}, bf16[3,3,3,128,16]{3,4,2,1,0:T(8,128)(2,1)}, u32[]{:S(2)}) copy-start(bf16[3,3,3,128,16]{3,4,2,1,0:T(8,128)(2,1)} %param.8) | copy-start | bytes 331780
  0.0 11.9 %copy-start = (bf16[2,4,128,128]{3,2,1,0:T(8,128)(2,1)S(1)}, bf16[2,4,128,128]{3,2,1,0:T(8,128)(2,1)}, u32[]{:S(2)}) copy-start(bf16[2,4,128,128]{3,2,1,0:T(8,128)(2,1)} %vol.1) | copy-start | bytes 786436
  0.0 23.1 %copy-start.1 = (bf16[3,3,3,128,128]{4,3,2,1,0:T(8,128)(2,1)S(1)}, bf16[3,3,3,128,128]{4,3,2,1,0:T(8,128)(2,1)}, u32[]{:S(2)}) copy-start(bf16[3,3,3,128,128]{4,3,2,1,0:T(8,128)(2,1)} %w.1) | copy-start | bytes 2654212
  1.1 17.8 %collective-permute-start = (bf16[4,128,128]{2,1,0:T(8,128)(2,1)S(1)}, bf16[4,128,128]{2,1,0:T(8,128)(2,1)S(1)}, u32[]{:S(2)}, u32[]{:S(2)}) collective-permute-start(bf16[4,128,128]{2,1,0:T(8,128)(2,1)S(1)} %get-tuple-element.24), channel_id=1, source_target_pairs={{0,0},{16,32},{32,16},{48,64},{64,48},{80,96},{96,80},{112,128},{1... | collective-permute-start | bytes 393224 | tf_op jit(solution)/shard_map/ppermute | solution.py:276
  3.3 15.6 %collective-permute-start.1 = (bf16[4,128,128]{2,1,0:T(8,128)(2,1)S(1)}, bf16[4,128,128]{2,1,0:T(8,128)(2,1)S(1)}, u32[]{:S(2)}, u32[]{:S(2)}) collective-permute-start(bf16[4,128,128]{2,1,0:T(8,128)(2,1)S(1)} %get-tuple-element.23), channel_id=1, source_target_pairs={{0,16},{16,0},{32,48},{48,32},{64,80},{80,64},{96,112},{112,96},{1... | collective-permute-start | bytes 393224 | tf_op jit(solution)/shard_map/ppermute | solution.py:277
  10.3 5.6 %collective-permute-start.7 = (bf16[27,16,128]{2,1,0:T(8,128)(2,1)S(1)}, bf16[27,16,128]{2,1,0:T(8,128)(2,1)S(1)}, u32[]{:S(2)}, u32[]{:S(2)}) collective-permute-start(bf16[27,16,128]{2,1,0:T(8,128)(2,1)S(1)} %bitcast.28), channel_id=1, source_target_pairs={{0,4},{1,5},{2,6},{3,7},{4,0},{5,1},{6,2},{7,3},{8,12},{9,13},{10,... | collective-permute-start | bytes 331784 | tf_op jit(solution)/shard_map/ppermute | solution.py:291
  11.9 11.0 %collective-permute-start.2 = (bf16[2,128,128]{2,1,0:T(8,128)(2,1)S(1)}, bf16[2,128,128]{2,1,0:T(8,128)(2,1)S(1)}, u32[]{:S(2)}, u32[]{:S(2)}) collective-permute-start(bf16[2,128,128]{2,1,0:T(8,128)(2,1)S(1)} %get-tuple-element.22), channel_id=1, source_target_pairs={{0,0},{1,2},{2,1},{3,4},{4,3},{5,6},{6,5},{7,8},{8,7},{9,10},{10,9... | collective-permute-start | bytes 196616 | tf_op jit(solution)/shard_map/ppermute | solution.py:278
  12.6 10.4 %collective-permute-start.3 = (bf16[2,128,128]{2,1,0:T(8,128)(2,1)S(1)}, bf16[2,128,128]{2,1,0:T(8,128)(2,1)S(1)}, u32[]{:S(2)}, u32[]{:S(2)}) collective-permute-start(bf16[2,128,128]{2,1,0:T(8,128)(2,1)S(1)} %get-tuple-element.21), channel_id=1, source_target_pairs={{0,1},{1,0},{2,3},{3,2},{4,5},{5,4},{6,7},{7,6},{8,9},{9,8},{10,11... | collective-permute-start | bytes 196616 | tf_op jit(solution)/shard_map/ppermute | solution.py:279
  16.0 8.9 %collective-permute-start.8 = (bf16[2,27,16,128]{3,2,1,0:T(8,128)(2,1)S(1)}, bf16[2,27,16,128]{3,2,1,0:T(8,128)(2,1)S(1)}, u32[]{:S(2)}, u32[]{:S(2)}) collective-permute-start(bf16[2,27,16,128]{3,2,1,0:T(8,128)(2,1)S(1)} %pad_maximum_fusion.pair), channel_id=1, source_target_pairs={{0,12},{1,13},{2,14},{3,15},{4,8},{5,9},{6,10},{7,11},{8,4},{9,5},... | collective-permute-start | bytes 663560 | tf_op jit(solution)/shard_map/ppermute | solution.py:292
  18.9 5.7 %collective-permute-start.4 = (bf16[128,128]{1,0:T(8,128)(2,1)S(1)}, bf16[128,128]{1,0:T(8,128)(2,1)S(1)}, u32[]{:S(2)}, u32[]{:S(2)}) collective-permute-start(bf16[128,128]{1,0:T(8,128)(2,1)S(1)} %get-tuple-element.20.far_row), channel_id=1, source_target_pairs={{0,0},{1,2},{2,1},{3,4},{4,3},{5,6},{6,5},{7,8},{8,7},{9,10},{10,9... | collective-permute-start | bytes 98312 | tf_op jit(solution)/shard_map/ppermute | solution.py:283
  19.6 3.5 %copy-start.3 = (f32[128]{0:T(128)S(1)}, f32[128]{0:T(128)}, u32[]{:S(2)}) copy-start(f32[128]{0:T(128)} %param.7) | copy-start | bytes 1540
  19.6 5.2 %collective-permute-start.5 = (bf16[128,128]{1,0:T(8,128)(2,1)S(1)}, bf16[128,128]{1,0:T(8,128)(2,1)S(1)}, u32[]{:S(2)}, u32[]{:S(2)}) collective-permute-start(bf16[128,128]{1,0:T(8,128)(2,1)S(1)} %get-tuple-element.19.near_row), channel_id=1, source_target_pairs={{0,1},{1,0},{2,3},{3,2},{4,5},{5,4},{6,7},{7,6},{8,9},{9,8},{10,11... | collective-permute-start | bytes 98312 | tf_op jit(solution)/shard_map/ppermute | solution.py:284
  23.0 1.9 %collective-permute-start.6 = (bf16[2,128,128]{2,1,0:T(8,128)(2,1)S(1)}, bf16[2,128,128]{2,1,0:T(8,128)(2,1)S(1)}, u32[]{:S(2)}, u32[]{:S(2)}) collective-permute-start(bf16[2,128,128]{2,1,0:T(8,128)(2,1)S(1)} %shard_map.56), channel_id=1, source_target_pairs={{0,16},{16,0},{32,48},{48,32},{64,80},{80,64},{96,112},{112,96},{1... | collective-permute-start | bytes 196616 | tf_op jit(solution)/shard_map/ppermute | solution.py:285
  39.1 3.3 %collective-permute-start.9 = (bf16[4,2,64,128]{3,2,1,0:T(8,128)(2,1)S(1)}, bf16[4,2,64,128]{3,2,1,0:T(8,128)(2,1)S(1)}, u32[]{:S(2)}, u32[]{:S(2)}) collective-permute-start(bf16[4,2,64,128]{3,2,1,0:T(8,128)(2,1)S(1)} %dynamic-slice_bitcast_fusion), channel_id=1, source_target_pairs={{0,16},{16,0},{32,48},{48,32},{64,80},{80,64},{96,112},{112,96},{1... | collective-permute-start | bytes 393224 | tf_op jit(solution)/shard_map/ppermute | solution.py:299
  42.8 5.6 %collective-permute-start.10 = (f32[16,640]{1,0:T(8,128)S(1)}, f32[16,640]{1,0:T(8,128)S(1)}, u32[]{:S(2)}, u32[]{:S(2)}) collective-permute-start(f32[16,640]{1,0:T(8,128)S(1)} %get-tuple-element.16), channel_id=1, source_target_pairs={{0,8},{1,9},{2,10},{3,11},{4,12},{5,13},{6,14},{7,15},{8,0},{9,1},... | collective-permute-start | bytes 122888 | tf_op jit(solution)/shard_map/ppermute | solution.py:301
  46.1 5.2 %collective-permute-start.11 = (f32[16,640]{1,0:T(8,128)S(1)}, f32[16,640]{1,0:T(8,128)S(1)}, u32[]{:S(2)}, u32[]{:S(2)}) collective-permute-start(f32[16,640]{1,0:T(8,128)S(1)} %get-tuple-element.17), channel_id=1, source_target_pairs={{0,12},{1,13},{2,14},{3,15},{4,8},{5,9},{6,10},{7,11},{8,4},{9,5},... | collective-permute-start | bytes 122888 | tf_op jit(solution)/shard_map/ppermute | solution.py:301
  47.7 4.0 %copy-start.4 = (f32[16]{0:T(128)S(1)}, f32[16]{0:T(128)}, u32[]{:S(2)}) copy-start(f32[16]{0:T(128)} %param.9) | copy-start | bytes 196
  47.7 4.0 %collective-permute-start.12 = (f32[16,640]{1,0:T(8,128)S(1)}, f32[16,640]{1,0:T(8,128)S(1)}, u32[]{:S(2)}, u32[]{:S(2)}) collective-permute-start(f32[16,640]{1,0:T(8,128)S(1)} %get-tuple-element.18), channel_id=1, source_target_pairs={{0,4},{1,5},{2,6},{3,7},{4,0},{5,1},{6,2},{7,3},{8,12},{9,13},{10,... | collective-permute-start | bytes 122888 | tf_op jit(solution)/shard_map/ppermute | solution.py:301

commit v19 on v18

--- a/solution.py
+++ b/solution.py
@@ -157,7 +157,7 @@
         [
             jnp.concatenate([w[m, 9 * a + 3 * b + c] for a in taps for b in range(3)], axis=1)
             for c in range(3)
-            for w, m in ((pair, 0), (pair, 1), (other, 1), (other, 0))
+            for w, m in ((pair, 0), (other, 0), (other, 1), (pair, 1))
         ],
         axis=0,
     )
@@ -288,8 +288,8 @@
         return [(i, i ^ (4 * k)) for i in range(16)]
 
     w = jnp.transpose(coarse_filters, (0, 1, 2, 4, 3)).reshape(27, 16, 128)
-    pair = jnp.stack([w, lax.ppermute(w, "rows", along_y(1))])
-    other = lax.ppermute(pair, "rows", along_y(3))
+    pair = jnp.stack([w, lax.ppermute(w, "rows", along_y(3))])
+    other = lax.ppermute(pair, "rows", along_y(1))
     main = fine_level(volume, x2, x1, r2, r1, fine_filters, jnp.broadcast_to(fine_bias, (8, 128)))
     pooled = finish(main, c2, c1, e, other)
 

time: 52.6 us -> 52.3 us (level)
  transfers between devices with their start and end apart: 13 -> 13, of which waited for: 5 -> 4; matrix products, arithmetic and copies ran while one was open for 0% -> 0% of each run, Pallas kernels for 4% -> 4%
where the time goes in v19:
time: 52.3 us; the launch traced here: 52 us
  starting transfers between devices  28.7 us (55%)
  blocking collectives  13.7 us (26%)
  waiting for transfers between devices  4.77 us (9%)
  Pallas kernels  3.49 us (7%)
  local copies, waits for them, and re-layouts  1.2 us (2%)
    all_to_all x1, blocking collectives, body(): lax.all_to_all(pooled, ('depth', 'rows'), 0, 0, axis_index_groups=far_and...  13.7 us
    ppermute x1, starting transfers between devices, body(): lax.ppermute(lax.dynamic_index_in_dim(volume, 1 - pd, 0, False), 'depth',...  7.04 us
    ppermute x3, starting transfers between devices, body(): lax.ppermute(sums[k], 'rows', along_y(k))  4.59 us
    ppermute x3, waiting for transfers between devices, body(): lax.ppermute(sums[k], 'rows', along_y(k))  4 us
    ppermute x1, starting transfers between devices, body(): lax.ppermute(lax.dynamic_index_in_dim(volume, 3 - 3 * pr, 1, False), 'row...  3.37 us
    ppermute x1, starting transfers between devices, body(): c1 = lax.ppermute(near_row, 'rows', rows_near)  3.34 us
    ppermute x1, starting transfers between devices, body(): pair = jnp.stack([w, lax.ppermute(w, 'rows', along_y(3))])  3.01 us
    ppermute x1, starting transfers between devices, body(): lax.ppermute(lax.dynamic_index_in_dim(both, 1 - pd, 0, False), 'depth', d...  2.32 us
  transfers between devices with their start and end apart: 13, of which 4 were waited for; matrix products, arithmetic and copies ran while one was open for 0% of the time, Pallas kernels for 4%

profile of v19, /device:TPU:6, one launch (start us, length us, event | category | flops | bytes accessed | tf_op | source)
XLA Modules:
  0.0 52.0 jit_solution(4534344134147907251)
XLA Ops:
  0.0 1.1 %dynamic-slice_bitcast_fusion.1 = (bf16[4,128,128]{2,1,0:T(8,128)(2,1)S(1)}, bf16[4,128,128]{2,1,0:T(8,128)(2,1)S(1)}) fusion(bf16[2,4,128,128]{3,2,1,0:T(8,128)(2,1)} %vol.1, s32[]{:T(128)S(6)} %select_n.19, s32[]{:T(128)S(6)} %select_n.18), kind=kLoop, calls=%fused_computation.6 | loop fusion | bytes 524296 | tf_op jit(solution)/shard_map/jit(dynamic_index_in_dim)/squeeze | solution.py:277
  1.1 2.2 %collective-permute-start = (bf16[4,128,128]{2,1,0:T(8,128)(2,1)S(1)}, bf16[4,128,128]{2,1,0:T(8,128)(2,1)S(1)}, u32[]{:S(2)}, u32[]{:S(2)}) collective-permute-start(bf16[4,128,128]{2,1,0:T(8,128)(2,1)S(1)} %get-tuple-element.24), channel_id=1, source_target_pairs={{0,0},{16,32},{32,16},{48,64},{64,48},{80,96},{96,80},{112,128},{1... | collective-permute-start | bytes 393224 | tf_op jit(solution)/shard_map/ppermute | solution.py:276
  3.3 7.0 %collective-permute-start.1 = (bf16[4,128,128]{2,1,0:T(8,128)(2,1)S(1)}, bf16[4,128,128]{2,1,0:T(8,128)(2,1)S(1)}, u32[]{:S(2)}, u32[]{:S(2)}) collective-permute-start(bf16[4,128,128]{2,1,0:T(8,128)(2,1)S(1)} %get-tuple-element.23), channel_id=1, source_target_pairs={{0,16},{16,0},{32,48},{48,32},{64,80},{80,64},{96,112},{112,96},{1... | collective-permute-start | bytes 393224 | tf_op jit(solution)/shard_map/ppermute | solution.py:277
  10.3 3.0 %collective-permute-start.7 = (bf16[27,16,128]{2,1,0:T(8,128)(2,1)S(1)}, bf16[27,16,128]{2,1,0:T(8,128)(2,1)S(1)}, u32[]{:S(2)}, u32[]{:S(2)}) collective-permute-start(bf16[27,16,128]{2,1,0:T(8,128)(2,1)S(1)} %bitcast.28), channel_id=1, source_target_pairs={{0,12},{1,13},{2,14},{3,15},{4,8},{5,9},{6,10},{7,11},{8,4},{9,5},... | collective-permute-start | bytes 331784 | tf_op jit(solution)/shard_map/ppermute | solution.py:291
  13.4 0.7 %collective-permute-start.2 = (bf16[2,128,128]{2,1,0:T(8,128)(2,1)S(1)}, bf16[2,128,128]{2,1,0:T(8,128)(2,1)S(1)}, u32[]{:S(2)}, u32[]{:S(2)}) collective-permute-start(bf16[2,128,128]{2,1,0:T(8,128)(2,1)S(1)} %get-tuple-element.22), channel_id=1, source_target_pairs={{0,0},{1,2},{2,1},{3,4},{4,3},{5,6},{6,5},{7,8},{8,7},{9,10},{10,9... | collective-permute-start | bytes 196616 | tf_op jit(solution)/shard_map/ppermute | solution.py:278
  14.0 3.4 %collective-permute-start.3 = (bf16[2,128,128]{2,1,0:T(8,128)(2,1)S(1)}, bf16[2,128,128]{2,1,0:T(8,128)(2,1)S(1)}, u32[]{:S(2)}, u32[]{:S(2)}) collective-permute-start(bf16[2,128,128]{2,1,0:T(8,128)(2,1)S(1)} %get-tuple-element.21), channel_id=1, source_target_pairs={{0,1},{1,0},{2,3},{3,2},{4,5},{5,4},{6,7},{7,6},{8,9},{9,8},{10,11... | collective-permute-start | bytes 196616 | tf_op jit(solution)/shard_map/ppermute | solution.py:279
  17.4 1.5 %collective-permute-start.8 = (bf16[2,27,16,128]{3,2,1,0:T(8,128)(2,1)S(1)}, bf16[2,27,16,128]{3,2,1,0:T(8,128)(2,1)S(1)}, u32[]{:S(2)}, u32[]{:S(2)}) collective-permute-start(bf16[2,27,16,128]{3,2,1,0:T(8,128)(2,1)S(1)} %pad_maximum_fusion.pair), channel_id=1, source_target_pairs={{0,4},{1,5},{2,6},{3,7},{4,0},{5,1},{6,2},{7,3},{8,12},{9,13},{10,... | collective-permute-start | bytes 663560 | tf_op jit(solution)/shard_map/ppermute | solution.py:292
  18.9 0.7 %collective-permute-start.4 = (bf16[128,128]{1,0:T(8,128)(2,1)S(1)}, bf16[128,128]{1,0:T(8,128)(2,1)S(1)}, u32[]{:S(2)}, u32[]{:S(2)}) collective-permute-start(bf16[128,128]{1,0:T(8,128)(2,1)S(1)} %get-tuple-element.20.far_row), channel_id=1, source_target_pairs={{0,0},{1,2},{2,1},{3,4},{4,3},{5,6},{6,5},{7,8},{8,7},{9,10},{10,9... | collective-permute-start | bytes 98312 | tf_op jit(solution)/shard_map/ppermute | solution.py:283
  19.6 3.3 %collective-permute-start.5 = (bf16[128,128]{1,0:T(8,128)(2,1)S(1)}, bf16[128,128]{1,0:T(8,128)(2,1)S(1)}, u32[]{:S(2)}, u32[]{:S(2)}) collective-permute-start(bf16[128,128]{1,0:T(8,128)(2,1)S(1)} %get-tuple-element.19.near_row), channel_id=1, source_target_pairs={{0,1},{1,0},{2,3},{3,2},{4,5},{5,4},{6,7},{7,6},{8,9},{9,8},{10,11... | collective-permute-start | bytes 98312 | tf_op jit(solution)/shard_map/ppermute | solution.py:284
  23.0 0.1 collective-permute-start.6
  23.1 1.5 %shard_map.55 = (f32[2,2,128,128]{3,2,1,0:T(8,128)S(1)}, f32[2,128,128]{2,1,0:T(8,128)S(1)}, bf16[2,2,128,384]{3,2,1,0:T(8,128)(2,1)S(1)}) custom-call(bf16[2,4,128,128]{3,2,1,0:T(8,128)(2,1)S(1)} %copy-done, bf16[4,128,128]{2,1,0:T(8,128)(2,1)S(1)} %collective-permute-done.x2, bf16[4,128,128]{2,1,0:T(8,128)(2,1)S(1)} %collective-permute-done.1.x1, ...), custom_call_target="tpu_custom_call" | custom-call | flops 20000000000 | tf_op jit(solution)/shard_map/pallas_call | solution.py:88
  24.6 0.4 collective-permute-done.5.c1
  25.0 0.3 shard_map.57
  25.3 13.7 %all_to_all.5 = bf16[8,2,64,128]{3,2,1,0:T(8,128)(2,1)S(1)} all-to-all(bf16[8,2,64,128]{3,2,1,0:T(8,128)(2,1)S(1)} %shard_map.57), channel_id=1, replica_groups={{16,17,18,19,32,33,34,35},{20,21,22,23,36,37,38,39},{24,25,26,27,40,41,..., dimensions={0} | all-to-all | bytes 524288 | tf_op jit(solution)/shard_map/all_to_all | solution.py:296
  38.9 2.3 %collective-permute-start.9 = (bf16[4,2,64,128]{3,2,1,0:T(8,128)(2,1)S(1)}, bf16[4,2,64,128]{3,2,1,0:T(8,128)(2,1)S(1)}, u32[]{:S(2)}, u32[]{:S(2)}) collective-permute-start(bf16[4,2,64,128]{3,2,1,0:T(8,128)(2,1)S(1)} %dynamic-slice_bitcast_fusion), channel_id=1, source_target_pairs={{0,16},{16,0},{32,48},{48,32},{64,80},{80,64},{96,112},{112,96},{1... | collective-permute-start | bytes 393224 | tf_op jit(solution)/shard_map/ppermute | solution.py:299
  41.2 0.6 %shard_map.58.sums = f32[64,640]{1,0:T(8,128)S(1)} custom-call(bf16[2,4,2,64,128]{4,3,2,1,0:T(8,128)(2,1)S(1)} %bitcast.25, bf16[2,27,16,128]{3,2,1,0:T(8,128)(2,1)S(1)} %pad_maximum_fusion.pair, bf16[2,27,16,128]{3,2,1,0:T(8,128)(2,1)S(1)} %collective-permute-done.8.other), custom_call_target="tpu_custom_call" | custom-call | flops 150000000 | tf_op jit(solution)/shard_map/pallas_call | solution.py:202
  41.8 0.4 collective-permute-done.9.near
  42.2 0.4 shard_map.59
  42.7 3.4 %collective-permute-start.10 = (f32[16,640]{1,0:T(8,128)S(1)}, f32[16,640]{1,0:T(8,128)S(1)}, u32[]{:S(2)}, u32[]{:S(2)}) collective-permute-start(f32[16,640]{1,0:T(8,128)S(1)} %get-tuple-element.16), channel_id=1, source_target_pairs={{0,8},{1,9},{2,10},{3,11},{4,12},{5,13},{6,14},{7,15},{8,0},{9,1},... | collective-permute-start | bytes 122888 | tf_op jit(solution)/shard_map/ppermute | solution.py:301
  46.1 1.2 %collective-permute-start.11 = (f32[16,640]{1,0:T(8,128)S(1)}, f32[16,640]{1,0:T(8,128)S(1)}, u32[]{:S(2)}, u32[]{:S(2)}) collective-permute-start(f32[16,640]{1,0:T(8,128)S(1)} %get-tuple-element.17), channel_id=1, source_target_pairs={{0,12},{1,13},{2,14},{3,15},{4,8},{5,9},{6,10},{7,11},{8,4},{9,5},... | collective-permute-start | bytes 122888 | tf_op jit(solution)/shard_map/ppermute | solution.py:301
  47.3 1.0 %collective-permute-done.10.s2 = f32[16,640]{1,0:T(8,128)S(1)} collective-permute-done((f32[16,640]{1,0:T(8,128)S(1)}, f32[16,640]{1,0:T(8,128)S(1)}, u32[]{:S(2)}, u32[]{:S(2)}) %collective-permute-start.10) | collective-permute-done | bytes 40992 | tf_op jit(solution)/shard_map/ppermute | solution.py:301
  48.3 3.0 %collective-permute-done.11.s3 = f32[16,640]{1,0:T(8,128)S(1)} collective-permute-done((f32[16,640]{1,0:T(8,128)S(1)}, f32[16,640]{1,0:T(8,128)S(1)}, u32[]{:S(2)}, u32[]{:S(2)}) %collective-permute-start.11) | collective-permute-done | bytes 40992 | tf_op jit(solution)/shard_map/ppermute | solution.py:301
  51.3 0.1 broadcast_in_dim.10.bias
  51.3 0.7 %shard_map.60 = bf16[16,2048]{1,0:T(8,128)(2,1)} custom-call(f32[16,640]{1,0:T(8,128)S(1)} %get-tuple-element.15.s0, f32[16,640]{1,0:T(8,128)S(1)} %collective-permute-done.10.s2, f32[16,640]{1,0:T(8,128)S(1)} %collective-permute-done.11.s3, f32[16,640]{1,0:T(8,128)S(1)} %collective-permute-done.12.s1, f32[16,128]{1,0:T(8,128)S(1)} %broadcast_in_dim.10.bias), custom_call_target="tpu_custom_call" | custom-call | tf_op jit(solution)/shard_map/pallas_call | solution.py:258
  (26 shorter events, 0.1 us)
Async XLA Ops:
  0.0 10.3 %copy-start.2 = (bf16[3,3,3,128,16]{3,4,2,1,0:T(8,128)(2,1)S(1)}, bf16[3,3,3,128,16]{3,4,2,1,0:T(8,128)(2,1)}, u32[]{:S(2)}) copy-start(bf16[3,3,3,128,16]{3,4,2,1,0:T(8,128)(2,1)} %param.8) | copy-start | bytes 331780
  0.0 13.3 %copy-start = (bf16[2,4,128,128]{3,2,1,0:T(8,128)(2,1)S(1)}, bf16[2,4,128,128]{3,2,1,0:T(8,128)(2,1)}, u32[]{:S(2)}) copy-start(bf16[2,4,128,128]{3,2,1,0:T(8,128)(2,1)} %vol.1) | copy-start | bytes 786436
  0.0 23.1 %copy-start.1 = (bf16[3,3,3,128,128]{4,3,2,1,0:T(8,128)(2,1)S(1)}, bf16[3,3,3,128,128]{4,3,2,1,0:T(8,128)(2,1)}, u32[]{:S(2)}) copy-start(bf16[3,3,3,128,128]{4,3,2,1,0:T(8,128)(2,1)} %w.1) | copy-start | bytes 2654212
  1.1 17.8 %collective-permute-start = (bf16[4,128,128]{2,1,0:T(8,128)(2,1)S(1)}, bf16[4,128,128]{2,1,0:T(8,128)(2,1)S(1)}, u32[]{:S(2)}, u32[]{:S(2)}) collective-permute-start(bf16[4,128,128]{2,1,0:T(8,128)(2,1)S(1)} %get-tuple-element.24), channel_id=1, source_target_pairs={{0,0},{16,32},{32,16},{48,64},{64,48},{80,96},{96,80},{112,128},{1... | collective-permute-start | bytes 393224 | tf_op jit(solution)/shard_map/ppermute | solution.py:276
  3.3 15.6 %collective-permute-start.1 = (bf16[4,128,128]{2,1,0:T(8,128)(2,1)S(1)}, bf16[4,128,128]{2,1,0:T(8,128)(2,1)S(1)}, u32[]{:S(2)}, u32[]{:S(2)}) collective-permute-start(bf16[4,128,128]{2,1,0:T(8,128)(2,1)S(1)} %get-tuple-element.23), channel_id=1, source_target_pairs={{0,16},{16,0},{32,48},{48,32},{64,80},{80,64},{96,112},{112,96},{1... | collective-permute-start | bytes 393224 | tf_op jit(solution)/shard_map/ppermute | solution.py:277
  10.3 7.1 %collective-permute-start.7 = (bf16[27,16,128]{2,1,0:T(8,128)(2,1)S(1)}, bf16[27,16,128]{2,1,0:T(8,128)(2,1)S(1)}, u32[]{:S(2)}, u32[]{:S(2)}) collective-permute-start(bf16[27,16,128]{2,1,0:T(8,128)(2,1)S(1)} %bitcast.28), channel_id=1, source_target_pairs={{0,12},{1,13},{2,14},{3,15},{4,8},{5,9},{6,10},{7,11},{8,4},{9,5},... | collective-permute-start | bytes 331784 | tf_op jit(solution)/shard_map/ppermute | solution.py:291
  13.4 9.6 %collective-permute-start.2 = (bf16[2,128,128]{2,1,0:T(8,128)(2,1)S(1)}, bf16[2,128,128]{2,1,0:T(8,128)(2,1)S(1)}, u32[]{:S(2)}, u32[]{:S(2)}) collective-permute-start(bf16[2,128,128]{2,1,0:T(8,128)(2,1)S(1)} %get-tuple-element.22), channel_id=1, source_target_pairs={{0,0},{1,2},{2,1},{3,4},{4,3},{5,6},{6,5},{7,8},{8,7},{9,10},{10,9... | collective-permute-start | bytes 196616 | tf_op jit(solution)/shard_map/ppermute | solution.py:278
  14.0 8.9 %collective-permute-start.3 = (bf16[2,128,128]{2,1,0:T(8,128)(2,1)S(1)}, bf16[2,128,128]{2,1,0:T(8,128)(2,1)S(1)}, u32[]{:S(2)}, u32[]{:S(2)}) collective-permute-start(bf16[2,128,128]{2,1,0:T(8,128)(2,1)S(1)} %get-tuple-element.21), channel_id=1, source_target_pairs={{0,1},{1,0},{2,3},{3,2},{4,5},{5,4},{6,7},{7,6},{8,9},{9,8},{10,11... | collective-permute-start | bytes 196616 | tf_op jit(solution)/shard_map/ppermute | solution.py:279
  17.4 7.5 %collective-permute-start.8 = (bf16[2,27,16,128]{3,2,1,0:T(8,128)(2,1)S(1)}, bf16[2,27,16,128]{3,2,1,0:T(8,128)(2,1)S(1)}, u32[]{:S(2)}, u32[]{:S(2)}) collective-permute-start(bf16[2,27,16,128]{3,2,1,0:T(8,128)(2,1)S(1)} %pad_maximum_fusion.pair), channel_id=1, source_target_pairs={{0,4},{1,5},{2,6},{3,7},{4,0},{5,1},{6,2},{7,3},{8,12},{9,13},{10,... | collective-permute-start | bytes 663560 | tf_op jit(solution)/shard_map/ppermute | solution.py:292
  18.9 5.7 %collective-permute-start.4 = (bf16[128,128]{1,0:T(8,128)(2,1)S(1)}, bf16[128,128]{1,0:T(8,128)(2,1)S(1)}, u32[]{:S(2)}, u32[]{:S(2)}) collective-permute-start(bf16[128,128]{1,0:T(8,128)(2,1)S(1)} %get-tuple-element.20.far_row), channel_id=1, source_target_pairs={{0,0},{1,2},{2,1},{3,4},{4,3},{5,6},{6,5},{7,8},{8,7},{9,10},{10,9... | collective-permute-start | bytes 98312 | tf_op jit(solution)/shard_map/ppermute | solution.py:283
  19.6 3.5 %copy-start.3 = (f32[128]{0:T(128)S(1)}, f32[128]{0:T(128)}, u32[]{:S(2)}) copy-start(f32[128]{0:T(128)} %param.7) | copy-start | bytes 1540
  19.6 5.4 %collective-permute-start.5 = (bf16[128,128]{1,0:T(8,128)(2,1)S(1)}, bf16[128,128]{1,0:T(8,128)(2,1)S(1)}, u32[]{:S(2)}, u32[]{:S(2)}) collective-permute-start(bf16[128,128]{1,0:T(8,128)(2,1)S(1)} %get-tuple-element.19.near_row), channel_id=1, source_target_pairs={{0,1},{1,0},{2,3},{3,2},{4,5},{5,4},{6,7},{7,6},{8,9},{9,8},{10,11... | collective-permute-start | bytes 98312 | tf_op jit(solution)/shard_map/ppermute | solution.py:284
  23.0 2.0 %collective-permute-start.6 = (bf16[2,128,128]{2,1,0:T(8,128)(2,1)S(1)}, bf16[2,128,128]{2,1,0:T(8,128)(2,1)S(1)}, u32[]{:S(2)}, u32[]{:S(2)}) collective-permute-start(bf16[2,128,128]{2,1,0:T(8,128)(2,1)S(1)} %shard_map.56), channel_id=1, source_target_pairs={{0,16},{16,0},{32,48},{48,32},{64,80},{80,64},{96,112},{112,96},{1... | collective-permute-start | bytes 196616 | tf_op jit(solution)/shard_map/ppermute | solution.py:285
  38.9 3.3 %collective-permute-start.9 = (bf16[4,2,64,128]{3,2,1,0:T(8,128)(2,1)S(1)}, bf16[4,2,64,128]{3,2,1,0:T(8,128)(2,1)S(1)}, u32[]{:S(2)}, u32[]{:S(2)}) collective-permute-start(bf16[4,2,64,128]{3,2,1,0:T(8,128)(2,1)S(1)} %dynamic-slice_bitcast_fusion), channel_id=1, source_target_pairs={{0,16},{16,0},{32,48},{48,32},{64,80},{80,64},{96,112},{112,96},{1... | collective-permute-start | bytes 393224 | tf_op jit(solution)/shard_map/ppermute | solution.py:299
  42.7 5.6 %collective-permute-start.10 = (f32[16,640]{1,0:T(8,128)S(1)}, f32[16,640]{1,0:T(8,128)S(1)}, u32[]{:S(2)}, u32[]{:S(2)}) collective-permute-start(f32[16,640]{1,0:T(8,128)S(1)} %get-tuple-element.16), channel_id=1, source_target_pairs={{0,8},{1,9},{2,10},{3,11},{4,12},{5,13},{6,14},{7,15},{8,0},{9,1},... | collective-permute-start | bytes 122888 | tf_op jit(solution)/shard_map/ppermute | solution.py:301
  46.1 5.2 %collective-permute-start.11 = (f32[16,640]{1,0:T(8,128)S(1)}, f32[16,640]{1,0:T(8,128)S(1)}, u32[]{:S(2)}, u32[]{:S(2)}) collective-permute-start(f32[16,640]{1,0:T(8,128)S(1)} %get-tuple-element.17), channel_id=1, source_target_pairs={{0,12},{1,13},{2,14},{3,15},{4,8},{5,9},{6,10},{7,11},{8,4},{9,5},... | collective-permute-start | bytes 122888 | tf_op jit(solution)/shard_map/ppermute | solution.py:301
  47.3 4.0 %copy-start.4 = (f32[16]{0:T(128)S(1)}, f32[16]{0:T(128)}, u32[]{:S(2)}) copy-start(f32[16]{0:T(128)} %param.9) | copy-start | bytes 196
  47.3 4.0 %collective-permute-start.12 = (f32[16,640]{1,0:T(8,128)S(1)}, f32[16,640]{1,0:T(8,128)S(1)}, u32[]{:S(2)}, u32[]{:S(2)}) collective-permute-start(f32[16,640]{1,0:T(8,128)S(1)} %get-tuple-element.18), channel_id=1, source_target_pairs={{0,4},{1,5},{2,6},{3,7},{4,0},{5,1},{6,2},{7,3},{8,12},{9,13},{10,... | collective-permute-start | bytes 122888 | tf_op jit(solution)/shard_map/ppermute | solution.py:301

commit v20 on v19

--- a/solution.py
+++ b/solution.py
@@ -237,11 +237,12 @@
     )(near, sums, pair, other)
 
 
-def join_kernel(s0, s2, s3, s1, bias, out, held):
+def join_kernel(s0, s2, s3, s1, bias, out, held, ready, done):
     y = lax.div(lax.axis_index("rows"), 4)
     for k, part in enumerate((s0, s1, s2, s3)):
         held[y ^ k] = part[...]
     low = lax.broadcasted_iota(jnp.int32, (16, 128), 1) < 64
+    copies = []
     for m in range(4):
         tiles = [held[m, :, 128 * i : 128 * i + 128] for i in range(4)]
         if m > 0:
@@ -250,7 +251,12 @@
             tiles[3] = tiles[3] + jnp.where(low, 0.0, held[m + 1, :, 512:])
         for i in range(4):
             value = jnp.maximum(tiles[i] + bias[...], 0.0).astype(BF16)
-            out[:, 512 * m + 128 * i : 512 * m + 128 * i + 128] = value
+            ready[:, 512 * m + 128 * i : 512 * m + 128 * i + 128] = value
+        columns = pl.ds(512 * m, 512)
+        copies.append(pltpu.make_async_copy(ready.at[:, columns], out.at[:, columns], done.at[m]))
+        copies[m].start()
+    for copy in copies:
+        copy.wait()
 
 
 def join(parts, bias):
@@ -259,8 +265,12 @@
         join_kernel,
         out_shape=jax.ShapeDtypeStruct((16, 2048), BF16),
         in_specs=[vmem] * 5,
-        out_specs=vmem,
-        scratch_shapes=[pltpu.VMEM((4, 16, 640), F32)],
+        out_specs=pl.BlockSpec(memory_space=pl.ANY),
+        scratch_shapes=[
+            pltpu.VMEM((4, 16, 640), F32),
+            pltpu.VMEM((16, 2048), BF16),
+            pltpu.SemaphoreType.DMA((4,)),
+        ],
         compiler_params=pltpu.CompilerParams(vmem_limit_bytes=4 * 1024 * 1024),
     )(*parts, bias)
 

time: 52.3 us -> 52.3 us (level)
  no operation moved by 1% of the time
where the time goes in v20:
time: 52.3 us; the launch traced here: 52 us
  starting transfers between devices  28.7 us (55%)
  blocking collectives  13.7 us (26%)
  waiting for transfers between devices  4.77 us (9%)
  Pallas kernels  3.5 us (7%)
  local copies, waits for them, and re-layouts  1.2 us (2%)
    all_to_all x1, blocking collectives, body(): lax.all_to_all(pooled, ('depth', 'rows'), 0, 0, axis_index_groups=far_and...  13.7 us
    ppermute x1, starting transfers between devices, body(): lax.ppermute(lax.dynamic_index_in_dim(volume, 1 - pd, 0, False), 'depth',...  7.04 us
    ppermute x3, starting transfers between devices, body(): lax.ppermute(sums[k], 'rows', along_y(k))  4.59 us
    ppermute x3, waiting for transfers between devices, body(): lax.ppermute(sums[k], 'rows', along_y(k))  4 us
    ppermute x1, starting transfers between devices, body(): lax.ppermute(lax.dynamic_index_in_dim(volume, 3 - 3 * pr, 1, False), 'row...  3.37 us
    ppermute x1, starting transfers between devices, body(): c1 = lax.ppermute(near_row, 'rows', rows_near)  3.34 us
    ppermute x1, starting transfers between devices, body(): pair = jnp.stack([w, lax.ppermute(w, 'rows', along_y(3))])  3.01 us
    ppermute x1, starting transfers between devices, body(): lax.ppermute(lax.dynamic_index_in_dim(both, 1 - pd, 0, False), 'depth', d...  2.32 us
  transfers between devices with their start and end apart: 13, of which 4 were waited for; matrix products, arithmetic and copies ran while one was open for 0% of the time, Pallas kernels for 4%

profile of v20, /device:TPU:6, one launch (start us, length us, event | category | flops | bytes accessed | tf_op | source)
XLA Modules:
  0.0 52.0 jit_solution(2835722459920221125)
XLA Ops:
  0.0 1.1 %dynamic-slice_bitcast_fusion.1 = (bf16[4,128,128]{2,1,0:T(8,128)(2,1)S(1)}, bf16[4,128,128]{2,1,0:T(8,128)(2,1)S(1)}) fusion(bf16[2,4,128,128]{3,2,1,0:T(8,128)(2,1)} %vol.1, s32[]{:T(128)S(6)} %select_n.19, s32[]{:T(128)S(6)} %select_n.18), kind=kLoop, calls=%fused_computation.6 | loop fusion | bytes 524296 | tf_op jit(solution)/shard_map/jit(dynamic_index_in_dim)/squeeze | solution.py:287
  1.1 2.2 %collective-permute-start = (bf16[4,128,128]{2,1,0:T(8,128)(2,1)S(1)}, bf16[4,128,128]{2,1,0:T(8,128)(2,1)S(1)}, u32[]{:S(2)}, u32[]{:S(2)}) collective-permute-start(bf16[4,128,128]{2,1,0:T(8,128)(2,1)S(1)} %get-tuple-element.24), channel_id=1, source_target_pairs={{0,0},{16,32},{32,16},{48,64},{64,48},{80,96},{96,80},{112,128},{1... | collective-permute-start | bytes 393224 | tf_op jit(solution)/shard_map/ppermute | solution.py:286
  3.3 7.0 %collective-permute-start.1 = (bf16[4,128,128]{2,1,0:T(8,128)(2,1)S(1)}, bf16[4,128,128]{2,1,0:T(8,128)(2,1)S(1)}, u32[]{:S(2)}, u32[]{:S(2)}) collective-permute-start(bf16[4,128,128]{2,1,0:T(8,128)(2,1)S(1)} %get-tuple-element.23), channel_id=1, source_target_pairs={{0,16},{16,0},{32,48},{48,32},{64,80},{80,64},{96,112},{112,96},{1... | collective-permute-start | bytes 393224 | tf_op jit(solution)/shard_map/ppermute | solution.py:287
  10.3 3.0 %collective-permute-start.7 = (bf16[27,16,128]{2,1,0:T(8,128)(2,1)S(1)}, bf16[27,16,128]{2,1,0:T(8,128)(2,1)S(1)}, u32[]{:S(2)}, u32[]{:S(2)}) collective-permute-start(bf16[27,16,128]{2,1,0:T(8,128)(2,1)S(1)} %bitcast.28), channel_id=1, source_target_pairs={{0,12},{1,13},{2,14},{3,15},{4,8},{5,9},{6,10},{7,11},{8,4},{9,5},... | collective-permute-start | bytes 331784 | tf_op jit(solution)/shard_map/ppermute | solution.py:301
  13.4 0.7 %collective-permute-start.2 = (bf16[2,128,128]{2,1,0:T(8,128)(2,1)S(1)}, bf16[2,128,128]{2,1,0:T(8,128)(2,1)S(1)}, u32[]{:S(2)}, u32[]{:S(2)}) collective-permute-start(bf16[2,128,128]{2,1,0:T(8,128)(2,1)S(1)} %get-tuple-element.22), channel_id=1, source_target_pairs={{0,0},{1,2},{2,1},{3,4},{4,3},{5,6},{6,5},{7,8},{8,7},{9,10},{10,9... | collective-permute-start | bytes 196616 | tf_op jit(solution)/shard_map/ppermute | solution.py:288
  14.0 3.4 %collective-permute-start.3 = (bf16[2,128,128]{2,1,0:T(8,128)(2,1)S(1)}, bf16[2,128,128]{2,1,0:T(8,128)(2,1)S(1)}, u32[]{:S(2)}, u32[]{:S(2)}) collective-permute-start(bf16[2,128,128]{2,1,0:T(8,128)(2,1)S(1)} %get-tuple-element.21), channel_id=1, source_target_pairs={{0,1},{1,0},{2,3},{3,2},{4,5},{5,4},{6,7},{7,6},{8,9},{9,8},{10,11... | collective-permute-start | bytes 196616 | tf_op jit(solution)/shard_map/ppermute | solution.py:289
  17.4 1.5 %collective-permute-start.8 = (bf16[2,27,16,128]{3,2,1,0:T(8,128)(2,1)S(1)}, bf16[2,27,16,128]{3,2,1,0:T(8,128)(2,1)S(1)}, u32[]{:S(2)}, u32[]{:S(2)}) collective-permute-start(bf16[2,27,16,128]{3,2,1,0:T(8,128)(2,1)S(1)} %pad_maximum_fusion.pair), channel_id=1, source_target_pairs={{0,4},{1,5},{2,6},{3,7},{4,0},{5,1},{6,2},{7,3},{8,12},{9,13},{10,... | collective-permute-start | bytes 663560 | tf_op jit(solution)/shard_map/ppermute | solution.py:302
  18.9 0.7 %collective-permute-start.4 = (bf16[128,128]{1,0:T(8,128)(2,1)S(1)}, bf16[128,128]{1,0:T(8,128)(2,1)S(1)}, u32[]{:S(2)}, u32[]{:S(2)}) collective-permute-start(bf16[128,128]{1,0:T(8,128)(2,1)S(1)} %get-tuple-element.20.far_row), channel_id=1, source_target_pairs={{0,0},{1,2},{2,1},{3,4},{4,3},{5,6},{6,5},{7,8},{8,7},{9,10},{10,9... | collective-permute-start | bytes 98312 | tf_op jit(solution)/shard_map/ppermute | solution.py:293
  19.6 3.3 %collective-permute-start.5 = (bf16[128,128]{1,0:T(8,128)(2,1)S(1)}, bf16[128,128]{1,0:T(8,128)(2,1)S(1)}, u32[]{:S(2)}, u32[]{:S(2)}) collective-permute-start(bf16[128,128]{1,0:T(8,128)(2,1)S(1)} %get-tuple-element.19.near_row), channel_id=1, source_target_pairs={{0,1},{1,0},{2,3},{3,2},{4,5},{5,4},{6,7},{7,6},{8,9},{9,8},{10,11... | collective-permute-start | bytes 98312 | tf_op jit(solution)/shard_map/ppermute | solution.py:294
  23.0 0.1 collective-permute-start.6
  23.1 1.5 %shard_map.55 = (f32[2,2,128,128]{3,2,1,0:T(8,128)S(1)}, f32[2,128,128]{2,1,0:T(8,128)S(1)}, bf16[2,2,128,384]{3,2,1,0:T(8,128)(2,1)S(1)}) custom-call(bf16[2,4,128,128]{3,2,1,0:T(8,128)(2,1)S(1)} %copy-done, bf16[4,128,128]{2,1,0:T(8,128)(2,1)S(1)} %collective-permute-done.x2, bf16[4,128,128]{2,1,0:T(8,128)(2,1)S(1)} %collective-permute-done.1.x1, ...), custom_call_target="tpu_custom_call" | custom-call | flops 20000000000 | tf_op jit(solution)/shard_map/pallas_call | solution.py:88
  24.6 0.4 collective-permute-done.5.c1
  25.0 0.3 shard_map.57
  25.3 13.7 %all_to_all.5 = bf16[8,2,64,128]{3,2,1,0:T(8,128)(2,1)S(1)} all-to-all(bf16[8,2,64,128]{3,2,1,0:T(8,128)(2,1)S(1)} %shard_map.57), channel_id=1, replica_groups={{16,17,18,19,32,33,34,35},{20,21,22,23,36,37,38,39},{24,25,26,27,40,41,..., dimensions={0} | all-to-all | bytes 524288 | tf_op jit(solution)/shard_map/all_to_all | solution.py:306
  38.9 2.3 %collective-permute-start.9 = (bf16[4,2,64,128]{3,2,1,0:T(8,128)(2,1)S(1)}, bf16[4,2,64,128]{3,2,1,0:T(8,128)(2,1)S(1)}, u32[]{:S(2)}, u32[]{:S(2)}) collective-permute-start(bf16[4,2,64,128]{3,2,1,0:T(8,128)(2,1)S(1)} %dynamic-slice_bitcast_fusion), channel_id=1, source_target_pairs={{0,16},{16,0},{32,48},{48,32},{64,80},{80,64},{96,112},{112,96},{1... | collective-permute-start | bytes 393224 | tf_op jit(solution)/shard_map/ppermute | solution.py:309
  41.2 0.6 %shard_map.58.sums = f32[64,640]{1,0:T(8,128)S(1)} custom-call(bf16[2,4,2,64,128]{4,3,2,1,0:T(8,128)(2,1)S(1)} %bitcast.25, bf16[2,27,16,128]{3,2,1,0:T(8,128)(2,1)S(1)} %pad_maximum_fusion.pair, bf16[2,27,16,128]{3,2,1,0:T(8,128)(2,1)S(1)} %collective-permute-done.8.other), custom_call_target="tpu_custom_call" | custom-call | flops 150000000 | tf_op jit(solution)/shard_map/pallas_call | solution.py:202
  41.8 0.4 collective-permute-done.9.near
  42.2 0.4 shard_map.59
  42.7 3.4 %collective-permute-start.10 = (f32[16,640]{1,0:T(8,128)S(1)}, f32[16,640]{1,0:T(8,128)S(1)}, u32[]{:S(2)}, u32[]{:S(2)}) collective-permute-start(f32[16,640]{1,0:T(8,128)S(1)} %get-tuple-element.16), channel_id=1, source_target_pairs={{0,8},{1,9},{2,10},{3,11},{4,12},{5,13},{6,14},{7,15},{8,0},{9,1},... | collective-permute-start | bytes 122888 | tf_op jit(solution)/shard_map/ppermute | solution.py:311
  46.1 1.2 %collective-permute-start.11 = (f32[16,640]{1,0:T(8,128)S(1)}, f32[16,640]{1,0:T(8,128)S(1)}, u32[]{:S(2)}, u32[]{:S(2)}) collective-permute-start(f32[16,640]{1,0:T(8,128)S(1)} %get-tuple-element.17), channel_id=1, source_target_pairs={{0,12},{1,13},{2,14},{3,15},{4,8},{5,9},{6,10},{7,11},{8,4},{9,5},... | collective-permute-start | bytes 122888 | tf_op jit(solution)/shard_map/ppermute | solution.py:311
  47.3 1.0 %collective-permute-done.10.s2 = f32[16,640]{1,0:T(8,128)S(1)} collective-permute-done((f32[16,640]{1,0:T(8,128)S(1)}, f32[16,640]{1,0:T(8,128)S(1)}, u32[]{:S(2)}, u32[]{:S(2)}) %collective-permute-start.10) | collective-permute-done | bytes 40992 | tf_op jit(solution)/shard_map/ppermute | solution.py:311
  48.3 3.0 %collective-permute-done.11.s3 = f32[16,640]{1,0:T(8,128)S(1)} collective-permute-done((f32[16,640]{1,0:T(8,128)S(1)}, f32[16,640]{1,0:T(8,128)S(1)}, u32[]{:S(2)}, u32[]{:S(2)}) %collective-permute-start.11) | collective-permute-done | bytes 40992 | tf_op jit(solution)/shard_map/ppermute | solution.py:311
  51.3 0.1 broadcast_in_dim.10.bias
  51.3 0.7 %shard_map.60 = bf16[16,2048]{1,0:T(8,128)(2,1)} custom-call(f32[16,640]{1,0:T(8,128)S(1)} %get-tuple-element.15.s0, f32[16,640]{1,0:T(8,128)S(1)} %collective-permute-done.10.s2, f32[16,640]{1,0:T(8,128)S(1)} %collective-permute-done.11.s3, f32[16,640]{1,0:T(8,128)S(1)} %collective-permute-done.12.s1, f32[16,128]{1,0:T(8,128)S(1)} %broadcast_in_dim.10.bias), custom_call_target="tpu_custom_call" | custom-call | tf_op jit(solution)/shard_map/pallas_call | solution.py:264
  (26 shorter events, 0.1 us)
Async XLA Ops:
  0.0 10.3 %copy-start.2 = (bf16[3,3,3,128,16]{3,4,2,1,0:T(8,128)(2,1)S(1)}, bf16[3,3,3,128,16]{3,4,2,1,0:T(8,128)(2,1)}, u32[]{:S(2)}) copy-start(bf16[3,3,3,128,16]{3,4,2,1,0:T(8,128)(2,1)} %param.8) | copy-start | bytes 331780
  0.0 13.3 %copy-start = (bf16[2,4,128,128]{3,2,1,0:T(8,128)(2,1)S(1)}, bf16[2,4,128,128]{3,2,1,0:T(8,128)(2,1)}, u32[]{:S(2)}) copy-start(bf16[2,4,128,128]{3,2,1,0:T(8,128)(2,1)} %vol.1) | copy-start | bytes 786436
  0.0 23.1 %copy-start.1 = (bf16[3,3,3,128,128]{4,3,2,1,0:T(8,128)(2,1)S(1)}, bf16[3,3,3,128,128]{4,3,2,1,0:T(8,128)(2,1)}, u32[]{:S(2)}) copy-start(bf16[3,3,3,128,128]{4,3,2,1,0:T(8,128)(2,1)} %w.1) | copy-start | bytes 2654212
  1.1 17.8 %collective-permute-start = (bf16[4,128,128]{2,1,0:T(8,128)(2,1)S(1)}, bf16[4,128,128]{2,1,0:T(8,128)(2,1)S(1)}, u32[]{:S(2)}, u32[]{:S(2)}) collective-permute-start(bf16[4,128,128]{2,1,0:T(8,128)(2,1)S(1)} %get-tuple-element.24), channel_id=1, source_target_pairs={{0,0},{16,32},{32,16},{48,64},{64,48},{80,96},{96,80},{112,128},{1... | collective-permute-start | bytes 393224 | tf_op jit(solution)/shard_map/ppermute | solution.py:286
  3.3 15.6 %collective-permute-start.1 = (bf16[4,128,128]{2,1,0:T(8,128)(2,1)S(1)}, bf16[4,128,128]{2,1,0:T(8,128)(2,1)S(1)}, u32[]{:S(2)}, u32[]{:S(2)}) collective-permute-start(bf16[4,128,128]{2,1,0:T(8,128)(2,1)S(1)} %get-tuple-element.23), channel_id=1, source_target_pairs={{0,16},{16,0},{32,48},{48,32},{64,80},{80,64},{96,112},{112,96},{1... | collective-permute-start | bytes 393224 | tf_op jit(solution)/shard_map/ppermute | solution.py:287
  10.3 7.1 %collective-permute-start.7 = (bf16[27,16,128]{2,1,0:T(8,128)(2,1)S(1)}, bf16[27,16,128]{2,1,0:T(8,128)(2,1)S(1)}, u32[]{:S(2)}, u32[]{:S(2)}) collective-permute-start(bf16[27,16,128]{2,1,0:T(8,128)(2,1)S(1)} %bitcast.28), channel_id=1, source_target_pairs={{0,12},{1,13},{2,14},{3,15},{4,8},{5,9},{6,10},{7,11},{8,4},{9,5},... | collective-permute-start | bytes 331784 | tf_op jit(solution)/shard_map/ppermute | solution.py:301
  13.4 9.6 %collective-permute-start.2 = (bf16[2,128,128]{2,1,0:T(8,128)(2,1)S(1)}, bf16[2,128,128]{2,1,0:T(8,128)(2,1)S(1)}, u32[]{:S(2)}, u32[]{:S(2)}) collective-permute-start(bf16[2,128,128]{2,1,0:T(8,128)(2,1)S(1)} %get-tuple-element.22), channel_id=1, source_target_pairs={{0,0},{1,2},{2,1},{3,4},{4,3},{5,6},{6,5},{7,8},{8,7},{9,10},{10,9... | collective-permute-start | bytes 196616 | tf_op jit(solution)/shard_map/ppermute | solution.py:288
  14.0 8.9 %collective-permute-start.3 = (bf16[2,128,128]{2,1,0:T(8,128)(2,1)S(1)}, bf16[2,128,128]{2,1,0:T(8,128)(2,1)S(1)}, u32[]{:S(2)}, u32[]{:S(2)}) collective-permute-start(bf16[2,128,128]{2,1,0:T(8,128)(2,1)S(1)} %get-tuple-element.21), channel_id=1, source_target_pairs={{0,1},{1,0},{2,3},{3,2},{4,5},{5,4},{6,7},{7,6},{8,9},{9,8},{10,11... | collective-permute-start | bytes 196616 | tf_op jit(solution)/shard_map/ppermute | solution.py:289
  17.4 7.5 %collective-permute-start.8 = (bf16[2,27,16,128]{3,2,1,0:T(8,128)(2,1)S(1)}, bf16[2,27,16,128]{3,2,1,0:T(8,128)(2,1)S(1)}, u32[]{:S(2)}, u32[]{:S(2)}) collective-permute-start(bf16[2,27,16,128]{3,2,1,0:T(8,128)(2,1)S(1)} %pad_maximum_fusion.pair), channel_id=1, source_target_pairs={{0,4},{1,5},{2,6},{3,7},{4,0},{5,1},{6,2},{7,3},{8,12},{9,13},{10,... | collective-permute-start | bytes 663560 | tf_op jit(solution)/shard_map/ppermute | solution.py:302
  18.9 5.7 %collective-permute-start.4 = (bf16[128,128]{1,0:T(8,128)(2,1)S(1)}, bf16[128,128]{1,0:T(8,128)(2,1)S(1)}, u32[]{:S(2)}, u32[]{:S(2)}) collective-permute-start(bf16[128,128]{1,0:T(8,128)(2,1)S(1)} %get-tuple-element.20.far_row), channel_id=1, source_target_pairs={{0,0},{1,2},{2,1},{3,4},{4,3},{5,6},{6,5},{7,8},{8,7},{9,10},{10,9... | collective-permute-start | bytes 98312 | tf_op jit(solution)/shard_map/ppermute | solution.py:293
  19.6 3.5 %copy-start.3 = (f32[128]{0:T(128)S(1)}, f32[128]{0:T(128)}, u32[]{:S(2)}) copy-start(f32[128]{0:T(128)} %param.7) | copy-start | bytes 1540
  19.6 5.4 %collective-permute-start.5 = (bf16[128,128]{1,0:T(8,128)(2,1)S(1)}, bf16[128,128]{1,0:T(8,128)(2,1)S(1)}, u32[]{:S(2)}, u32[]{:S(2)}) collective-permute-start(bf16[128,128]{1,0:T(8,128)(2,1)S(1)} %get-tuple-element.19.near_row), channel_id=1, source_target_pairs={{0,1},{1,0},{2,3},{3,2},{4,5},{5,4},{6,7},{7,6},{8,9},{9,8},{10,11... | collective-permute-start | bytes 98312 | tf_op jit(solution)/shard_map/ppermute | solution.py:294
  23.0 2.0 %collective-permute-start.6 = (bf16[2,128,128]{2,1,0:T(8,128)(2,1)S(1)}, bf16[2,128,128]{2,1,0:T(8,128)(2,1)S(1)}, u32[]{:S(2)}, u32[]{:S(2)}) collective-permute-start(bf16[2,128,128]{2,1,0:T(8,128)(2,1)S(1)} %shard_map.56), channel_id=1, source_target_pairs={{0,16},{16,0},{32,48},{48,32},{64,80},{80,64},{96,112},{112,96},{1... | collective-permute-start | bytes 196616 | tf_op jit(solution)/shard_map/ppermute | solution.py:295
  38.9 3.3 %collective-permute-start.9 = (bf16[4,2,64,128]{3,2,1,0:T(8,128)(2,1)S(1)}, bf16[4,2,64,128]{3,2,1,0:T(8,128)(2,1)S(1)}, u32[]{:S(2)}, u32[]{:S(2)}) collective-permute-start(bf16[4,2,64,128]{3,2,1,0:T(8,128)(2,1)S(1)} %dynamic-slice_bitcast_fusion), channel_id=1, source_target_pairs={{0,16},{16,0},{32,48},{48,32},{64,80},{80,64},{96,112},{112,96},{1... | collective-permute-start | bytes 393224 | tf_op jit(solution)/shard_map/ppermute | solution.py:309
  42.7 5.6 %collective-permute-start.10 = (f32[16,640]{1,0:T(8,128)S(1)}, f32[16,640]{1,0:T(8,128)S(1)}, u32[]{:S(2)}, u32[]{:S(2)}) collective-permute-start(f32[16,640]{1,0:T(8,128)S(1)} %get-tuple-element.16), channel_id=1, source_target_pairs={{0,8},{1,9},{2,10},{3,11},{4,12},{5,13},{6,14},{7,15},{8,0},{9,1},... | collective-permute-start | bytes 122888 | tf_op jit(solution)/shard_map/ppermute | solution.py:311
  46.1 5.2 %collective-permute-start.11 = (f32[16,640]{1,0:T(8,128)S(1)}, f32[16,640]{1,0:T(8,128)S(1)}, u32[]{:S(2)}, u32[]{:S(2)}) collective-permute-start(f32[16,640]{1,0:T(8,128)S(1)} %get-tuple-element.17), channel_id=1, source_target_pairs={{0,12},{1,13},{2,14},{3,15},{4,8},{5,9},{6,10},{7,11},{8,4},{9,5},... | collective-permute-start | bytes 122888 | tf_op jit(solution)/shard_map/ppermute | solution.py:311
  47.3 4.0 %copy-start.4 = (f32[16]{0:T(128)S(1)}, f32[16]{0:T(128)}, u32[]{:S(2)}) copy-start(f32[16]{0:T(128)} %param.9) | copy-start | bytes 196
  47.3 4.0 %collective-permute-start.12 = (f32[16,640]{1,0:T(8,128)S(1)}, f32[16,640]{1,0:T(8,128)S(1)}, u32[]{:S(2)}, u32[]{:S(2)}) collective-permute-start(f32[16,640]{1,0:T(8,128)S(1)} %get-tuple-element.18), channel_id=1, source_target_pairs={{0,4},{1,5},{2,6},{3,7},{4,0},{5,1},{6,2},{7,3},{8,12},{9,13},{10,... | collective-permute-start | bytes 122888 | tf_op jit(solution)/shard_map/ppermute | solution.py:311

commit v21 on v19

--- a/solution.py
+++ b/solution.py
@@ -237,7 +237,7 @@
     )(near, sums, pair, other)
 
 
-def join_kernel(s0, s2, s3, s1, bias, out, held):
+def join_kernel(s0, s3, s2, s1, bias, out, held):
     y = lax.div(lax.axis_index("rows"), 4)
     for k, part in enumerate((s0, s1, s2, s3)):
         held[y ^ k] = part[...]
@@ -298,7 +298,7 @@
     ).reshape(2, 4, 2, 64, 128)
     near = lax.ppermute(lax.dynamic_index_in_dim(both, 1 - pd, 0, False), "depth", depth_near)
     sums = near_level(near, coarse_level(both, pair, other), pair, other)
-    parts = [sums[0]] + [lax.ppermute(sums[k], "rows", along_y(k)) for k in (2, 3, 1)]
+    parts = [sums[0]] + [lax.ppermute(sums[k], "rows", along_y(k)) for k in (3, 2, 1)]
     result = join(parts, jnp.broadcast_to(coarse_bias[:, None], (16, 128)))
     return result.reshape(16, 1, 2048)
 

time: 52.3 us -> 52.7 us (level)
  waiting for transfers between devices: 4.77 us -> 5.31 us
    ppermute x3, waiting for transfers between devices: 4 us -> 4.55 us  [body(): lax.ppermute(sums[k], 'rows', along_y(k))]
where the time goes in v21:
time: 52.7 us; the launch traced here: 52.5 us
  starting transfers between devices  28.6 us (54%)
  blocking collectives  13.7 us (26%)
  waiting for transfers between devices  5.31 us (10%)
  Pallas kernels  3.49 us (7%)
  local copies, waits for them, and re-layouts  1.2 us (2%)
    all_to_all x1, blocking collectives, body(): lax.all_to_all(pooled, ('depth', 'rows'), 0, 0, axis_index_groups=far_and...  13.7 us
    ppermute x1, starting transfers between devices, body(): lax.ppermute(lax.dynamic_index_in_dim(volume, 1 - pd, 0, False), 'depth',...  7.04 us
    ppermute x3, waiting for transfers between devices, body(): lax.ppermute(sums[k], 'rows', along_y(k))  4.55 us
    ppermute x3, starting transfers between devices, body(): lax.ppermute(sums[k], 'rows', along_y(k))  4.48 us
    ppermute x1, starting transfers between devices, body(): lax.ppermute(lax.dynamic_index_in_dim(volume, 3 - 3 * pr, 1, False), 'row...  3.37 us
    ppermute x1, starting transfers between devices, body(): c1 = lax.ppermute(near_row, 'rows', rows_near)  3.34 us
    ppermute x1, starting transfers between devices, body(): pair = jnp.stack([w, lax.ppermute(w, 'rows', along_y(3))])  3.01 us
    ppermute x1, starting transfers between devices, body(): lax.ppermute(lax.dynamic_index_in_dim(both, 1 - pd, 0, False), 'depth', d...  2.32 us
  transfers between devices with their start and end apart: 13, of which 4 were waited for; matrix products, arithmetic and copies ran while one was open for 0% of the time, Pallas kernels for 4%

profile of v21, /device:TPU:6, one launch (start us, length us, event | category | flops | bytes accessed | tf_op | source)
XLA Modules:
  0.0 52.5 jit_solution(18300086703563539754)
XLA Ops:
  0.0 1.1 %dynamic-slice_bitcast_fusion.1 = (bf16[4,128,128]{2,1,0:T(8,128)(2,1)S(1)}, bf16[4,128,128]{2,1,0:T(8,128)(2,1)S(1)}) fusion(bf16[2,4,128,128]{3,2,1,0:T(8,128)(2,1)} %vol.1, s32[]{:T(128)S(6)} %select_n.19, s32[]{:T(128)S(6)} %select_n.18), kind=kLoop, calls=%fused_computation.6 | loop fusion | bytes 524296 | tf_op jit(solution)/shard_map/jit(dynamic_index_in_dim)/squeeze | solution.py:277
  1.1 2.2 %collective-permute-start = (bf16[4,128,128]{2,1,0:T(8,128)(2,1)S(1)}, bf16[4,128,128]{2,1,0:T(8,128)(2,1)S(1)}, u32[]{:S(2)}, u32[]{:S(2)}) collective-permute-start(bf16[4,128,128]{2,1,0:T(8,128)(2,1)S(1)} %get-tuple-element.24), channel_id=1, source_target_pairs={{0,0},{16,32},{32,16},{48,64},{64,48},{80,96},{96,80},{112,128},{1... | collective-permute-start | bytes 393224 | tf_op jit(solution)/shard_map/ppermute | solution.py:276
  3.3 7.0 %collective-permute-start.1 = (bf16[4,128,128]{2,1,0:T(8,128)(2,1)S(1)}, bf16[4,128,128]{2,1,0:T(8,128)(2,1)S(1)}, u32[]{:S(2)}, u32[]{:S(2)}) collective-permute-start(bf16[4,128,128]{2,1,0:T(8,128)(2,1)S(1)} %get-tuple-element.23), channel_id=1, source_target_pairs={{0,16},{16,0},{32,48},{48,32},{64,80},{80,64},{96,112},{112,96},{1... | collective-permute-start | bytes 393224 | tf_op jit(solution)/shard_map/ppermute | solution.py:277
  10.3 3.0 %collective-permute-start.7 = (bf16[27,16,128]{2,1,0:T(8,128)(2,1)S(1)}, bf16[27,16,128]{2,1,0:T(8,128)(2,1)S(1)}, u32[]{:S(2)}, u32[]{:S(2)}) collective-permute-start(bf16[27,16,128]{2,1,0:T(8,128)(2,1)S(1)} %bitcast.28), channel_id=1, source_target_pairs={{0,12},{1,13},{2,14},{3,15},{4,8},{5,9},{6,10},{7,11},{8,4},{9,5},... | collective-permute-start | bytes 331784 | tf_op jit(solution)/shard_map/ppermute | solution.py:291
  13.4 0.7 %collective-permute-start.2 = (bf16[2,128,128]{2,1,0:T(8,128)(2,1)S(1)}, bf16[2,128,128]{2,1,0:T(8,128)(2,1)S(1)}, u32[]{:S(2)}, u32[]{:S(2)}) collective-permute-start(bf16[2,128,128]{2,1,0:T(8,128)(2,1)S(1)} %get-tuple-element.22), channel_id=1, source_target_pairs={{0,0},{1,2},{2,1},{3,4},{4,3},{5,6},{6,5},{7,8},{8,7},{9,10},{10,9... | collective-permute-start | bytes 196616 | tf_op jit(solution)/shard_map/ppermute | solution.py:278
  14.0 3.4 %collective-permute-start.3 = (bf16[2,128,128]{2,1,0:T(8,128)(2,1)S(1)}, bf16[2,128,128]{2,1,0:T(8,128)(2,1)S(1)}, u32[]{:S(2)}, u32[]{:S(2)}) collective-permute-start(bf16[2,128,128]{2,1,0:T(8,128)(2,1)S(1)} %get-tuple-element.21), channel_id=1, source_target_pairs={{0,1},{1,0},{2,3},{3,2},{4,5},{5,4},{6,7},{7,6},{8,9},{9,8},{10,11... | collective-permute-start | bytes 196616 | tf_op jit(solution)/shard_map/ppermute | solution.py:279
  17.4 1.5 %collective-permute-start.8 = (bf16[2,27,16,128]{3,2,1,0:T(8,128)(2,1)S(1)}, bf16[2,27,16,128]{3,2,1,0:T(8,128)(2,1)S(1)}, u32[]{:S(2)}, u32[]{:S(2)}) collective-permute-start(bf16[2,27,16,128]{3,2,1,0:T(8,128)(2,1)S(1)} %pad_maximum_fusion.pair), channel_id=1, source_target_pairs={{0,4},{1,5},{2,6},{3,7},{4,0},{5,1},{6,2},{7,3},{8,12},{9,13},{10,... | collective-permute-start | bytes 663560 | tf_op jit(solution)/shard_map/ppermute | solution.py:292
  18.9 0.7 %collective-permute-start.4 = (bf16[128,128]{1,0:T(8,128)(2,1)S(1)}, bf16[128,128]{1,0:T(8,128)(2,1)S(1)}, u32[]{:S(2)}, u32[]{:S(2)}) collective-permute-start(bf16[128,128]{1,0:T(8,128)(2,1)S(1)} %get-tuple-element.20.far_row), channel_id=1, source_target_pairs={{0,0},{1,2},{2,1},{3,4},{4,3},{5,6},{6,5},{7,8},{8,7},{9,10},{10,9... | collective-permute-start | bytes 98312 | tf_op jit(solution)/shard_map/ppermute | solution.py:283
  19.6 3.3 %collective-permute-start.5 = (bf16[128,128]{1,0:T(8,128)(2,1)S(1)}, bf16[128,128]{1,0:T(8,128)(2,1)S(1)}, u32[]{:S(2)}, u32[]{:S(2)}) collective-permute-start(bf16[128,128]{1,0:T(8,128)(2,1)S(1)} %get-tuple-element.19.near_row), channel_id=1, source_target_pairs={{0,1},{1,0},{2,3},{3,2},{4,5},{5,4},{6,7},{7,6},{8,9},{9,8},{10,11... | collective-permute-start | bytes 98312 | tf_op jit(solution)/shard_map/ppermute | solution.py:284
  23.0 0.1 collective-permute-start.6
  23.1 1.5 %shard_map.55 = (f32[2,2,128,128]{3,2,1,0:T(8,128)S(1)}, f32[2,128,128]{2,1,0:T(8,128)S(1)}, bf16[2,2,128,384]{3,2,1,0:T(8,128)(2,1)S(1)}) custom-call(bf16[2,4,128,128]{3,2,1,0:T(8,128)(2,1)S(1)} %copy-done, bf16[4,128,128]{2,1,0:T(8,128)(2,1)S(1)} %collective-permute-done.x2, bf16[4,128,128]{2,1,0:T(8,128)(2,1)S(1)} %collective-permute-done.1.x1, ...), custom_call_target="tpu_custom_call" | custom-call | flops 20000000000 | tf_op jit(solution)/shard_map/pallas_call | solution.py:88
  24.6 0.4 collective-permute-done.5.c1
  25.0 0.3 shard_map.57
  25.3 13.7 %all_to_all.5 = bf16[8,2,64,128]{3,2,1,0:T(8,128)(2,1)S(1)} all-to-all(bf16[8,2,64,128]{3,2,1,0:T(8,128)(2,1)S(1)} %shard_map.57), channel_id=1, replica_groups={{16,17,18,19,32,33,34,35},{20,21,22,23,36,37,38,39},{24,25,26,27,40,41,..., dimensions={0} | all-to-all | bytes 524288 | tf_op jit(solution)/shard_map/all_to_all | solution.py:296
  38.9 2.3 %collective-permute-start.9 = (bf16[4,2,64,128]{3,2,1,0:T(8,128)(2,1)S(1)}, bf16[4,2,64,128]{3,2,1,0:T(8,128)(2,1)S(1)}, u32[]{:S(2)}, u32[]{:S(2)}) collective-permute-start(bf16[4,2,64,128]{3,2,1,0:T(8,128)(2,1)S(1)} %dynamic-slice_bitcast_fusion), channel_id=1, source_target_pairs={{0,16},{16,0},{32,48},{48,32},{64,80},{80,64},{96,112},{112,96},{1... | collective-permute-start | bytes 393224 | tf_op jit(solution)/shard_map/ppermute | solution.py:299
  41.2 0.6 %shard_map.58.sums = f32[64,640]{1,0:T(8,128)S(1)} custom-call(bf16[2,4,2,64,128]{4,3,2,1,0:T(8,128)(2,1)S(1)} %bitcast.25, bf16[2,27,16,128]{3,2,1,0:T(8,128)(2,1)S(1)} %pad_maximum_fusion.pair, bf16[2,27,16,128]{3,2,1,0:T(8,128)(2,1)S(1)} %collective-permute-done.8.other), custom_call_target="tpu_custom_call" | custom-call | flops 150000000 | tf_op jit(solution)/shard_map/pallas_call | solution.py:202
  41.8 0.4 collective-permute-done.9.near
  42.2 0.4 shard_map.59
  42.7 3.5 %collective-permute-start.10 = (f32[16,640]{1,0:T(8,128)S(1)}, f32[16,640]{1,0:T(8,128)S(1)}, u32[]{:S(2)}, u32[]{:S(2)}) collective-permute-start(f32[16,640]{1,0:T(8,128)S(1)} %get-tuple-element.16), channel_id=1, source_target_pairs={{0,12},{1,13},{2,14},{3,15},{4,8},{5,9},{6,10},{7,11},{8,4},{9,5},... | collective-permute-start | bytes 122888 | tf_op jit(solution)/shard_map/ppermute | solution.py:301
  46.2 0.5 collective-permute-start.11
  46.7 0.5 collective-permute-start.12
  47.2 1.3 %collective-permute-done.10.s3 = f32[16,640]{1,0:T(8,128)S(1)} collective-permute-done((f32[16,640]{1,0:T(8,128)S(1)}, f32[16,640]{1,0:T(8,128)S(1)}, u32[]{:S(2)}, u32[]{:S(2)}) %collective-permute-start.10) | collective-permute-done | bytes 40992 | tf_op jit(solution)/shard_map/ppermute | solution.py:301
  48.5 3.3 %collective-permute-done.11.s2 = f32[16,640]{1,0:T(8,128)S(1)} collective-permute-done((f32[16,640]{1,0:T(8,128)S(1)}, f32[16,640]{1,0:T(8,128)S(1)}, u32[]{:S(2)}, u32[]{:S(2)}) %collective-permute-start.11) | collective-permute-done | bytes 40992 | tf_op jit(solution)/shard_map/ppermute | solution.py:301
  51.8 0.7 %shard_map.60 = bf16[16,2048]{1,0:T(8,128)(2,1)} custom-call(f32[16,640]{1,0:T(8,128)S(1)} %get-tuple-element.15.s0, f32[16,640]{1,0:T(8,128)S(1)} %collective-permute-done.10.s3, f32[16,640]{1,0:T(8,128)S(1)} %collective-permute-done.11.s2, f32[16,640]{1,0:T(8,128)S(1)} %collective-permute-done.12.s1, f32[16,128]{1,0:T(8,128)S(1)} %broadcast_in_dim.10.bias), custom_call_target="tpu_custom_call" | custom-call | tf_op jit(solution)/shard_map/pallas_call | solution.py:258
  (26 shorter events, 0.2 us)
Async XLA Ops:
  0.0 10.3 %copy-start.2 = (bf16[3,3,3,128,16]{3,4,2,1,0:T(8,128)(2,1)S(1)}, bf16[3,3,3,128,16]{3,4,2,1,0:T(8,128)(2,1)}, u32[]{:S(2)}) copy-start(bf16[3,3,3,128,16]{3,4,2,1,0:T(8,128)(2,1)} %param.8) | copy-start | bytes 331780
  0.0 13.3 %copy-start = (bf16[2,4,128,128]{3,2,1,0:T(8,128)(2,1)S(1)}, bf16[2,4,128,128]{3,2,1,0:T(8,128)(2,1)}, u32[]{:S(2)}) copy-start(bf16[2,4,128,128]{3,2,1,0:T(8,128)(2,1)} %vol.1) | copy-start | bytes 786436
  0.0 23.1 %copy-start.1 = (bf16[3,3,3,128,128]{4,3,2,1,0:T(8,128)(2,1)S(1)}, bf16[3,3,3,128,128]{4,3,2,1,0:T(8,128)(2,1)}, u32[]{:S(2)}) copy-start(bf16[3,3,3,128,128]{4,3,2,1,0:T(8,128)(2,1)} %w.1) | copy-start | bytes 2654212
  1.1 17.8 %collective-permute-start = (bf16[4,128,128]{2,1,0:T(8,128)(2,1)S(1)}, bf16[4,128,128]{2,1,0:T(8,128)(2,1)S(1)}, u32[]{:S(2)}, u32[]{:S(2)}) collective-permute-start(bf16[4,128,128]{2,1,0:T(8,128)(2,1)S(1)} %get-tuple-element.24), channel_id=1, source_target_pairs={{0,0},{16,32},{32,16},{48,64},{64,48},{80,96},{96,80},{112,128},{1... | collective-permute-start | bytes 393224 | tf_op jit(solution)/shard_map/ppermute | solution.py:276
  3.3 15.6 %collective-permute-start.1 = (bf16[4,128,128]{2,1,0:T(8,128)(2,1)S(1)}, bf16[4,128,128]{2,1,0:T(8,128)(2,1)S(1)}, u32[]{:S(2)}, u32[]{:S(2)}) collective-permute-start(bf16[4,128,128]{2,1,0:T(8,128)(2,1)S(1)} %get-tuple-element.23), channel_id=1, source_target_pairs={{0,16},{16,0},{32,48},{48,32},{64,80},{80,64},{96,112},{112,96},{1... | collective-permute-start | bytes 393224 | tf_op jit(solution)/shard_map/ppermute | solution.py:277
  10.3 7.1 %collective-permute-start.7 = (bf16[27,16,128]{2,1,0:T(8,128)(2,1)S(1)}, bf16[27,16,128]{2,1,0:T(8,128)(2,1)S(1)}, u32[]{:S(2)}, u32[]{:S(2)}) collective-permute-start(bf16[27,16,128]{2,1,0:T(8,128)(2,1)S(1)} %bitcast.28), channel_id=1, source_target_pairs={{0,12},{1,13},{2,14},{3,15},{4,8},{5,9},{6,10},{7,11},{8,4},{9,5},... | collective-permute-start | bytes 331784 | tf_op jit(solution)/shard_map/ppermute | solution.py:291
  13.4 9.6 %collective-permute-start.2 = (bf16[2,128,128]{2,1,0:T(8,128)(2,1)S(1)}, bf16[2,128,128]{2,1,0:T(8,128)(2,1)S(1)}, u32[]{:S(2)}, u32[]{:S(2)}) collective-permute-start(bf16[2,128,128]{2,1,0:T(8,128)(2,1)S(1)} %get-tuple-element.22), channel_id=1, source_target_pairs={{0,0},{1,2},{2,1},{3,4},{4,3},{5,6},{6,5},{7,8},{8,7},{9,10},{10,9... | collective-permute-start | bytes 196616 | tf_op jit(solution)/shard_map/ppermute | solution.py:278
  14.0 8.9 %collective-permute-start.3 = (bf16[2,128,128]{2,1,0:T(8,128)(2,1)S(1)}, bf16[2,128,128]{2,1,0:T(8,128)(2,1)S(1)}, u32[]{:S(2)}, u32[]{:S(2)}) collective-permute-start(bf16[2,128,128]{2,1,0:T(8,128)(2,1)S(1)} %get-tuple-element.21), channel_id=1, source_target_pairs={{0,1},{1,0},{2,3},{3,2},{4,5},{5,4},{6,7},{7,6},{8,9},{9,8},{10,11... | collective-permute-start | bytes 196616 | tf_op jit(solution)/shard_map/ppermute | solution.py:279
  17.4 7.5 %collective-permute-start.8 = (bf16[2,27,16,128]{3,2,1,0:T(8,128)(2,1)S(1)}, bf16[2,27,16,128]{3,2,1,0:T(8,128)(2,1)S(1)}, u32[]{:S(2)}, u32[]{:S(2)}) collective-permute-start(bf16[2,27,16,128]{3,2,1,0:T(8,128)(2,1)S(1)} %pad_maximum_fusion.pair), channel_id=1, source_target_pairs={{0,4},{1,5},{2,6},{3,7},{4,0},{5,1},{6,2},{7,3},{8,12},{9,13},{10,... | collective-permute-start | bytes 663560 | tf_op jit(solution)/shard_map/ppermute | solution.py:292
  18.9 5.7 %collective-permute-start.4 = (bf16[128,128]{1,0:T(8,128)(2,1)S(1)}, bf16[128,128]{1,0:T(8,128)(2,1)S(1)}, u32[]{:S(2)}, u32[]{:S(2)}) collective-permute-start(bf16[128,128]{1,0:T(8,128)(2,1)S(1)} %get-tuple-element.20.far_row), channel_id=1, source_target_pairs={{0,0},{1,2},{2,1},{3,4},{4,3},{5,6},{6,5},{7,8},{8,7},{9,10},{10,9... | collective-permute-start | bytes 98312 | tf_op jit(solution)/shard_map/ppermute | solution.py:283
  19.6 3.5 %copy-start.3 = (f32[128]{0:T(128)S(1)}, f32[128]{0:T(128)}, u32[]{:S(2)}) copy-start(f32[128]{0:T(128)} %param.7) | copy-start | bytes 1540
  19.6 5.4 %collective-permute-start.5 = (bf16[128,128]{1,0:T(8,128)(2,1)S(1)}, bf16[128,128]{1,0:T(8,128)(2,1)S(1)}, u32[]{:S(2)}, u32[]{:S(2)}) collective-permute-start(bf16[128,128]{1,0:T(8,128)(2,1)S(1)} %get-tuple-element.19.near_row), channel_id=1, source_target_pairs={{0,1},{1,0},{2,3},{3,2},{4,5},{5,4},{6,7},{7,6},{8,9},{9,8},{10,11... | collective-permute-start | bytes 98312 | tf_op jit(solution)/shard_map/ppermute | solution.py:284
  23.0 2.0 %collective-permute-start.6 = (bf16[2,128,128]{2,1,0:T(8,128)(2,1)S(1)}, bf16[2,128,128]{2,1,0:T(8,128)(2,1)S(1)}, u32[]{:S(2)}, u32[]{:S(2)}) collective-permute-start(bf16[2,128,128]{2,1,0:T(8,128)(2,1)S(1)} %shard_map.56), channel_id=1, source_target_pairs={{0,16},{16,0},{32,48},{48,32},{64,80},{80,64},{96,112},{112,96},{1... | collective-permute-start | bytes 196616 | tf_op jit(solution)/shard_map/ppermute | solution.py:285
  38.9 3.3 %collective-permute-start.9 = (bf16[4,2,64,128]{3,2,1,0:T(8,128)(2,1)S(1)}, bf16[4,2,64,128]{3,2,1,0:T(8,128)(2,1)S(1)}, u32[]{:S(2)}, u32[]{:S(2)}) collective-permute-start(bf16[4,2,64,128]{3,2,1,0:T(8,128)(2,1)S(1)} %dynamic-slice_bitcast_fusion), channel_id=1, source_target_pairs={{0,16},{16,0},{32,48},{48,32},{64,80},{80,64},{96,112},{112,96},{1... | collective-permute-start | bytes 393224 | tf_op jit(solution)/shard_map/ppermute | solution.py:299
  42.7 5.8 %collective-permute-start.10 = (f32[16,640]{1,0:T(8,128)S(1)}, f32[16,640]{1,0:T(8,128)S(1)}, u32[]{:S(2)}, u32[]{:S(2)}) collective-permute-start(f32[16,640]{1,0:T(8,128)S(1)} %get-tuple-element.16), channel_id=1, source_target_pairs={{0,12},{1,13},{2,14},{3,15},{4,8},{5,9},{6,10},{7,11},{8,4},{9,5},... | collective-permute-start | bytes 122888 | tf_op jit(solution)/shard_map/ppermute | solution.py:301
  46.2 5.5 %collective-permute-start.11 = (f32[16,640]{1,0:T(8,128)S(1)}, f32[16,640]{1,0:T(8,128)S(1)}, u32[]{:S(2)}, u32[]{:S(2)}) collective-permute-start(f32[16,640]{1,0:T(8,128)S(1)} %get-tuple-element.17), channel_id=1, source_target_pairs={{0,8},{1,9},{2,10},{3,11},{4,12},{5,13},{6,14},{7,15},{8,0},{9,1},... | collective-permute-start | bytes 122888 | tf_op jit(solution)/shard_map/ppermute | solution.py:301
  46.7 5.1 %copy-start.4 = (f32[16]{0:T(128)S(1)}, f32[16]{0:T(128)}, u32[]{:S(2)}) copy-start(f32[16]{0:T(128)} %param.9) | copy-start | bytes 196
  46.7 5.1 %collective-permute-start.12 = (f32[16,640]{1,0:T(8,128)S(1)}, f32[16,640]{1,0:T(8,128)S(1)}, u32[]{:S(2)}, u32[]{:S(2)}) collective-permute-start(f32[16,640]{1,0:T(8,128)S(1)} %get-tuple-element.18), channel_id=1, source_target_pairs={{0,4},{1,5},{2,6},{3,7},{4,0},{5,1},{6,2},{7,3},{8,12},{9,13},{10,... | collective-permute-start | bytes 122888 | tf_op jit(solution)/shard_map/ppermute | solution.py:301

commit v22 on v19

--- a/solution.py
+++ b/solution.py
@@ -54,26 +54,25 @@
             if j == 0:
                 piece = jnp.where(inner_d, piece, zero)
             cells[j, i] = piece
-    taps = [(a, b) for a in range(3) for b in range(3)]
-    groups = [taps[i : i + 2] for i in range(0, 9, 2)]
-    col = lax.broadcasted_iota(jnp.int32, (128, 128), 0)
-    for s in range(2):
+    def tap(a, b):
+        return [w[a + pd * (2 - 2 * a), b + pr * (2 - 2 * b), c] for c in range(3)]
+
+    def line_sums(pieces, outs):
         total = None
-        for group in groups:
-            lhs = jnp.concatenate(
-                [cells[s + a, b : b + 4].reshape(512, 128) for a, b in group], axis=1
-            )
+        for i in range(0, len(pieces), 2):
+            group = pieces[i : i + 2]
+            lhs = jnp.concatenate([cells[j, b : b + 4].reshape(512, 128) for j, b in group], axis=1)
             rhs = jnp.concatenate(
-                [
-                    jnp.concatenate(
-                        [w[a + pd * (2 - 2 * a), b + pr * (2 - 2 * b), c] for c in range(3)], axis=1
-                    )
-                    for a, b in group
-                ],
-                axis=0,
+                [jnp.concatenate(sum([tap(j - s, b) for s in outs], []), axis=1) for j, b in group], axis=0
             )
             term = jnp.dot(lhs, rhs, preferred_element_type=F32)
             total = term if total is None else total + term
+        return total
+
+    col = lax.broadcasted_iota(jnp.int32, (128, 128), 0)
+    shared = line_sums([(j, b) for j in (1, 2) for b in range(3)], (0, 1))
+    for s in range(2):
+        total = shared[:, 384 * s : 384 * s + 384] + line_sums([(3 * s, b) for b in range(3)], (s,))
         for q in range(2):
             ends[s, q] = spread(total[3 * q * 128 : (3 * q + 1) * 128], col) + bias[:1]
             middle = spread(total[(q + 1) * 128 : (q + 2) * 128], col) + bias[:1]

time: 52.3 us -> 52.3 us (level)
  no operation moved by 1% of the time
where the time goes in v22:
time: 52.3 us; the launch traced here: 52 us
  starting transfers between devices  28.7 us (55%)
  blocking collectives  13.7 us (26%)
  waiting for transfers between devices  4.99 us (10%)
  Pallas kernels  3.27 us (6%)
  local copies, waits for them, and re-layouts  1.2 us (2%)
    all_to_all x1, blocking collectives, body(): lax.all_to_all(pooled, ('depth', 'rows'), 0, 0, axis_index_groups=far_and...  13.7 us
    ppermute x1, starting transfers between devices, body(): lax.ppermute(lax.dynamic_index_in_dim(volume, 1 - pd, 0, False), 'depth',...  7.04 us
    ppermute x3, starting transfers between devices, body(): lax.ppermute(sums[k], 'rows', along_y(k))  4.59 us
    ppermute x3, waiting for transfers between devices, body(): lax.ppermute(sums[k], 'rows', along_y(k))  4 us
    ppermute x1, starting transfers between devices, body(): lax.ppermute(lax.dynamic_index_in_dim(volume, 3 - 3 * pr, 1, False), 'row...  3.37 us
    ppermute x1, starting transfers between devices, body(): c1 = lax.ppermute(near_row, 'rows', rows_near)  3.34 us
    ppermute x1, starting transfers between devices, body(): pair = jnp.stack([w, lax.ppermute(w, 'rows', along_y(3))])  3.01 us
    ppermute x1, starting transfers between devices, body(): lax.ppermute(lax.dynamic_index_in_dim(both, 1 - pd, 0, False), 'depth', d...  2.32 us
  transfers between devices with their start and end apart: 13, of which 4 were waited for; matrix products, arithmetic and copies ran while one was open for 0% of the time, Pallas kernels for 4%

profile of v22, /device:TPU:6, one launch (start us, length us, event | category | flops | bytes accessed | tf_op | source)
XLA Modules:
  0.0 52.0 jit_solution(3235297182818846768)
XLA Ops:
  0.0 1.1 %dynamic-slice_bitcast_fusion.1 = (bf16[4,128,128]{2,1,0:T(8,128)(2,1)S(1)}, bf16[4,128,128]{2,1,0:T(8,128)(2,1)S(1)}) fusion(bf16[2,4,128,128]{3,2,1,0:T(8,128)(2,1)} %vol.1, s32[]{:T(128)S(6)} %select_n.19, s32[]{:T(128)S(6)} %select_n.18), kind=kLoop, calls=%fused_computation.6 | loop fusion | bytes 524296 | tf_op jit(solution)/shard_map/jit(dynamic_index_in_dim)/squeeze | solution.py:276
  1.1 2.2 %collective-permute-start = (bf16[4,128,128]{2,1,0:T(8,128)(2,1)S(1)}, bf16[4,128,128]{2,1,0:T(8,128)(2,1)S(1)}, u32[]{:S(2)}, u32[]{:S(2)}) collective-permute-start(bf16[4,128,128]{2,1,0:T(8,128)(2,1)S(1)} %get-tuple-element.24), channel_id=1, source_target_pairs={{0,0},{16,32},{32,16},{48,64},{64,48},{80,96},{96,80},{112,128},{1... | collective-permute-start | bytes 393224 | tf_op jit(solution)/shard_map/ppermute | solution.py:275
  3.3 7.0 %collective-permute-start.1 = (bf16[4,128,128]{2,1,0:T(8,128)(2,1)S(1)}, bf16[4,128,128]{2,1,0:T(8,128)(2,1)S(1)}, u32[]{:S(2)}, u32[]{:S(2)}) collective-permute-start(bf16[4,128,128]{2,1,0:T(8,128)(2,1)S(1)} %get-tuple-element.23), channel_id=1, source_target_pairs={{0,16},{16,0},{32,48},{48,32},{64,80},{80,64},{96,112},{112,96},{1... | collective-permute-start | bytes 393224 | tf_op jit(solution)/shard_map/ppermute | solution.py:276
  10.3 3.0 %collective-permute-start.7 = (bf16[27,16,128]{2,1,0:T(8,128)(2,1)S(1)}, bf16[27,16,128]{2,1,0:T(8,128)(2,1)S(1)}, u32[]{:S(2)}, u32[]{:S(2)}) collective-permute-start(bf16[27,16,128]{2,1,0:T(8,128)(2,1)S(1)} %bitcast.28), channel_id=1, source_target_pairs={{0,12},{1,13},{2,14},{3,15},{4,8},{5,9},{6,10},{7,11},{8,4},{9,5},... | collective-permute-start | bytes 331784 | tf_op jit(solution)/shard_map/ppermute | solution.py:290
  13.4 0.7 %collective-permute-start.2 = (bf16[2,128,128]{2,1,0:T(8,128)(2,1)S(1)}, bf16[2,128,128]{2,1,0:T(8,128)(2,1)S(1)}, u32[]{:S(2)}, u32[]{:S(2)}) collective-permute-start(bf16[2,128,128]{2,1,0:T(8,128)(2,1)S(1)} %get-tuple-element.22), channel_id=1, source_target_pairs={{0,0},{1,2},{2,1},{3,4},{4,3},{5,6},{6,5},{7,8},{8,7},{9,10},{10,9... | collective-permute-start | bytes 196616 | tf_op jit(solution)/shard_map/ppermute | solution.py:277
  14.0 3.4 %collective-permute-start.3 = (bf16[2,128,128]{2,1,0:T(8,128)(2,1)S(1)}, bf16[2,128,128]{2,1,0:T(8,128)(2,1)S(1)}, u32[]{:S(2)}, u32[]{:S(2)}) collective-permute-start(bf16[2,128,128]{2,1,0:T(8,128)(2,1)S(1)} %get-tuple-element.21), channel_id=1, source_target_pairs={{0,1},{1,0},{2,3},{3,2},{4,5},{5,4},{6,7},{7,6},{8,9},{9,8},{10,11... | collective-permute-start | bytes 196616 | tf_op jit(solution)/shard_map/ppermute | solution.py:278
  17.4 1.5 %collective-permute-start.8 = (bf16[2,27,16,128]{3,2,1,0:T(8,128)(2,1)S(1)}, bf16[2,27,16,128]{3,2,1,0:T(8,128)(2,1)S(1)}, u32[]{:S(2)}, u32[]{:S(2)}) collective-permute-start(bf16[2,27,16,128]{3,2,1,0:T(8,128)(2,1)S(1)} %pad_maximum_fusion.pair), channel_id=1, source_target_pairs={{0,4},{1,5},{2,6},{3,7},{4,0},{5,1},{6,2},{7,3},{8,12},{9,13},{10,... | collective-permute-start | bytes 663560 | tf_op jit(solution)/shard_map/ppermute | solution.py:291
  18.9 0.7 %collective-permute-start.4 = (bf16[128,128]{1,0:T(8,128)(2,1)S(1)}, bf16[128,128]{1,0:T(8,128)(2,1)S(1)}, u32[]{:S(2)}, u32[]{:S(2)}) collective-permute-start(bf16[128,128]{1,0:T(8,128)(2,1)S(1)} %get-tuple-element.20.far_row), channel_id=1, source_target_pairs={{0,0},{1,2},{2,1},{3,4},{4,3},{5,6},{6,5},{7,8},{8,7},{9,10},{10,9... | collective-permute-start | bytes 98312 | tf_op jit(solution)/shard_map/ppermute | solution.py:282
  19.6 3.3 %collective-permute-start.5 = (bf16[128,128]{1,0:T(8,128)(2,1)S(1)}, bf16[128,128]{1,0:T(8,128)(2,1)S(1)}, u32[]{:S(2)}, u32[]{:S(2)}) collective-permute-start(bf16[128,128]{1,0:T(8,128)(2,1)S(1)} %get-tuple-element.19.near_row), channel_id=1, source_target_pairs={{0,1},{1,0},{2,3},{3,2},{4,5},{5,4},{6,7},{7,6},{8,9},{9,8},{10,11... | collective-permute-start | bytes 98312 | tf_op jit(solution)/shard_map/ppermute | solution.py:283
  23.0 0.1 collective-permute-start.6
  23.1 1.3 %shard_map.55 = (f32[2,2,128,128]{3,2,1,0:T(8,128)S(1)}, f32[2,128,128]{2,1,0:T(8,128)S(1)}, bf16[2,2,128,384]{3,2,1,0:T(8,128)(2,1)S(1)}) custom-call(bf16[2,4,128,128]{3,2,1,0:T(8,128)(2,1)S(1)} %copy-done, bf16[4,128,128]{2,1,0:T(8,128)(2,1)S(1)} %collective-permute-done.x2, bf16[4,128,128]{2,1,0:T(8,128)(2,1)S(1)} %collective-permute-done.1.x1, ...), custom_call_target="tpu_custom_call" | custom-call | flops 20000000000 | tf_op jit(solution)/shard_map/pallas_call | solution.py:87
  24.4 0.6 %collective-permute-done.5.c1 = bf16[128,128]{1,0:T(8,128)(2,1)S(1)} collective-permute-done((bf16[128,128]{1,0:T(8,128)(2,1)S(1)}, bf16[128,128]{1,0:T(8,128)(2,1)S(1)}, u32[]{:S(2)}, u32[]{:S(2)}) %collective-permute-start.5) | collective-permute-done | bytes 32800 | tf_op jit(solution)/shard_map/ppermute | solution.py:283
  25.0 0.3 shard_map.57
  25.3 13.7 %all_to_all.5 = bf16[8,2,64,128]{3,2,1,0:T(8,128)(2,1)S(1)} all-to-all(bf16[8,2,64,128]{3,2,1,0:T(8,128)(2,1)S(1)} %shard_map.57), channel_id=1, replica_groups={{16,17,18,19,32,33,34,35},{20,21,22,23,36,37,38,39},{24,25,26,27,40,41,..., dimensions={0} | all-to-all | bytes 524288 | tf_op jit(solution)/shard_map/all_to_all | solution.py:295
  38.9 2.3 %collective-permute-start.9 = (bf16[4,2,64,128]{3,2,1,0:T(8,128)(2,1)S(1)}, bf16[4,2,64,128]{3,2,1,0:T(8,128)(2,1)S(1)}, u32[]{:S(2)}, u32[]{:S(2)}) collective-permute-start(bf16[4,2,64,128]{3,2,1,0:T(8,128)(2,1)S(1)} %dynamic-slice_bitcast_fusion), channel_id=1, source_target_pairs={{0,16},{16,0},{32,48},{48,32},{64,80},{80,64},{96,112},{112,96},{1... | collective-permute-start | bytes 393224 | tf_op jit(solution)/shard_map/ppermute | solution.py:298
  41.2 0.6 %shard_map.58.sums = f32[64,640]{1,0:T(8,128)S(1)} custom-call(bf16[2,4,2,64,128]{4,3,2,1,0:T(8,128)(2,1)S(1)} %bitcast.25, bf16[2,27,16,128]{3,2,1,0:T(8,128)(2,1)S(1)} %pad_maximum_fusion.pair, bf16[2,27,16,128]{3,2,1,0:T(8,128)(2,1)S(1)} %collective-permute-done.8.other), custom_call_target="tpu_custom_call" | custom-call | flops 150000000 | tf_op jit(solution)/shard_map/pallas_call | solution.py:201
  41.8 0.4 collective-permute-done.9.near
  42.2 0.4 shard_map.59
  42.7 3.4 %collective-permute-start.10 = (f32[16,640]{1,0:T(8,128)S(1)}, f32[16,640]{1,0:T(8,128)S(1)}, u32[]{:S(2)}, u32[]{:S(2)}) collective-permute-start(f32[16,640]{1,0:T(8,128)S(1)} %get-tuple-element.16), channel_id=1, source_target_pairs={{0,8},{1,9},{2,10},{3,11},{4,12},{5,13},{6,14},{7,15},{8,0},{9,1},... | collective-permute-start | bytes 122888 | tf_op jit(solution)/shard_map/ppermute | solution.py:300
  46.1 1.2 %collective-permute-start.11 = (f32[16,640]{1,0:T(8,128)S(1)}, f32[16,640]{1,0:T(8,128)S(1)}, u32[]{:S(2)}, u32[]{:S(2)}) collective-permute-start(f32[16,640]{1,0:T(8,128)S(1)} %get-tuple-element.17), channel_id=1, source_target_pairs={{0,12},{1,13},{2,14},{3,15},{4,8},{5,9},{6,10},{7,11},{8,4},{9,5},... | collective-permute-start | bytes 122888 | tf_op jit(solution)/shard_map/ppermute | solution.py:300
  47.3 1.0 %collective-permute-done.10.s2 = f32[16,640]{1,0:T(8,128)S(1)} collective-permute-done((f32[16,640]{1,0:T(8,128)S(1)}, f32[16,640]{1,0:T(8,128)S(1)}, u32[]{:S(2)}, u32[]{:S(2)}) %collective-permute-start.10) | collective-permute-done | bytes 40992 | tf_op jit(solution)/shard_map/ppermute | solution.py:300
  48.3 3.0 %collective-permute-done.11.s3 = f32[16,640]{1,0:T(8,128)S(1)} collective-permute-done((f32[16,640]{1,0:T(8,128)S(1)}, f32[16,640]{1,0:T(8,128)S(1)}, u32[]{:S(2)}, u32[]{:S(2)}) %collective-permute-start.11) | collective-permute-done | bytes 40992 | tf_op jit(solution)/shard_map/ppermute | solution.py:300
  51.3 0.1 broadcast_in_dim.10.bias
  51.3 0.7 %shard_map.60 = bf16[16,2048]{1,0:T(8,128)(2,1)} custom-call(f32[16,640]{1,0:T(8,128)S(1)} %get-tuple-element.15.s0, f32[16,640]{1,0:T(8,128)S(1)} %collective-permute-done.10.s2, f32[16,640]{1,0:T(8,128)S(1)} %collective-permute-done.11.s3, f32[16,640]{1,0:T(8,128)S(1)} %collective-permute-done.12.s1, f32[16,128]{1,0:T(8,128)S(1)} %broadcast_in_dim.10.bias), custom_call_target="tpu_custom_call" | custom-call | tf_op jit(solution)/shard_map/pallas_call | solution.py:257
  (26 shorter events, 0.1 us)
Async XLA Ops:
  0.0 10.3 %copy-start.2 = (bf16[3,3,3,128,16]{3,4,2,1,0:T(8,128)(2,1)S(1)}, bf16[3,3,3,128,16]{3,4,2,1,0:T(8,128)(2,1)}, u32[]{:S(2)}) copy-start(bf16[3,3,3,128,16]{3,4,2,1,0:T(8,128)(2,1)} %param.8) | copy-start | bytes 331780
  0.0 13.3 %copy-start = (bf16[2,4,128,128]{3,2,1,0:T(8,128)(2,1)S(1)}, bf16[2,4,128,128]{3,2,1,0:T(8,128)(2,1)}, u32[]{:S(2)}) copy-start(bf16[2,4,128,128]{3,2,1,0:T(8,128)(2,1)} %vol.1) | copy-start | bytes 786436
  0.0 23.1 %copy-start.1 = (bf16[3,3,3,128,128]{4,3,2,1,0:T(8,128)(2,1)S(1)}, bf16[3,3,3,128,128]{4,3,2,1,0:T(8,128)(2,1)}, u32[]{:S(2)}) copy-start(bf16[3,3,3,128,128]{4,3,2,1,0:T(8,128)(2,1)} %w.1) | copy-start | bytes 2654212
  1.1 17.8 %collective-permute-start = (bf16[4,128,128]{2,1,0:T(8,128)(2,1)S(1)}, bf16[4,128,128]{2,1,0:T(8,128)(2,1)S(1)}, u32[]{:S(2)}, u32[]{:S(2)}) collective-permute-start(bf16[4,128,128]{2,1,0:T(8,128)(2,1)S(1)} %get-tuple-element.24), channel_id=1, source_target_pairs={{0,0},{16,32},{32,16},{48,64},{64,48},{80,96},{96,80},{112,128},{1... | collective-permute-start | bytes 393224 | tf_op jit(solution)/shard_map/ppermute | solution.py:275
  3.3 15.6 %collective-permute-start.1 = (bf16[4,128,128]{2,1,0:T(8,128)(2,1)S(1)}, bf16[4,128,128]{2,1,0:T(8,128)(2,1)S(1)}, u32[]{:S(2)}, u32[]{:S(2)}) collective-permute-start(bf16[4,128,128]{2,1,0:T(8,128)(2,1)S(1)} %get-tuple-element.23), channel_id=1, source_target_pairs={{0,16},{16,0},{32,48},{48,32},{64,80},{80,64},{96,112},{112,96},{1... | collective-permute-start | bytes 393224 | tf_op jit(solution)/shard_map/ppermute | solution.py:276
  10.3 7.1 %collective-permute-start.7 = (bf16[27,16,128]{2,1,0:T(8,128)(2,1)S(1)}, bf16[27,16,128]{2,1,0:T(8,128)(2,1)S(1)}, u32[]{:S(2)}, u32[]{:S(2)}) collective-permute-start(bf16[27,16,128]{2,1,0:T(8,128)(2,1)S(1)} %bitcast.28), channel_id=1, source_target_pairs={{0,12},{1,13},{2,14},{3,15},{4,8},{5,9},{6,10},{7,11},{8,4},{9,5},... | collective-permute-start | bytes 331784 | tf_op jit(solution)/shard_map/ppermute | solution.py:290
  13.4 9.6 %collective-permute-start.2 = (bf16[2,128,128]{2,1,0:T(8,128)(2,1)S(1)}, bf16[2,128,128]{2,1,0:T(8,128)(2,1)S(1)}, u32[]{:S(2)}, u32[]{:S(2)}) collective-permute-start(bf16[2,128,128]{2,1,0:T(8,128)(2,1)S(1)} %get-tuple-element.22), channel_id=1, source_target_pairs={{0,0},{1,2},{2,1},{3,4},{4,3},{5,6},{6,5},{7,8},{8,7},{9,10},{10,9... | collective-permute-start | bytes 196616 | tf_op jit(solution)/shard_map/ppermute | solution.py:277
  14.0 8.9 %collective-permute-start.3 = (bf16[2,128,128]{2,1,0:T(8,128)(2,1)S(1)}, bf16[2,128,128]{2,1,0:T(8,128)(2,1)S(1)}, u32[]{:S(2)}, u32[]{:S(2)}) collective-permute-start(bf16[2,128,128]{2,1,0:T(8,128)(2,1)S(1)} %get-tuple-element.21), channel_id=1, source_target_pairs={{0,1},{1,0},{2,3},{3,2},{4,5},{5,4},{6,7},{7,6},{8,9},{9,8},{10,11... | collective-permute-start | bytes 196616 | tf_op jit(solution)/shard_map/ppermute | solution.py:278
  17.4 7.5 %collective-permute-start.8 = (bf16[2,27,16,128]{3,2,1,0:T(8,128)(2,1)S(1)}, bf16[2,27,16,128]{3,2,1,0:T(8,128)(2,1)S(1)}, u32[]{:S(2)}, u32[]{:S(2)}) collective-permute-start(bf16[2,27,16,128]{3,2,1,0:T(8,128)(2,1)S(1)} %pad_maximum_fusion.pair), channel_id=1, source_target_pairs={{0,4},{1,5},{2,6},{3,7},{4,0},{5,1},{6,2},{7,3},{8,12},{9,13},{10,... | collective-permute-start | bytes 663560 | tf_op jit(solution)/shard_map/ppermute | solution.py:291
  18.9 5.5 %collective-permute-start.4 = (bf16[128,128]{1,0:T(8,128)(2,1)S(1)}, bf16[128,128]{1,0:T(8,128)(2,1)S(1)}, u32[]{:S(2)}, u32[]{:S(2)}) collective-permute-start(bf16[128,128]{1,0:T(8,128)(2,1)S(1)} %get-tuple-element.20.far_row), channel_id=1, source_target_pairs={{0,0},{1,2},{2,1},{3,4},{4,3},{5,6},{6,5},{7,8},{8,7},{9,10},{10,9... | collective-permute-start | bytes 98312 | tf_op jit(solution)/shard_map/ppermute | solution.py:282
  19.6 3.5 %copy-start.3 = (f32[128]{0:T(128)S(1)}, f32[128]{0:T(128)}, u32[]{:S(2)}) copy-start(f32[128]{0:T(128)} %param.7) | copy-start | bytes 1540
  19.6 5.4 %collective-permute-start.5 = (bf16[128,128]{1,0:T(8,128)(2,1)S(1)}, bf16[128,128]{1,0:T(8,128)(2,1)S(1)}, u32[]{:S(2)}, u32[]{:S(2)}) collective-permute-start(bf16[128,128]{1,0:T(8,128)(2,1)S(1)} %get-tuple-element.19.near_row), channel_id=1, source_target_pairs={{0,1},{1,0},{2,3},{3,2},{4,5},{5,4},{6,7},{7,6},{8,9},{9,8},{10,11... | collective-permute-start | bytes 98312 | tf_op jit(solution)/shard_map/ppermute | solution.py:283
  23.0 2.0 %collective-permute-start.6 = (bf16[2,128,128]{2,1,0:T(8,128)(2,1)S(1)}, bf16[2,128,128]{2,1,0:T(8,128)(2,1)S(1)}, u32[]{:S(2)}, u32[]{:S(2)}) collective-permute-start(bf16[2,128,128]{2,1,0:T(8,128)(2,1)S(1)} %shard_map.56), channel_id=1, source_target_pairs={{0,16},{16,0},{32,48},{48,32},{64,80},{80,64},{96,112},{112,96},{1... | collective-permute-start | bytes 196616 | tf_op jit(solution)/shard_map/ppermute | solution.py:284
  38.9 3.3 %collective-permute-start.9 = (bf16[4,2,64,128]{3,2,1,0:T(8,128)(2,1)S(1)}, bf16[4,2,64,128]{3,2,1,0:T(8,128)(2,1)S(1)}, u32[]{:S(2)}, u32[]{:S(2)}) collective-permute-start(bf16[4,2,64,128]{3,2,1,0:T(8,128)(2,1)S(1)} %dynamic-slice_bitcast_fusion), channel_id=1, source_target_pairs={{0,16},{16,0},{32,48},{48,32},{64,80},{80,64},{96,112},{112,96},{1... | collective-permute-start | bytes 393224 | tf_op jit(solution)/shard_map/ppermute | solution.py:298
  42.7 5.6 %collective-permute-start.10 = (f32[16,640]{1,0:T(8,128)S(1)}, f32[16,640]{1,0:T(8,128)S(1)}, u32[]{:S(2)}, u32[]{:S(2)}) collective-permute-start(f32[16,640]{1,0:T(8,128)S(1)} %get-tuple-element.16), channel_id=1, source_target_pairs={{0,8},{1,9},{2,10},{3,11},{4,12},{5,13},{6,14},{7,15},{8,0},{9,1},... | collective-permute-start | bytes 122888 | tf_op jit(solution)/shard_map/ppermute | solution.py:300
  46.1 5.2 %collective-permute-start.11 = (f32[16,640]{1,0:T(8,128)S(1)}, f32[16,640]{1,0:T(8,128)S(1)}, u32[]{:S(2)}, u32[]{:S(2)}) collective-permute-start(f32[16,640]{1,0:T(8,128)S(1)} %get-tuple-element.17), channel_id=1, source_target_pairs={{0,12},{1,13},{2,14},{3,15},{4,8},{5,9},{6,10},{7,11},{8,4},{9,5},... | collective-permute-start | bytes 122888 | tf_op jit(solution)/shard_map/ppermute | solution.py:300
  47.3 4.0 %copy-start.4 = (f32[16]{0:T(128)S(1)}, f32[16]{0:T(128)}, u32[]{:S(2)}) copy-start(f32[16]{0:T(128)} %param.9) | copy-start | bytes 196
  47.3 4.0 %collective-permute-start.12 = (f32[16,640]{1,0:T(8,128)S(1)}, f32[16,640]{1,0:T(8,128)S(1)}, u32[]{:S(2)}, u32[]{:S(2)}) collective-permute-start(f32[16,640]{1,0:T(8,128)S(1)} %get-tuple-element.18), channel_id=1, source_target_pairs={{0,4},{1,5},{2,6},{3,7},{4,0},{5,1},{6,2},{7,3},{8,12},{9,13},{10,... | collective-permute-start | bytes 122888 | tf_op jit(solution)/shard_map/ppermute | solution.py:300

commit v23 on v22

--- a/solution.py
+++ b/solution.py
@@ -179,7 +179,8 @@
         add(start, size, term[64:128] + left + right)
 
 
-def coarse_kernel(both, pair, other, out, cells):
+def coarse_kernel(both, pair, other, bias, out, kept, cells):
+    kept[...] = bias[...]
     pd = lax.rem(lax.axis_index("depth"), 2)
     inner_d = inner("depth")
     for a in range(2):
@@ -196,17 +197,17 @@
     coarse_sums(cells, (2 * pd, 1), pair, other, put)
 
 
-def coarse_level(both, pair, other):
+def coarse_level(both, pair, other, bias):
     vmem = pl.BlockSpec(memory_space=pltpu.VMEM)
     return pl.pallas_call(
         coarse_kernel,
-        out_shape=jax.ShapeDtypeStruct((64, 640), F32),
-        in_specs=[vmem] * 3,
-        out_specs=vmem,
+        out_shape=[jax.ShapeDtypeStruct((64, 640), F32), jax.ShapeDtypeStruct((16, 128), F32)],
+        in_specs=[vmem] * 4,
+        out_specs=[vmem] * 2,
         scratch_shapes=[pltpu.VMEM((2, 12, 64, 128), BF16)],
         compiler_params=pltpu.CompilerParams(vmem_limit_bytes=6 * 1024 * 1024),
         cost_estimate=pl.CostEstimate(flops=150_000_000, bytes_accessed=0, transcendentals=0),
-    )(both, pair, other)
+    )(both, pair, other, bias)
 
 
 def near_kernel(near, sums, pair, other, o0, o1, o2, o3, cells):
@@ -296,9 +297,12 @@
         pooled, ("depth", "rows"), 0, 0, axis_index_groups=far_and_z(), tiled=True
     ).reshape(2, 4, 2, 64, 128)
     near = lax.ppermute(lax.dynamic_index_in_dim(both, 1 - pd, 0, False), "depth", depth_near)
-    sums = near_level(near, coarse_level(both, pair, other), pair, other)
+    inner_sums, bias = coarse_level(
+        both, pair, other, jnp.broadcast_to(coarse_bias[:, None], (16, 128))
+    )
+    sums = near_level(near, inner_sums, pair, other)
     parts = [sums[0]] + [lax.ppermute(sums[k], "rows", along_y(k)) for k in (2, 3, 1)]
-    result = join(parts, jnp.broadcast_to(coarse_bias[:, None], (16, 128)))
+    result = join(parts, bias)
     return result.reshape(16, 1, 2048)
 
 

time: 52.3 us -> 52.2 us (level)
  no operation moved by 1% of the time
where the time goes in v23:
time: 52.2 us; the launch traced here: 51.9 us
  starting transfers between devices  28.7 us (55%)
  blocking collectives  13.7 us (26%)
  waiting for transfers between devices  4.91 us (9%)
  Pallas kernels  3.28 us (6%)
  local copies, waits for them, and re-layouts  1.2 us (2%)
    all_to_all x1, blocking collectives, body(): lax.all_to_all(pooled, ('depth', 'rows'), 0, 0, axis_index_groups=far_and...  13.7 us
    ppermute x1, starting transfers between devices, body(): lax.ppermute(lax.dynamic_index_in_dim(volume, 1 - pd, 0, False), 'depth',...  7.04 us
    ppermute x3, starting transfers between devices, body(): lax.ppermute(sums[k], 'rows', along_y(k))  4.59 us
    ppermute x3, waiting for transfers between devices, body(): lax.ppermute(sums[k], 'rows', along_y(k))  4.01 us
    ppermute x1, starting transfers between devices, body(): lax.ppermute(lax.dynamic_index_in_dim(volume, 3 - 3 * pr, 1, False), 'row...  3.37 us
    ppermute x1, starting transfers between devices, body(): c1 = lax.ppermute(near_row, 'rows', rows_near)  3.34 us
    ppermute x1, starting transfers between devices, body(): pair = jnp.stack([w, lax.ppermute(w, 'rows', along_y(3))])  3.01 us
    ppermute x1, starting transfers between devices, body(): lax.ppermute(lax.dynamic_index_in_dim(both, 1 - pd, 0, False), 'depth', d...  2.32 us
  transfers between devices with their start and end apart: 13, of which 4 were waited for; matrix products, arithmetic and copies ran while one was open for 0% of the time, Pallas kernels for 4%

profile of v23, /device:TPU:6, one launch (start us, length us, event | category | flops | bytes accessed | tf_op | source)
XLA Modules:
  0.0 51.9 jit_solution(11034103060752229726)
XLA Ops:
  0.0 1.1 %dynamic-slice_bitcast_fusion.1 = (bf16[4,128,128]{2,1,0:T(8,128)(2,1)S(1)}, bf16[4,128,128]{2,1,0:T(8,128)(2,1)S(1)}) fusion(bf16[2,4,128,128]{3,2,1,0:T(8,128)(2,1)} %vol.1, s32[]{:T(128)S(6)} %select_n.19, s32[]{:T(128)S(6)} %select_n.18), kind=kLoop, calls=%fused_computation.6 | loop fusion | bytes 524296 | tf_op jit(solution)/shard_map/jit(dynamic_index_in_dim)/squeeze | solution.py:277
  1.1 2.2 %collective-permute-start = (bf16[4,128,128]{2,1,0:T(8,128)(2,1)S(1)}, bf16[4,128,128]{2,1,0:T(8,128)(2,1)S(1)}, u32[]{:S(2)}, u32[]{:S(2)}) collective-permute-start(bf16[4,128,128]{2,1,0:T(8,128)(2,1)S(1)} %get-tuple-element.28), channel_id=1, source_target_pairs={{0,0},{16,32},{32,16},{48,64},{64,48},{80,96},{96,80},{112,128},{1... | collective-permute-start | bytes 393224 | tf_op jit(solution)/shard_map/ppermute | solution.py:276
  3.3 7.0 %collective-permute-start.1 = (bf16[4,128,128]{2,1,0:T(8,128)(2,1)S(1)}, bf16[4,128,128]{2,1,0:T(8,128)(2,1)S(1)}, u32[]{:S(2)}, u32[]{:S(2)}) collective-permute-start(bf16[4,128,128]{2,1,0:T(8,128)(2,1)S(1)} %get-tuple-element.27), channel_id=1, source_target_pairs={{0,16},{16,0},{32,48},{48,32},{64,80},{80,64},{96,112},{112,96},{1... | collective-permute-start | bytes 393224 | tf_op jit(solution)/shard_map/ppermute | solution.py:277
  10.3 3.0 %collective-permute-start.7 = (bf16[27,16,128]{2,1,0:T(8,128)(2,1)S(1)}, bf16[27,16,128]{2,1,0:T(8,128)(2,1)S(1)}, u32[]{:S(2)}, u32[]{:S(2)}) collective-permute-start(bf16[27,16,128]{2,1,0:T(8,128)(2,1)S(1)} %bitcast.28), channel_id=1, source_target_pairs={{0,12},{1,13},{2,14},{3,15},{4,8},{5,9},{6,10},{7,11},{8,4},{9,5},... | collective-permute-start | bytes 331784 | tf_op jit(solution)/shard_map/ppermute | solution.py:291
  13.4 0.7 %collective-permute-start.2 = (bf16[2,128,128]{2,1,0:T(8,128)(2,1)S(1)}, bf16[2,128,128]{2,1,0:T(8,128)(2,1)S(1)}, u32[]{:S(2)}, u32[]{:S(2)}) collective-permute-start(bf16[2,128,128]{2,1,0:T(8,128)(2,1)S(1)} %get-tuple-element.26), channel_id=1, source_target_pairs={{0,0},{1,2},{2,1},{3,4},{4,3},{5,6},{6,5},{7,8},{8,7},{9,10},{10,9... | collective-permute-start | bytes 196616 | tf_op jit(solution)/shard_map/ppermute | solution.py:278
  14.0 3.4 %collective-permute-start.3 = (bf16[2,128,128]{2,1,0:T(8,128)(2,1)S(1)}, bf16[2,128,128]{2,1,0:T(8,128)(2,1)S(1)}, u32[]{:S(2)}, u32[]{:S(2)}) collective-permute-start(bf16[2,128,128]{2,1,0:T(8,128)(2,1)S(1)} %get-tuple-element.25), channel_id=1, source_target_pairs={{0,1},{1,0},{2,3},{3,2},{4,5},{5,4},{6,7},{7,6},{8,9},{9,8},{10,11... | collective-permute-start | bytes 196616 | tf_op jit(solution)/shard_map/ppermute | solution.py:279
  17.4 1.5 %collective-permute-start.8 = (bf16[2,27,16,128]{3,2,1,0:T(8,128)(2,1)S(1)}, bf16[2,27,16,128]{3,2,1,0:T(8,128)(2,1)S(1)}, u32[]{:S(2)}, u32[]{:S(2)}) collective-permute-start(bf16[2,27,16,128]{3,2,1,0:T(8,128)(2,1)S(1)} %pad_maximum_fusion.pair), channel_id=1, source_target_pairs={{0,4},{1,5},{2,6},{3,7},{4,0},{5,1},{6,2},{7,3},{8,12},{9,13},{10,... | collective-permute-start | bytes 663560 | tf_op jit(solution)/shard_map/ppermute | solution.py:292
  18.9 0.7 %collective-permute-start.4 = (bf16[128,128]{1,0:T(8,128)(2,1)S(1)}, bf16[128,128]{1,0:T(8,128)(2,1)S(1)}, u32[]{:S(2)}, u32[]{:S(2)}) collective-permute-start(bf16[128,128]{1,0:T(8,128)(2,1)S(1)} %get-tuple-element.24.far_row), channel_id=1, source_target_pairs={{0,0},{1,2},{2,1},{3,4},{4,3},{5,6},{6,5},{7,8},{8,7},{9,10},{10,9... | collective-permute-start | bytes 98312 | tf_op jit(solution)/shard_map/ppermute | solution.py:283
  19.6 3.3 %collective-permute-start.5 = (bf16[128,128]{1,0:T(8,128)(2,1)S(1)}, bf16[128,128]{1,0:T(8,128)(2,1)S(1)}, u32[]{:S(2)}, u32[]{:S(2)}) collective-permute-start(bf16[128,128]{1,0:T(8,128)(2,1)S(1)} %get-tuple-element.23.near_row), channel_id=1, source_target_pairs={{0,1},{1,0},{2,3},{3,2},{4,5},{5,4},{6,7},{7,6},{8,9},{9,8},{10,11... | collective-permute-start | bytes 98312 | tf_op jit(solution)/shard_map/ppermute | solution.py:284
  23.0 0.1 collective-permute-start.6
  23.1 1.3 %shard_map.55 = (f32[2,2,128,128]{3,2,1,0:T(8,128)S(1)}, f32[2,128,128]{2,1,0:T(8,128)S(1)}, bf16[2,2,128,384]{3,2,1,0:T(8,128)(2,1)S(1)}) custom-call(bf16[2,4,128,128]{3,2,1,0:T(8,128)(2,1)S(1)} %copy-done, bf16[4,128,128]{2,1,0:T(8,128)(2,1)S(1)} %collective-permute-done.x2, bf16[4,128,128]{2,1,0:T(8,128)(2,1)S(1)} %collective-permute-done.1.x1, ...), custom_call_target="tpu_custom_call" | custom-call | flops 20000000000 | tf_op jit(solution)/shard_map/pallas_call | solution.py:87
  24.4 0.6 %collective-permute-done.5.c1 = bf16[128,128]{1,0:T(8,128)(2,1)S(1)} collective-permute-done((bf16[128,128]{1,0:T(8,128)(2,1)S(1)}, bf16[128,128]{1,0:T(8,128)(2,1)S(1)}, u32[]{:S(2)}, u32[]{:S(2)}) %collective-permute-start.5) | collective-permute-done | bytes 32800 | tf_op jit(solution)/shard_map/ppermute | solution.py:284
  25.0 0.3 shard_map.57
  25.3 13.7 %all_to_all.5 = bf16[8,2,64,128]{3,2,1,0:T(8,128)(2,1)S(1)} all-to-all(bf16[8,2,64,128]{3,2,1,0:T(8,128)(2,1)S(1)} %shard_map.57), channel_id=1, replica_groups={{16,17,18,19,32,33,34,35},{20,21,22,23,36,37,38,39},{24,25,26,27,40,41,..., dimensions={0} | all-to-all | bytes 524288 | tf_op jit(solution)/shard_map/all_to_all | solution.py:296
  38.9 2.3 %collective-permute-start.9 = (bf16[4,2,64,128]{3,2,1,0:T(8,128)(2,1)S(1)}, bf16[4,2,64,128]{3,2,1,0:T(8,128)(2,1)S(1)}, u32[]{:S(2)}, u32[]{:S(2)}) collective-permute-start(bf16[4,2,64,128]{3,2,1,0:T(8,128)(2,1)S(1)} %dynamic-slice_bitcast_fusion), channel_id=1, source_target_pairs={{0,16},{16,0},{32,48},{48,32},{64,80},{80,64},{96,112},{112,96},{1... | collective-permute-start | bytes 393224 | tf_op jit(solution)/shard_map/ppermute | solution.py:299
  41.3 0.1 broadcast_in_dim.10.bias
  41.3 0.6 %shard_map.58 = (f32[64,640]{1,0:T(8,128)S(1)}, f32[16,128]{1,0:T(8,128)S(1)}) custom-call(bf16[2,4,2,64,128]{4,3,2,1,0:T(8,128)(2,1)S(1)} %bitcast.25, bf16[2,27,16,128]{3,2,1,0:T(8,128)(2,1)S(1)} %pad_maximum_fusion.pair, bf16[2,27,16,128]{3,2,1,0:T(8,128)(2,1)S(1)} %collective-permute-done.8.other, f32[16,128]{1,0:T(8,128)S(1)} %broadcast_in_dim.10.bias), custom_call_target="tpu_custom_call" | custom-call | flops 150000000 | tf_op jit(solution)/shard_map/pallas_call | solution.py:202
  41.9 0.3 collective-permute-done.9.near
  42.2 0.4 shard_map.59
  42.7 3.4 %collective-permute-start.10 = (f32[16,640]{1,0:T(8,128)S(1)}, f32[16,640]{1,0:T(8,128)S(1)}, u32[]{:S(2)}, u32[]{:S(2)}) collective-permute-start(f32[16,640]{1,0:T(8,128)S(1)} %get-tuple-element.19), channel_id=1, source_target_pairs={{0,8},{1,9},{2,10},{3,11},{4,12},{5,13},{6,14},{7,15},{8,0},{9,1},... | collective-permute-start | bytes 122888 | tf_op jit(solution)/shard_map/ppermute | solution.py:304
  46.1 1.2 %collective-permute-start.11 = (f32[16,640]{1,0:T(8,128)S(1)}, f32[16,640]{1,0:T(8,128)S(1)}, u32[]{:S(2)}, u32[]{:S(2)}) collective-permute-start(f32[16,640]{1,0:T(8,128)S(1)} %get-tuple-element.20), channel_id=1, source_target_pairs={{0,12},{1,13},{2,14},{3,15},{4,8},{5,9},{6,10},{7,11},{8,4},{9,5},... | collective-permute-start | bytes 122888 | tf_op jit(solution)/shard_map/ppermute | solution.py:304
  47.3 1.0 %collective-permute-done.10.s2 = f32[16,640]{1,0:T(8,128)S(1)} collective-permute-done((f32[16,640]{1,0:T(8,128)S(1)}, f32[16,640]{1,0:T(8,128)S(1)}, u32[]{:S(2)}, u32[]{:S(2)}) %collective-permute-start.10) | collective-permute-done | bytes 40992 | tf_op jit(solution)/shard_map/ppermute | solution.py:304
  48.3 3.0 %collective-permute-done.11.s3 = f32[16,640]{1,0:T(8,128)S(1)} collective-permute-done((f32[16,640]{1,0:T(8,128)S(1)}, f32[16,640]{1,0:T(8,128)S(1)}, u32[]{:S(2)}, u32[]{:S(2)}) %collective-permute-start.11) | collective-permute-done | bytes 40992 | tf_op jit(solution)/shard_map/ppermute | solution.py:304
  51.3 0.7 %shard_map.60 = bf16[16,2048]{1,0:T(8,128)(2,1)} custom-call(f32[16,640]{1,0:T(8,128)S(1)} %get-tuple-element.18.s0, f32[16,640]{1,0:T(8,128)S(1)} %collective-permute-done.10.s2, f32[16,640]{1,0:T(8,128)S(1)} %collective-permute-done.11.s3, f32[16,640]{1,0:T(8,128)S(1)} %collective-permute-done.12.s1, f32[16,128]{1,0:T(8,128)S(1)} %get-tuple-element.22.bias), custom_call_target="tpu_custom_call" | custom-call | tf_op jit(solution)/shard_map/pallas_call | solution.py:258
  (26 shorter events, 0.1 us)
Async XLA Ops:
  0.0 10.3 %copy-start.2 = (bf16[3,3,3,128,16]{3,4,2,1,0:T(8,128)(2,1)S(1)}, bf16[3,3,3,128,16]{3,4,2,1,0:T(8,128)(2,1)}, u32[]{:S(2)}) copy-start(bf16[3,3,3,128,16]{3,4,2,1,0:T(8,128)(2,1)} %param.8) | copy-start | bytes 331780
  0.0 13.3 %copy-start = (bf16[2,4,128,128]{3,2,1,0:T(8,128)(2,1)S(1)}, bf16[2,4,128,128]{3,2,1,0:T(8,128)(2,1)}, u32[]{:S(2)}) copy-start(bf16[2,4,128,128]{3,2,1,0:T(8,128)(2,1)} %vol.1) | copy-start | bytes 786436
  0.0 23.1 %copy-start.1 = (bf16[3,3,3,128,128]{4,3,2,1,0:T(8,128)(2,1)S(1)}, bf16[3,3,3,128,128]{4,3,2,1,0:T(8,128)(2,1)}, u32[]{:S(2)}) copy-start(bf16[3,3,3,128,128]{4,3,2,1,0:T(8,128)(2,1)} %w.1) | copy-start | bytes 2654212
  1.1 17.8 %collective-permute-start = (bf16[4,128,128]{2,1,0:T(8,128)(2,1)S(1)}, bf16[4,128,128]{2,1,0:T(8,128)(2,1)S(1)}, u32[]{:S(2)}, u32[]{:S(2)}) collective-permute-start(bf16[4,128,128]{2,1,0:T(8,128)(2,1)S(1)} %get-tuple-element.28), channel_id=1, source_target_pairs={{0,0},{16,32},{32,16},{48,64},{64,48},{80,96},{96,80},{112,128},{1... | collective-permute-start | bytes 393224 | tf_op jit(solution)/shard_map/ppermute | solution.py:276
  3.3 15.6 %collective-permute-start.1 = (bf16[4,128,128]{2,1,0:T(8,128)(2,1)S(1)}, bf16[4,128,128]{2,1,0:T(8,128)(2,1)S(1)}, u32[]{:S(2)}, u32[]{:S(2)}) collective-permute-start(bf16[4,128,128]{2,1,0:T(8,128)(2,1)S(1)} %get-tuple-element.27), channel_id=1, source_target_pairs={{0,16},{16,0},{32,48},{48,32},{64,80},{80,64},{96,112},{112,96},{1... | collective-permute-start | bytes 393224 | tf_op jit(solution)/shard_map/ppermute | solution.py:277
  10.3 7.1 %collective-permute-start.7 = (bf16[27,16,128]{2,1,0:T(8,128)(2,1)S(1)}, bf16[27,16,128]{2,1,0:T(8,128)(2,1)S(1)}, u32[]{:S(2)}, u32[]{:S(2)}) collective-permute-start(bf16[27,16,128]{2,1,0:T(8,128)(2,1)S(1)} %bitcast.28), channel_id=1, source_target_pairs={{0,12},{1,13},{2,14},{3,15},{4,8},{5,9},{6,10},{7,11},{8,4},{9,5},... | collective-permute-start | bytes 331784 | tf_op jit(solution)/shard_map/ppermute | solution.py:291
  13.4 9.6 %collective-permute-start.2 = (bf16[2,128,128]{2,1,0:T(8,128)(2,1)S(1)}, bf16[2,128,128]{2,1,0:T(8,128)(2,1)S(1)}, u32[]{:S(2)}, u32[]{:S(2)}) collective-permute-start(bf16[2,128,128]{2,1,0:T(8,128)(2,1)S(1)} %get-tuple-element.26), channel_id=1, source_target_pairs={{0,0},{1,2},{2,1},{3,4},{4,3},{5,6},{6,5},{7,8},{8,7},{9,10},{10,9... | collective-permute-start | bytes 196616 | tf_op jit(solution)/shard_map/ppermute | solution.py:278
  14.0 8.9 %collective-permute-start.3 = (bf16[2,128,128]{2,1,0:T(8,128)(2,1)S(1)}, bf16[2,128,128]{2,1,0:T(8,128)(2,1)S(1)}, u32[]{:S(2)}, u32[]{:S(2)}) collective-permute-start(bf16[2,128,128]{2,1,0:T(8,128)(2,1)S(1)} %get-tuple-element.25), channel_id=1, source_target_pairs={{0,1},{1,0},{2,3},{3,2},{4,5},{5,4},{6,7},{7,6},{8,9},{9,8},{10,11... | collective-permute-start | bytes 196616 | tf_op jit(solution)/shard_map/ppermute | solution.py:279
  17.4 7.5 %collective-permute-start.8 = (bf16[2,27,16,128]{3,2,1,0:T(8,128)(2,1)S(1)}, bf16[2,27,16,128]{3,2,1,0:T(8,128)(2,1)S(1)}, u32[]{:S(2)}, u32[]{:S(2)}) collective-permute-start(bf16[2,27,16,128]{3,2,1,0:T(8,128)(2,1)S(1)} %pad_maximum_fusion.pair), channel_id=1, source_target_pairs={{0,4},{1,5},{2,6},{3,7},{4,0},{5,1},{6,2},{7,3},{8,12},{9,13},{10,... | collective-permute-start | bytes 663560 | tf_op jit(solution)/shard_map/ppermute | solution.py:292
  18.9 5.5 %collective-permute-start.4 = (bf16[128,128]{1,0:T(8,128)(2,1)S(1)}, bf16[128,128]{1,0:T(8,128)(2,1)S(1)}, u32[]{:S(2)}, u32[]{:S(2)}) collective-permute-start(bf16[128,128]{1,0:T(8,128)(2,1)S(1)} %get-tuple-element.24.far_row), channel_id=1, source_target_pairs={{0,0},{1,2},{2,1},{3,4},{4,3},{5,6},{6,5},{7,8},{8,7},{9,10},{10,9... | collective-permute-start | bytes 98312 | tf_op jit(solution)/shard_map/ppermute | solution.py:283
  19.6 3.5 %copy-start.3 = (f32[128]{0:T(128)S(1)}, f32[128]{0:T(128)}, u32[]{:S(2)}) copy-start(f32[128]{0:T(128)} %param.7) | copy-start | bytes 1540
  19.6 5.4 %collective-permute-start.5 = (bf16[128,128]{1,0:T(8,128)(2,1)S(1)}, bf16[128,128]{1,0:T(8,128)(2,1)S(1)}, u32[]{:S(2)}, u32[]{:S(2)}) collective-permute-start(bf16[128,128]{1,0:T(8,128)(2,1)S(1)} %get-tuple-element.23.near_row), channel_id=1, source_target_pairs={{0,1},{1,0},{2,3},{3,2},{4,5},{5,4},{6,7},{7,6},{8,9},{9,8},{10,11... | collective-permute-start | bytes 98312 | tf_op jit(solution)/shard_map/ppermute | solution.py:284
  23.0 2.0 %collective-permute-start.6 = (bf16[2,128,128]{2,1,0:T(8,128)(2,1)S(1)}, bf16[2,128,128]{2,1,0:T(8,128)(2,1)S(1)}, u32[]{:S(2)}, u32[]{:S(2)}) collective-permute-start(bf16[2,128,128]{2,1,0:T(8,128)(2,1)S(1)} %shard_map.56), channel_id=1, source_target_pairs={{0,16},{16,0},{32,48},{48,32},{64,80},{80,64},{96,112},{112,96},{1... | collective-permute-start | bytes 196616 | tf_op jit(solution)/shard_map/ppermute | solution.py:285
  38.9 2.3 %copy-start.4 = (f32[16]{0:T(128)S(1)}, f32[16]{0:T(128)}, u32[]{:S(2)}) copy-start(f32[16]{0:T(128)} %param.9) | copy-start | bytes 196
  38.9 3.3 %collective-permute-start.9 = (bf16[4,2,64,128]{3,2,1,0:T(8,128)(2,1)S(1)}, bf16[4,2,64,128]{3,2,1,0:T(8,128)(2,1)S(1)}, u32[]{:S(2)}, u32[]{:S(2)}) collective-permute-start(bf16[4,2,64,128]{3,2,1,0:T(8,128)(2,1)S(1)} %dynamic-slice_bitcast_fusion), channel_id=1, source_target_pairs={{0,16},{16,0},{32,48},{48,32},{64,80},{80,64},{96,112},{112,96},{1... | collective-permute-start | bytes 393224 | tf_op jit(solution)/shard_map/ppermute | solution.py:299
  42.7 5.6 %collective-permute-start.10 = (f32[16,640]{1,0:T(8,128)S(1)}, f32[16,640]{1,0:T(8,128)S(1)}, u32[]{:S(2)}, u32[]{:S(2)}) collective-permute-start(f32[16,640]{1,0:T(8,128)S(1)} %get-tuple-element.19), channel_id=1, source_target_pairs={{0,8},{1,9},{2,10},{3,11},{4,12},{5,13},{6,14},{7,15},{8,0},{9,1},... | collective-permute-start | bytes 122888 | tf_op jit(solution)/shard_map/ppermute | solution.py:304
  46.1 5.2 %collective-permute-start.11 = (f32[16,640]{1,0:T(8,128)S(1)}, f32[16,640]{1,0:T(8,128)S(1)}, u32[]{:S(2)}, u32[]{:S(2)}) collective-permute-start(f32[16,640]{1,0:T(8,128)S(1)} %get-tuple-element.20), channel_id=1, source_target_pairs={{0,12},{1,13},{2,14},{3,15},{4,8},{5,9},{6,10},{7,11},{8,4},{9,5},... | collective-permute-start | bytes 122888 | tf_op jit(solution)/shard_map/ppermute | solution.py:304
  47.3 4.0 %collective-permute-start.12 = (f32[16,640]{1,0:T(8,128)S(1)}, f32[16,640]{1,0:T(8,128)S(1)}, u32[]{:S(2)}, u32[]{:S(2)}) collective-permute-start(f32[16,640]{1,0:T(8,128)S(1)} %get-tuple-element.21), channel_id=1, source_target_pairs={{0,4},{1,5},{2,6},{3,7},{4,0},{5,1},{6,2},{7,3},{8,12},{9,13},{10,... | collective-permute-start | bytes 122888 | tf_op jit(solution)/shard_map/ppermute | solution.py:304
